TPU v7x, 32 devices: a whole 2x2x4 slice. The times are simulated.
32 devices in a mesh: groups: 2 (over x), blk: 16 (over z, y, core).
Axes of the slice: x: 2, y: 2, z: 4, core: 2. Of those that a mesh axis runs over, the one named last changes fastest.
Arguments:
- embeddings: bfloat16 [32768, 1024], P(('groups', 'blk')), parts along dimension 0
- order: int32 [32768], P(('groups', 'blk')), parts along dimension 0, may hold values from 0 to 1023, as said below
- pad_counts: int32 [32], P('groups'), parts along dimension 0, may hold values from 0 to 256
Outputs:
- max_sim: float32 [32768], P(('groups', 'blk')), parts along dimension 0
There are 2 independent parts, one for each index of `groups`. A program takes and returns all parts, laid end to end along the dimension named above; each array names one. Nothing has to cross between parts.
Inputs may be any that keep to these rules, and one draw needn't show every extreme that they name: `order`: each aligned block of 1024 entries is a permutation of 0 .. 1023.
All inputs are finite; a program needn't handle non-finite values.
Results may differ from a plain program's by a relative error of at most 0.00066.
Values may be sent and summed in bfloat16 or wider, within the bound.
No kernel may reach another device: no remote copies, remote signals or barrier semaphores. Data moves between devices by JAX's collectives and lax.ppermute only.
A program may use at most 64 MiB of HBM per device.

v0:
```python
import jax
import jax.numpy as jnp
from jax import lax
from jax.sharding import PartitionSpec as P

STEPS = 6


def passed_along(value, axis, by):
    devices = lax.axis_size(axis)
    return lax.ppermute(value, axis, [(i, (i + by) % devices) for i in range(devices)])


def tile_maxima(own, own_valid, other, other_valid, diagonal):
    scores = lax.dot_general(
        own, other, (((1,), (1,)), ((), ())), preferred_element_type=jnp.float32
    )
    keep = own_valid[:, None] & other_valid[None, :]
    if diagonal:
        count = own.shape[0]
        keep = keep & (jnp.arange(count)[:, None] != jnp.arange(count)[None, :])
    scores = jnp.where(keep, scores, jnp.float32(-2.0))
    return (jnp.max(scores, axis=1), jnp.max(scores, axis=0))


def local(embeddings, order, pad_counts):
    rows = embeddings.shape[0]
    ordered = jnp.take(embeddings, order, axis=0).astype(jnp.float32)
    unit = (ordered * lax.rsqrt(jnp.sum(ordered * ordered, axis=1, keepdims=True) + 1e-06)).astype(
        jnp.bfloat16
    )
    nblocks = lax.axis_size("blk")
    here = lax.axis_index("blk")
    positions = jnp.arange(rows, dtype=jnp.int32)

    def valid_of(offset):
        index = (here + offset) % nblocks
        return positions < rows - pad_counts[index]

    own_valid = valid_of(0)
    rowbest, unused = tile_maxima(unit, own_valid, unit, own_valid, True)
    colbest = jnp.full((rows,), -2.0, jnp.float32)
    chains = list(range(1, STEPS + 1))
    visitor = unit
    previous = 0
    for offset in chains:
        visitor = passed_along(visitor, "blk", previous - offset)
        rowpart, colpart = tile_maxima(unit, own_valid, visitor, valid_of(offset), False)
        rowbest = jnp.maximum(rowbest, rowpart)
        colbest = jnp.maximum(colbest, passed_along(colpart, "blk", offset))
        previous = offset
    return jnp.where(own_valid, jnp.maximum(rowbest, colbest), jnp.float32(0.0))


def solution(mesh):
    in_specs = (P(("groups", "blk"), None), P(("groups", "blk")), P("groups"))
    out_specs = P(("groups", "blk"))
    return jax.shard_map(local, mesh=mesh, in_specs=in_specs, out_specs=out_specs, check_vma=False)
```

profile of v0, /device:TPU:0, one launch (start us, length us, event | category | flops | bytes accessed | tf_op | source)
XLA Modules:
  0.0 207.1 jit_solution(15465330399465840089)
XLA Ops:
  1.6 5.4 %gather_fusion = bf16[1024,1024]{1,0:T(8,128)(2,1)} fusion(bf16[1024,1024]{1,0:T(8,128)(2,1)S(1)} %copy-done, s32[1024]{0:T(1024)S(1)} %fusion.15), kind=kCustom, calls=%fused_computation | custom fusion | bytes 4198400 | tf_op jit(solution)/shard_map/jit(_take)/gather | solution.py:28
  7.0 2.5 %fusion = f32[1024]{0:T(1024)S(1)} fusion(bf16[1024,1024]{1,0:T(8,128)(2,1)} %gather_fusion, pred[1024]{0:T(1024)(128)(4,1)S(1)} %compare_and_fusion), kind=kLoop, calls=%fused_computation.3 | loop fusion | flops 4193280 | bytes 2102272 | tf_op jit(solution)/shard_map/reduce_sum | solution.py:29
  11.4 5.4 %collective-permute-start = (bf16[1024,1024]{1,0:T(8,128)(2,1)S(1)}, bf16[1024,1024]{1,0:T(8,128)(2,1)S(1)}, u32[]{:S(2)}, u32[]{:S(2)}) collective-permute-start(bf16[1024,1024]{1,0:T(8,128)(2,1)S(1)} %fusion.1), channel_id=1, source_target_pairs={{0,15},{1,0},{2,1},{3,2},{4,3},{5,4},{6,5},{7,6},{8,7},{9,8},{10,9... | collective-permute-start | bytes 6291464 | tf_op jit(solution)/shard_map/ppermute | solution.py:11
  16.8 23.6 %collective-permute-done = bf16[1024,1024]{1,0:T(8,128)(2,1)S(1)} collective-permute-done((bf16[1024,1024]{1,0:T(8,128)(2,1)S(1)}, bf16[1024,1024]{1,0:T(8,128)(2,1)S(1)}, u32[]{:S(2)}, u32[]{:S(2)}) %collective-permute-start) | collective-permute-done | bytes 2097184 | tf_op jit(solution)/shard_map/ppermute | solution.py:11
  40.4 4.6 %collective-permute-start.1 = (bf16[1024,1024]{1,0:T(8,128)(2,1)S(1)}, bf16[1024,1024]{1,0:T(8,128)(2,1)S(1)}, u32[]{:S(2)}, u32[]{:S(2)}) collective-permute-start(bf16[1024,1024]{1,0:T(8,128)(2,1)S(1)} %collective-permute-done), channel_id=1, source_target_pairs={{0,15},{1,0},{2,1},{3,2},{4,3},{5,4},{6,5},{7,6},{8,7},{9,8},{10,9... | collective-permute-start | bytes 6291464 | tf_op jit(solution)/shard_map/ppermute | solution.py:11
  45.0 23.6 %collective-permute-done.1 = bf16[1024,1024]{1,0:T(8,128)(2,1)S(1)} collective-permute-done((bf16[1024,1024]{1,0:T(8,128)(2,1)S(1)}, bf16[1024,1024]{1,0:T(8,128)(2,1)S(1)}, u32[]{:S(2)}, u32[]{:S(2)}) %collective-permute-start.1) | collective-permute-done | bytes 2097184 | tf_op jit(solution)/shard_map/ppermute | solution.py:11
  70.0 4.6 %collective-permute-start.2 = (bf16[1024,1024]{1,0:T(8,128)(2,1)S(1)}, bf16[1024,1024]{1,0:T(8,128)(2,1)S(1)}, u32[]{:S(2)}, u32[]{:S(2)}) collective-permute-start(bf16[1024,1024]{1,0:T(8,128)(2,1)S(1)} %collective-permute-done.1), channel_id=1, source_target_pairs={{0,15},{1,0},{2,1},{3,2},{4,3},{5,4},{6,5},{7,6},{8,7},{9,8},{10,9... | collective-permute-start | bytes 6291464 | tf_op jit(solution)/shard_map/ppermute | solution.py:11
  74.6 23.6 %collective-permute-done.2 = bf16[1024,1024]{1,0:T(8,128)(2,1)S(1)} collective-permute-done((bf16[1024,1024]{1,0:T(8,128)(2,1)S(1)}, bf16[1024,1024]{1,0:T(8,128)(2,1)S(1)}, u32[]{:S(2)}, u32[]{:S(2)}) %collective-permute-start.2) | collective-permute-done | bytes 2097184 | tf_op jit(solution)/shard_map/ppermute | solution.py:11
  98.1 4.6 %collective-permute-start.3 = (bf16[1024,1024]{1,0:T(8,128)(2,1)S(1)}, bf16[1024,1024]{1,0:T(8,128)(2,1)}, u32[]{:S(2)}, u32[]{:S(2)}) collective-permute-start(bf16[1024,1024]{1,0:T(8,128)(2,1)S(1)} %collective-permute-done.2), channel_id=1, source_target_pairs={{0,15},{1,0},{2,1},{3,2},{4,3},{5,4},{6,5},{7,6},{8,7},{9,8},{10,9... | collective-permute-start | bytes 6291464 | tf_op jit(solution)/shard_map/ppermute | solution.py:11
  102.7 23.6 %collective-permute-done.3 = bf16[1024,1024]{1,0:T(8,128)(2,1)} collective-permute-done((bf16[1024,1024]{1,0:T(8,128)(2,1)S(1)}, bf16[1024,1024]{1,0:T(8,128)(2,1)}, u32[]{:S(2)}, u32[]{:S(2)}) %collective-permute-start.3) | collective-permute-done | bytes 2097184 | tf_op jit(solution)/shard_map/ppermute | solution.py:11
  126.3 4.7 %collective-permute-start.4 = (bf16[1024,1024]{1,0:T(8,128)(2,1)}, bf16[1024,1024]{1,0:T(8,128)(2,1)}, u32[]{:S(2)}, u32[]{:S(2)}) collective-permute-start(bf16[1024,1024]{1,0:T(8,128)(2,1)} %collective-permute-done.3), channel_id=1, source_target_pairs={{0,15},{1,0},{2,1},{3,2},{4,3},{5,4},{6,5},{7,6},{8,7},{9,8},{10,9... | collective-permute-start | bytes 6291464 | tf_op jit(solution)/shard_map/ppermute | solution.py:11
  136.1 4.7 %fusion.17 = f32[1024,1024]{0,1:T(8,128)S(1)} fusion(bf16[1024,1024]{1,0:T(8,128)(2,1)} %copy-done.2, bf16[1024,1024]{1,0:T(8,128)(2,1)} %copy-done.7), kind=kOutput, calls=%fused_computation.40 | convolution fusion | flops 2147483648 | bytes 8388608 | tf_op jit(solution)/shard_map/dot_general | solution.py:15
  140.9 14.0 %collective-permute-done.4 = bf16[1024,1024]{1,0:T(8,128)(2,1)} collective-permute-done((bf16[1024,1024]{1,0:T(8,128)(2,1)}, bf16[1024,1024]{1,0:T(8,128)(2,1)}, u32[]{:S(2)}, u32[]{:S(2)}) %collective-permute-start.4) | collective-permute-done | bytes 2097184 | tf_op jit(solution)/shard_map/ppermute | solution.py:11
  154.9 4.6 %collective-permute-start.5 = (bf16[1024,1024]{1,0:T(8,128)(2,1)}, bf16[1024,1024]{1,0:T(8,128)(2,1)S(1)}, u32[]{:S(2)}, u32[]{:S(2)}) collective-permute-start(bf16[1024,1024]{1,0:T(8,128)(2,1)} %collective-permute-done.4), channel_id=1, source_target_pairs={{0,15},{1,0},{2,1},{3,2},{4,3},{5,4},{6,5},{7,6},{8,7},{9,8},{10,9... | collective-permute-start | bytes 6291464 | tf_op jit(solution)/shard_map/ppermute | solution.py:11
  159.5 2.4 %fusion.18 = f32[1024,1024]{0,1:T(8,128)S(1)} fusion(bf16[1024,1024]{1,0:T(8,128)(2,1)S(1)} %copy-done.3, bf16[1024,1024]{1,0:T(8,128)(2,1)S(1)} %copy-done.6), kind=kOutput, calls=%fused_computation.41 | convolution fusion | flops 2147483648 | bytes 8388608 | tf_op jit(solution)/shard_map/dot_general | solution.py:15
  161.8 2.4 %fusion.19 = f32[1024,1024]{0,1:T(8,128)S(1)} fusion(bf16[1024,1024]{1,0:T(8,128)(2,1)S(1)} %copy-done.3, bf16[1024,1024]{1,0:T(8,128)(2,1)S(1)} %copy-done.9), kind=kOutput, calls=%fused_computation.42 | convolution fusion | flops 2147483648 | bytes 8388608 | tf_op jit(solution)/shard_map/dot_general | solution.py:15
  164.2 4.0 %fusion.20 = f32[1024,1024]{0,1:T(8,128)S(1)} fusion(bf16[1024,1024]{1,0:T(8,128)(2,1)S(1)} %copy-done.3, bf16[1024,1024]{1,0:T(8,128)(2,1)} %collective-permute-done.3), kind=kOutput, calls=%fused_computation.43 | convolution fusion | flops 2147483648 | bytes 8388608 | tf_op jit(solution)/shard_map/dot_general | solution.py:15
  168.2 5.9 %fusion.21 = f32[1024,1024]{0,1:T(8,128)} fusion(bf16[1024,1024]{1,0:T(8,128)(2,1)S(1)} %copy-done.3, bf16[1024,1024]{1,0:T(8,128)(2,1)} %collective-permute-done.4), kind=kOutput, calls=%fused_computation.44 | convolution fusion | flops 2147483648 | bytes 8388608 | tf_op jit(solution)/shard_map/dot_general | solution.py:15
  174.1 9.3 %collective-permute-done.5 = bf16[1024,1024]{1,0:T(8,128)(2,1)S(1)} collective-permute-done((bf16[1024,1024]{1,0:T(8,128)(2,1)}, bf16[1024,1024]{1,0:T(8,128)(2,1)S(1)}, u32[]{:S(2)}, u32[]{:S(2)}) %collective-permute-start.5) | collective-permute-done | bytes 2097184 | tf_op jit(solution)/shard_map/ppermute | solution.py:11
  183.3 10.9 %fusion.4 = (f32[1024]{0:T(1024)S(1)}, f32[1024]{0:T(1024)S(1)}, f32[1024]{0:T(1024)S(1)}, f32[1024]{0:T(1024)S(1)}, f32[1024]{0:T(1024)S(1)}, /*index=5*/f32[10...) fusion(f32[1024,1024]{0,1:T(8,128)S(1)} %fusion.17, ...), kind=kOutput, calls=%fused_computation.15 | convolution fusion | flops 2172637184 | bytes 25222144 | tf_op jit(solution)/shard_map/dot_general | solution.py:15
  194.5 5.6 %collective-permute-start.11 = (f32[1024]{0:T(1024)S(1)}, f32[1024]{0:T(1024)S(1)}, u32[]{:S(2)}, u32[]{:S(2)}) collective-permute-start(f32[1024]{0:T(1024)S(1)} %get-tuple-element.23), channel_id=1, source_target_pairs={{0,6},{1,7},{2,8},{3,9},{4,10},{5,11},{6,12},{7,13},{8,14},{9,15},... | collective-permute-start | bytes 12296 | tf_op jit(solution)/shard_map/ppermute | solution.py:11
  200.2 1.4 collective-permute-start.7
  201.6 2.5 %select_reduce_fusion = f32[1024]{0:T(1024)S(1)} fusion(pred[1024]{0:T(1024)(128)(4,1)S(1)} %iota_compare_fusion.7, bf16[1024,1024]{1,0:T(8,128)(2,1)S(1)} %copy-done.3), kind=kOutput, calls=%fused_computation.5 | convolution fusion | flops 2152725504 | bytes 2102272 | tf_op jit(solution)/shard_map/dot_general | solution.py:15
  204.1 2.3 %collective-permute-done.7 = f32[1024]{0:T(1024)S(1)} collective-permute-done((f32[1024]{0:T(1024)S(1)}, f32[1024]{0:T(1024)S(1)}, u32[]{:S(2)}, u32[]{:S(2)}) %collective-permute-start.7) | collective-permute-done | bytes 4128 | tf_op jit(solution)/shard_map/ppermute | solution.py:11
  (39 shorter events, 6.5 us)
Async XLA Ops:
  0.0 1.6 copy-start
  7.0 2.5 %copy-start.1 = (bf16[1024,1024]{1,0:T(8,128)(2,1)S(1)}, bf16[1024,1024]{1,0:T(8,128)(2,1)}, u32[]{:S(2)}) copy-start(bf16[1024,1024]{1,0:T(8,128)(2,1)} %gather_fusion) | copy-start | bytes 6291460
  9.5 121.5 %copy-start.4 = (s32[16]{0:T(128)S(1)}, s32[16]{0:T(128)}, u32[]{:S(2)}) copy-start(s32[16]{0:T(128)} %param.5) | copy-start | bytes 196
  10.1 1.4 copy-start.2
  11.4 29.0 %collective-permute-start = (bf16[1024,1024]{1,0:T(8,128)(2,1)S(1)}, bf16[1024,1024]{1,0:T(8,128)(2,1)S(1)}, u32[]{:S(2)}, u32[]{:S(2)}) collective-permute-start(bf16[1024,1024]{1,0:T(8,128)(2,1)S(1)} %fusion.1), channel_id=1, source_target_pairs={{0,15},{1,0},{2,1},{3,2},{4,3},{5,4},{6,5},{7,6},{8,7},{9,8},{10,9... | collective-permute-start | bytes 6291464 | tf_op jit(solution)/shard_map/ppermute | solution.py:11
  40.4 57.7 %copy-start.7 = (bf16[1024,1024]{1,0:T(8,128)(2,1)}, bf16[1024,1024]{1,0:T(8,128)(2,1)S(1)}, u32[]{:S(2)}) copy-start(bf16[1024,1024]{1,0:T(8,128)(2,1)S(1)} %collective-permute-done) | copy-start | bytes 6291460
  40.4 28.2 %collective-permute-start.1 = (bf16[1024,1024]{1,0:T(8,128)(2,1)S(1)}, bf16[1024,1024]{1,0:T(8,128)(2,1)S(1)}, u32[]{:S(2)}, u32[]{:S(2)}) collective-permute-start(bf16[1024,1024]{1,0:T(8,128)(2,1)S(1)} %collective-permute-done), channel_id=1, source_target_pairs={{0,15},{1,0},{2,1},{3,2},{4,3},{5,4},{6,5},{7,6},{8,7},{9,8},{10,9... | collective-permute-start | bytes 6291464 | tf_op jit(solution)/shard_map/ppermute | solution.py:11
  68.6 1.4 copy-start.5
  70.0 28.2 %collective-permute-start.2 = (bf16[1024,1024]{1,0:T(8,128)(2,1)S(1)}, bf16[1024,1024]{1,0:T(8,128)(2,1)S(1)}, u32[]{:S(2)}, u32[]{:S(2)}) collective-permute-start(bf16[1024,1024]{1,0:T(8,128)(2,1)S(1)} %collective-permute-done.1), channel_id=1, source_target_pairs={{0,15},{1,0},{2,1},{3,2},{4,3},{5,4},{6,5},{7,6},{8,7},{9,8},{10,9... | collective-permute-start | bytes 6291464 | tf_op jit(solution)/shard_map/ppermute | solution.py:11
  98.1 4.6 %copy-start.8 = (bf16[1024,1024]{1,0:T(8,128)(2,1)}, bf16[1024,1024]{1,0:T(8,128)(2,1)S(1)}, u32[]{:S(2)}) copy-start(bf16[1024,1024]{1,0:T(8,128)(2,1)S(1)} %collective-permute-done.2) | copy-start | bytes 6291460
  98.1 28.2 %collective-permute-start.3 = (bf16[1024,1024]{1,0:T(8,128)(2,1)S(1)}, bf16[1024,1024]{1,0:T(8,128)(2,1)}, u32[]{:S(2)}, u32[]{:S(2)}) collective-permute-start(bf16[1024,1024]{1,0:T(8,128)(2,1)S(1)} %collective-permute-done.2), channel_id=1, source_target_pairs={{0,15},{1,0},{2,1},{3,2},{4,3},{5,4},{6,5},{7,6},{8,7},{9,8},{10,9... | collective-permute-start | bytes 6291464 | tf_op jit(solution)/shard_map/ppermute | solution.py:11
  126.3 28.6 %collective-permute-start.4 = (bf16[1024,1024]{1,0:T(8,128)(2,1)}, bf16[1024,1024]{1,0:T(8,128)(2,1)}, u32[]{:S(2)}, u32[]{:S(2)}) collective-permute-start(bf16[1024,1024]{1,0:T(8,128)(2,1)} %collective-permute-done.3), channel_id=1, source_target_pairs={{0,15},{1,0},{2,1},{3,2},{4,3},{5,4},{6,5},{7,6},{8,7},{9,8},{10,9... | collective-permute-start | bytes 6291464 | tf_op jit(solution)/shard_map/ppermute | solution.py:11
  136.1 23.4 %copy-start.3 = (bf16[1024,1024]{1,0:T(8,128)(2,1)S(1)}, bf16[1024,1024]{1,0:T(8,128)(2,1)}, u32[]{:S(2)}) copy-start(bf16[1024,1024]{1,0:T(8,128)(2,1)} %copy-done.2) | copy-start | bytes 6291460
  136.1 23.4 %copy-start.6 = (bf16[1024,1024]{1,0:T(8,128)(2,1)S(1)}, bf16[1024,1024]{1,0:T(8,128)(2,1)}, u32[]{:S(2)}) copy-start(bf16[1024,1024]{1,0:T(8,128)(2,1)} %copy-done.5) | copy-start | bytes 6291460
  140.8 21.0 %copy-start.9 = (bf16[1024,1024]{1,0:T(8,128)(2,1)S(1)}, bf16[1024,1024]{1,0:T(8,128)(2,1)}, u32[]{:S(2)}) copy-start(bf16[1024,1024]{1,0:T(8,128)(2,1)} %copy-done.8) | copy-start | bytes 6291460
  154.9 28.5 %collective-permute-start.5 = (bf16[1024,1024]{1,0:T(8,128)(2,1)}, bf16[1024,1024]{1,0:T(8,128)(2,1)S(1)}, u32[]{:S(2)}, u32[]{:S(2)}) collective-permute-start(bf16[1024,1024]{1,0:T(8,128)(2,1)} %collective-permute-done.4), channel_id=1, source_target_pairs={{0,15},{1,0},{2,1},{3,2},{4,3},{5,4},{6,5},{7,6},{8,7},{9,8},{10,9... | collective-permute-start | bytes 6291464 | tf_op jit(solution)/shard_map/ppermute | solution.py:11
  194.3 5.9 %collective-permute-start.6 = (f32[1024]{0:T(1024)S(1)}, f32[1024]{0:T(1024)S(1)}, u32[]{:S(2)}, u32[]{:S(2)}) collective-permute-start(f32[1024]{0:T(1024)S(1)} %get-tuple-element.6), channel_id=1, source_target_pairs={{0,1},{1,2},{2,3},{3,4},{4,5},{5,6},{6,7},{7,8},{8,9},{9,10},{10,1... | collective-permute-start | bytes 12296 | tf_op jit(solution)/shard_map/ppermute | solution.py:11
  194.3 9.7 %collective-permute-start.8 = (f32[1024]{0:T(1024)S(1)}, f32[1024]{0:T(1024)S(1)}, u32[]{:S(2)}, u32[]{:S(2)}) collective-permute-start(f32[1024]{0:T(1024)S(1)} %get-tuple-element.17), channel_id=1, source_target_pairs={{0,3},{1,4},{2,5},{3,6},{4,7},{5,8},{6,9},{7,10},{8,11},{9,12},{10... | collective-permute-start | bytes 12296 | tf_op jit(solution)/shard_map/ppermute | solution.py:11
  194.4 9.7 %collective-permute-start.9 = (f32[1024]{0:T(1024)S(1)}, f32[1024]{0:T(1024)S(1)}, u32[]{:S(2)}, u32[]{:S(2)}) collective-permute-start(f32[1024]{0:T(1024)S(1)} %get-tuple-element.19), channel_id=1, source_target_pairs={{0,4},{1,5},{2,6},{3,7},{4,8},{5,9},{6,10},{7,11},{8,12},{9,13},{1... | collective-permute-start | bytes 12296 | tf_op jit(solution)/shard_map/ppermute | solution.py:11
  194.5 9.6 %collective-permute-start.10 = (f32[1024]{0:T(1024)S(1)}, f32[1024]{0:T(1024)S(1)}, u32[]{:S(2)}, u32[]{:S(2)}) collective-permute-start(f32[1024]{0:T(1024)S(1)} %get-tuple-element.21), channel_id=1, source_target_pairs={{0,5},{1,6},{2,7},{3,8},{4,9},{5,10},{6,11},{7,12},{8,13},{9,14},{... | collective-permute-start | bytes 12296 | tf_op jit(solution)/shard_map/ppermute | solution.py:11
  194.5 9.6 %collective-permute-start.11 = (f32[1024]{0:T(1024)S(1)}, f32[1024]{0:T(1024)S(1)}, u32[]{:S(2)}, u32[]{:S(2)}) collective-permute-start(f32[1024]{0:T(1024)S(1)} %get-tuple-element.23), channel_id=1, source_target_pairs={{0,6},{1,7},{2,8},{3,9},{4,10},{5,11},{6,12},{7,13},{8,14},{9,15},... | collective-permute-start | bytes 12296 | tf_op jit(solution)/shard_map/ppermute | solution.py:11
  200.2 6.3 %collective-permute-start.7 = (f32[1024]{0:T(1024)S(1)}, f32[1024]{0:T(1024)S(1)}, u32[]{:S(2)}, u32[]{:S(2)}) collective-permute-start(f32[1024]{0:T(1024)S(1)} %get-tuple-element.25), channel_id=1, source_target_pairs={{0,2},{1,3},{2,4},{3,5},{4,6},{5,7},{6,8},{7,9},{8,10},{9,11},{10,... | collective-permute-start | bytes 12296 | tf_op jit(solution)/shard_map/ppermute | solution.py:11
where the time goes:
time: 207 us
  waiting for transfers between devices  120 us (58%)
  starting transfers between devices  35.8 us (17%)
  matrix products  32.8 us (16%)
  local copies, waits for them, and re-layouts  8.86 us (4%)
  other arithmetic  5.22 us (3%)
  between operations  4.58 us (2%)
    ppermute x12, waiting for transfers between devices, passed_along(): lax.ppermute(value, axis, [(i, (i + by) % devices) for i in range(devices)])  120 us
    ppermute x12, starting transfers between devices, passed_along(): lax.ppermute(value, axis, [(i, (i + by) % devices) for i in range(devices)])  35.8 us
    dot_general x7, matrix products, tile_maxima(): lax.dot_general(own, other, (((1,), (1,)), ((), ())), preferred_element_t...  32.8 us
    gather x1, local copies, waits for them, and re-layouts, local(): ordered = jnp.take(embeddings, order, axis=0).astype(jnp.float32)  5.35 us
  transfers between devices with their start and end apart: 12, of which 7 were waited for; matrix products, arithmetic and copies ran while one was open for 11% of the time, Pallas kernels for 0%

commit v1 on v0

v1 whole, which is shorter than its diff:
```python
import functools

import jax
import jax.numpy as jnp
from jax import lax
from jax.experimental import pallas as pl
from jax.experimental.pallas import tpu as pltpu
from jax.sharding import PartitionSpec as P

STEPS = 6
CHUNKS = 4
VMEM = 48 * 2**20


def unit_kernel(first_row, pads, order_smem, order, embeddings, everything, unit, tile, sem):
    rows = order.shape[1]
    count = unit.shape[0]
    valid_count = rows - pads[lax.axis_index("blk")]
    first = order_smem[0]
    base = pl.multiple_of((first // 16) * 16, 16)
    copy = pltpu.make_async_copy(everything.at[pl.ds(base, 16)], tile, sem)
    copy.start()
    position = lax.broadcasted_iota(jnp.int32, (1, rows), 1)
    kept = jnp.where(position < valid_count, order[...], -1)
    row = first_row + lax.broadcasted_iota(jnp.int32, (count, 1), 0)
    valid = jnp.max(jnp.where(kept == row, 1.0, 0.0), axis=1, keepdims=True) > 0.0
    copy.wait()
    among = lax.broadcasted_iota(jnp.int32, (16, 1), 0) == first - base
    filler = jnp.sum(jnp.where(among, tile[...].astype(jnp.float32), 0.0), axis=0, keepdims=True)
    value = jnp.where(valid, embeddings[...].astype(jnp.float32), filler)
    scale = lax.rsqrt(jnp.sum(value * value, axis=1, keepdims=True) + 1e-06)
    unit[...] = (value * scale).astype(jnp.bfloat16)


def unit_chunk(embeddings, order, pad_counts, chunk):
    rows, depth = embeddings.shape
    count = rows // CHUNKS
    return pl.pallas_call(
        functools.partial(unit_kernel, chunk * count),
        out_shape=jax.ShapeDtypeStruct((count, depth), jnp.bfloat16),
        grid=(1,),
        in_specs=[
            pl.BlockSpec(memory_space=pltpu.SMEM),
            pl.BlockSpec(memory_space=pltpu.SMEM),
            pl.BlockSpec((1, rows), lambda i: (0, 0)),
            pl.BlockSpec((count, depth), lambda i: (chunk, 0)),
            pl.BlockSpec(memory_space=pl.ANY),
        ],
        out_specs=pl.BlockSpec((count, depth), lambda i: (0, 0)),
        scratch_shapes=[pltpu.VMEM((16, depth), jnp.bfloat16), pltpu.SemaphoreType.DMA],
        compiler_params=pltpu.CompilerParams(vmem_limit_bytes=VMEM),
        cost_estimate=pl.CostEstimate(
            flops=4 * count * depth, bytes_accessed=4 * count * depth, transcendentals=count
        ),
        name="unit_chunk",
    )(pad_counts, order, order.reshape(1, rows), embeddings, embeddings)


def folded(scores):
    return jnp.max(scores.reshape(-1, 8, scores.shape[1]), axis=0)


def own_kernel(pads, order, *refs):
    units, own, best = refs[:-2], refs[-2], refs[-1]
    rows = order.shape[1]
    count = units[0].shape[0]
    valid_count = rows - pads[lax.axis_index("blk")]
    position = lax.broadcasted_iota(jnp.int32, (1, rows), 1)
    kept = jnp.where(position < valid_count, order[...], -1)
    total = None
    for index, unit in enumerate(units):
        row = index * count + lax.broadcasted_iota(jnp.int32, (count, 1), 0)
        placed = (order[...] == row).astype(jnp.bfloat16)
        part = lax.dot_general(
            unit[...], placed, (((0,), (0,)), ((), ())), preferred_element_type=jnp.float32
        )
        if index == 0:
            total = part
        else:
            total = total + part
    own[...] = total.astype(jnp.bfloat16)
    running = jnp.full((8, rows), -2.0, jnp.float32)
    for index, unit in enumerate(units):
        row = index * count + lax.broadcasted_iota(jnp.int32, (count, 1), 0)
        valid = jnp.max(jnp.where(kept == row, 1.0, 0.0), axis=1, keepdims=True) > 0.0
        scores = jnp.dot(unit[...], own[...], preferred_element_type=jnp.float32)
        scores = jnp.where(valid & (order[...] != row), scores, -2.0)
        running = jnp.maximum(running, folded(scores))
    best[...] = running


def own_block(units, order, pad_counts):
    count, depth = units[0].shape
    rows = order.shape[0]
    whole = pl.BlockSpec(memory_space=pltpu.VMEM)
    return pl.pallas_call(
        own_kernel,
        out_shape=(
            jax.ShapeDtypeStruct((depth, rows), jnp.bfloat16),
            jax.ShapeDtypeStruct((8, rows), jnp.float32),
        ),
        in_specs=[pl.BlockSpec(memory_space=pltpu.SMEM), whole] + [whole] * len(units),
        out_specs=(whole, whole),
        compiler_params=pltpu.CompilerParams(vmem_limit_bytes=VMEM),
        cost_estimate=pl.CostEstimate(
            flops=4 * rows * rows * depth, bytes_accessed=4 * rows * depth, transcendentals=0
        ),
        name="own_block",
    )(pad_counts, order.reshape(1, rows), *units)


def tile_kernel(last, table, pads, own, best, blocks, out, running):
    step = pl.program_id(0)
    rows = own.shape[1]

    @pl.when(step == 0)
    def _():
        running[...] = best[...]

    for column in range(0, rows, 256):
        part = pl.ds(column, 256)
        scores = jnp.dot(blocks[0], own[:, part], preferred_element_type=jnp.float32)
        running[:, part] = jnp.maximum(running[:, part], folded(scores))

    @pl.when(step == pl.num_programs(0) - 1)
    def _():
        if last:
            valid_count = rows - pads[lax.axis_index("blk")]
            position = lax.broadcasted_iota(jnp.int32, (1, rows), 1)
            found = jnp.max(running[...], axis=0, keepdims=True)
            out[...] = jnp.where(position < valid_count, found, 0.0)
        else:
            out[...] = running[...]


def scored(table, pad_counts, own, best, blocks, last):
    depth, rows = own.shape
    count = blocks.shape[1]
    steps = table.shape[0]
    out_rows = 1 if last else 8
    return pl.pallas_call(
        functools.partial(tile_kernel, last),
        out_shape=jax.ShapeDtypeStruct((out_rows, rows), jnp.float32),
        grid_spec=pltpu.PrefetchScalarGridSpec(
            num_scalar_prefetch=2,
            grid=(steps,),
            in_specs=[
                pl.BlockSpec((depth, rows), lambda i, table, pads: (0, 0)),
                pl.BlockSpec((8, rows), lambda i, table, pads: (0, 0)),
                pl.BlockSpec((1, count, depth), lambda i, table, pads: (table[i], 0, 0)),
            ],
            out_specs=pl.BlockSpec((out_rows, rows), lambda i, table, pads: (0, 0)),
            scratch_shapes=[pltpu.VMEM((8, rows), jnp.float32)],
        ),
        compiler_params=pltpu.CompilerParams(vmem_limit_bytes=VMEM),
        cost_estimate=pl.CostEstimate(
            flops=2 * steps * count * rows * depth,
            bytes_accessed=2 * (steps * count + rows) * depth,
            transcendentals=0,
        ),
        name="scored",
    )(table, pad_counts, own, best, blocks)


def local(embeddings, order, pad_counts):
    rows, depth = embeddings.shape
    count = rows // CHUNKS
    nblocks = lax.axis_size("blk")
    here = lax.axis_index("blk")
    offsets = [k for step in range(1, STEPS + 1) for k in (step, -step)]
    units = [unit_chunk(embeddings, order, pad_counts, chunk) for chunk in range(CHUNKS)]
    if nblocks <= 16:
        arrived = [lax.all_gather(unit, "blk") for unit in units]
        table = (here + jnp.array(offsets, jnp.int32)) % nblocks
        rounds = [(table, blocks) for blocks in arrived]
    else:
        own_unit = jnp.concatenate(units)[None]
        rounds = []
        for offset in offsets:
            pairs = [(i, (i + offset) % nblocks) for i in range(nblocks)]
            rounds.append((jnp.zeros((1,), jnp.int32), lax.ppermute(own_unit, "blk", pairs)))
    own, best = own_block(units, order, pad_counts)
    for index, (table, blocks) in enumerate(rounds):
        best = scored(table, pad_counts, own, best, blocks, index == len(rounds) - 1)
    return best.reshape(rows)


def solution(mesh):
    in_specs = (P(("groups", "blk"), None), P(("groups", "blk")), P("groups"))
    out_specs = P(("groups", "blk"))
    return jax.shard_map(local, mesh=mesh, in_specs=in_specs, out_specs=out_specs, check_vma=False)
```

time: 207 us -> 336 us (1.62)
  waiting for transfers between devices: 120 us -> 249 us
  Pallas kernels: 0 us -> 63.4 us
  starting transfers between devices: 35.8 us -> 0.13 us
  matrix products: 32.8 us -> 0 us
  between operations: 4.58 us -> 13.3 us
  other arithmetic: 5.22 us -> 0.01 us
    all_gather x0 -> x4, waiting for transfers between devices: none -> 249 us  [local(): arrived = [lax.all_gather(unit, 'blk') for unit in units]]
    ppermute x12 -> x0, waiting for transfers between devices: 120 us -> none  [passed_along(): lax.ppermute(value, axis, [(i, (i + by) % devices) for i in range(devices)])]
    pallas_call x0 -> x9, Pallas kernels: none -> 63.4 us  [the longest x4 49.4 us: scored(): pl.pallas_call(functools.partial(tile_kernel, last), out_shape=jax.ShapeD...]
    ppermute x12 -> x0, starting transfers between devices: 35.8 us -> none  [passed_along(): lax.ppermute(value, axis, [(i, (i + by) % devices) for i in range(devices)])]
    dot_general x7 -> x0, matrix products: 32.8 us -> none  [tile_maxima(): lax.dot_general(own, other, (((1,), (1,)), ((), ())), preferred_element_t...]
    unnamed x20 -> x24, local copies, waits for them, and re-layouts: 2.84 us -> 8.78 us
    gather x1 -> x0, local copies, waits for them, and re-layouts: 5.35 us -> none  [local(): ordered = jnp.take(embeddings, order, axis=0).astype(jnp.float32)]
  transfers between devices with their start and end apart: 12 -> 4, of which waited for: 7 -> 4; matrix products, arithmetic and copies ran while one was open for 11% -> 0% of each run, Pallas kernels for 0% -> 15%
where the time goes in v1:
time: 336 us; the launch traced here: 335 us
  waiting for transfers between devices  249 us (74%)
  Pallas kernels  63.4 us (19%)
  between operations  13.3 us (4%)
  local copies, waits for them, and re-layouts  8.78 us (3%)
    all_gather x4, waiting for transfers between devices, local(): arrived = [lax.all_gather(unit, 'blk') for unit in units]  249 us
    pallas_call x4, Pallas kernels, scored(): pl.pallas_call(functools.partial(tile_kernel, last), out_shape=jax.ShapeD...  49.4 us
    unnamed x24, local copies, waits for them, and re-layouts  8.78 us
    pallas_call x4, Pallas kernels, unit_chunk(): pl.pallas_call(functools.partial(unit_kernel, chunk * count), out_shape=j...  7.61 us
  transfers between devices with their start and end apart: 4, of which 4 were waited for; matrix products, arithmetic and copies ran while one was open for 0% of the time, Pallas kernels for 15%

profile of v1, /device:TPU:0, one launch (start us, length us, event | category | flops | bytes accessed | tf_op | source)
XLA Modules:
  0.0 334.5 jit_solution(11164032838742595785)
XLA Ops:
  6.5 1.6 copy-done
  8.1 0.7 copy-done.3
  8.8 0.7 copy-done.6
  9.5 1.9 unit_chunk.4.refs_0_
  11.4 0.0 all-gather.11.cloned.1.call-start
  11.5 1.6 copy-done.1
  13.1 0.7 copy-done.4
  13.8 0.7 copy-done.7
  14.4 1.9 unit_chunk.5.refs_1_
  16.4 0.0 all-gather.13.cloned.1.call-start
  16.4 1.9 unit_chunk.6.refs_2_
  18.4 0.0 all-gather.15.cloned.1.call-start
  18.4 1.9 unit_chunk.7.refs_3_
  20.4 6.5 %own_block.1 = (bf16[1024,1024]{1,0:T(8,128)(2,1)S(1)}, f32[8,1024]{1,0:T(8,128)S(1)}) custom-call(s32[16]{0:T(128)S(1)} %copy-done.8, s32[1,1024]{1,0:T(1,128)S(1)} %bitcast.10, bf16[256,1024]{1,0:T(8,128)(2,1)} %unit_chunk.4.refs_0_, bf16[256,1024]{1,0:T(8,128)(2,1)} %unit_chunk.5.refs_1_, bf16[256,1024]{1,0:T(8,128)(2,1)} %unit_chunk.6.refs_2_, ...), custom_call_target="tpu_custom_call" | custom-call | flops 4294967296 | bytes 4194304 | tf_op jit(solution)/shard_map/own_block/pallas_call | solution.py:96
  26.9 1.3 copy-done.9
  28.2 61.1 %all-gather.9.cloned.1.call-done = bf16[4096,1024]{1,0:T(8,128)(2,1)} async-done(((bf16[256,1024]{1,0:T(8,128)(2,1)}), bf16[4096,1024]{1,0:T(8,128)(2,1)}) %all-gather.9.cloned.1.call-update) | async-done | bytes 8388624 | tf_op jit(solution)/shard_map/all_gather | solution.py:173
  89.2 1.6 copy-done.10
  90.8 12.2 %scored.4.best = f32[8,1024]{1,0:T(8,128)S(1)} custom-call(s32[12]{0:T(128)S(1)} %and_select_fusion.table, s32[16]{0:T(128)S(1)} %copy-done.8, bf16[1024,1024]{1,0:T(8,128)(2,1)S(1)} %copy-done.10, f32[8,1024]{1,0:T(8,128)S(1)} %get-tuple-element.8.best, bf16[16,256,1024]{2,1,0:T(8,128)(2,1)} %bitcast.11), custom_call_target="tpu_custom_call" | custom-call | flops 6442450944 | bytes 8388608 | tf_op jit(solution)/shard_map/scored/pallas_call | solution.py:141
  103.0 61.5 %all-gather.11.cloned.1.call-done = bf16[4096,1024]{1,0:T(8,128)(2,1)} async-done(((bf16[256,1024]{1,0:T(8,128)(2,1)}), bf16[4096,1024]{1,0:T(8,128)(2,1)}) %all-gather.11.cloned.1.call-update) | async-done | bytes 8388624 | tf_op jit(solution)/shard_map/all_gather | solution.py:173
  164.6 12.2 %scored.5.best = f32[8,1024]{1,0:T(8,128)S(1)} custom-call(s32[12]{0:T(128)S(1)} %and_select_fusion.table, s32[16]{0:T(128)S(1)} %copy-done.8, bf16[1024,1024]{1,0:T(8,128)(2,1)S(1)} %copy-done.10, f32[8,1024]{1,0:T(8,128)S(1)} %scored.4.best, bf16[16,256,1024]{2,1,0:T(8,128)(2,1)} %bitcast.12), custom_call_target="tpu_custom_call" | custom-call | flops 6442450944 | bytes 8388608 | tf_op jit(solution)/shard_map/scored/pallas_call | solution.py:141
  176.8 63.2 %all-gather.13.cloned.1.call-done = bf16[4096,1024]{1,0:T(8,128)(2,1)} async-done(((bf16[256,1024]{1,0:T(8,128)(2,1)}), bf16[4096,1024]{1,0:T(8,128)(2,1)}) %all-gather.13.cloned.1.call-update) | async-done | bytes 8388624 | tf_op jit(solution)/shard_map/all_gather | solution.py:173
  240.0 12.2 %scored.6.best = f32[8,1024]{1,0:T(8,128)S(1)} custom-call(s32[12]{0:T(128)S(1)} %and_select_fusion.table, s32[16]{0:T(128)S(1)} %copy-done.8, bf16[1024,1024]{1,0:T(8,128)(2,1)S(1)} %copy-done.10, f32[8,1024]{1,0:T(8,128)S(1)} %scored.5.best, bf16[16,256,1024]{2,1,0:T(8,128)(2,1)} %bitcast.13), custom_call_target="tpu_custom_call" | custom-call | flops 6442450944 | bytes 8388608 | tf_op jit(solution)/shard_map/scored/pallas_call | solution.py:141
  252.2 63.0 %all-gather.15.cloned.1.call-done = bf16[4096,1024]{1,0:T(8,128)(2,1)} async-done(((bf16[256,1024]{1,0:T(8,128)(2,1)}), bf16[4096,1024]{1,0:T(8,128)(2,1)}) %all-gather.15.cloned.1.call-update) | async-done | bytes 8388624 | tf_op jit(solution)/shard_map/all_gather | solution.py:173
  315.2 12.8 %scored.7 = f32[1,1024]{1,0:T(1,128)} custom-call(s32[12]{0:T(128)S(1)} %and_select_fusion.table, s32[16]{0:T(128)S(1)} %copy-done.8, bf16[1024,1024]{1,0:T(8,128)(2,1)S(1)} %copy-done.10, f32[8,1024]{1,0:T(8,128)S(1)} %scored.6.best, bf16[16,256,1024]{2,1,0:T(8,128)(2,1)} %bitcast.14), custom_call_target="tpu_custom_call" | custom-call | flops 6442450944 | bytes 8388608 | tf_op jit(solution)/shard_map/scored/pallas_call | solution.py:141
  (22 shorter events, 0.1 us)
Async XLA Ops:
  6.5 9.9 %copy-start.8 = (s32[16]{0:T(128)S(1)}, s32[16]{0:T(128)}, u32[]{:S(2)}) copy-start(s32[16]{0:T(128)} %pads.17) | copy-start | bytes 196
  6.5 82.7 %all-gather.9.cloned.1.call-start = ((), (), s32[]{:S(2)}) async-start(), calls=%async_computation | async-start | bytes 8912896 | tf_op jit(solution)/shard_map/all_gather | solution.py:173
  6.5 1.6 copy-start
  8.1 0.7 copy-start.3
  8.8 0.7 copy-start.6
  9.5 6.9 %copy-start.2 = (bf16[1024,1024]{1,0:T(8,128)(2,1)S(1)}, bf16[1024,1024]{1,0:T(8,128)(2,1)}, u32[]{:S(2)}) copy-start(bf16[1024,1024]{1,0:T(8,128)(2,1)} %everything.7) | copy-start | bytes 6291460
  9.5 6.9 %copy-start.5 = (s32[1024]{0:T(1024)S(1)}, s32[1024]{0:T(1024)}, u32[]{:S(2)}) copy-start(s32[1024]{0:T(1024)} %order_smem.7) | copy-start | bytes 12292
  11.4 9.0 %copy-start.11 = (s32[12]{0:T(128)S(1)}, s32[12]{0:T(128)}, u32[]{:S(2)}) copy-start(s32[12]{0:T(128)} %constant.21.clone) | copy-start | bytes 148
  11.4 153.1 %all-gather.11.cloned.1.call-start = ((), (), s32[]{:S(2)}) async-start(), calls=%async_computation.1 | async-start | bytes 8912896 | tf_op jit(solution)/shard_map/all_gather | solution.py:173
  11.5 1.6 copy-start.1
  13.1 0.7 copy-start.4
  13.8 0.7 copy-start.7
  16.4 223.7 %all-gather.13.cloned.1.call-start = ((), (), s32[]{:S(2)}) async-start(), calls=%async_computation.2 | async-start | bytes 8912896 | tf_op jit(solution)/shard_map/all_gather | solution.py:173
  18.4 296.8 %all-gather.15.cloned.1.call-start = ((), (), s32[]{:S(2)}) async-start(), calls=%async_computation.3 | async-start | bytes 8912896 | tf_op jit(solution)/shard_map/all_gather | solution.py:173
  26.8 1.3 copy-start.9
  89.2 1.6 copy-start.10
Sparse Core Ops, SparseCore 0:
  11.6 77.6 all-gather.8
  91.4 73.1 all-gather.10
  166.7 73.2 all-gather.12
  242.0 73.1 all-gather.14

commit v2 on v0

v2 whole, which is shorter than its diff:
```python
import functools

import jax
import jax.numpy as jnp
import numpy as np
from jax import lax
from jax.experimental import pallas as pl
from jax.experimental.pallas import tpu as pltpu
from jax.sharding import PartitionSpec as P

STEPS = 6
VMEM = 56 * 2**20
FLOOR = -2.0


class Move:
    def __init__(self, name, source, pairs, stage, after=()):
        self.name, self.source, self.pairs = name, source, pairs
        self.stage, self.after = stage, after


def near(first, second, count):
    gap = (first - second) % count
    return min(gap, count - gap) <= STEPS


def grid_moves():
    def at(z, y, lane):
        return 4 * z + 2 * y + (y if lane == 0 else 1 - y)

    def rows(links):
        return [
            (at(z, y, lane), at(to, y, land)) for y in (0, 1) for (z, lane), (to, land) in links
        ]

    def across(planes, lane):
        return [(at(z, y, lane), at(z, 1 - y, lane)) for z in planes for y in (0, 1)]

    every = range(4)
    return [
        Move("R1", "own", rows([((0, 0), (2, 0)), ((2, 0), (3, 0)), ((3, 0), (1, 0)), ((1, 0), (0, 0))])
             + across(every, 1), 1),
        Move("R2a", "own", rows([((3, 1), (1, 1)), ((1, 1), (0, 1)), ((1, 0), (2, 0))]), 1),
        Move("R2b", "own", rows([((0, 1), (1, 1))]) + across(every, 0), 1),
        Move("A", "own", rows([((z, lane), (z, 1 - lane)) for z in every for lane in (0, 1)]), 0),
        Move("H", "R2b", across([1], 1), 3),
        Move("G", "R1", rows([((2, 0), (3, 0))]), 3),
        Move("R3", "own", rows([((1, 1), (2, 1)), ((2, 1), (3, 1)), ((2, 0), (1, 1))]), 3, ("R1",)),
        Move("FI", "R2b", rows([((z, 0), (z, 1)) for z in every] + [((1, 1), (1, 0))]), 2),
        Move("FK", "R1", rows([((z, 1), (z, 0)) for z in every] + [((1, 0), (1, 1))]), 2),
    ]


def ring_moves(count):
    return [
        Move("N%d" % k, "own", [((i + k) % count, i) for i in range(count)], k)
        for k in range(1, STEPS + 1)
    ]


def planned(count):
    moves = grid_moves() if count == 16 else ring_moves(count)
    holds = {"own": {d: d for d in range(count)}}
    stage_of = {"own": 0}
    for move in moves:
        holds[move.name] = {to: holds[move.source][of] for of, to in move.pairs if of in holds[move.source]}
        stage_of[move.name] = move.stage
    slots = ["own"] + [move.name for move in moves]
    stages = 1 + max(stage_of.values())
    where = {}
    for device in range(count):
        held = [(slot, holds[slot][device]) for slot in slots if device in holds[slot]]
        for i, (slot, block) in enumerate(held):
            for other, visitor in held[:i]:
                if block != visitor and near(block, visitor, count):
                    pair = (min(block, visitor), max(block, visitor))
                    stage = max(stage_of[slot], stage_of[other])
                    where.setdefault(pair, []).append((stage, device, slot, other, block, visitor))
    need = [(b, (b + k) % count) for b in range(count) for k in range(1, STEPS + 1)]
    need = sorted({(min(pair), max(pair)) for pair in need})
    load = np.zeros((stages, count), np.int64)
    work = [[[] for _ in range(count)] for _ in range(stages)]
    for pair in sorted(need, key=lambda p: (len({w[1] for w in where[p]}), p)):
        choice = min(
            where[pair],
            key=lambda w: (w[0], load[w[0], w[1]], load[:, w[1]].sum(), w[1]),
        )
        stage, device = choice[:2]
        load[stage, device] += 1
        work[stage][device].append(choice[2:])
    return moves, slots, work


def unit_kernel(pads, order_smem, order, embeddings, everything, unit, mask, tile, sem):
    rows = order.shape[1]
    count = unit.shape[0]
    valid_count = rows - pads[lax.axis_index("blk")]
    first = order_smem[0]
    base = pl.multiple_of((first // 16) * 16, 16)

    @pl.when(pl.program_id(0) == 0)
    def _():
        copy = pltpu.make_async_copy(everything.at[pl.ds(base, 16)], tile, sem)
        copy.start()
        copy.wait()

    position = lax.broadcasted_iota(jnp.int32, (1, rows), 1)
    kept = jnp.where(position < valid_count, order[...], -1)
    row = pl.program_id(0) * count + lax.broadcasted_iota(jnp.int32, (count, 1), 0)
    found = jnp.max(jnp.where(kept == row, 1.0, 0.0), axis=1, keepdims=True)
    among = lax.broadcasted_iota(jnp.int32, (16, 1), 0) == first - base
    filler = jnp.sum(jnp.where(among, tile[...].astype(jnp.float32), 0.0), axis=0, keepdims=True)
    value = jnp.where(found > 0.0, embeddings[...].astype(jnp.float32), filler)
    scale = lax.rsqrt(jnp.sum(value * value, axis=1, keepdims=True) + 1e-06)
    unit[...] = (value * scale).astype(jnp.bfloat16)
    mask[...] = jnp.broadcast_to(found, mask.shape)


def normalized(embeddings, order, pad_counts):
    rows, depth = embeddings.shape
    count = 256
    return pl.pallas_call(
        unit_kernel,
        out_shape=(
            jax.ShapeDtypeStruct((rows, depth), jnp.bfloat16),
            jax.ShapeDtypeStruct((rows, 128), jnp.float32),
        ),
        grid=(rows // count,),
        in_specs=[
            pl.BlockSpec(memory_space=pltpu.SMEM),
            pl.BlockSpec(memory_space=pltpu.SMEM),
            pl.BlockSpec((1, rows), lambda i: (0, 0)),
            pl.BlockSpec((count, depth), lambda i: (i, 0)),
            pl.BlockSpec(memory_space=pl.ANY),
        ],
        out_specs=(
            pl.BlockSpec((count, depth), lambda i: (i, 0)),
            pl.BlockSpec((count, 128), lambda i: (i, 0)),
        ),
        scratch_shapes=[pltpu.VMEM((16, depth), jnp.bfloat16), pltpu.SemaphoreType.DMA],
        compiler_params=pltpu.CompilerParams(vmem_limit_bytes=VMEM),
        cost_estimate=pl.CostEstimate(
            flops=4 * rows * depth, bytes_accessed=4 * rows * depth, transcendentals=rows
        ),
        name="normalized",
    )(pad_counts, order, order.reshape(1, rows), embeddings, embeddings)


def product(left, right):
    return lax.dot_general(left, right, (((1,), (1,)), ((), ())), preferred_element_type=jnp.float32)


def own_kernel(unit, mask, best):
    rows = unit.shape[0]
    best[...] = jnp.full(best.shape, FLOOR, jnp.float32)
    total = None
    for start in range(0, rows, 256):
        scores = product(unit[pl.ds(start, 256), :], unit[...])
        row = start + lax.broadcasted_iota(jnp.int32, (256, 1), 0)
        column = lax.broadcasted_iota(jnp.int32, (1, rows), 1)
        keep = (mask[pl.ds(start, 256), :1] > 0.0) & (row != column)
        found = jnp.max(jnp.where(keep, scores, FLOOR), axis=0, keepdims=True)
        total = found if total is None else jnp.maximum(total, found)
    best[pl.ds(lax.axis_index("blk"), 1), :] = total


def own_block(unit, mask, nblocks):
    rows, depth = unit.shape
    return pl.pallas_call(
        own_kernel,
        out_shape=jax.ShapeDtypeStruct((nblocks, rows), jnp.float32),
        in_specs=[pl.BlockSpec(memory_space=pltpu.VMEM)] * 2,
        out_specs=pl.BlockSpec(memory_space=pltpu.VMEM),
        compiler_params=pltpu.CompilerParams(vmem_limit_bytes=VMEM),
        cost_estimate=pl.CostEstimate(
            flops=2 * rows * rows * depth, bytes_accessed=2 * rows * depth, transcendentals=0
        ),
        name="own_block",
    )(unit, mask)


def pairs_kernel(nslots, table, best, *refs):
    slots, out, held, sems = refs[:nslots], refs[nslots], refs[nslots + 1], refs[nslots + 2]
    rows = out.shape[1]
    here = lax.axis_index("blk")
    steps = table[here, 0, 0]
    out[...] = best[...]

    def fetch(step):
        for side in range(2):
            wanted = table[here, step + 1, side]
            for index, slot in enumerate(slots):
                @pl.when(wanted == index)
                def _(slot=slot, side=side):
                    pltpu.make_async_copy(slot, held.at[step % 2, side], sems.at[step % 2, side]).start()

    def arrived(step):
        for side in range(2):
            pltpu.make_async_copy(slots[0], held.at[step % 2, side], sems.at[step % 2, side]).wait()

    @pl.when(steps > 0)
    def _():
        fetch(0)

    @pl.loop(0, steps)
    def _(step):
        arrived(step)

        @pl.when(step + 1 < steps)
        def _():
            fetch(step + 1)

        now = step % 2
        total = None
        first = pl.ds(table[here, step + 1, 2], 1)
        second = pl.ds(table[here, step + 1, 3], 1)
        for start in range(0, rows, 256):
            scores = product(held[now, 0, pl.ds(start, 256), :], held[now, 1])
            down = jnp.max(scores.reshape(32, 8, rows), axis=0)
            total = down if total is None else jnp.maximum(total, down)
            along = scores[:, :128]
            for lane in range(128, rows, 128):
                along = jnp.maximum(along, scores[:, lane : lane + 128])
            found = jnp.max(along.T, axis=0, keepdims=True)
            part = pl.ds(start, 256)
            out[first, part] = jnp.maximum(out[first, part], found)
        out[second, :] = jnp.maximum(out[second, :], jnp.max(total, axis=0, keepdims=True))


def scored(best, slots, work):
    names = sorted({slot for pairs in work for pair in pairs for slot in pair[:2]})
    most = max(len(pairs) for pairs in work)
    table = np.zeros((len(work), most + 1, 4), np.int32)
    for device, pairs in enumerate(work):
        table[device, 0, 0] = len(pairs)
        for step, (slot, other, block, visitor) in enumerate(pairs):
            table[device, step + 1] = (names.index(slot), names.index(other), block, visitor)
    given = [slots[name] for name in names]
    rows, depth = given[0].shape
    return pl.pallas_call(
        functools.partial(pairs_kernel, len(given)),
        out_shape=jax.ShapeDtypeStruct(best.shape, jnp.float32),
        in_specs=[pl.BlockSpec(memory_space=pltpu.SMEM), pl.BlockSpec(memory_space=pltpu.VMEM)]
        + [pl.BlockSpec(memory_space=pl.ANY)] * len(given),
        out_specs=pl.BlockSpec(memory_space=pltpu.VMEM),
        scratch_shapes=[
            pltpu.VMEM((2, 2, rows, depth), jnp.bfloat16),
            pltpu.SemaphoreType.DMA((2, 2)),
        ],
        compiler_params=pltpu.CompilerParams(vmem_limit_bytes=VMEM),
        cost_estimate=pl.CostEstimate(
            flops=2 * most * rows * rows * depth,
            bytes_accessed=4 * most * rows * depth,
            transcendentals=0,
        ),
        name="scored",
    )(jnp.asarray(table), best, *given)


def placed_kernel(pads, order, found, out):
    rows = order.shape[1]
    valid_count = rows - pads[lax.axis_index("blk")]
    best = jnp.max(found[...], axis=0, keepdims=True)
    column = jnp.broadcast_to(best, (128, rows)).T[:, :1]
    row = lax.broadcasted_iota(jnp.int32, (rows, 1), 0)
    sorted_best = jnp.max(jnp.where(order[...] == row, column, FLOOR), axis=0, keepdims=True)
    position = lax.broadcasted_iota(jnp.int32, (1, rows), 1)
    out[...] = jnp.where(position < valid_count, sorted_best, 0.0)


def placed(found, order, pad_counts):
    rows = order.shape[0]
    whole = pl.BlockSpec(memory_space=pltpu.VMEM)
    return pl.pallas_call(
        placed_kernel,
        out_shape=jax.ShapeDtypeStruct((1, rows), jnp.float32),
        in_specs=[pl.BlockSpec(memory_space=pltpu.SMEM), whole, whole],
        out_specs=whole,
        compiler_params=pltpu.CompilerParams(vmem_limit_bytes=VMEM),
        name="placed",
    )(pad_counts, order.reshape(1, rows), found).reshape(rows)


def local(embeddings, order, pad_counts):
    nblocks = lax.axis_size("blk")
    moves, names, work = planned(nblocks)
    unit, mask = normalized(embeddings, order, pad_counts)
    slots = {"own": unit}
    for move in moves:
        value = slots[move.source]
        if move.after:
            value = lax.optimization_barrier((value, *[slots[name] for name in move.after]))[0]
        slots[move.name] = lax.ppermute(value, "blk", move.pairs)
    best = own_block(unit, mask, nblocks)
    for pairs in work:
        if any(pairs):
            best = scored(best, slots, pairs)
    return placed(lax.all_to_all(best, "blk", 0, 0, tiled=True), order, pad_counts)


def solution(mesh):
    in_specs = (P(("groups", "blk"), None), P(("groups", "blk")), P("groups"))
    out_specs = P(("groups", "blk"))
    return jax.shard_map(local, mesh=mesh, in_specs=in_specs, out_specs=out_specs, check_vma=False)
```

time: 207 us -> 143 us (0.69)
  waiting for transfers between devices: 120 us -> 40.7 us
  blocking collectives: 0 us -> 44.5 us
  Pallas kernels: 0 us -> 37 us
  matrix products: 32.8 us -> 0 us
  starting transfers between devices: 35.8 us -> 17.9 us
  local copies, waits for them, and re-layouts: 8.86 us -> 1.56 us
  other arithmetic: 5.22 us -> 0 us
  between operations: 4.58 us -> 0.12 us
    ppermute x12 -> x9, waiting for transfers between devices: 120 us -> 40.7 us  [local(): slots[move.name] = lax.ppermute(value, 'blk', move.pairs)]
    all_to_all x0 -> x1, blocking collectives: none -> 44.5 us  [local(): lax.all_to_all(best, 'blk', 0, 0, tiled=True)]
    pallas_call x0 -> x7, Pallas kernels: none -> 37 us  [the longest x4 24.8 us: scored(): pl.pallas_call(functools.partial(pairs_kernel, len(given)), out_shape=jax...]
    dot_general x7 -> x0, matrix products: 32.8 us -> none  [tile_maxima(): lax.dot_general(own, other, (((1,), (1,)), ((), ())), preferred_element_t...]
    ppermute x12 -> x9, starting transfers between devices: 35.8 us -> 17.9 us  [local(): slots[move.name] = lax.ppermute(value, 'blk', move.pairs)]
    gather x1 -> x0, local copies, waits for them, and re-layouts: 5.35 us -> none  [local(): ordered = jnp.take(embeddings, order, axis=0).astype(jnp.float32)]
    reduce_sum x1 -> x0, other arithmetic: 2.48 us -> none  [local(): jnp.sum(ordered * ordered, axis=1, keepdims=True) + 1e-06]
    unnamed x20 -> x7, local copies, waits for them, and re-layouts: 2.84 us -> 0.66 us
  transfers between devices with their start and end apart: 12 -> 9, of which waited for: 7 -> 1; matrix products, arithmetic and copies ran while one was open for 11% -> 0% of each run, Pallas kernels for 0% -> 19%
where the time goes in v2:
time: 143 us; the launch traced here: 142 us
  blocking collectives  44.5 us (31%)
  waiting for transfers between devices  40.7 us (28%)
  Pallas kernels  37 us (26%)
  starting transfers between devices  17.9 us (13%)
  local copies, waits for them, and re-layouts  1.56 us (1%)
    all_to_all x1, blocking collectives, local(): lax.all_to_all(best, 'blk', 0, 0, tiled=True)  44.5 us
    ppermute x9, waiting for transfers between devices, local(): slots[move.name] = lax.ppermute(value, 'blk', move.pairs)  40.7 us
    pallas_call x4, Pallas kernels, scored(): pl.pallas_call(functools.partial(pairs_kernel, len(given)), out_shape=jax...  24.8 us
    ppermute x9, starting transfers between devices, local(): slots[move.name] = lax.ppermute(value, 'blk', move.pairs)  17.9 us
    pallas_call x1, Pallas kernels, normalized(): pl.pallas_call(unit_kernel, out_shape=(jax.ShapeDtypeStruct((rows, depth)...  5.28 us
    pallas_call x1, Pallas kernels, own_block(): pl.pallas_call(own_kernel, out_shape=jax.ShapeDtypeStruct((nblocks, rows)...  4.69 us
  transfers between devices with their start and end apart: 9, of which 1 were waited for; matrix products, arithmetic and copies ran while one was open for 0% of the time, Pallas kernels for 19%

profile of v2, /device:TPU:0, one launch (start us, length us, event | category | flops | bytes accessed | tf_op | source)
XLA Modules:
  0.0 141.8 jit_solution(3081223058109309898)
XLA Ops:
  0.0 5.3 %normalized.1 = (bf16[1024,1024]{1,0:T(8,128)(2,1)}, f32[1024,128]{1,0:T(8,128)}) custom-call(s32[16]{0:T(128)} %pads.3, s32[1024]{0:T(1024)} %order_smem.1, s32[1,1024]{1,0:T(1,128)} %bitcast.8, bf16[1024,1024]{1,0:T(8,128)(2,1)} %everything.1, bf16[1024,1024]{1,0:T(8,128)(2,1)} %everything.1), custom_call_target="tpu_custom_call" | custom-call | flops 4194304 | bytes 4194304 | tf_op jit(solution)/shard_map/normalized/pallas_call | solution.py:122
  5.3 4.3 %collective-permute-start.3 = (bf16[1024,1024]{1,0:T(8,128)(2,1)}, bf16[1024,1024]{1,0:T(8,128)(2,1)S(1)}, u32[]{:S(2)}, u32[]{:S(2)}) collective-permute-start(bf16[1024,1024]{1,0:T(8,128)(2,1)} %get-tuple-element.10.unit.refs_1_.refs_4_.refs_9_), channel_id=1, source_target_pairs={{1,5},{2,6},{0,3},{3,0},{4,7},{7,4},{8,11},{11,8},{12,15},{15,12},... | collective-permute-start | bytes 6291464 | tf_op jit(solution)/shard_map/ppermute | solution.py:293
  9.6 2.6 %collective-permute-start.1 = (bf16[1024,1024]{1,0:T(8,128)(2,1)}, bf16[1024,1024]{1,0:T(8,128)(2,1)S(1)}, u32[]{:S(2)}, u32[]{:S(2)}) collective-permute-start(bf16[1024,1024]{1,0:T(8,128)(2,1)} %get-tuple-element.10.unit.refs_1_.refs_4_.refs_9_), channel_id=1, source_target_pairs={{0,8},{8,12},{12,4},{4,0},{3,11},{11,15},{15,7},{7,3},{1,2},{2,1},... | collective-permute-start | bytes 6291464 | tf_op jit(solution)/shard_map/ppermute | solution.py:293
  12.3 0.8 collective-permute-start.2
  13.0 0.4 collective-permute-start
  13.4 40.7 %collective-permute-done.3.refs_3_.refs_7_ = bf16[1024,1024]{1,0:T(8,128)(2,1)S(1)} collective-permute-done((bf16[1024,1024]{1,0:T(8,128)(2,1)}, bf16[1024,1024]{1,0:T(8,128)(2,1)S(1)}, u32[]{:S(2)}, u32[]{:S(2)}) %collective-permute-start.3) | collective-permute-done | bytes 2097184 | tf_op jit(solution)/shard_map/ppermute | solution.py:293
  54.1 2.6 %collective-permute-start.4 = (bf16[1024,1024]{1,0:T(8,128)(2,1)S(1)}, bf16[1024,1024]{1,0:T(8,128)(2,1)}, u32[]{:S(2)}, u32[]{:S(2)}) collective-permute-start(bf16[1024,1024]{1,0:T(8,128)(2,1)S(1)} %collective-permute-done.3.refs_3_.refs_7_), channel_id=1, source_target_pairs={{0,1},{4,5},{8,9},{12,13},{5,4},{3,2},{7,6},{11,10},{15,14},{6,7},... | collective-permute-start | bytes 6291464 | tf_op jit(solution)/shard_map/ppermute | solution.py:293
  56.7 0.0 collective-permute-done.1.refs_1_.refs_2_.refs_5_
  56.7 1.3 collective-permute-start.5
  58.0 2.0 %collective-permute-start.8 = (bf16[1024,1024]{1,0:T(8,128)(2,1)}, bf16[1024,1024]{1,0:T(8,128)(2,1)}, u32[]{:S(2)}, u32[]{:S(2)}) collective-permute-start(bf16[1024,1024]{1,0:T(8,128)(2,1)} %get-tuple-element.10.unit.refs_1_.refs_4_.refs_9_), channel_id=1, source_target_pairs={{5,9},{9,13},{8,5},{6,10},{10,14},{11,6},{21,25},{25,29},{24,21},{... | collective-permute-start | bytes 6291464 | tf_op jit(solution)/shard_map/ppermute | solution.py:293
  60.0 0.0 collective-permute-done.2.refs_2_.refs_3_.refs_6_
  60.0 2.0 %collective-permute-start.7 = (bf16[1024,1024]{1,0:T(8,128)(2,1)S(1)}, bf16[1024,1024]{1,0:T(8,128)(2,1)}, u32[]{:S(2)}, u32[]{:S(2)}) collective-permute-start(bf16[1024,1024]{1,0:T(8,128)(2,1)S(1)} %collective-permute-done.3.refs_3_.refs_7_), channel_id=1, source_target_pairs={{5,6},{6,5},{21,22},{22,21}} | collective-permute-start | bytes 6291464 | tf_op jit(solution)/shard_map/ppermute | solution.py:293
  62.0 0.0 collective-permute-done.refs_0_
  62.0 2.0 %collective-permute-start.6 = (bf16[1024,1024]{1,0:T(8,128)(2,1)S(1)}, bf16[1024,1024]{1,0:T(8,128)(2,1)}, u32[]{:S(2)}, u32[]{:S(2)}) collective-permute-start(bf16[1024,1024]{1,0:T(8,128)(2,1)S(1)} %collective-permute-done.1.refs_1_.refs_2_.refs_5_), channel_id=1, source_target_pairs={{8,12},{11,15},{24,28},{27,31}} | collective-permute-start | bytes 6291464 | tf_op jit(solution)/shard_map/ppermute | solution.py:293
  63.9 4.7 %own_block.1.best = f32[16,1024]{1,0:T(8,128)} custom-call(bf16[1024,1024]{1,0:T(8,128)(2,1)} %get-tuple-element.10.unit.refs_1_.refs_4_.refs_9_, f32[1024,128]{1,0:T(8,128)} %get-tuple-element.9.mask), custom_call_target="tpu_custom_call" | custom-call | flops 2147483648 | bytes 2097152 | tf_op jit(solution)/shard_map/own_block/pallas_call | solution.py:169
  68.6 6.3 %scored.4.best = f32[16,1024]{1,0:T(8,128)} custom-call(s32[16,2,4]{2,1,0:T(2,128)} %constant.8.clone.table, f32[16,1024]{1,0:T(8,128)} %own_block.1.best, bf16[1024,1024]{1,0:T(8,128)(2,1)} %collective-permute-done.refs_0_, bf16[1024,1024]{1,0:T(8,128)(2,1)} %get-tuple-element.10.unit.refs_1_.refs_4_.refs_9_), custom_call_target="tpu_custom_call" | custom-call | flops 2147483648 | bytes 4194304 | tf_op jit(solution)/shard_map/scored/pallas_call | solution.py:240
  74.9 9.6 %scored.5.best = f32[16,1024]{1,0:T(8,128)} custom-call(s32[16,5,4]{2,1,0:T(8,128)} %constant.9.clone.table, f32[16,1024]{1,0:T(8,128)} %scored.4.best, bf16[1024,1024]{1,0:T(8,128)(2,1)} %collective-permute-done.refs_0_, bf16[1024,1024]{1,0:T(8,128)(2,1)} %copy-done.1, bf16[1024,1024]{1,0:T(8,128)(2,1)} %copy-done.2, bf16[1024,1024]{1,0:T(8,128)(2,1)} %copy-done, ...), custom_call_target="tpu_custom_call" | custom-call | flops 8589934592 | bytes 16777216 | tf_op jit(solution)/shard_map/scored/pallas_call | solution.py:240
  84.5 6.6 %scored.6.best = f32[16,1024]{1,0:T(8,128)} custom-call(s32[16,3,4]{2,1,0:T(4,128)} %constant.10.clone.table, f32[16,1024]{1,0:T(8,128)} %scored.5.best, bf16[1024,1024]{1,0:T(8,128)(2,1)} %collective-permute-done.4.refs_0_.refs_1_, bf16[1024,1024]{1,0:T(8,128)(2,1)} %collective-permute-done.5.refs_1_.refs_2_, bf16[1024,1024]{1,0:T(8,128)(2,1)} %copy-done.1, ...), custom_call_target="tpu_custom_call" | custom-call | flops 4294967296 | bytes 8388608 | tf_op jit(solution)/shard_map/scored/pallas_call | solution.py:240
  91.1 0.0 collective-permute-done.7.refs_4_
  91.1 2.4 %scored.7 = f32[16,1024]{1,0:T(8,128)} custom-call(s32[16,5,4]{2,1,0:T(8,128)} %constant.11.clone.table, f32[16,1024]{1,0:T(8,128)} %scored.6.best, bf16[1024,1024]{1,0:T(8,128)(2,1)} %collective-permute-done.refs_0_, bf16[1024,1024]{1,0:T(8,128)(2,1)} %collective-permute-done.4.refs_0_.refs_1_, bf16[1024,1024]{1,0:T(8,128)(2,1)} %collective-permute-done.5.refs_1_.refs_2_, ...), custom_call_target="tpu_custom_call" | custom-call | flops 8589934592 | bytes 16777216 | tf_op jit(solution)/shard_map/scored/pallas_call | solution.py:240
  93.6 0.9 copy.8
  94.5 44.5 %all_to_all.11 = f32[16,1,1024]{2,1,0:T(1,128)S(1)} all-to-all(f32[16,1,1024]{2,1,0:T(1,128)S(1)} %copy.8), channel_id=1, replica_groups=mesh['groups'=2,'blk'=16] {'blk'}, dimensions={0} | all-to-all | bytes 131072 | tf_op jit(solution)/shard_map/all_to_all | solution.py:298
  139.0 0.6 copy.11
  139.7 2.2 %placed.1 = f32[1,1024]{1,0:T(1,128)} custom-call(s32[16]{0:T(128)} %pads.3, s32[1,1024]{1,0:T(1,128)} %bitcast.9, f32[16,1024]{1,0:T(8,128)} %bitcast.6), custom_call_target="tpu_custom_call" | custom-call | tf_op jit(solution)/shard_map/placed/pallas_call | solution.py:274
  (10 shorter events, 0.0 us)
Async XLA Ops:
  5.3 48.8 %collective-permute-start.3 = (bf16[1024,1024]{1,0:T(8,128)(2,1)}, bf16[1024,1024]{1,0:T(8,128)(2,1)S(1)}, u32[]{:S(2)}, u32[]{:S(2)}) collective-permute-start(bf16[1024,1024]{1,0:T(8,128)(2,1)} %get-tuple-element.10.unit.refs_1_.refs_4_.refs_9_), channel_id=1, source_target_pairs={{1,5},{2,6},{0,3},{3,0},{4,7},{7,4},{8,11},{11,8},{12,15},{15,12},... | collective-permute-start | bytes 6291464 | tf_op jit(solution)/shard_map/ppermute | solution.py:293
  9.6 47.1 %collective-permute-start.1 = (bf16[1024,1024]{1,0:T(8,128)(2,1)}, bf16[1024,1024]{1,0:T(8,128)(2,1)S(1)}, u32[]{:S(2)}, u32[]{:S(2)}) collective-permute-start(bf16[1024,1024]{1,0:T(8,128)(2,1)} %get-tuple-element.10.unit.refs_1_.refs_4_.refs_9_), channel_id=1, source_target_pairs={{0,8},{8,12},{12,4},{4,0},{3,11},{11,15},{15,7},{7,3},{1,2},{2,1},... | collective-permute-start | bytes 6291464 | tf_op jit(solution)/shard_map/ppermute | solution.py:293
  12.3 47.7 %collective-permute-start.2 = (bf16[1024,1024]{1,0:T(8,128)(2,1)}, bf16[1024,1024]{1,0:T(8,128)(2,1)S(1)}, u32[]{:S(2)}, u32[]{:S(2)}) collective-permute-start(bf16[1024,1024]{1,0:T(8,128)(2,1)} %get-tuple-element.10.unit.refs_1_.refs_4_.refs_9_), channel_id=1, source_target_pairs={{13,5},{5,1},{4,8},{14,6},{6,2},{7,11},{29,21},{21,17},{20,24},{30... | collective-permute-start | bytes 6291464 | tf_op jit(solution)/shard_map/ppermute | solution.py:293
  13.0 48.9 %collective-permute-start = (bf16[1024,1024]{1,0:T(8,128)(2,1)}, bf16[1024,1024]{1,0:T(8,128)(2,1)}, u32[]{:S(2)}, u32[]{:S(2)}) collective-permute-start(bf16[1024,1024]{1,0:T(8,128)(2,1)} %get-tuple-element.10.unit.refs_1_.refs_4_.refs_9_), channel_id=1, source_target_pairs={{0,1},{1,0},{4,5},{5,4},{8,9},{9,8},{12,13},{13,12},{3,2},{2,3},{7... | collective-permute-start | bytes 6291464 | tf_op jit(solution)/shard_map/ppermute | solution.py:293
  54.1 14.5 %copy-start = (bf16[1024,1024]{1,0:T(8,128)(2,1)}, bf16[1024,1024]{1,0:T(8,128)(2,1)S(1)}, u32[]{:S(2)}) copy-start(bf16[1024,1024]{1,0:T(8,128)(2,1)S(1)} %collective-permute-done.3.refs_3_.refs_7_) | copy-start | bytes 6291460
  54.1 30.4 %collective-permute-start.4 = (bf16[1024,1024]{1,0:T(8,128)(2,1)S(1)}, bf16[1024,1024]{1,0:T(8,128)(2,1)}, u32[]{:S(2)}, u32[]{:S(2)}) collective-permute-start(bf16[1024,1024]{1,0:T(8,128)(2,1)S(1)} %collective-permute-done.3.refs_3_.refs_7_), channel_id=1, source_target_pairs={{0,1},{4,5},{8,9},{12,13},{5,4},{3,2},{7,6},{11,10},{15,14},{6,7},... | collective-permute-start | bytes 6291464 | tf_op jit(solution)/shard_map/ppermute | solution.py:293
  56.7 11.9 %copy-start.1 = (bf16[1024,1024]{1,0:T(8,128)(2,1)}, bf16[1024,1024]{1,0:T(8,128)(2,1)S(1)}, u32[]{:S(2)}) copy-start(bf16[1024,1024]{1,0:T(8,128)(2,1)S(1)} %collective-permute-done.1.refs_1_.refs_2_.refs_5_) | copy-start | bytes 6291460
  56.7 27.8 %collective-permute-start.5 = (bf16[1024,1024]{1,0:T(8,128)(2,1)S(1)}, bf16[1024,1024]{1,0:T(8,128)(2,1)}, u32[]{:S(2)}, u32[]{:S(2)}) collective-permute-start(bf16[1024,1024]{1,0:T(8,128)(2,1)S(1)} %collective-permute-done.1.refs_1_.refs_2_.refs_5_), channel_id=1, source_target_pairs={{1,0},{5,4},{9,8},{13,12},{4,5},{2,3},{6,7},{10,11},{14,15},{7,6},... | collective-permute-start | bytes 6291464 | tf_op jit(solution)/shard_map/ppermute | solution.py:293
  58.0 33.1 %collective-permute-start.8 = (bf16[1024,1024]{1,0:T(8,128)(2,1)}, bf16[1024,1024]{1,0:T(8,128)(2,1)}, u32[]{:S(2)}, u32[]{:S(2)}) collective-permute-start(bf16[1024,1024]{1,0:T(8,128)(2,1)} %get-tuple-element.10.unit.refs_1_.refs_4_.refs_9_), channel_id=1, source_target_pairs={{5,9},{9,13},{8,5},{6,10},{10,14},{11,6},{21,25},{25,29},{24,21},{... | collective-permute-start | bytes 6291464 | tf_op jit(solution)/shard_map/ppermute | solution.py:293
  60.0 8.6 %copy-start.2 = (bf16[1024,1024]{1,0:T(8,128)(2,1)}, bf16[1024,1024]{1,0:T(8,128)(2,1)S(1)}, u32[]{:S(2)}) copy-start(bf16[1024,1024]{1,0:T(8,128)(2,1)S(1)} %collective-permute-done.2.refs_2_.refs_3_.refs_6_) | copy-start | bytes 6291460
  60.0 31.1 %collective-permute-start.7 = (bf16[1024,1024]{1,0:T(8,128)(2,1)S(1)}, bf16[1024,1024]{1,0:T(8,128)(2,1)}, u32[]{:S(2)}, u32[]{:S(2)}) collective-permute-start(bf16[1024,1024]{1,0:T(8,128)(2,1)S(1)} %collective-permute-done.3.refs_3_.refs_7_), channel_id=1, source_target_pairs={{5,6},{6,5},{21,22},{22,21}} | collective-permute-start | bytes 6291464 | tf_op jit(solution)/shard_map/ppermute | solution.py:293
  62.0 29.1 %collective-permute-start.6 = (bf16[1024,1024]{1,0:T(8,128)(2,1)S(1)}, bf16[1024,1024]{1,0:T(8,128)(2,1)}, u32[]{:S(2)}, u32[]{:S(2)}) collective-permute-start(bf16[1024,1024]{1,0:T(8,128)(2,1)S(1)} %collective-permute-done.1.refs_1_.refs_2_.refs_5_), channel_id=1, source_target_pairs={{8,12},{11,15},{24,28},{27,31}} | collective-permute-start | bytes 6291464 | tf_op jit(solution)/shard_map/ppermute | solution.py:293

commit v3 on v2

v3 whole, which is shorter than its diff:
```python
import functools

import jax
import jax.numpy as jnp
import numpy as np
from jax import lax
from jax.experimental import pallas as pl
from jax.experimental.pallas import tpu as pltpu
from jax.sharding import PartitionSpec as P

STEPS = 6
VMEM = 56 * 2**20
FLOOR = -2.0


class Move:
    def __init__(self, name, source, pairs, stage):
        self.name, self.source, self.pairs, self.stage = name, source, pairs, stage


def grid_moves():
    def at(z, y, lane):
        return 4 * z + 2 * y + (y if lane == 0 else 1 - y)

    def rows(links):
        return [
            (at(z, y, lane), at(to, y, land)) for y in (0, 1) for (z, lane), (to, land) in links
        ]

    def across(planes):
        return [(at(z, y, lane), at(z, 1 - y, lane)) for z, lane in planes for y in (0, 1)]

    every = [(z, lane) for z in range(4) for lane in range(2)]
    cores = rows([((z, lane), (z, 1 - lane)) for z, lane in every])
    first = [((0, 0), (2, 0)), ((2, 0), (3, 0)), ((3, 0), (1, 0)), ((1, 0), (0, 0)), ((0, 1), (1, 1))]
    second = [((3, 1), (1, 1)), ((1, 1), (0, 1)), ((2, 1), (3, 1)), ((1, 0), (2, 0))]
    return [
        Move("R1", "own", rows(first), 1),
        Move("R2", "own", rows(second), 1),
        Move("Y", "own", across(every), 1),
        Move("A", "own", cores, 0),
        Move("V", "R1", rows([((2, 0), (3, 0))]) + across([(1, 1)]), 3),
        Move("R3", "late", rows([((1, 1), (2, 1)), ((2, 0), (1, 1))]), 3),
        Move("F", "Y", cores, 2),
        Move("W", "R1", rows([((1, 0), (1, 1)), ((1, 1), (1, 0))]), 2),
    ]


GRID_PAIRS = (
    ((0, 2), (0, 4), (1, 4), (2, 4), (3, 4)),
    ((0, 1), (0, 3), (0, 5), (3, 5)),
    ((0, 6), (1, 2), (1, 6), (3, 6)),
    ((1, 3), (1, 7), (2, 3), (3, 7)),
    ((1, 12), (4, 5), (4, 7), (5, 7), (6, 12), (7, 12)),
    ((1, 5), (1, 13), (2, 5), (2, 8), (2, 12), (2, 13), (5, 6), (6, 7), (7, 13)),
    ((1, 11), (1, 14), (1, 15), (2, 6), (2, 14), (4, 14), (5, 15), (11, 14)),
    ((2, 7), (2, 15), (4, 6), (4, 15)),
    ((0, 10), (0, 11), (4, 8), (4, 9), (4, 10)),
    ((5, 8), (5, 9), (5, 10), (5, 11), (8, 10), (8, 11), (9, 10)),
    ((6, 8), (6, 9), (6, 10), (6, 11), (8, 9), (9, 11)),
    ((3, 8), (3, 9), (7, 8), (7, 9), (7, 10), (7, 11), (10, 11)),
    ((0, 12), (0, 13), (0, 14), (0, 15), (8, 12), (8, 13), (8, 14), (12, 13), (13, 14)),
    ((9, 12), (9, 13), (9, 14), (9, 15), (12, 14)),
    ((10, 12), (10, 13), (10, 14), (10, 15), (12, 15), (14, 15)),
    ((3, 13), (3, 14), (3, 15), (11, 12), (11, 13), (11, 15), (13, 15)),
)


def ring_moves(count):
    return [
        Move("N%d" % k, "own", [((i + k) % count, i) for i in range(count)], k)
        for k in range(1, STEPS + 1)
    ]


def planned(count):
    if count == 16:
        moves, placed_pairs, sending = grid_moves(), GRID_PAIRS, (2, 3)
    else:
        moves, sending = ring_moves(count), (STEPS,)
        placed_pairs = [[(b, (b + k) % count) for k in range(1, STEPS + 1)] for b in range(count)]
    holds = {"own": {d: d for d in range(count)}}
    holds["late"] = holds["own"]
    stage_of = {"own": 0}
    for move in moves:
        holds[move.name] = {to: holds[move.source][of] for of, to in move.pairs}
        stage_of[move.name] = move.stage
    stages = 1 + max(stage_of.values())
    work = [[[] for _ in range(count)] for _ in range(stages)]
    for device, pairs in enumerate(placed_pairs):
        slot_of = {}
        for slot in sorted(stage_of, key=stage_of.get):
            if device in holds[slot]:
                slot_of.setdefault(holds[slot][device], slot)
        for block, visitor in pairs:
            slot, other = slot_of[block], slot_of[visitor]
            stage = max(stage_of[slot], stage_of[other])
            work[stage][device].append((slot, other, block, visitor))
    scored_pairs = sorted(tuple(sorted(pair)) for pairs in placed_pairs for pair in pairs)
    needed = {tuple(sorted((b, (b + k) % count))) for b in range(count) for k in range(1, STEPS + 1)}
    assert scored_pairs == sorted(needed)
    return moves, work, sending


def colored(edges, count):
    sends, takes = [{} for _ in range(count)], [{} for _ in range(count)]
    for of, to in edges:
        a = next(c for c in range(len(edges)) if c not in sends[of])
        b = next(c for c in range(len(edges)) if c not in takes[to])
        path, node, tables, colour = [], to, (takes, sends), a
        while a != b and colour in tables[0][node]:
            end = tables[0][node][colour]
            path.append(((end, node) if tables[0] is takes else (node, end), colour))
            node, tables, colour = end, tables[::-1], a + b - colour
        for (first, second), colour in path:
            del sends[first][colour], takes[second][colour]
        for (first, second), colour in path:
            sends[first][a + b - colour], takes[second][a + b - colour] = second, first
        sends[of][a], takes[to][a] = to, of
    return [
        [(of, to[c]) for of, to in enumerate(sends) if c in to]
        for c in range(max((c + 1 for to in sends for c in to), default=0))
    ]


def unit_kernel(order_smem, pads, order, embeddings, tile, unit):
    count = unit.shape[0]
    found = valid_rows(pads, order, pl.program_id(0) * count, count)
    among = lax.broadcasted_iota(jnp.int32, (16, 1), 0) == lax.rem(order_smem[0], 16)
    filler = jnp.sum(jnp.where(among, tile[...].astype(jnp.float32), 0.0), axis=0, keepdims=True)
    value = jnp.where(found, embeddings[...].astype(jnp.float32), filler)
    scale = lax.rsqrt(jnp.sum(value * value, axis=1, keepdims=True) + 1e-06)
    unit[...] = (value * scale).astype(jnp.bfloat16)


def valid_rows(pads, order, start, count):
    rows = order.shape[1]
    valid_count = rows - pads[lax.axis_index("blk")]
    position = lax.broadcasted_iota(jnp.int32, (1, rows), 1)
    kept = jnp.where(position < valid_count, order[...], -1)
    row = start + lax.broadcasted_iota(jnp.int32, (count, 1), 0)
    return jnp.max(jnp.where(kept == row, 1.0, 0.0), axis=1, keepdims=True) > 0.0


def normalized(embeddings, order, pad_counts):
    rows, depth = embeddings.shape
    count = 256
    return pl.pallas_call(
        unit_kernel,
        out_shape=jax.ShapeDtypeStruct((rows, depth), jnp.bfloat16),
        grid_spec=pltpu.PrefetchScalarGridSpec(
            num_scalar_prefetch=2,
            grid=(rows // count,),
            in_specs=[
                pl.BlockSpec((1, rows), lambda i, order, pads: (0, 0)),
                pl.BlockSpec((count, depth), lambda i, order, pads: (i, 0)),
                pl.BlockSpec((16, depth), lambda i, order, pads: (order[0] // 16, 0)),
            ],
            out_specs=pl.BlockSpec((count, depth), lambda i, order, pads: (i, 0)),
        ),
        compiler_params=pltpu.CompilerParams(vmem_limit_bytes=VMEM),
        cost_estimate=pl.CostEstimate(
            flops=4 * rows * depth, bytes_accessed=4 * rows * depth, transcendentals=rows
        ),
        name="normalized",
    )(order, pad_counts, order.reshape(1, rows), embeddings, embeddings)


def product(left, right):
    return lax.dot_general(left, right, (((1,), (1,)), ((), ())), preferred_element_type=jnp.float32)


def own_kernel(pads, order, unit, best):
    rows = unit.shape[0]
    best[...] = jnp.full(best.shape, FLOOR, jnp.float32)
    valid = valid_rows(pads, order, 0, rows)
    row = lax.broadcasted_iota(jnp.int32, (rows, 1), 0)
    here = pl.ds(lax.axis_index("blk"), 1)
    for start in range(0, rows, 256):
        part = pl.ds(start, 256)
        scores = product(unit[...], unit[part, :])
        column = start + lax.broadcasted_iota(jnp.int32, (1, 256), 1)
        scores = jnp.where(valid & (row != column), scores, FLOOR)
        best[here, part] = jnp.max(scores, axis=0, keepdims=True)


def own_block(unit, order, pad_counts, nblocks):
    rows, depth = unit.shape
    whole = pl.BlockSpec(memory_space=pltpu.VMEM)
    return pl.pallas_call(
        own_kernel,
        out_shape=jax.ShapeDtypeStruct((nblocks, rows), jnp.float32),
        in_specs=[pl.BlockSpec(memory_space=pltpu.SMEM), whole, whole],
        out_specs=whole,
        compiler_params=pltpu.CompilerParams(vmem_limit_bytes=VMEM),
        cost_estimate=pl.CostEstimate(
            flops=2 * rows * rows * depth, bytes_accessed=2 * rows * depth, transcendentals=0
        ),
        name="own_block",
    )(pad_counts, order.reshape(1, rows), unit)


def pairs_kernel(nslots, nsends, most, table, best, *refs):
    slots, out, sent = refs[:nslots], refs[nslots], refs[nslots + 1 : nslots + 1 + nsends]
    held, across, sems = refs[nslots + 1 + nsends :]
    rows = out.shape[1]
    at = lax.axis_index("blk") * (1 + nsends + 4 * most)
    steps = table[at]
    out[...] = best[...]

    def entry(step, which):
        return table[at + 1 + nsends + 4 * step + which]

    def fetch(step):
        for side in range(2):
            wanted = entry(step, side)
            for index, slot in enumerate(slots):
                @pl.when(wanted == index)
                def _(slot=slot, side=side):
                    pltpu.make_async_copy(slot, held.at[step % 2, side], sems.at[step % 2, side]).start()

    def arrived(step):
        for side in range(2):
            pltpu.make_async_copy(slots[0], held.at[step % 2, side], sems.at[step % 2, side]).wait()

    @pl.when(steps > 0)
    def _():
        fetch(0)

    @pl.loop(0, steps)
    def _(step):
        arrived(step)

        @pl.when(step + 1 < steps)
        def _():
            fetch(step + 1)

        now = step % 2
        first, second = pl.ds(entry(step, 2), 1), pl.ds(entry(step, 3), 1)
        for start in range(0, rows, 256):
            part = pl.ds(start, 256)
            scores = product(held[now, 0], held[now, 1, part, :])
            down = jnp.max(scores, axis=0, keepdims=True)
            out[second, part] = jnp.maximum(out[second, part], down)
            along = jnp.maximum(scores[:, :128], scores[:, 128:])
            across[...] = along if start == 0 else jnp.maximum(across[...], along)
        found = jnp.max(across[...].T, axis=0, keepdims=True)
        out[first, :] = jnp.maximum(out[first, :], found)

    for index, row in enumerate(sent):
        row[...] = out[pl.ds(table[at + 1 + index], 1), :]


def scored(best, slots, work, sends):
    names = sorted({slot for pairs in work for pair in pairs for slot in pair[:2]})
    most = max(len(pairs) for pairs in work)
    table = []
    for device, pairs in enumerate(work):
        table.append(len(pairs))
        table += [dict(permute).get(device, device) for permute in sends]
        for slot, other, block, visitor in pairs + [(names[0], names[0], 0, 0)] * (most - len(pairs)):
            table += [names.index(slot), names.index(other), block, visitor]
    given = [slots[name] for name in names]
    rows, depth = given[0].shape
    whole = pl.BlockSpec(memory_space=pltpu.VMEM)
    return pl.pallas_call(
        functools.partial(pairs_kernel, len(given), len(sends), most),
        out_shape=[jax.ShapeDtypeStruct(best.shape, jnp.float32)]
        + [jax.ShapeDtypeStruct((1, rows), jnp.float32)] * len(sends),
        in_specs=[pl.BlockSpec(memory_space=pltpu.SMEM), whole]
        + [pl.BlockSpec(memory_space=pl.ANY)] * len(given),
        out_specs=[whole] * (1 + len(sends)),
        scratch_shapes=[
            pltpu.VMEM((2, 2, rows, depth), jnp.bfloat16),
            pltpu.VMEM((rows, 128), jnp.float32),
            pltpu.SemaphoreType.DMA((2, 2)),
        ],
        compiler_params=pltpu.CompilerParams(vmem_limit_bytes=VMEM),
        cost_estimate=pl.CostEstimate(
            flops=2 * most * rows * rows * depth,
            bytes_accessed=4 * most * rows * depth,
            transcendentals=0,
        ),
        name="scored",
    )(jnp.asarray(np.array(table, np.int32)), best, *given)


def placed_kernel(taken, pads, order, best, *refs):
    found, out = refs[:-1], refs[-1]
    rows = order.shape[1]
    here = lax.axis_index("blk")
    total = best[pl.ds(here, 1), :]
    for index, row in enumerate(found):
        total = jnp.where(taken[here * len(found) + index] > 0, jnp.maximum(total, row[...]), total)
    column = jnp.broadcast_to(total, (128, rows)).T[:, :1]
    row = lax.broadcasted_iota(jnp.int32, (rows, 1), 0)
    in_order = jnp.max(jnp.where(order[...] == row, column, FLOOR), axis=0, keepdims=True)
    position = lax.broadcasted_iota(jnp.int32, (1, rows), 1)
    out[...] = jnp.where(position < rows - pads[here], in_order, 0.0)


def placed(best, found, permutes, order, pad_counts):
    rows = order.shape[0]
    taken = np.zeros((best.shape[0], len(permutes)), np.int32)
    for index, permute in enumerate(permutes):
        taken[[to for _, to in permute], index] = 1
    whole, scalars = pl.BlockSpec(memory_space=pltpu.VMEM), pl.BlockSpec(memory_space=pltpu.SMEM)
    return pl.pallas_call(
        placed_kernel,
        out_shape=jax.ShapeDtypeStruct((1, rows), jnp.float32),
        in_specs=[scalars, scalars] + [whole] * (2 + len(found)),
        out_specs=whole,
        compiler_params=pltpu.CompilerParams(vmem_limit_bytes=VMEM),
        name="placed",
    )(jnp.asarray(taken.reshape(-1)), pad_counts, order.reshape(1, rows), best, *found).reshape(rows)


def local(embeddings, order, pad_counts):
    nblocks = lax.axis_size("blk")
    moves, work, sending = planned(nblocks)
    unit = normalized(embeddings, order, pad_counts)
    slots = {"own": unit}
    best = own_block(unit, order, pad_counts, nblocks)
    touched, permutes, found = [set() for _ in range(nblocks)], [], []
    waiting = list(moves)
    for stage, pairs in enumerate(work):
        if stage == 1 and nblocks == 16:
            slots["late"], slots["R1"], best = lax.optimization_barrier((unit, slots["R1"], best))
        while waiting and waiting[0].source in slots:
            move = waiting.pop(0)
            slots[move.name] = lax.ppermute(slots[move.source], "blk", move.pairs)
            if move.name == "A":
                break
        for device, mine in enumerate(pairs):
            touched[device] |= {block for pair in mine for block in pair[2:] if block != device}
        sends = []
        if stage in sending:
            sends = colored([(of, to) for of in range(nblocks) for to in sorted(touched[of])], nblocks)
            touched = [set() for _ in range(nblocks)]
        if any(pairs):
            best, *rows = scored(best, slots, pairs, sends)
            found += [lax.ppermute(row, "blk", permute) for row, permute in zip(rows, sends)]
            permutes += sends
    return placed(best, found, permutes, order, pad_counts)


def solution(mesh):
    in_specs = (P(("groups", "blk"), None), P(("groups", "blk")), P("groups"))
    out_specs = P(("groups", "blk"))
    return jax.shard_map(local, mesh=mesh, in_specs=in_specs, out_specs=out_specs, check_vma=False)
```

time: 143 us -> 126 us (0.88)
  blocking collectives: 44.5 us -> 0 us
  starting transfers between devices: 17.9 us -> 44.5 us
  Pallas kernels: 37 us -> 35.2 us
  waiting for transfers between devices: 40.7 us -> 42.4 us
  local copies, waits for them, and re-layouts: 1.56 us -> 3.25 us
    all_to_all x1 -> x0, blocking collectives: 44.5 us -> none  [local(): lax.all_to_all(best, 'blk', 0, 0, tiled=True)]
    ppermute x9 -> x17, starting transfers between devices: 17.9 us -> 44.5 us  [the longest x9 30 us: local(): lax.ppermute(row, 'blk', permute)]
    unnamed x7 -> x36, local copies, waits for them, and re-layouts: 0.66 us -> 3.25 us
    pallas_call x5, Pallas kernels: 30.1 us -> 28.1 us  [the longest x4 23 us: scored(): pl.pallas_call(functools.partial(pairs_kernel, len(given), len(sends), mo...]
    ppermute x9 -> x17, waiting for transfers between devices: 40.7 us -> 42.4 us  [the longest x8 35.6 us: local(): slots[move.name] = lax.ppermute(slots[move.source], 'blk', move.pairs)]
  transfers between devices with their start and end apart: 9 -> 17, of which waited for: 1 -> 4; matrix products, arithmetic and copies ran while one was open for 0% -> 0% of each run, Pallas kernels for 19% -> 21%
where the time goes in v3:
time: 126 us
  starting transfers between devices  44.5 us (35%)
  waiting for transfers between devices  42.4 us (34%)
  Pallas kernels  35.2 us (28%)
  local copies, waits for them, and re-layouts  3.25 us (3%)
    ppermute x8, waiting for transfers between devices, local(): slots[move.name] = lax.ppermute(slots[move.source], 'blk', move.pairs)  35.6 us
    ppermute x9, starting transfers between devices, local(): lax.ppermute(row, 'blk', permute)  30 us
    pallas_call x4, Pallas kernels, scored(): pl.pallas_call(functools.partial(pairs_kernel, len(given), len(sends), mo...  23 us
    ppermute x8, starting transfers between devices, local(): slots[move.name] = lax.ppermute(slots[move.source], 'blk', move.pairs)  14.5 us
    ppermute x9, waiting for transfers between devices, local(): lax.ppermute(row, 'blk', permute)  6.83 us
    pallas_call x1, Pallas kernels, normalized(): pl.pallas_call(unit_kernel, out_shape=jax.ShapeDtypeStruct((rows, depth),...  5.16 us
    pallas_call x1, Pallas kernels, own_block(): pl.pallas_call(own_kernel, out_shape=jax.ShapeDtypeStruct((nblocks, rows)...  4.88 us
    unnamed x36, local copies, waits for them, and re-layouts  3.25 us
  transfers between devices with their start and end apart: 17, of which 4 were waited for; matrix products, arithmetic and copies ran while one was open for 0% of the time, Pallas kernels for 21%

profile of v3, /device:TPU:0, one launch (start us, length us, event | category | flops | bytes accessed | tf_op | source)
XLA Modules:
  0.0 125.8 jit_solution(13031063480172200493)
XLA Ops:
  0.0 5.2 %normalized.1.unit.refs_1_.refs_4_.refs_6_.refs_7_ = bf16[1024,1024]{1,0:T(8,128)(2,1)} custom-call(s32[1024]{0:T(1024)} %order_smem.1, s32[16]{0:T(128)} %pads.5, s32[1,1024]{1,0:T(1,128)} %bitcast.2, bf16[1024,1024]{1,0:T(8,128)(2,1)} %tile.1, bf16[1024,1024]{1,0:T(8,128)(2,1)} %tile.1), custom_call_target="tpu_custom_call" | custom-call | flops 4194304 | bytes 4194304 | tf_op jit(solution)/shard_map/normalized/pallas_call | solution.py:148
  5.6 5.5 %collective-permute-start = (bf16[1024,1024]{1,0:T(8,128)(2,1)}, bf16[1024,1024]{1,0:T(8,128)(2,1)}, u32[]{:S(2)}, u32[]{:S(2)}) collective-permute-start(bf16[1024,1024]{1,0:T(8,128)(2,1)} %normalized.1.unit.refs_1_.refs_4_.refs_6_.refs_7_), channel_id=1, source_target_pairs={{0,8},{8,12},{12,4},{4,0},{1,5},{3,11},{11,15},{15,7},{7,3},{2,6},... | collective-permute-start | bytes 6291464 | tf_op jit(solution)/shard_map/ppermute | solution.py:331
  11.1 1.4 %collective-permute-start.3 = (bf16[1024,1024]{1,0:T(8,128)(2,1)}, bf16[1024,1024]{1,0:T(8,128)(2,1)S(1)}, u32[]{:S(2)}, u32[]{:S(2)}) collective-permute-start(bf16[1024,1024]{1,0:T(8,128)(2,1)} %normalized.1.unit.refs_1_.refs_4_.refs_6_.refs_7_), channel_id=1, source_target_pairs={{0,3},{3,0},{1,2},{2,1},{4,7},{7,4},{5,6},{6,5},{8,11},{11,8},{9,1... | collective-permute-start | bytes 6291464 | tf_op jit(solution)/shard_map/ppermute | solution.py:331
  12.5 2.0 %collective-permute-start.2 = (bf16[1024,1024]{1,0:T(8,128)(2,1)}, bf16[1024,1024]{1,0:T(8,128)(2,1)}, u32[]{:S(2)}, u32[]{:S(2)}) collective-permute-start(bf16[1024,1024]{1,0:T(8,128)(2,1)} %normalized.1.unit.refs_1_.refs_4_.refs_6_.refs_7_), channel_id=1, source_target_pairs={{13,5},{5,1},{9,13},{4,8},{14,6},{6,2},{10,14},{7,11},{29,21},{21,... | collective-permute-start | bytes 6291464 | tf_op jit(solution)/shard_map/ppermute | solution.py:331
  14.5 4.9 %own_block.1.best = f32[16,1024]{1,0:T(8,128)} custom-call(s32[16]{0:T(128)} %pads.5, s32[1,1024]{1,0:T(1,128)} %bitcast.3, bf16[1024,1024]{1,0:T(8,128)(2,1)} %normalized.1.unit.refs_1_.refs_4_.refs_6_.refs_7_), custom_call_target="tpu_custom_call" | custom-call | flops 2147483648 | bytes 2097152 | tf_op jit(solution)/shard_map/own_block/pallas_call | solution.py:190
  19.4 1.4 %copy-done.10 = bf16[1024,1024]{1,0:T(8,128)(2,1)} copy-done((bf16[1024,1024]{1,0:T(8,128)(2,1)}, bf16[1024,1024]{1,0:T(8,128)(2,1)S(1)}, u32[]{:S(2)}) %copy-start.10) | copy-done | bytes 2097176
  20.8 1.5 %scored.4.best = f32[16,1024]{1,0:T(8,128)} custom-call(s32[80]{0:T(128)} %constant.10.clone.table, f32[16,1024]{1,0:T(8,128)} %own_block.1.best, bf16[1024,1024]{1,0:T(8,128)(2,1)} %copy-done.10, bf16[1024,1024]{1,0:T(8,128)(2,1)} %normalized.1.unit.refs_1_.refs_4_.refs_6_.refs_7_), custom_call_target="tpu_custom_call" | custom-call | flops 2147483648 | bytes 4194304 | tf_op jit(solution)/shard_map/scored/pallas_call | solution.py:266
  22.3 33.7 %collective-permute-done.refs_1_.refs_2_ = bf16[1024,1024]{1,0:T(8,128)(2,1)} collective-permute-done((bf16[1024,1024]{1,0:T(8,128)(2,1)}, bf16[1024,1024]{1,0:T(8,128)(2,1)}, u32[]{:S(2)}, u32[]{:S(2)}) %collective-permute-start) | collective-permute-done | bytes 2097184 | tf_op jit(solution)/shard_map/ppermute | solution.py:331
  56.0 0.8 collective-permute-start.5
  56.8 1.9 %collective-permute-done.3.refs_3_.refs_5_.refs_6_ = bf16[1024,1024]{1,0:T(8,128)(2,1)S(1)} collective-permute-done((bf16[1024,1024]{1,0:T(8,128)(2,1)}, bf16[1024,1024]{1,0:T(8,128)(2,1)S(1)}, u32[]{:S(2)}, u32[]{:S(2)}) %collective-permute-start.3) | collective-permute-done | bytes 2097184 | tf_op jit(solution)/shard_map/ppermute | solution.py:331
  59.1 2.0 %collective-permute-start.7 = (bf16[1024,1024]{1,0:T(8,128)(2,1)}, bf16[1024,1024]{1,0:T(8,128)(2,1)}, u32[]{:S(2)}, u32[]{:S(2)}) collective-permute-start(bf16[1024,1024]{1,0:T(8,128)(2,1)} %collective-permute-done.refs_1_.refs_2_), channel_id=1, source_target_pairs={{8,12},{11,15},{5,6},{6,5},{24,28},{27,31},{21,22},{22,21}} | collective-permute-start | bytes 6291464 | tf_op jit(solution)/shard_map/ppermute | solution.py:331
  61.1 2.0 %collective-permute-start.6 = (bf16[1024,1024]{1,0:T(8,128)(2,1)S(1)}, bf16[1024,1024]{1,0:T(8,128)(2,1)}, u32[]{:S(2)}, u32[]{:S(2)}) collective-permute-start(bf16[1024,1024]{1,0:T(8,128)(2,1)S(1)} %copy-done), channel_id=1, source_target_pairs={{5,9},{8,5},{6,10},{11,6},{21,25},{24,21},{22,26},{27,22}} | collective-permute-start | bytes 6291464 | tf_op jit(solution)/shard_map/ppermute | solution.py:331
  63.1 11.1 %scored.5.best = f32[16,1024]{1,0:T(8,128)} custom-call(s32[272]{0:T(512)} %constant.11.clone.table, f32[16,1024]{1,0:T(8,128)} %scored.4.best, bf16[1024,1024]{1,0:T(8,128)(2,1)} %copy-done.10, bf16[1024,1024]{1,0:T(8,128)(2,1)} %collective-permute-done.refs_1_.refs_2_, bf16[1024,1024]{1,0:T(8,128)(2,1)} %collective-permute-done.2.refs_2_.refs_3_, ...), custom_call_target="tpu_custom_call" | custom-call | flops 8589934592 | bytes 16777216 | tf_op jit(solution)/shard_map/scored/pallas_call | solution.py:266
  74.3 1.3 %copy-done.12 = bf16[1024,1024]{1,0:T(8,128)(2,1)} copy-done((bf16[1024,1024]{1,0:T(8,128)(2,1)}, bf16[1024,1024]{1,0:T(8,128)(2,1)S(1)}, u32[]{:S(2)}) %copy-start.12) | copy-done | bytes 2097176
  75.6 8.7 %scored.6 = (f32[16,1024]{1,0:T(8,128)}, f32[1,1024]{1,0:T(1,128)}, f32[1,1024]{1,0:T(1,128)}, f32[1,1024]{1,0:T(1,128)}, f32[1,1024]{1,0:T(1,128)}, /*index=5*/f32[1,1024]{1,0:T(1,128)}) custom-call(s32[224]{0:T(256)} %constant.12.clone.table, f32[16,1024]{1,0:T(8,128)} %scored.5.best, bf16[1024,1024]{1,0:T(8,128)(2,1)} %copy-done.10, ...), custom_call_target="tpu_custom_call" | custom-call | flops 4294967296 | bytes 8388608 | tf_op jit(solution)/shard_map/scored/pallas_call | solution.py:266
  84.4 1.6 %scored.7 = (f32[16,1024]{1,0:T(8,128)}, f32[1,1024]{1,0:T(1,128)}, f32[1,1024]{1,0:T(1,128)}, f32[1,1024]{1,0:T(1,128)}, f32[1,1024]{1,0:T(1,128)}) custom-call(s32[336]{0:T(512)} %constant.13.clone.table, f32[16,1024]{1,0:T(8,128)} %get-tuple-element.21.best, bf16[1024,1024]{1,0:T(8,128)(2,1)} %copy-done.10, ...), custom_call_target="tpu_custom_call" | custom-call | flops 8589934592 | bytes 16777216 | tf_op jit(solution)/shard_map/scored/pallas_call | solution.py:266
  86.7 1.3 %collective-permute-start.14 = (f32[1,1024]{1,0:T(1,128)}, f32[1,1024]{1,0:T(1,128)S(1)}, u32[]{:S(2)}, u32[]{:S(2)}) collective-permute-start(f32[1,1024]{1,0:T(1,128)} %get-tuple-element.30), channel_id=1, source_target_pairs={{5,2},{6,11},{9,10},{10,8},{12,0},{15,13},{21,18},{22,27},{25,26},... | collective-permute-start | bytes 12296 | tf_op jit(solution)/shard_map/ppermute | solution.py:342
  89.3 1.9 %collective-permute-start.10 = (f32[1,1024]{1,0:T(1,128)S(1)}, f32[1,1024]{1,0:T(1,128)S(1)}, u32[]{:S(2)}, u32[]{:S(2)}) collective-permute-start(f32[1,1024]{1,0:T(1,128)S(1)} %copy-done.17), channel_id=1, source_target_pairs={{0,1},{1,5},{2,0},{4,7},{5,6},{6,4},{7,2},{8,9},{9,11},{11,3},{12,... | collective-permute-start | bytes 12296 | tf_op jit(solution)/shard_map/ppermute | solution.py:342
  91.3 13.5 %collective-permute-start.11 = (f32[1,1024]{1,0:T(1,128)S(1)}, f32[1,1024]{1,0:T(1,128)S(1)}, u32[]{:S(2)}, u32[]{:S(2)}) collective-permute-start(f32[1,1024]{1,0:T(1,128)S(1)} %copy-done.16), channel_id=1, source_target_pairs={{0,3},{2,1},{3,7},{4,6},{5,13},{6,2},{7,15},{8,4},{10,8},{11,9},{1... | collective-permute-start | bytes 12296 | tf_op jit(solution)/shard_map/ppermute | solution.py:342
  104.7 2.0 %collective-permute-done.14.refs_6_ = f32[1,1024]{1,0:T(1,128)S(1)} collective-permute-done((f32[1,1024]{1,0:T(1,128)}, f32[1,1024]{1,0:T(1,128)S(1)}, u32[]{:S(2)}, u32[]{:S(2)}) %collective-permute-start.14) | collective-permute-done | bytes 4128 | tf_op jit(solution)/shard_map/ppermute | solution.py:342
  107.5 9.9 %collective-permute-start.8 = (f32[1,1024]{1,0:T(1,128)S(1)}, f32[1,1024]{1,0:T(1,128)S(1)}, u32[]{:S(2)}, u32[]{:S(2)}) collective-permute-start(f32[1,1024]{1,0:T(1,128)S(1)} %copy-done.14), channel_id=1, source_target_pairs={{0,2},{1,3},{2,6},{3,1},{4,12},{5,7},{6,5},{7,4},{8,0},{9,10},{10,... | collective-permute-start | bytes 12296 | tf_op jit(solution)/shard_map/ppermute | solution.py:342
  117.4 0.7 collective-permute-start.9
  118.2 4.8 %collective-permute-done.8.refs_0_ = f32[1,1024]{1,0:T(1,128)S(1)} collective-permute-done((f32[1,1024]{1,0:T(1,128)S(1)}, f32[1,1024]{1,0:T(1,128)S(1)}, u32[]{:S(2)}, u32[]{:S(2)}) %collective-permute-start.8) | collective-permute-done | bytes 4128 | tf_op jit(solution)/shard_map/ppermute | solution.py:342
  123.6 2.2 %placed.1 = f32[1,1024]{1,0:T(1,128)} custom-call(s32[144]{0:T(256)} %constant.14.clone.taken, s32[16]{0:T(128)} %pads.5, s32[1,1024]{1,0:T(1,128)} %bitcast.4, f32[16,1024]{1,0:T(8,128)} %get-tuple-element.23.best, f32[1,1024]{1,0:T(1,128)} %copy-done.8, f32[1,1024]{1,0:T(1,128)} %copy-done.9, f32[1,1024]{1,0:T(1,128)} %copy-done.5, f32[1,1024]{1,0:T(1,128)} %copy-done.6, ...), custom_call_target="tpu_custom_call" | custom-call | tf_op jit(solution)/shard_map/placed/pallas_call | solution.py:308
  (53 shorter events, 4.1 us)
Async XLA Ops:
  5.2 14.2 %collective-permute-start.1 = (bf16[1024,1024]{1,0:T(8,128)(2,1)}, bf16[1024,1024]{1,0:T(8,128)(2,1)S(1)}, u32[]{:S(2)}, u32[]{:S(2)}) collective-permute-start(bf16[1024,1024]{1,0:T(8,128)(2,1)} %normalized.1.unit.refs_1_.refs_4_.refs_6_.refs_7_), channel_id=1, source_target_pairs={{0,1},{1,0},{4,5},{5,4},{8,9},{9,8},{12,13},{13,12},{3,2},{2,3},{7... | collective-permute-start | bytes 6291464 | tf_op jit(solution)/shard_map/ppermute | solution.py:331
  5.6 50.4 %collective-permute-start = (bf16[1024,1024]{1,0:T(8,128)(2,1)}, bf16[1024,1024]{1,0:T(8,128)(2,1)}, u32[]{:S(2)}, u32[]{:S(2)}) collective-permute-start(bf16[1024,1024]{1,0:T(8,128)(2,1)} %normalized.1.unit.refs_1_.refs_4_.refs_6_.refs_7_), channel_id=1, source_target_pairs={{0,8},{8,12},{12,4},{4,0},{1,5},{3,11},{11,15},{15,7},{7,3},{2,6},... | collective-permute-start | bytes 6291464 | tf_op jit(solution)/shard_map/ppermute | solution.py:331
  11.1 47.6 %collective-permute-start.3 = (bf16[1024,1024]{1,0:T(8,128)(2,1)}, bf16[1024,1024]{1,0:T(8,128)(2,1)S(1)}, u32[]{:S(2)}, u32[]{:S(2)}) collective-permute-start(bf16[1024,1024]{1,0:T(8,128)(2,1)} %normalized.1.unit.refs_1_.refs_4_.refs_6_.refs_7_), channel_id=1, source_target_pairs={{0,3},{3,0},{1,2},{2,1},{4,7},{7,4},{5,6},{6,5},{8,11},{11,8},{9,1... | collective-permute-start | bytes 6291464 | tf_op jit(solution)/shard_map/ppermute | solution.py:331
  12.5 50.6 %collective-permute-start.2 = (bf16[1024,1024]{1,0:T(8,128)(2,1)}, bf16[1024,1024]{1,0:T(8,128)(2,1)}, u32[]{:S(2)}, u32[]{:S(2)}) collective-permute-start(bf16[1024,1024]{1,0:T(8,128)(2,1)} %normalized.1.unit.refs_1_.refs_4_.refs_6_.refs_7_), channel_id=1, source_target_pairs={{13,5},{5,1},{9,13},{4,8},{14,6},{6,2},{10,14},{7,11},{29,21},{21,... | collective-permute-start | bytes 6291464 | tf_op jit(solution)/shard_map/ppermute | solution.py:331
  19.4 41.7 %copy-start = (bf16[1024,1024]{1,0:T(8,128)(2,1)S(1)}, bf16[1024,1024]{1,0:T(8,128)(2,1)}, u32[]{:S(2)}) copy-start(bf16[1024,1024]{1,0:T(8,128)(2,1)} %normalized.1.unit.refs_1_.refs_4_.refs_6_.refs_7_) | copy-start | bytes 6291460
  56.0 18.3 %collective-permute-start.5 = (bf16[1024,1024]{1,0:T(8,128)(2,1)}, bf16[1024,1024]{1,0:T(8,128)(2,1)S(1)}, u32[]{:S(2)}, u32[]{:S(2)}) collective-permute-start(bf16[1024,1024]{1,0:T(8,128)(2,1)} %collective-permute-done.refs_1_.refs_2_), channel_id=1, source_target_pairs={{4,5},{5,4},{7,6},{6,7},{20,21},{21,20},{23,22},{22,23}} | collective-permute-start | bytes 6291464 | tf_op jit(solution)/shard_map/ppermute | solution.py:331
  58.7 15.6 %collective-permute-start.4 = (bf16[1024,1024]{1,0:T(8,128)(2,1)S(1)}, bf16[1024,1024]{1,0:T(8,128)(2,1)}, u32[]{:S(2)}, u32[]{:S(2)}) collective-permute-start(bf16[1024,1024]{1,0:T(8,128)(2,1)S(1)} %collective-permute-done.3.refs_3_.refs_5_.refs_6_), channel_id=1, source_target_pairs={{0,1},{1,0},{4,5},{5,4},{8,9},{9,8},{12,13},{13,12},{3,2},{2,3},{7... | collective-permute-start | bytes 6291464 | tf_op jit(solution)/shard_map/ppermute | solution.py:331
  59.1 25.2 %collective-permute-start.7 = (bf16[1024,1024]{1,0:T(8,128)(2,1)}, bf16[1024,1024]{1,0:T(8,128)(2,1)}, u32[]{:S(2)}, u32[]{:S(2)}) collective-permute-start(bf16[1024,1024]{1,0:T(8,128)(2,1)} %collective-permute-done.refs_1_.refs_2_), channel_id=1, source_target_pairs={{8,12},{11,15},{5,6},{6,5},{24,28},{27,31},{21,22},{22,21}} | collective-permute-start | bytes 6291464 | tf_op jit(solution)/shard_map/ppermute | solution.py:331
  61.1 23.2 %collective-permute-start.6 = (bf16[1024,1024]{1,0:T(8,128)(2,1)S(1)}, bf16[1024,1024]{1,0:T(8,128)(2,1)}, u32[]{:S(2)}, u32[]{:S(2)}) collective-permute-start(bf16[1024,1024]{1,0:T(8,128)(2,1)S(1)} %copy-done), channel_id=1, source_target_pairs={{5,9},{8,5},{6,10},{11,6},{21,25},{24,21},{22,26},{27,22}} | collective-permute-start | bytes 6291464 | tf_op jit(solution)/shard_map/ppermute | solution.py:331
  84.4 22.4 %copy-start.15 = (f32[1,1024]{1,0:T(1,128)S(1)}, f32[1,1024]{1,0:T(1,128)}, u32[]{:S(2)}) copy-start(f32[1,1024]{1,0:T(1,128)} %get-tuple-element.28) | copy-start | bytes 12292
  84.4 23.1 %copy-start.14 = (f32[1,1024]{1,0:T(1,128)S(1)}, f32[1,1024]{1,0:T(1,128)}, u32[]{:S(2)}) copy-start(f32[1,1024]{1,0:T(1,128)} %get-tuple-element.24) | copy-start | bytes 12292
  84.4 33.1 %copy-start.13 = (f32[1,1024]{1,0:T(1,128)S(1)}, f32[1,1024]{1,0:T(1,128)}, u32[]{:S(2)}) copy-start(f32[1,1024]{1,0:T(1,128)} %get-tuple-element.25) | copy-start | bytes 12292
  86.0 5.2 %collective-permute-start.13 = (f32[1,1024]{1,0:T(1,128)}, f32[1,1024]{1,0:T(1,128)S(1)}, u32[]{:S(2)}, u32[]{:S(2)}) collective-permute-start(f32[1,1024]{1,0:T(1,128)} %get-tuple-element.29), channel_id=1, source_target_pairs={{5,8},{6,15},{9,11},{10,6},{12,14},{15,3},{21,24},{22,31},{25,27},... | collective-permute-start | bytes 12296 | tf_op jit(solution)/shard_map/ppermute | solution.py:342
  86.7 20.1 %collective-permute-start.14 = (f32[1,1024]{1,0:T(1,128)}, f32[1,1024]{1,0:T(1,128)S(1)}, u32[]{:S(2)}, u32[]{:S(2)}) collective-permute-start(f32[1,1024]{1,0:T(1,128)} %get-tuple-element.30), channel_id=1, source_target_pairs={{5,2},{6,11},{9,10},{10,8},{12,0},{15,13},{21,18},{22,27},{25,26},... | collective-permute-start | bytes 12296 | tf_op jit(solution)/shard_map/ppermute | solution.py:342
  88.0 19.5 %collective-permute-start.15 = (f32[1,1024]{1,0:T(1,128)}, f32[1,1024]{1,0:T(1,128)S(1)}, u32[]{:S(2)}, u32[]{:S(2)}) collective-permute-start(f32[1,1024]{1,0:T(1,128)} %get-tuple-element.31), channel_id=1, source_target_pairs={{5,12},{6,1},{9,8},{10,9},{12,13},{15,14},{21,28},{22,17},{25,24},... | collective-permute-start | bytes 12296 | tf_op jit(solution)/shard_map/ppermute | solution.py:342
  88.6 28.8 %collective-permute-start.16 = (f32[1,1024]{1,0:T(1,128)}, f32[1,1024]{1,0:T(1,128)S(1)}, u32[]{:S(2)}, u32[]{:S(2)}) collective-permute-start(f32[1,1024]{1,0:T(1,128)} %get-tuple-element.32), channel_id=1, source_target_pairs={{5,13},{6,14},{9,5},{10,11},{12,15},{21,29},{22,30},{25,21},{26,27... | collective-permute-start | bytes 12296 | tf_op jit(solution)/shard_map/ppermute | solution.py:342
  89.3 28.9 %collective-permute-start.10 = (f32[1,1024]{1,0:T(1,128)S(1)}, f32[1,1024]{1,0:T(1,128)S(1)}, u32[]{:S(2)}, u32[]{:S(2)}) collective-permute-start(f32[1,1024]{1,0:T(1,128)S(1)} %copy-done.17), channel_id=1, source_target_pairs={{0,1},{1,5},{2,0},{4,7},{5,6},{6,4},{7,2},{8,9},{9,11},{11,3},{12,... | collective-permute-start | bytes 12296 | tf_op jit(solution)/shard_map/ppermute | solution.py:342
  91.2 31.7 %copy-start.1 = (f32[1,1024]{1,0:T(1,128)}, f32[1,1024]{1,0:T(1,128)S(1)}, u32[]{:S(2)}) copy-start(f32[1,1024]{1,0:T(1,128)S(1)} %collective-permute-done.13.refs_5_) | copy-start | bytes 12292
  91.3 26.9 %collective-permute-start.11 = (f32[1,1024]{1,0:T(1,128)S(1)}, f32[1,1024]{1,0:T(1,128)S(1)}, u32[]{:S(2)}, u32[]{:S(2)}) collective-permute-start(f32[1,1024]{1,0:T(1,128)S(1)} %copy-done.16), channel_id=1, source_target_pairs={{0,3},{2,1},{3,7},{4,6},{5,13},{6,2},{7,15},{8,4},{10,8},{11,9},{1... | collective-permute-start | bytes 12296 | tf_op jit(solution)/shard_map/ppermute | solution.py:342
  106.8 16.2 %copy-start.2 = (f32[1,1024]{1,0:T(1,128)}, f32[1,1024]{1,0:T(1,128)S(1)}, u32[]{:S(2)}) copy-start(f32[1,1024]{1,0:T(1,128)S(1)} %collective-permute-done.14.refs_6_) | copy-start | bytes 12292
  106.8 11.4 %collective-permute-start.12 = (f32[1,1024]{1,0:T(1,128)S(1)}, f32[1,1024]{1,0:T(1,128)S(1)}, u32[]{:S(2)}, u32[]{:S(2)}) collective-permute-start(f32[1,1024]{1,0:T(1,128)S(1)} %copy-done.15), channel_id=1, source_target_pairs={{4,1},{6,15},{8,11},{11,10},{20,17},{22,31},{24,27},{27,26}} | collective-permute-start | bytes 12296 | tf_op jit(solution)/shard_map/ppermute | solution.py:342
  107.5 15.5 %copy-start.3 = (f32[1,1024]{1,0:T(1,128)}, f32[1,1024]{1,0:T(1,128)S(1)}, u32[]{:S(2)}) copy-start(f32[1,1024]{1,0:T(1,128)S(1)} %collective-permute-done.15.refs_7_) | copy-start | bytes 12292
  107.5 15.5 %collective-permute-start.8 = (f32[1,1024]{1,0:T(1,128)S(1)}, f32[1,1024]{1,0:T(1,128)S(1)}, u32[]{:S(2)}, u32[]{:S(2)}) collective-permute-start(f32[1,1024]{1,0:T(1,128)S(1)} %copy-done.14), channel_id=1, source_target_pairs={{0,2},{1,3},{2,6},{3,1},{4,12},{5,7},{6,5},{7,4},{8,0},{9,10},{10,... | collective-permute-start | bytes 12296 | tf_op jit(solution)/shard_map/ppermute | solution.py:342
  117.4 5.5 %collective-permute-start.9 = (f32[1,1024]{1,0:T(1,128)S(1)}, f32[1,1024]{1,0:T(1,128)S(1)}, u32[]{:S(2)}, u32[]{:S(2)}) collective-permute-start(f32[1,1024]{1,0:T(1,128)S(1)} %copy-done.13), channel_id=1, source_target_pairs={{0,4},{1,0},{2,3},{3,2},{4,5},{5,1},{6,14},{7,6},{8,10},{9,8},{10,... | collective-permute-start | bytes 12296 | tf_op jit(solution)/shard_map/ppermute | solution.py:342
  (11 other events, 40.3 us)

commit v4 on v3

--- a/solution.py
+++ b/solution.py
@@ -9,13 +9,14 @@
 from jax.sharding import PartitionSpec as P
 
 STEPS = 6
-VMEM = 56 * 2**20
+VMEM = 62 * 2**20
 FLOOR = -2.0
 
 
 class Move:
-    def __init__(self, name, source, pairs, stage):
-        self.name, self.source, self.pairs, self.stage = name, source, pairs, stage
+    def __init__(self, name, source, pairs, begins, stage, *after):
+        self.name, self.source, self.pairs = name, source, pairs
+        self.begins, self.stage, self.needs = begins, stage, (source, *after)
 
 
 def grid_moves():
@@ -27,48 +28,50 @@
             (at(z, y, lane), at(to, y, land)) for y in (0, 1) for (z, lane), (to, land) in links
         ]
 
-    def across(planes):
-        return [(at(z, y, lane), at(z, 1 - y, lane)) for z, lane in planes for y in (0, 1)]
-
-    every = [(z, lane) for z in range(4) for lane in range(2)]
-    cores = rows([((z, lane), (z, 1 - lane)) for z, lane in every])
+    def across(planes, lane):
+        return [(at(z, y, lane), at(z, 1 - y, lane)) for z in planes for y in (0, 1)]
+
+    planes = range(4)
     first = [((0, 0), (2, 0)), ((2, 0), (3, 0)), ((3, 0), (1, 0)), ((1, 0), (0, 0)), ((0, 1), (1, 1))]
     second = [((3, 1), (1, 1)), ((1, 1), (0, 1)), ((2, 1), (3, 1)), ((1, 0), (2, 0))]
+    swap = [((z, lane), (z, 1 - lane)) for z in planes for lane in (0, 1)]
     return [
-        Move("R1", "own", rows(first), 1),
-        Move("R2", "own", rows(second), 1),
-        Move("Y", "own", across(every), 1),
-        Move("A", "own", cores, 0),
-        Move("V", "R1", rows([((2, 0), (3, 0))]) + across([(1, 1)]), 3),
-        Move("R3", "late", rows([((1, 1), (2, 1)), ((2, 0), (1, 1))]), 3),
-        Move("F", "Y", cores, 2),
-        Move("W", "R1", rows([((1, 0), (1, 1)), ((1, 1), (1, 0))]), 2),
+        Move("A", "own", rows(swap), 0, 0),
+        Move("R1", "own", rows(first), 0, 1),
+        Move("YX", "own", across(planes, 0), 0, 1),
+        Move("R2", "own", rows(second), 1, 2, "R1"),
+        Move("YN", "own", across(planes, 1), 1, 2, "R1"),
+        Move("V", "R1", rows([((2, 0), (3, 0))]) + across([1], 1), 1, 2),
+        Move("W", "R1", rows([((1, 0), (1, 1)), ((1, 1), (1, 0))]), 1, 1),
+        Move("FX", "YX", rows([((z, 0), (z, 1)) for z in planes]), 1, 1),
+        Move("R3", "own", rows([((1, 1), (2, 1)), ((2, 0), (1, 1))]), 2, 3, "R2"),
+        Move("FN", "YN", rows([((z, 1), (z, 0)) for z in planes]), 2, 2),
     ]
 
 
 GRID_PAIRS = (
-    ((0, 2), (0, 4), (1, 4), (2, 4), (3, 4)),
-    ((0, 1), (0, 3), (0, 5), (3, 5)),
-    ((0, 6), (1, 2), (1, 6), (3, 6)),
-    ((1, 3), (1, 7), (2, 3), (3, 7)),
-    ((1, 12), (4, 5), (4, 7), (5, 7), (6, 12), (7, 12)),
-    ((1, 5), (1, 13), (2, 5), (2, 8), (2, 12), (2, 13), (5, 6), (6, 7), (7, 13)),
-    ((1, 11), (1, 14), (1, 15), (2, 6), (2, 14), (4, 14), (5, 15), (11, 14)),
-    ((2, 7), (2, 15), (4, 6), (4, 15)),
-    ((0, 10), (0, 11), (4, 8), (4, 9), (4, 10)),
-    ((5, 8), (5, 9), (5, 10), (5, 11), (8, 10), (8, 11), (9, 10)),
-    ((6, 8), (6, 9), (6, 10), (6, 11), (8, 9), (9, 11)),
-    ((3, 8), (3, 9), (7, 8), (7, 9), (7, 10), (7, 11), (10, 11)),
-    ((0, 12), (0, 13), (0, 14), (0, 15), (8, 12), (8, 13), (8, 14), (12, 13), (13, 14)),
-    ((9, 12), (9, 13), (9, 14), (9, 15), (12, 14)),
-    ((10, 12), (10, 13), (10, 14), (10, 15), (12, 15), (14, 15)),
-    ((3, 13), (3, 14), (3, 15), (11, 12), (11, 13), (11, 15), (13, 15)),
+    ((0, 1), (0, 4), (1, 4), (3, 4)),
+    ((0, 5), (1, 3), (3, 5)),
+    ((0, 2), (0, 3), (0, 6), (2, 3), (3, 6)),
+    ((1, 2), (2, 7), (3, 7)),
+    ((1, 5), (1, 6), (1, 12), (4, 5), (6, 12)),
+    ((1, 7), (1, 13), (2, 8), (2, 12), (2, 13), (5, 7), (5, 8), (7, 12), (7, 13)),
+    ((1, 11), (1, 14), (1, 15), (2, 6), (2, 14), (2, 15), (4, 14), (4, 15), (6, 11)),
+    ((2, 4), (2, 5), (4, 6), (4, 7), (5, 6), (5, 15), (6, 7)),
+    ((0, 10), (0, 11), (4, 8), (4, 9), (4, 10), (8, 9), (8, 11), (9, 11)),
+    ((5, 9), (5, 10), (5, 11), (9, 10)),
+    ((6, 8), (6, 9), (6, 10)),
+    ((3, 8), (3, 9), (7, 8), (7, 9), (7, 10), (7, 11), (8, 10), (10, 11)),
+    ((0, 12), (0, 13), (0, 14), (0, 15), (8, 12), (8, 13), (8, 14)),
+    ((9, 12), (9, 13), (9, 14), (9, 15), (12, 13), (13, 15)),
+    ((10, 12), (10, 13), (10, 14), (10, 15), (12, 14), (12, 15)),
+    ((3, 13), (3, 14), (3, 15), (11, 12), (11, 13), (11, 14), (11, 15), (13, 14), (14, 15)),
 )
 
 
 def ring_moves(count):
     return [
-        Move("N%d" % k, "own", [((i + k) % count, i) for i in range(count)], k)
+        Move("N%d" % k, "own", [((i + k) % count, i) for i in range(count)], 0, k)
         for k in range(1, STEPS + 1)
     ]
 
@@ -80,7 +83,6 @@
         moves, sending = ring_moves(count), (STEPS,)
         placed_pairs = [[(b, (b + k) % count) for k in range(1, STEPS + 1)] for b in range(count)]
     holds = {"own": {d: d for d in range(count)}}
-    holds["late"] = holds["own"]
     stage_of = {"own": 0}
     for move in moves:
         holds[move.name] = {to: holds[move.source][of] for of, to in move.pairs}
@@ -123,14 +125,36 @@
     ]
 
 
-def unit_kernel(order_smem, pads, order, embeddings, tile, unit):
-    count = unit.shape[0]
-    found = valid_rows(pads, order, pl.program_id(0) * count, count)
-    among = lax.broadcasted_iota(jnp.int32, (16, 1), 0) == lax.rem(order_smem[0], 16)
+def unit_kernel(pads, order_smem, order, embeddings, unit, value, result, tile, into, out, sem):
+    rows = unit.shape[0]
+    count = rows // into.shape[0]
+    parts = [pl.ds(start, count) for start in range(0, rows, count)]
+    loads = [
+        pltpu.make_async_copy(embeddings.at[part], value.at[part], into.at[index])
+        for index, part in enumerate(parts)
+    ]
+    stores = [
+        pltpu.make_async_copy(result.at[part], unit.at[part], out.at[index])
+        for index, part in enumerate(parts)
+    ]
+    first = order_smem[0]
+    base = pl.multiple_of((first // 16) * 16, 16)
+    filling = pltpu.make_async_copy(embeddings.at[pl.ds(base, 16)], tile, sem)
+    filling.start()
+    for load in loads:
+        load.start()
+    filling.wait()
+    among = lax.broadcasted_iota(jnp.int32, (16, 1), 0) == first - base
     filler = jnp.sum(jnp.where(among, tile[...].astype(jnp.float32), 0.0), axis=0, keepdims=True)
-    value = jnp.where(found, embeddings[...].astype(jnp.float32), filler)
-    scale = lax.rsqrt(jnp.sum(value * value, axis=1, keepdims=True) + 1e-06)
-    unit[...] = (value * scale).astype(jnp.bfloat16)
+    for index, part in enumerate(parts):
+        found = valid_rows(pads, order, index * count, count)
+        loads[index].wait()
+        chunk = jnp.where(found, value[part, :].astype(jnp.float32), filler)
+        scale = lax.rsqrt(jnp.sum(chunk * chunk, axis=1, keepdims=True) + 1e-06)
+        result[part, :] = (chunk * scale).astype(jnp.bfloat16)
+        stores[index].start()
+    for store in stores:
+        store.wait()
 
 
 def valid_rows(pads, order, start, count):
@@ -144,26 +168,32 @@
 
 def normalized(embeddings, order, pad_counts):
     rows, depth = embeddings.shape
-    count = 256
+    chunks = 4
+    scalars = pl.BlockSpec(memory_space=pltpu.SMEM)
     return pl.pallas_call(
         unit_kernel,
         out_shape=jax.ShapeDtypeStruct((rows, depth), jnp.bfloat16),
-        grid_spec=pltpu.PrefetchScalarGridSpec(
-            num_scalar_prefetch=2,
-            grid=(rows // count,),
-            in_specs=[
-                pl.BlockSpec((1, rows), lambda i, order, pads: (0, 0)),
-                pl.BlockSpec((count, depth), lambda i, order, pads: (i, 0)),
-                pl.BlockSpec((16, depth), lambda i, order, pads: (order[0] // 16, 0)),
-            ],
-            out_specs=pl.BlockSpec((count, depth), lambda i, order, pads: (i, 0)),
-        ),
+        in_specs=[
+            scalars,
+            scalars,
+            pl.BlockSpec(memory_space=pltpu.VMEM),
+            pl.BlockSpec(memory_space=pl.ANY),
+        ],
+        out_specs=pl.BlockSpec(memory_space=pl.ANY),
+        scratch_shapes=[
+            pltpu.VMEM((rows, depth), jnp.bfloat16),
+            pltpu.VMEM((rows, depth), jnp.bfloat16),
+            pltpu.VMEM((16, depth), jnp.bfloat16),
+            pltpu.SemaphoreType.DMA((chunks,)),
+            pltpu.SemaphoreType.DMA((chunks,)),
+            pltpu.SemaphoreType.DMA,
+        ],
         compiler_params=pltpu.CompilerParams(vmem_limit_bytes=VMEM),
         cost_estimate=pl.CostEstimate(
             flops=4 * rows * depth, bytes_accessed=4 * rows * depth, transcendentals=rows
         ),
         name="normalized",
-    )(order, pad_counts, order.reshape(1, rows), embeddings, embeddings)
+    )(pad_counts, order, order.reshape(1, rows), embeddings)
 
 
 def product(left, right):
@@ -200,16 +230,20 @@
     )(pad_counts, order.reshape(1, rows), unit)
 
 
-def pairs_kernel(nslots, nsends, most, table, best, *refs):
-    slots, out, sent = refs[:nslots], refs[nslots], refs[nslots + 1 : nslots + 1 + nsends]
-    held, across, sems = refs[nslots + 1 + nsends :]
+def pairs_kernel(ntaken, nslots, nsends, most, table, best, *refs):
+    refs = list(refs)
+    arrivals, slots, (out, *sent) = (
+        [refs.pop(0) for _ in range(count)] for count in (ntaken, nslots, 1 + nsends)
+    )
+    held, across, sems = refs
     rows = out.shape[1]
-    at = lax.axis_index("blk") * (1 + nsends + 4 * most)
+    here = lax.axis_index("blk")
+    fixed = 1 + nsends + ntaken
+    at = here * (fixed + 4 * most)
     steps = table[at]
-    out[...] = best[...]
 
     def entry(step, which):
-        return table[at + 1 + nsends + 4 * step + which]
+        return table[at + fixed + 4 * step + which]
 
     def fetch(step):
         for side in range(2):
@@ -226,6 +260,12 @@
     @pl.when(steps > 0)
     def _():
         fetch(0)
+
+    out[...] = best[...]
+    own = pl.ds(here, 1)
+    for index, row in enumerate(arrivals):
+        taken = table[at + 1 + nsends + index] > 0
+        out[own, :] = jnp.where(taken, jnp.maximum(out[own, :], row[...]), out[own, :])
 
     @pl.loop(0, steps)
     def _(step):
@@ -251,23 +291,25 @@
         row[...] = out[pl.ds(table[at + 1 + index], 1), :]
 
 
-def scored(best, slots, work, sends):
+def scored(best, found, permutes, slots, work, sends):
     names = sorted({slot for pairs in work for pair in pairs for slot in pair[:2]})
     most = max(len(pairs) for pairs in work)
     table = []
     for device, pairs in enumerate(work):
         table.append(len(pairs))
         table += [dict(permute).get(device, device) for permute in sends]
+        table += [int(device in dict(permute).values()) for permute in permutes]
         for slot, other, block, visitor in pairs + [(names[0], names[0], 0, 0)] * (most - len(pairs)):
             table += [names.index(slot), names.index(other), block, visitor]
     given = [slots[name] for name in names]
     rows, depth = given[0].shape
     whole = pl.BlockSpec(memory_space=pltpu.VMEM)
     return pl.pallas_call(
-        functools.partial(pairs_kernel, len(given), len(sends), most),
+        functools.partial(pairs_kernel, len(found), len(given), len(sends), most),
         out_shape=[jax.ShapeDtypeStruct(best.shape, jnp.float32)]
         + [jax.ShapeDtypeStruct((1, rows), jnp.float32)] * len(sends),
-        in_specs=[pl.BlockSpec(memory_space=pltpu.SMEM), whole]
+        in_specs=[pl.BlockSpec(memory_space=pltpu.SMEM)]
+        + [whole] * (1 + len(found))
         + [pl.BlockSpec(memory_space=pl.ANY)] * len(given),
         out_specs=[whole] * (1 + len(sends)),
         scratch_shapes=[
@@ -282,7 +324,7 @@
             transcendentals=0,
         ),
         name="scored",
-    )(jnp.asarray(np.array(table, np.int32)), best, *given)
+    )(jnp.asarray(np.array(table, np.int32)), best, *found, *given)
 
 
 def placed_kernel(taken, pads, order, best, *refs):
@@ -319,18 +361,20 @@
     nblocks = lax.axis_size("blk")
     moves, work, sending = planned(nblocks)
     unit = normalized(embeddings, order, pad_counts)
-    slots = {"own": unit}
-    best = own_block(unit, order, pad_counts, nblocks)
+    slots, best = {"own": unit}, None
     touched, permutes, found = [set() for _ in range(nblocks)], [], []
-    waiting = list(moves)
     for stage, pairs in enumerate(work):
-        if stage == 1 and nblocks == 16:
-            slots["late"], slots["R1"], best = lax.optimization_barrier((unit, slots["R1"], best))
-        while waiting and waiting[0].source in slots:
-            move = waiting.pop(0)
-            slots[move.name] = lax.ppermute(slots[move.source], "blk", move.pairs)
-            if move.name == "A":
-                break
+        starting = [move for move in moves if move.begins == stage]
+        for needs in sorted({move.needs for move in starting}):
+            values = [slots[name] for name in needs]
+            if best is not None:
+                *values, best = lax.optimization_barrier((*values, best))
+            for move in starting:
+                if move.needs == needs:
+                    value = values[needs.index(move.source)]
+                    slots[move.name] = lax.ppermute(value, "blk", move.pairs)
+        if stage == 0:
+            best = own_block(unit, order, pad_counts, nblocks)
         for device, mine in enumerate(pairs):
             touched[device] |= {block for pair in mine for block in pair[2:] if block != device}
         sends = []
@@ -338,9 +382,9 @@
             sends = colored([(of, to) for of in range(nblocks) for to in sorted(touched[of])], nblocks)
             touched = [set() for _ in range(nblocks)]
         if any(pairs):
-            best, *rows = scored(best, slots, pairs, sends)
-            found += [lax.ppermute(row, "blk", permute) for row, permute in zip(rows, sends)]
-            permutes += sends
+            best, *rows = scored(best, found, permutes, slots, pairs, sends)
+            found = [lax.ppermute(row, "blk", permute) for row, permute in zip(rows, sends)]
+            permutes = sends
     return placed(best, found, permutes, order, pad_counts)
 
 

time: 126 us -> 162 us (1.29)
  the two profiles are of different devices: /device:TPU:0 before, /device:TPU:17 now
where the time goes in v4:
time: 162 us; the launch traced here: 161 us
  starting transfers between devices  71.4 us (44%)
  waiting for transfers between devices  56.7 us (35%)
  Pallas kernels  31.9 us (20%)
    ppermute x10, waiting for transfers between devices, local(): slots[move.name] = lax.ppermute(value, 'blk', move.pairs)  53.6 us
    ppermute x10, starting transfers between devices, local(): slots[move.name] = lax.ppermute(value, 'blk', move.pairs)  40.5 us
    ppermute x8, starting transfers between devices, local(): lax.ppermute(row, 'blk', permute)  30.8 us
    pallas_call x4, Pallas kernels, scored(): pl.pallas_call(functools.partial(pairs_kernel, len(found), len(given), le...  20.5 us
    pallas_call x1, Pallas kernels, own_block(): pl.pallas_call(own_kernel, out_shape=jax.ShapeDtypeStruct((nblocks, rows)...  4.86 us
    pallas_call x1, Pallas kernels, normalized(): pl.pallas_call(unit_kernel, out_shape=jax.ShapeDtypeStruct((rows, depth),...  4.42 us
  transfers between devices with their start and end apart: 18, of which 4 were waited for; matrix products, arithmetic and copies ran while one was open for 0% of the time, Pallas kernels for 9%

profile of v4, /device:TPU:17, one launch (start us, length us, event | category | flops | bytes accessed | tf_op | source)
XLA Modules:
  0.0 161.5 jit_solution(13085512128848767330)
XLA Ops:
  0.0 4.4 %normalized.1.unit.refs_1_.refs_5_.refs_9_ = bf16[1024,1024]{1,0:T(8,128)(2,1)} custom-call(s32[16]{0:T(128)} %pads.5, s32[1024]{0:T(1024)} %order_smem.1, s32[1,1024]{1,0:T(1,128)} %bitcast.2, bf16[1024,1024]{1,0:T(8,128)(2,1)} %embeddings.1), custom_call_target="tpu_custom_call" | custom-call | flops 4194304 | bytes 4194304 | tf_op jit(solution)/shard_map/normalized/pallas_call | solution.py:173
  5.2 2.0 %collective-permute-start = (bf16[1024,1024]{1,0:T(8,128)(2,1)}, bf16[1024,1024]{1,0:T(8,128)(2,1)}, u32[]{:S(2)}, u32[]{:S(2)}) collective-permute-start(bf16[1024,1024]{1,0:T(8,128)(2,1)} %normalized.1.unit.refs_1_.refs_5_.refs_9_), channel_id=1, source_target_pairs={{0,8},{8,12},{12,4},{4,0},{1,5},{3,11},{11,15},{15,7},{7,3},{2,6},... | collective-permute-start | bytes 6291464 | tf_op jit(solution)/shard_map/ppermute | solution.py:375
  7.1 2.0 %collective-permute-start.1 = (bf16[1024,1024]{1,0:T(8,128)(2,1)}, bf16[1024,1024]{1,0:T(8,128)(2,1)}, u32[]{:S(2)}, u32[]{:S(2)}) collective-permute-start(bf16[1024,1024]{1,0:T(8,128)(2,1)} %normalized.1.unit.refs_1_.refs_5_.refs_9_), channel_id=1, source_target_pairs={{0,3},{3,0},{4,7},{7,4},{8,11},{11,8},{12,15},{15,12},{16,19},{19,... | collective-permute-start | bytes 6291464 | tf_op jit(solution)/shard_map/ppermute | solution.py:375
  9.1 4.9 %own_block.1.best = f32[16,1024]{1,0:T(8,128)} custom-call(s32[16]{0:T(128)} %pads.5, s32[1,1024]{1,0:T(1,128)} %bitcast.3, bf16[1024,1024]{1,0:T(8,128)(2,1)} %normalized.1.unit.refs_1_.refs_5_.refs_9_), custom_call_target="tpu_custom_call" | custom-call | flops 2147483648 | bytes 2097152 | tf_op jit(solution)/shard_map/own_block/pallas_call | solution.py:220
  14.0 1.5 scored.4.best
  15.5 1.3 collective-permute-start.5
  16.8 2.0 %collective-permute-start.6 = (bf16[1024,1024]{1,0:T(8,128)(2,1)}, bf16[1024,1024]{1,0:T(8,128)(2,1)}, u32[]{:S(2)}, u32[]{:S(2)}) collective-permute-start(bf16[1024,1024]{1,0:T(8,128)(2,1)} %collective-permute-done.refs_2_.refs_3_), channel_id=1, source_target_pairs={{4,5},{5,4},{7,6},{6,7},{20,21},{21,20},{23,22},{22,23}} | collective-permute-start | bytes 6291464 | tf_op jit(solution)/shard_map/ppermute | solution.py:375
  18.8 3.1 %collective-permute-start.4 = (bf16[1024,1024]{1,0:T(8,128)(2,1)}, bf16[1024,1024]{1,0:T(8,128)(2,1)}, u32[]{:S(2)}, u32[]{:S(2)}) collective-permute-start(bf16[1024,1024]{1,0:T(8,128)(2,1)} %normalized.1.unit.refs_1_.refs_5_.refs_9_), channel_id=1, source_target_pairs={{1,2},{2,1},{5,6},{6,5},{9,10},{10,9},{13,14},{14,13},{17,18},{18,... | collective-permute-start | bytes 6291464 | tf_op jit(solution)/shard_map/ppermute | solution.py:375
  21.9 8.0 %collective-permute-start.3 = (bf16[1024,1024]{1,0:T(8,128)(2,1)}, bf16[1024,1024]{1,0:T(8,128)(2,1)}, u32[]{:S(2)}, u32[]{:S(2)}) collective-permute-start(bf16[1024,1024]{1,0:T(8,128)(2,1)} %normalized.1.unit.refs_1_.refs_5_.refs_9_), channel_id=1, source_target_pairs={{13,5},{5,1},{9,13},{4,8},{14,6},{6,2},{10,14},{7,11},{29,21},{21,... | collective-permute-start | bytes 6291464 | tf_op jit(solution)/shard_map/ppermute | solution.py:375
  29.9 2.0 %collective-permute-start.8 = (bf16[1024,1024]{1,0:T(8,128)(2,1)}, bf16[1024,1024]{1,0:T(8,128)(2,1)}, u32[]{:S(2)}, u32[]{:S(2)}) collective-permute-start(bf16[1024,1024]{1,0:T(8,128)(2,1)} %collective-permute-done.refs_2_.refs_3_), channel_id=1, source_target_pairs={{8,12},{11,15},{5,6},{6,5},{24,28},{27,31},{21,22},{22,21}} | collective-permute-start | bytes 6291464 | tf_op jit(solution)/shard_map/ppermute | solution.py:375
  32.0 28.6 %collective-permute-done.5.refs_1_.refs_2_.refs_5_ = bf16[1024,1024]{1,0:T(8,128)(2,1)} collective-permute-done((bf16[1024,1024]{1,0:T(8,128)(2,1)}, bf16[1024,1024]{1,0:T(8,128)(2,1)}, u32[]{:S(2)}, u32[]{:S(2)}) %collective-permute-start.5) | collective-permute-done | bytes 2097184 | tf_op jit(solution)/shard_map/ppermute | solution.py:375
  60.6 1.5 scored.5.best
  62.2 18.2 %collective-permute-start.7 = (bf16[1024,1024]{1,0:T(8,128)(2,1)}, bf16[1024,1024]{1,0:T(8,128)(2,1)}, u32[]{:S(2)}, u32[]{:S(2)}) collective-permute-start(bf16[1024,1024]{1,0:T(8,128)(2,1)} %collective-permute-done.4.refs_7_.refs_8_), channel_id=1, source_target_pairs={{1,0},{5,4},{9,8},{13,12},{2,3},{6,7},{10,11},{14,15},{17,16},{21,... | collective-permute-start | bytes 6291464 | tf_op jit(solution)/shard_map/ppermute | solution.py:375
  81.6 1.5 collective-permute-done.7.refs_1_
  83.1 6.2 %scored.6 = (f32[16,1024]{1,0:T(8,128)}, f32[1,1024]{1,0:T(1,128)}, f32[1,1024]{1,0:T(1,128)}, f32[1,1024]{1,0:T(1,128)}, f32[1,1024]{1,0:T(1,128)}, /*index=5*/f32[1,1024]{1,0:T(1,128)}) custom-call(s32[416]{0:T(512)} %constant.12.clone.table, f32[16,1024]{1,0:T(8,128)} %scored.5.best, bf16[1024,1024]{1,0:T(8,128)(2,1)} %collective-permute-done.2.refs_0_, ...), custom_call_target="tpu_custom_call" | custom-call | flops 10737418240 | bytes 20971520 | tf_op jit(solution)/shard_map/scored/pallas_call | solution.py:307
  89.3 1.3 collective-permute-start.10
  91.9 1.9 %collective-permute-start.12 = (f32[1,1024]{1,0:T(1,128)}, f32[1,1024]{1,0:T(1,128)S(1)}, u32[]{:S(2)}, u32[]{:S(2)}) collective-permute-start(f32[1,1024]{1,0:T(1,128)} %get-tuple-element.38), channel_id=1, source_target_pairs={{1,3},{3,1},{4,6},{5,12},{6,2},{7,4},{8,9},{9,10},{11,8},{12,0},{1... | collective-permute-start | bytes 12296 | tf_op jit(solution)/shard_map/ppermute | solution.py:386
  94.5 23.4 %collective-permute-done.14.refs_6_ = bf16[1024,1024]{1,0:T(8,128)(2,1)} collective-permute-done((bf16[1024,1024]{1,0:T(8,128)(2,1)}, bf16[1024,1024]{1,0:T(8,128)(2,1)}, u32[]{:S(2)}, u32[]{:S(2)}) %collective-permute-start.14) | collective-permute-done | bytes 2097184 | tf_op jit(solution)/shard_map/ppermute | solution.py:375
  119.3 11.2 %scored.7 = (f32[16,1024]{1,0:T(8,128)}, f32[1,1024]{1,0:T(1,128)}, f32[1,1024]{1,0:T(1,128)}, f32[1,1024]{1,0:T(1,128)}) custom-call(s32[336]{0:T(512)} %constant.13.clone.table, f32[16,1024]{1,0:T(8,128)} %get-tuple-element.34.best, f32[1,1024]{1,0:T(1,128)} %copy-done.7, f32[1,1024]{1,0:T(1,128)} %copy-done.3, f32[1,1024]{1,0:T(1,128)} %copy-done.4, ...), custom_call_target="tpu_custom_call" | custom-call | flops 6442450944 | bytes 12582912 | tf_op jit(solution)/shard_map/scored/pallas_call | solution.py:307
  130.5 20.2 %collective-permute-start.15 = (f32[1,1024]{1,0:T(1,128)}, f32[1,1024]{1,0:T(1,128)S(1)}, u32[]{:S(2)}, u32[]{:S(2)}) collective-permute-start(f32[1,1024]{1,0:T(1,128)} %get-tuple-element.42), channel_id=1, source_target_pairs={{5,8},{6,1},{9,5},{10,6},{21,24},{22,17},{25,21},{26,22}} | collective-permute-start | bytes 12296 | tf_op jit(solution)/shard_map/ppermute | solution.py:386
  150.7 2.8 %collective-permute-start.16 = (f32[1,1024]{1,0:T(1,128)}, f32[1,1024]{1,0:T(1,128)S(1)}, u32[]{:S(2)}, u32[]{:S(2)}) collective-permute-start(f32[1,1024]{1,0:T(1,128)} %get-tuple-element.43), channel_id=1, source_target_pairs={{5,2},{6,11},{9,10},{10,8},{21,18},{22,27},{25,26},{26,24}} | collective-permute-start | bytes 12296 | tf_op jit(solution)/shard_map/ppermute | solution.py:386
  153.6 1.9 %collective-permute-start.17 = (f32[1,1024]{1,0:T(1,128)}, f32[1,1024]{1,0:T(1,128)S(1)}, u32[]{:S(2)}, u32[]{:S(2)}) collective-permute-start(f32[1,1024]{1,0:T(1,128)} %get-tuple-element.44), channel_id=1, source_target_pairs={{9,11},{10,9},{25,27},{26,25}} | collective-permute-start | bytes 12296 | tf_op jit(solution)/shard_map/ppermute | solution.py:386
  155.5 3.2 %collective-permute-done.17.refs_2_ = f32[1,1024]{1,0:T(1,128)S(1)} collective-permute-done((f32[1,1024]{1,0:T(1,128)}, f32[1,1024]{1,0:T(1,128)S(1)}, u32[]{:S(2)}, u32[]{:S(2)}) %collective-permute-start.17) | collective-permute-done | bytes 4128 | tf_op jit(solution)/shard_map/ppermute | solution.py:386
  159.3 2.2 %placed.1 = f32[1,1024]{1,0:T(1,128)} custom-call(s32[48]{0:T(128)} %constant.14.clone.taken, s32[16]{0:T(128)} %pads.5, s32[1,1024]{1,0:T(1,128)} %bitcast.4, f32[16,1024]{1,0:T(8,128)} %get-tuple-element.41.best, f32[1,1024]{1,0:T(1,128)} %copy-done, f32[1,1024]{1,0:T(1,128)} %copy-done.1, f32[1,1024]{1,0:T(1,128)} %copy-done.2), custom_call_target="tpu_custom_call" | custom-call | tf_op jit(solution)/shard_map/placed/pallas_call | solution.py:350
  (35 shorter events, 5.8 us)
Async XLA Ops:
  4.4 9.5 %collective-permute-start.2 = (bf16[1024,1024]{1,0:T(8,128)(2,1)}, bf16[1024,1024]{1,0:T(8,128)(2,1)}, u32[]{:S(2)}, u32[]{:S(2)}) collective-permute-start(bf16[1024,1024]{1,0:T(8,128)(2,1)} %normalized.1.unit.refs_1_.refs_5_.refs_9_), channel_id=1, source_target_pairs={{0,1},{1,0},{4,5},{5,4},{8,9},{9,8},{12,13},{13,12},{3,2},{2,3},{7... | collective-permute-start | bytes 6291464 | tf_op jit(solution)/shard_map/ppermute | solution.py:375
  5.2 10.3 %collective-permute-start = (bf16[1024,1024]{1,0:T(8,128)(2,1)}, bf16[1024,1024]{1,0:T(8,128)(2,1)}, u32[]{:S(2)}, u32[]{:S(2)}) collective-permute-start(bf16[1024,1024]{1,0:T(8,128)(2,1)} %normalized.1.unit.refs_1_.refs_5_.refs_9_), channel_id=1, source_target_pairs={{0,8},{8,12},{12,4},{4,0},{1,5},{3,11},{11,15},{15,7},{7,3},{2,6},... | collective-permute-start | bytes 6291464 | tf_op jit(solution)/shard_map/ppermute | solution.py:375
  7.1 8.4 %collective-permute-start.1 = (bf16[1024,1024]{1,0:T(8,128)(2,1)}, bf16[1024,1024]{1,0:T(8,128)(2,1)}, u32[]{:S(2)}, u32[]{:S(2)}) collective-permute-start(bf16[1024,1024]{1,0:T(8,128)(2,1)} %normalized.1.unit.refs_1_.refs_5_.refs_9_), channel_id=1, source_target_pairs={{0,3},{3,0},{4,7},{7,4},{8,11},{11,8},{12,15},{15,12},{16,19},{19,... | collective-permute-start | bytes 6291464 | tf_op jit(solution)/shard_map/ppermute | solution.py:375
  15.5 45.1 %collective-permute-start.5 = (bf16[1024,1024]{1,0:T(8,128)(2,1)}, bf16[1024,1024]{1,0:T(8,128)(2,1)}, u32[]{:S(2)}, u32[]{:S(2)}) collective-permute-start(bf16[1024,1024]{1,0:T(8,128)(2,1)} %collective-permute-done.1.refs_4_.refs_8_), channel_id=1, source_target_pairs={{0,1},{4,5},{8,9},{12,13},{3,2},{7,6},{11,10},{15,14},{16,17},{20,... | collective-permute-start | bytes 6291464 | tf_op jit(solution)/shard_map/ppermute | solution.py:375
  16.8 43.8 %collective-permute-start.6 = (bf16[1024,1024]{1,0:T(8,128)(2,1)}, bf16[1024,1024]{1,0:T(8,128)(2,1)}, u32[]{:S(2)}, u32[]{:S(2)}) collective-permute-start(bf16[1024,1024]{1,0:T(8,128)(2,1)} %collective-permute-done.refs_2_.refs_3_), channel_id=1, source_target_pairs={{4,5},{5,4},{7,6},{6,7},{20,21},{21,20},{23,22},{22,23}} | collective-permute-start | bytes 6291464 | tf_op jit(solution)/shard_map/ppermute | solution.py:375
  18.8 43.3 %collective-permute-start.4 = (bf16[1024,1024]{1,0:T(8,128)(2,1)}, bf16[1024,1024]{1,0:T(8,128)(2,1)}, u32[]{:S(2)}, u32[]{:S(2)}) collective-permute-start(bf16[1024,1024]{1,0:T(8,128)(2,1)} %normalized.1.unit.refs_1_.refs_5_.refs_9_), channel_id=1, source_target_pairs={{1,2},{2,1},{5,6},{6,5},{9,10},{10,9},{13,14},{14,13},{17,18},{18,... | collective-permute-start | bytes 6291464 | tf_op jit(solution)/shard_map/ppermute | solution.py:375
  21.9 58.5 %collective-permute-start.3 = (bf16[1024,1024]{1,0:T(8,128)(2,1)}, bf16[1024,1024]{1,0:T(8,128)(2,1)}, u32[]{:S(2)}, u32[]{:S(2)}) collective-permute-start(bf16[1024,1024]{1,0:T(8,128)(2,1)} %normalized.1.unit.refs_1_.refs_5_.refs_9_), channel_id=1, source_target_pairs={{13,5},{5,1},{9,13},{4,8},{14,6},{6,2},{10,14},{7,11},{29,21},{21,... | collective-permute-start | bytes 6291464 | tf_op jit(solution)/shard_map/ppermute | solution.py:375
  29.9 51.7 %collective-permute-start.8 = (bf16[1024,1024]{1,0:T(8,128)(2,1)}, bf16[1024,1024]{1,0:T(8,128)(2,1)}, u32[]{:S(2)}, u32[]{:S(2)}) collective-permute-start(bf16[1024,1024]{1,0:T(8,128)(2,1)} %collective-permute-done.refs_2_.refs_3_), channel_id=1, source_target_pairs={{8,12},{11,15},{5,6},{6,5},{24,28},{27,31},{21,22},{22,21}} | collective-permute-start | bytes 6291464 | tf_op jit(solution)/shard_map/ppermute | solution.py:375
  62.2 20.9 %collective-permute-start.7 = (bf16[1024,1024]{1,0:T(8,128)(2,1)}, bf16[1024,1024]{1,0:T(8,128)(2,1)}, u32[]{:S(2)}, u32[]{:S(2)}) collective-permute-start(bf16[1024,1024]{1,0:T(8,128)(2,1)} %collective-permute-done.4.refs_7_.refs_8_), channel_id=1, source_target_pairs={{1,0},{5,4},{9,8},{13,12},{2,3},{6,7},{10,11},{14,15},{17,16},{21,... | collective-permute-start | bytes 6291464 | tf_op jit(solution)/shard_map/ppermute | solution.py:375
  80.3 37.6 %collective-permute-start.14 = (bf16[1024,1024]{1,0:T(8,128)(2,1)}, bf16[1024,1024]{1,0:T(8,128)(2,1)}, u32[]{:S(2)}, u32[]{:S(2)}) collective-permute-start(bf16[1024,1024]{1,0:T(8,128)(2,1)} %normalized.1.unit.refs_1_.refs_5_.refs_9_), channel_id=1, source_target_pairs={{5,9},{8,5},{6,10},{11,6},{21,25},{24,21},{22,26},{27,22}} | collective-permute-start | bytes 6291464 | tf_op jit(solution)/shard_map/ppermute | solution.py:375
  89.3 29.3 %collective-permute-start.10 = (f32[1,1024]{1,0:T(1,128)}, f32[1,1024]{1,0:T(1,128)S(1)}, u32[]{:S(2)}, u32[]{:S(2)}) collective-permute-start(f32[1,1024]{1,0:T(1,128)} %get-tuple-element.36), channel_id=1, source_target_pairs={{0,4},{1,5},{2,0},{3,2},{4,1},{5,7},{6,14},{7,15},{8,10},{11,3},{1... | collective-permute-start | bytes 12296 | tf_op jit(solution)/shard_map/ppermute | solution.py:386
  90.6 28.0 %collective-permute-start.11 = (f32[1,1024]{1,0:T(1,128)}, f32[1,1024]{1,0:T(1,128)S(1)}, u32[]{:S(2)}, u32[]{:S(2)}) collective-permute-start(f32[1,1024]{1,0:T(1,128)} %get-tuple-element.37), channel_id=1, source_target_pairs={{0,1},{2,3},{3,7},{5,2},{6,4},{7,5},{8,0},{11,9},{12,14},{13,15},{... | collective-permute-start | bytes 12296 | tf_op jit(solution)/shard_map/ppermute | solution.py:386
  91.9 26.7 %collective-permute-start.12 = (f32[1,1024]{1,0:T(1,128)}, f32[1,1024]{1,0:T(1,128)S(1)}, u32[]{:S(2)}, u32[]{:S(2)}) collective-permute-start(f32[1,1024]{1,0:T(1,128)} %get-tuple-element.38), channel_id=1, source_target_pairs={{1,3},{3,1},{4,6},{5,12},{6,2},{7,4},{8,9},{9,10},{11,8},{12,0},{1... | collective-permute-start | bytes 12296 | tf_op jit(solution)/shard_map/ppermute | solution.py:386
  93.8 24.8 %collective-permute-start.13 = (f32[1,1024]{1,0:T(1,128)}, f32[1,1024]{1,0:T(1,128)S(1)}, u32[]{:S(2)}, u32[]{:S(2)}) collective-permute-start(f32[1,1024]{1,0:T(1,128)} %get-tuple-element.39), channel_id=1, source_target_pairs={{0,3},{4,12},{5,13},{6,1},{7,6},{8,11},{11,10},{12,15},{15,14},{16... | collective-permute-start | bytes 12296 | tf_op jit(solution)/shard_map/ppermute | solution.py:386
  118.0 0.7 collective-permute-start.9
  118.6 0.6 copy-start.3
  118.6 0.6 copy-start.4
  118.7 0.6 copy-start.5
  118.7 0.6 copy-start.7
  130.5 25.0 %collective-permute-start.15 = (f32[1,1024]{1,0:T(1,128)}, f32[1,1024]{1,0:T(1,128)S(1)}, u32[]{:S(2)}, u32[]{:S(2)}) collective-permute-start(f32[1,1024]{1,0:T(1,128)} %get-tuple-element.42), channel_id=1, source_target_pairs={{5,8},{6,1},{9,5},{10,6},{21,24},{22,17},{25,21},{26,22}} | collective-permute-start | bytes 12296 | tf_op jit(solution)/shard_map/ppermute | solution.py:386
  150.7 4.8 %collective-permute-start.16 = (f32[1,1024]{1,0:T(1,128)}, f32[1,1024]{1,0:T(1,128)S(1)}, u32[]{:S(2)}, u32[]{:S(2)}) collective-permute-start(f32[1,1024]{1,0:T(1,128)} %get-tuple-element.43), channel_id=1, source_target_pairs={{5,2},{6,11},{9,10},{10,8},{21,18},{22,27},{25,26},{26,24}} | collective-permute-start | bytes 12296 | tf_op jit(solution)/shard_map/ppermute | solution.py:386
  153.6 5.1 %collective-permute-start.17 = (f32[1,1024]{1,0:T(1,128)}, f32[1,1024]{1,0:T(1,128)S(1)}, u32[]{:S(2)}, u32[]{:S(2)}) collective-permute-start(f32[1,1024]{1,0:T(1,128)} %get-tuple-element.44), channel_id=1, source_target_pairs={{9,11},{10,9},{25,27},{26,25}} | collective-permute-start | bytes 12296 | tf_op jit(solution)/shard_map/ppermute | solution.py:386
  155.5 3.2 %copy-start = (f32[1,1024]{1,0:T(1,128)}, f32[1,1024]{1,0:T(1,128)S(1)}, u32[]{:S(2)}) copy-start(f32[1,1024]{1,0:T(1,128)S(1)} %collective-permute-done.15.refs_0_) | copy-start | bytes 12292
  155.5 3.2 %copy-start.1 = (f32[1,1024]{1,0:T(1,128)}, f32[1,1024]{1,0:T(1,128)S(1)}, u32[]{:S(2)}) copy-start(f32[1,1024]{1,0:T(1,128)S(1)} %collective-permute-done.16.refs_1_) | copy-start | bytes 12292
  (2 other events, 1.2 us)

commit v5 on v4

--- a/solution.py
+++ b/solution.py
@@ -11,6 +11,7 @@
 STEPS = 6
 VMEM = 62 * 2**20
 FLOOR = -2.0
+MOST_PADS = 256
 
 
 class Move:
@@ -28,44 +29,42 @@
             (at(z, y, lane), at(to, y, land)) for y in (0, 1) for (z, lane), (to, land) in links
         ]
 
-    def across(planes, lane):
-        return [(at(z, y, lane), at(z, 1 - y, lane)) for z in planes for y in (0, 1)]
-
-    planes = range(4)
+    def across(planes):
+        return [(at(z, y, lane), at(z, 1 - y, lane)) for z, lane in planes for y in (0, 1)]
+
+    every = [(z, lane) for z in range(4) for lane in (0, 1)]
+    swap = rows([((z, lane), (z, 1 - lane)) for z, lane in every])
     first = [((0, 0), (2, 0)), ((2, 0), (3, 0)), ((3, 0), (1, 0)), ((1, 0), (0, 0)), ((0, 1), (1, 1))]
     second = [((3, 1), (1, 1)), ((1, 1), (0, 1)), ((2, 1), (3, 1)), ((1, 0), (2, 0))]
-    swap = [((z, lane), (z, 1 - lane)) for z in planes for lane in (0, 1)]
     return [
-        Move("A", "own", rows(swap), 0, 0),
         Move("R1", "own", rows(first), 0, 1),
-        Move("YX", "own", across(planes, 0), 0, 1),
-        Move("R2", "own", rows(second), 1, 2, "R1"),
-        Move("YN", "own", across(planes, 1), 1, 2, "R1"),
-        Move("V", "R1", rows([((2, 0), (3, 0))]) + across([1], 1), 1, 2),
+        Move("R2", "own", rows(second), 0, 1),
+        Move("Y", "own", across(every), 0, 1),
+        Move("A", "own", swap, 0, 0),
+        Move("R3", "own", rows([((1, 1), (2, 1)), ((2, 0), (1, 1))]), 1, 2, "R1"),
+        Move("V", "R1", rows([((2, 0), (3, 0))]) + across([(1, 1)]), 1, 2),
+        Move("F", "Y", swap, 1, 1),
         Move("W", "R1", rows([((1, 0), (1, 1)), ((1, 1), (1, 0))]), 1, 1),
-        Move("FX", "YX", rows([((z, 0), (z, 1)) for z in planes]), 1, 1),
-        Move("R3", "own", rows([((1, 1), (2, 1)), ((2, 0), (1, 1))]), 2, 3, "R2"),
-        Move("FN", "YN", rows([((z, 1), (z, 0)) for z in planes]), 2, 2),
     ]
 
 
 GRID_PAIRS = (
-    ((0, 1), (0, 4), (1, 4), (3, 4)),
-    ((0, 5), (1, 3), (3, 5)),
-    ((0, 2), (0, 3), (0, 6), (2, 3), (3, 6)),
-    ((1, 2), (2, 7), (3, 7)),
-    ((1, 5), (1, 6), (1, 12), (4, 5), (6, 12)),
-    ((1, 7), (1, 13), (2, 8), (2, 12), (2, 13), (5, 7), (5, 8), (7, 12), (7, 13)),
-    ((1, 11), (1, 14), (1, 15), (2, 6), (2, 14), (2, 15), (4, 14), (4, 15), (6, 11)),
-    ((2, 4), (2, 5), (4, 6), (4, 7), (5, 6), (5, 15), (6, 7)),
-    ((0, 10), (0, 11), (4, 8), (4, 9), (4, 10), (8, 9), (8, 11), (9, 11)),
-    ((5, 9), (5, 10), (5, 11), (9, 10)),
-    ((6, 8), (6, 9), (6, 10)),
-    ((3, 8), (3, 9), (7, 8), (7, 9), (7, 10), (7, 11), (8, 10), (10, 11)),
-    ((0, 12), (0, 13), (0, 14), (0, 15), (8, 12), (8, 13), (8, 14)),
-    ((9, 12), (9, 13), (9, 14), (9, 15), (12, 13), (13, 15)),
-    ((10, 12), (10, 13), (10, 14), (10, 15), (12, 14), (12, 15)),
-    ((3, 13), (3, 14), (3, 15), (11, 12), (11, 13), (11, 14), (11, 15), (13, 14), (14, 15)),
+    ((0, 1), (0, 4), (1, 2), (1, 4), (3, 4)),
+    ((0, 5), (1, 5), (2, 5), (3, 5)),
+    ((0, 2), (0, 6), (1, 6), (2, 6), (3, 6)),
+    ((0, 3), (1, 3), (2, 3), (2, 7), (3, 7)),
+    ((1, 7), (4, 5), (4, 7), (5, 6), (7, 12)),
+    ((1, 12), (1, 13), (2, 8), (2, 12), (2, 13), (6, 12), (7, 13), (8, 13)),
+    ((1, 11), (1, 14), (1, 15), (2, 4), (2, 14), (4, 14), (4, 15), (6, 7), (11, 15)),
+    ((2, 15), (4, 6), (5, 7), (5, 15)),
+    ((0, 10), (0, 11), (4, 8), (4, 9), (4, 10)),
+    ((5, 8), (5, 9), (5, 10), (5, 11), (8, 9), (8, 11), (9, 11)),
+    ((6, 8), (6, 9), (6, 10), (6, 11), (8, 10), (9, 10)),
+    ((3, 8), (3, 9), (7, 8), (7, 9), (7, 10), (7, 11), (10, 11)),
+    ((0, 12), (0, 13), (0, 14), (0, 15), (8, 12), (8, 14), (12, 13), (13, 14), (13, 15)),
+    ((9, 12), (9, 13), (9, 14), (9, 15), (12, 14)),
+    ((10, 12), (10, 13), (10, 14), (10, 15)),
+    ((3, 13), (3, 14), (3, 15), (11, 12), (11, 13), (11, 14), (12, 15), (14, 15)),
 )
 
 
@@ -78,9 +77,9 @@
 
 def planned(count):
     if count == 16:
-        moves, placed_pairs, sending = grid_moves(), GRID_PAIRS, (2, 3)
+        moves, placed_pairs = grid_moves(), GRID_PAIRS
     else:
-        moves, sending = ring_moves(count), (STEPS,)
+        moves = ring_moves(count)
         placed_pairs = [[(b, (b + k) % count) for k in range(1, STEPS + 1)] for b in range(count)]
     holds = {"own": {d: d for d in range(count)}}
     stage_of = {"own": 0}
@@ -101,7 +100,7 @@
     scored_pairs = sorted(tuple(sorted(pair)) for pairs in placed_pairs for pair in pairs)
     needed = {tuple(sorted((b, (b + k) % count))) for b in range(count) for k in range(1, STEPS + 1)}
     assert scored_pairs == sorted(needed)
-    return moves, work, sending
+    return moves, work
 
 
 def colored(edges, count):
@@ -159,11 +158,12 @@
 
 def valid_rows(pads, order, start, count):
     rows = order.shape[1]
+    most = min(rows, MOST_PADS)
     valid_count = rows - pads[lax.axis_index("blk")]
-    position = lax.broadcasted_iota(jnp.int32, (1, rows), 1)
-    kept = jnp.where(position < valid_count, order[...], -1)
+    position = rows - most + lax.broadcasted_iota(jnp.int32, (1, most), 1)
+    padding = jnp.where(position < valid_count, -1, order[:, rows - most :])
     row = start + lax.broadcasted_iota(jnp.int32, (count, 1), 0)
-    return jnp.max(jnp.where(kept == row, 1.0, 0.0), axis=1, keepdims=True) > 0.0
+    return jnp.max(jnp.where(padding == row, 1.0, 0.0), axis=1, keepdims=True) < 1.0
 
 
 def normalized(embeddings, order, pad_counts):
@@ -230,16 +230,13 @@
     )(pad_counts, order.reshape(1, rows), unit)
 
 
-def pairs_kernel(ntaken, nslots, nsends, most, table, best, *refs):
+def pairs_kernel(nslots, nrows, most, fresh, table, *refs):
     refs = list(refs)
-    arrivals, slots, (out, *sent) = (
-        [refs.pop(0) for _ in range(count)] for count in (ntaken, nslots, 1 + nsends)
-    )
-    held, across, sems = refs
+    best = None if fresh else refs.pop(0)
+    slots, out, sent, (held, across, sems) = refs[:nslots], refs[nslots], refs[nslots + 1 : -3], refs[-3:]
     rows = out.shape[1]
-    here = lax.axis_index("blk")
-    fixed = 1 + nsends + ntaken
-    at = here * (fixed + 4 * most)
+    fixed = 1 + nrows
+    at = lax.axis_index("blk") * (fixed + 4 * most)
     steps = table[at]
 
     def entry(step, which):
@@ -261,11 +258,7 @@
     def _():
         fetch(0)
 
-    out[...] = best[...]
-    own = pl.ds(here, 1)
-    for index, row in enumerate(arrivals):
-        taken = table[at + 1 + nsends + index] > 0
-        out[own, :] = jnp.where(taken, jnp.maximum(out[own, :], row[...]), out[own, :])
+    out[...] = jnp.full(out.shape, FLOOR, jnp.float32) if fresh else best[...]
 
     @pl.loop(0, steps)
     def _(step):
@@ -277,41 +270,53 @@
 
         now = step % 2
         first, second = pl.ds(entry(step, 2), 1), pl.ds(entry(step, 3), 1)
-        for start in range(0, rows, 256):
+
+        def maxima(start, scores):
             part = pl.ds(start, 256)
-            scores = product(held[now, 0], held[now, 1, part, :])
             down = jnp.max(scores, axis=0, keepdims=True)
             out[second, part] = jnp.maximum(out[second, part], down)
             along = jnp.maximum(scores[:, :128], scores[:, 128:])
             across[...] = along if start == 0 else jnp.maximum(across[...], along)
+
+        last = None
+        for start in range(0, rows, 256):
+            scores = product(held[now, 0], held[now, 1, pl.ds(start, 256), :])
+            if last is not None:
+                maxima(*last)
+            last = (start, scores)
+        maxima(*last)
         found = jnp.max(across[...].T, axis=0, keepdims=True)
         out[first, :] = jnp.maximum(out[first, :], found)
 
-    for index, row in enumerate(sent):
-        row[...] = out[pl.ds(table[at + 1 + index], 1), :]
-
-
-def scored(best, found, permutes, slots, work, sends):
+    for index in range(nrows):
+        row = out[pl.ds(table[at + 1 + index], 1), :]
+        if len(sent) == nrows:
+            sent[index][...] = row
+        else:
+            sent[0][pl.ds(index, 1), :] = row
+
+
+def scored(best, slots, work, taken, split):
     names = sorted({slot for pairs in work for pair in pairs for slot in pair[:2]})
     most = max(len(pairs) for pairs in work)
+    nrows = max(len(blocks) for blocks in taken)
     table = []
     for device, pairs in enumerate(work):
-        table.append(len(pairs))
-        table += [dict(permute).get(device, device) for permute in sends]
-        table += [int(device in dict(permute).values()) for permute in permutes]
+        table += [len(pairs)] + list(taken[device]) + [device] * (nrows - len(taken[device]))
         for slot, other, block, visitor in pairs + [(names[0], names[0], 0, 0)] * (most - len(pairs)):
             table += [names.index(slot), names.index(other), block, visitor]
     given = [slots[name] for name in names]
     rows, depth = given[0].shape
     whole = pl.BlockSpec(memory_space=pltpu.VMEM)
-    return pl.pallas_call(
-        functools.partial(pairs_kernel, len(found), len(given), len(sends), most),
-        out_shape=[jax.ShapeDtypeStruct(best.shape, jnp.float32)]
-        + [jax.ShapeDtypeStruct((1, rows), jnp.float32)] * len(sends),
+    before = [] if best is None else [best]
+    out, *sent = pl.pallas_call(
+        functools.partial(pairs_kernel, len(given), nrows, most, best is None),
+        out_shape=[jax.ShapeDtypeStruct((len(work), rows), jnp.float32)]
+        + [jax.ShapeDtypeStruct((1 if split else nrows, rows), jnp.float32)] * (nrows if split else 1),
         in_specs=[pl.BlockSpec(memory_space=pltpu.SMEM)]
-        + [whole] * (1 + len(found))
+        + [whole] * len(before)
         + [pl.BlockSpec(memory_space=pl.ANY)] * len(given),
-        out_specs=[whole] * (1 + len(sends)),
+        out_specs=[whole] * (1 + (nrows if split else 1)),
         scratch_shapes=[
             pltpu.VMEM((2, 2, rows, depth), jnp.bfloat16),
             pltpu.VMEM((rows, 128), jnp.float32),
@@ -324,16 +329,28 @@
             transcendentals=0,
         ),
         name="scored",
-    )(jnp.asarray(np.array(table, np.int32)), best, *found, *given)
-
-
-def placed_kernel(taken, pads, order, best, *refs):
-    found, out = refs[:-1], refs[-1]
+    )(jnp.asarray(np.array(table, np.int32)), *before, *given)
+    return out, sent
+
+
+def placed_kernel(ngathered, taken, pads, order, *refs):
+    refs = list(refs)
+    out, gathered = refs.pop(), refs.pop(0) if ngathered else None
+    here = lax.axis_index("blk")
     rows = order.shape[1]
-    here = lax.axis_index("blk")
-    total = best[pl.ds(here, 1), :]
-    for index, row in enumerate(found):
-        total = jnp.where(taken[here * len(found) + index] > 0, jnp.maximum(total, row[...]), total)
+    own = [ref for ref in refs if ref.shape[0] > 1]
+    found = [ref for ref in refs if ref.shape[0] == 1]
+    at = here * (1 + 2 * ngathered + len(found))
+    total = jnp.full((1, rows), FLOOR, jnp.float32)
+    for ref in own:
+        total = jnp.maximum(total, ref[pl.ds(here, 1), :])
+    for index in range(ngathered):
+        entry = at + 1 + 2 * index
+        row = gathered[taken[entry], pl.ds(taken[entry + 1], 1), :]
+        total = jnp.where(index < taken[at], jnp.maximum(total, row), total)
+    for index, ref in enumerate(found):
+        handed = taken[at + 1 + 2 * ngathered + index] > 0
+        total = jnp.where(handed, jnp.maximum(total, ref[...]), total)
     column = jnp.broadcast_to(total, (128, rows)).T[:, :1]
     row = lax.broadcasted_iota(jnp.int32, (rows, 1), 0)
     in_order = jnp.max(jnp.where(order[...] == row, column, FLOOR), axis=0, keepdims=True)
@@ -341,28 +358,39 @@
     out[...] = jnp.where(position < rows - pads[here], in_order, 0.0)
 
 
-def placed(best, found, permutes, order, pad_counts):
+def placed(bests, gathered, handed, found, permutes, order, pad_counts):
     rows = order.shape[0]
-    taken = np.zeros((best.shape[0], len(permutes)), np.int32)
-    for index, permute in enumerate(permutes):
-        taken[[to for _, to in permute], index] = 1
+    count = bests[0].shape[0]
+    entries = [
+        [(device, index) for device in range(count) for index, b in enumerate(handed[device]) if b == mine]
+        for mine in range(count)
+    ]
+    most = max(len(mine) for mine in entries)
+    taken = []
+    for mine in range(count):
+        taken.append(len(entries[mine]))
+        for entry in entries[mine] + [(0, 0)] * (most - len(entries[mine])):
+            taken += entry
+        taken += [int(mine in dict(permute).values()) for permute in permutes]
     whole, scalars = pl.BlockSpec(memory_space=pltpu.VMEM), pl.BlockSpec(memory_space=pltpu.SMEM)
+    given = [order.reshape(1, rows)] + [gathered] * (most > 0) + bests + found
     return pl.pallas_call(
-        placed_kernel,
+        functools.partial(placed_kernel, most),
         out_shape=jax.ShapeDtypeStruct((1, rows), jnp.float32),
-        in_specs=[scalars, scalars] + [whole] * (2 + len(found)),
+        in_specs=[scalars, scalars] + [whole] * len(given),
         out_specs=whole,
         compiler_params=pltpu.CompilerParams(vmem_limit_bytes=VMEM),
         name="placed",
-    )(jnp.asarray(taken.reshape(-1)), pad_counts, order.reshape(1, rows), best, *found).reshape(rows)
+    )(jnp.asarray(np.array(taken, np.int32)), pad_counts, *given).reshape(rows)
 
 
 def local(embeddings, order, pad_counts):
     nblocks = lax.axis_size("blk")
-    moves, work, sending = planned(nblocks)
+    moves, work = planned(nblocks)
     unit = normalized(embeddings, order, pad_counts)
     slots, best = {"own": unit}, None
-    touched, permutes, found = [set() for _ in range(nblocks)], [], []
+    nothing = [[] for _ in range(nblocks)]
+    touched, gathered, handed, bests = [set() for _ in range(nblocks)], None, nothing, []
     for stage, pairs in enumerate(work):
         starting = [move for move in moves if move.begins == stage]
         for needs in sorted({move.needs for move in starting}):
@@ -377,15 +405,21 @@
             best = own_block(unit, order, pad_counts, nblocks)
         for device, mine in enumerate(pairs):
             touched[device] |= {block for pair in mine for block in pair[2:] if block != device}
-        sends = []
-        if stage in sending:
-            sends = colored([(of, to) for of in range(nblocks) for to in sorted(touched[of])], nblocks)
-            touched = [set() for _ in range(nblocks)]
-        if any(pairs):
-            best, *rows = scored(best, found, permutes, slots, pairs, sends)
-            found = [lax.ppermute(row, "blk", permute) for row, permute in zip(rows, sends)]
-            permutes = sends
-    return placed(best, found, permutes, order, pad_counts)
+        if stage == len(work) - 1:
+            edges = [(of, to) for of in range(nblocks) for to in sorted(touched[of])]
+            permutes = colored(edges, nblocks)
+            rows = [[dict(permute).get(device, device) for permute in permutes] for device in range(nblocks)]
+            bests = [best] * (gathered is not None)
+            best, sent = scored(None if bests else best, slots, pairs, rows, True)
+            found = [lax.ppermute(row, "blk", permute) for row, permute in zip(sent, permutes)]
+        elif any(pairs):
+            last = nblocks == 16 and stage == len(work) - 2
+            handed = [sorted(mine) for mine in touched] if last else nothing
+            best, sent = scored(best, slots, pairs, handed if last else [[d] for d in range(nblocks)], False)
+            if last:
+                gathered = lax.all_gather(sent[0], "blk")
+                touched = [set() for _ in range(nblocks)]
+    return placed(bests + [best], gathered, handed, found, permutes, order, pad_counts)
 
 
 def solution(mesh):

time: 162 us -> 145 us (0.90)
  the two profiles are of different devices: /device:TPU:17 before, /device:TPU:0 now
where the time goes in v5:
time: 145 us; the launch traced here: 144 us
  blocking collectives  58.2 us (40%)
  waiting for transfers between devices  33.6 us (23%)
  Pallas kernels  32.4 us (22%)
  starting transfers between devices  19.1 us (13%)
    all_gather x1, blocking collectives, local(): gathered = lax.all_gather(sent[0], 'blk')  58.2 us
    ppermute x8, waiting for transfers between devices, local(): slots[move.name] = lax.ppermute(value, 'blk', move.pairs)  33.5 us
    pallas_call x3, Pallas kernels, scored(): pl.pallas_call(functools.partial(pairs_kernel, len(given), nrows, most, b...  21.2 us
    ppermute x8, starting transfers between devices, local(): slots[move.name] = lax.ppermute(value, 'blk', move.pairs)  15.8 us
    pallas_call x1, Pallas kernels, own_block(): pl.pallas_call(own_kernel, out_shape=jax.ShapeDtypeStruct((nblocks, rows)...  4.64 us
    pallas_call x1, Pallas kernels, normalized(): pl.pallas_call(unit_kernel, out_shape=jax.ShapeDtypeStruct((rows, depth),...  4.13 us
    ppermute x4, starting transfers between devices, local(): lax.ppermute(row, 'blk', permute)  3.28 us
  transfers between devices with their start and end apart: 12, of which 3 were waited for; matrix products, arithmetic and copies ran while one was open for 0% of the time, Pallas kernels for 17%

profile of v5, /device:TPU:0, one launch (start us, length us, event | category | flops | bytes accessed | tf_op | source)
XLA Modules:
  0.0 144.0 jit_solution(5841508600587139823)
XLA Ops:
  0.0 4.1 %normalized.1.unit.refs_2_.refs_7_ = bf16[1024,1024]{1,0:T(8,128)(2,1)} custom-call(s32[16]{0:T(128)} %pads.5, s32[1024]{0:T(1024)} %order_smem.1, s32[1,1024]{1,0:T(1,128)} %bitcast.3, bf16[1024,1024]{1,0:T(8,128)(2,1)} %embeddings.1), custom_call_target="tpu_custom_call" | custom-call | flops 4194304 | bytes 4194304 | tf_op jit(solution)/shard_map/normalized/pallas_call | solution.py:173
  4.1 0.5 collective-permute-start.2
  4.7 5.5 %collective-permute-start = (bf16[1024,1024]{1,0:T(8,128)(2,1)}, bf16[1024,1024]{1,0:T(8,128)(2,1)}, u32[]{:S(2)}, u32[]{:S(2)}) collective-permute-start(bf16[1024,1024]{1,0:T(8,128)(2,1)} %normalized.1.unit.refs_2_.refs_7_), channel_id=1, source_target_pairs={{0,8},{8,12},{12,4},{4,0},{1,5},{3,11},{11,15},{15,7},{7,3},{2,6},... | collective-permute-start | bytes 6291464 | tf_op jit(solution)/shard_map/ppermute | solution.py:403
  10.2 1.4 collective-permute-start.1
  11.6 2.0 %collective-permute-start.4 = (bf16[1024,1024]{1,0:T(8,128)(2,1)}, bf16[1024,1024]{1,0:T(8,128)(2,1)}, u32[]{:S(2)}, u32[]{:S(2)}) collective-permute-start(bf16[1024,1024]{1,0:T(8,128)(2,1)} %normalized.1.unit.refs_2_.refs_7_), channel_id=1, source_target_pairs={{13,5},{5,1},{9,13},{4,8},{14,6},{6,2},{10,14},{7,11},{29,21},{21,... | collective-permute-start | bytes 6291464 | tf_op jit(solution)/shard_map/ppermute | solution.py:403
  13.6 4.6 %own_block.1.refs_0_ = f32[16,1024]{1,0:T(8,128)} custom-call(s32[16]{0:T(128)} %pads.5, s32[1,1024]{1,0:T(1,128)} %bitcast.4, bf16[1024,1024]{1,0:T(8,128)(2,1)} %normalized.1.unit.refs_2_.refs_7_), custom_call_target="tpu_custom_call" | custom-call | flops 2147483648 | bytes 2097152 | tf_op jit(solution)/shard_map/own_block/pallas_call | solution.py:220
  18.3 6.2 %scored.3 = (f32[16,1024]{1,0:T(8,128)}, f32[1,1024]{1,0:T(1,128)}) custom-call(s32[96]{0:T(128)} %constant.8.clone.table, f32[16,1024]{1,0:T(8,128)} %own_block.1.refs_0_, bf16[1024,1024]{1,0:T(8,128)(2,1)} %collective-permute-done.2.refs_1_.refs_0_, bf16[1024,1024]{1,0:T(8,128)(2,1)} %normalized.1.unit.refs_2_.refs_7_), custom_call_target="tpu_custom_call" | custom-call | flops 2147483648 | bytes 4194304 | tf_op jit(solution)/shard_map/scored/pallas_call | solution.py:312
  24.5 30.6 %collective-permute-done.refs_3_ = bf16[1024,1024]{1,0:T(8,128)(2,1)} collective-permute-done((bf16[1024,1024]{1,0:T(8,128)(2,1)}, bf16[1024,1024]{1,0:T(8,128)(2,1)}, u32[]{:S(2)}, u32[]{:S(2)}) %collective-permute-start) | collective-permute-done | bytes 2097184 | tf_op jit(solution)/shard_map/ppermute | solution.py:403
  55.0 2.8 %collective-permute-done.1.refs_6_ = bf16[1024,1024]{1,0:T(8,128)(2,1)} collective-permute-done((bf16[1024,1024]{1,0:T(8,128)(2,1)}, bf16[1024,1024]{1,0:T(8,128)(2,1)}, u32[]{:S(2)}, u32[]{:S(2)}) %collective-permute-start.1) | collective-permute-done | bytes 2097184 | tf_op jit(solution)/shard_map/ppermute | solution.py:403
  57.9 2.0 %collective-permute-start.6 = (bf16[1024,1024]{1,0:T(8,128)(2,1)}, bf16[1024,1024]{1,0:T(8,128)(2,1)}, u32[]{:S(2)}, u32[]{:S(2)}) collective-permute-start(bf16[1024,1024]{1,0:T(8,128)(2,1)} %normalized.1.unit.refs_2_.refs_7_), channel_id=1, source_target_pairs={{5,9},{8,5},{6,10},{11,6},{21,25},{24,21},{22,26},{27,22}} | collective-permute-start | bytes 6291464 | tf_op jit(solution)/shard_map/ppermute | solution.py:403
  59.8 0.4 collective-permute-start.3
  60.3 2.0 %collective-permute-start.7 = (bf16[1024,1024]{1,0:T(8,128)(2,1)}, bf16[1024,1024]{1,0:T(8,128)(2,1)}, u32[]{:S(2)}, u32[]{:S(2)}) collective-permute-start(bf16[1024,1024]{1,0:T(8,128)(2,1)} %collective-permute-done.refs_3_), channel_id=1, source_target_pairs={{8,12},{11,15},{5,6},{6,5},{24,28},{27,31},{21,22},{22,21}} | collective-permute-start | bytes 6291464 | tf_op jit(solution)/shard_map/ppermute | solution.py:403
  62.3 2.0 %collective-permute-start.5 = (bf16[1024,1024]{1,0:T(8,128)(2,1)}, bf16[1024,1024]{1,0:T(8,128)(2,1)}, u32[]{:S(2)}, u32[]{:S(2)}) collective-permute-start(bf16[1024,1024]{1,0:T(8,128)(2,1)} %collective-permute-done.refs_3_), channel_id=1, source_target_pairs={{4,5},{5,4},{7,6},{6,7},{20,21},{21,20},{23,22},{22,23}} | collective-permute-start | bytes 6291464 | tf_op jit(solution)/shard_map/ppermute | solution.py:403
  64.3 0.1 collective-permute-done.3.refs_2_.refs_1_
  64.4 1.4 scored.5
  65.8 0.7 collective-permute-start.8
  66.5 1.3 collective-permute-start.9
  67.8 0.7 collective-permute-start.10
  68.5 0.7 collective-permute-start.11
  69.1 13.6 %scored.4 = (f32[16,1024]{1,0:T(8,128)}, f32[5,1024]{1,0:T(8,128)}) custom-call(s32[480]{0:T(512)} %constant.9.clone.table, f32[16,1024]{1,0:T(8,128)} %get-tuple-element.22.refs_0_, bf16[1024,1024]{1,0:T(8,128)(2,1)} %collective-permute-done.2.refs_1_.refs_0_, bf16[1024,1024]{1,0:T(8,128)(2,1)} %collective-permute-done.3.refs_2_.refs_1_, ...), custom_call_target="tpu_custom_call" | custom-call | flops 12884901888 | bytes 25165824 | tf_op jit(solution)/shard_map/scored/pallas_call | solution.py:312
  82.8 58.2 %all-gather.1.refs_0_ = f32[16,5,1024]{2,1,0:T(8,128)} all-gather(f32[1,5,1024]{2,1,0:T(8,128)} %bitcast.6), channel_id=2, replica_groups=mesh['groups'=2,'blk'=16] {'blk'}, dimensions={0}, use_global_device_ids=true | all-gather | bytes 348160 | tf_op jit(solution)/shard_map/all_gather | solution.py:420
  141.0 0.5 copy-done
  141.6 0.0 copy-done.3
  141.6 2.4 %placed.1 = f32[1,1024]{1,0:T(1,128)} custom-call(s32[240]{0:T(256)} %constant.11.clone.taken, s32[16]{0:T(128)} %pads.5, s32[1,1024]{1,0:T(1,128)} %bitcast.5, f32[16,5,1024]{2,1,0:T(8,128)} %all-gather.1.refs_0_, f32[16,1024]{1,0:T(8,128)} %get-tuple-element.26.refs_1_, f32[16,1024]{1,0:T(8,128)} %get-tuple-element.28.refs_2_, f32[1,1024]{1,0:T(1,128)} %copy-done, ...), custom_call_target="tpu_custom_call" | custom-call | tf_op jit(solution)/shard_map/placed/pallas_call | solution.py:377
  (15 shorter events, 0.1 us)
Async XLA Ops:
  4.1 14.1 %collective-permute-start.2 = (bf16[1024,1024]{1,0:T(8,128)(2,1)}, bf16[1024,1024]{1,0:T(8,128)(2,1)}, u32[]{:S(2)}, u32[]{:S(2)}) collective-permute-start(bf16[1024,1024]{1,0:T(8,128)(2,1)} %normalized.1.unit.refs_2_.refs_7_), channel_id=1, source_target_pairs={{0,1},{1,0},{4,5},{5,4},{8,9},{9,8},{12,13},{13,12},{3,2},{2,3},{7... | collective-permute-start | bytes 6291464 | tf_op jit(solution)/shard_map/ppermute | solution.py:403
  4.7 50.4 %collective-permute-start = (bf16[1024,1024]{1,0:T(8,128)(2,1)}, bf16[1024,1024]{1,0:T(8,128)(2,1)}, u32[]{:S(2)}, u32[]{:S(2)}) collective-permute-start(bf16[1024,1024]{1,0:T(8,128)(2,1)} %normalized.1.unit.refs_2_.refs_7_), channel_id=1, source_target_pairs={{0,8},{8,12},{12,4},{4,0},{1,5},{3,11},{11,15},{15,7},{7,3},{2,6},... | collective-permute-start | bytes 6291464 | tf_op jit(solution)/shard_map/ppermute | solution.py:403
  10.2 47.7 %collective-permute-start.1 = (bf16[1024,1024]{1,0:T(8,128)(2,1)}, bf16[1024,1024]{1,0:T(8,128)(2,1)}, u32[]{:S(2)}, u32[]{:S(2)}) collective-permute-start(bf16[1024,1024]{1,0:T(8,128)(2,1)} %normalized.1.unit.refs_2_.refs_7_), channel_id=1, source_target_pairs={{0,3},{3,0},{1,2},{2,1},{4,7},{7,4},{5,6},{6,5},{8,11},{11,8},{9,1... | collective-permute-start | bytes 6291464 | tf_op jit(solution)/shard_map/ppermute | solution.py:403
  11.6 52.7 %collective-permute-start.4 = (bf16[1024,1024]{1,0:T(8,128)(2,1)}, bf16[1024,1024]{1,0:T(8,128)(2,1)}, u32[]{:S(2)}, u32[]{:S(2)}) collective-permute-start(bf16[1024,1024]{1,0:T(8,128)(2,1)} %normalized.1.unit.refs_2_.refs_7_), channel_id=1, source_target_pairs={{13,5},{5,1},{9,13},{4,8},{14,6},{6,2},{10,14},{7,11},{29,21},{21,... | collective-permute-start | bytes 6291464 | tf_op jit(solution)/shard_map/ppermute | solution.py:403
  57.9 6.4 %collective-permute-start.6 = (bf16[1024,1024]{1,0:T(8,128)(2,1)}, bf16[1024,1024]{1,0:T(8,128)(2,1)}, u32[]{:S(2)}, u32[]{:S(2)}) collective-permute-start(bf16[1024,1024]{1,0:T(8,128)(2,1)} %normalized.1.unit.refs_2_.refs_7_), channel_id=1, source_target_pairs={{5,9},{8,5},{6,10},{11,6},{21,25},{24,21},{22,26},{27,22}} | collective-permute-start | bytes 6291464 | tf_op jit(solution)/shard_map/ppermute | solution.py:403
  59.8 4.6 %collective-permute-start.3 = (bf16[1024,1024]{1,0:T(8,128)(2,1)}, bf16[1024,1024]{1,0:T(8,128)(2,1)}, u32[]{:S(2)}, u32[]{:S(2)}) collective-permute-start(bf16[1024,1024]{1,0:T(8,128)(2,1)} %collective-permute-done.1.refs_6_), channel_id=1, source_target_pairs={{0,1},{1,0},{4,5},{5,4},{8,9},{9,8},{12,13},{13,12},{3,2},{2,3},{7... | collective-permute-start | bytes 6291464 | tf_op jit(solution)/shard_map/ppermute | solution.py:403
  60.3 4.1 %collective-permute-start.7 = (bf16[1024,1024]{1,0:T(8,128)(2,1)}, bf16[1024,1024]{1,0:T(8,128)(2,1)}, u32[]{:S(2)}, u32[]{:S(2)}) collective-permute-start(bf16[1024,1024]{1,0:T(8,128)(2,1)} %collective-permute-done.refs_3_), channel_id=1, source_target_pairs={{8,12},{11,15},{5,6},{6,5},{24,28},{27,31},{21,22},{22,21}} | collective-permute-start | bytes 6291464 | tf_op jit(solution)/shard_map/ppermute | solution.py:403
  62.3 2.1 %collective-permute-start.5 = (bf16[1024,1024]{1,0:T(8,128)(2,1)}, bf16[1024,1024]{1,0:T(8,128)(2,1)}, u32[]{:S(2)}, u32[]{:S(2)}) collective-permute-start(bf16[1024,1024]{1,0:T(8,128)(2,1)} %collective-permute-done.refs_3_), channel_id=1, source_target_pairs={{4,5},{5,4},{7,6},{6,7},{20,21},{21,20},{23,22},{22,23}} | collective-permute-start | bytes 6291464 | tf_op jit(solution)/shard_map/ppermute | solution.py:403
  65.8 75.2 %collective-permute-start.8 = (f32[1,1024]{1,0:T(1,128)}, f32[1,1024]{1,0:T(1,128)S(1)}, u32[]{:S(2)}, u32[]{:S(2)}) collective-permute-start(f32[1,1024]{1,0:T(1,128)} %get-tuple-element.29), channel_id=1, source_target_pairs={{5,8},{6,15},{9,11},{10,6},{12,14},{15,3},{21,24},{22,31},{25,27},... | collective-permute-start | bytes 12296 | tf_op jit(solution)/shard_map/ppermute | solution.py:414
  66.5 74.5 %collective-permute-start.9 = (f32[1,1024]{1,0:T(1,128)}, f32[1,1024]{1,0:T(1,128)S(1)}, u32[]{:S(2)}, u32[]{:S(2)}) collective-permute-start(f32[1,1024]{1,0:T(1,128)} %get-tuple-element.30), channel_id=1, source_target_pairs={{5,2},{6,11},{9,10},{10,8},{12,0},{15,13},{21,18},{22,27},{25,26},... | collective-permute-start | bytes 12296 | tf_op jit(solution)/shard_map/ppermute | solution.py:414
  67.8 73.2 %collective-permute-start.10 = (f32[1,1024]{1,0:T(1,128)}, f32[1,1024]{1,0:T(1,128)S(1)}, u32[]{:S(2)}, u32[]{:S(2)}) collective-permute-start(f32[1,1024]{1,0:T(1,128)} %get-tuple-element.31), channel_id=1, source_target_pairs={{5,12},{6,1},{9,8},{10,9},{12,13},{15,14},{21,28},{22,17},{25,24},... | collective-permute-start | bytes 12296 | tf_op jit(solution)/shard_map/ppermute | solution.py:414
  68.5 72.6 %collective-permute-start.11 = (f32[1,1024]{1,0:T(1,128)}, f32[1,1024]{1,0:T(1,128)S(1)}, u32[]{:S(2)}, u32[]{:S(2)}) collective-permute-start(f32[1,1024]{1,0:T(1,128)} %get-tuple-element.32), channel_id=1, source_target_pairs={{5,13},{6,14},{9,5},{10,11},{12,15},{21,29},{22,30},{25,21},{26,27... | collective-permute-start | bytes 12296 | tf_op jit(solution)/shard_map/ppermute | solution.py:414
  141.0 0.6 copy-start
  141.0 0.6 copy-start.1
  141.0 0.6 copy-start.2
  141.0 0.6 copy-start.3

commit v6 on v4

--- a/solution.py
+++ b/solution.py
@@ -11,6 +11,8 @@
 STEPS = 6
 VMEM = 62 * 2**20
 FLOOR = -2.0
+MOST_PADS = 256
+AHEAD = 3
 
 
 class Move:
@@ -28,44 +30,42 @@
             (at(z, y, lane), at(to, y, land)) for y in (0, 1) for (z, lane), (to, land) in links
         ]
 
-    def across(planes, lane):
-        return [(at(z, y, lane), at(z, 1 - y, lane)) for z in planes for y in (0, 1)]
-
-    planes = range(4)
+    def across(planes):
+        return [(at(z, y, lane), at(z, 1 - y, lane)) for z, lane in planes for y in (0, 1)]
+
+    every = [(z, lane) for z in range(4) for lane in (0, 1)]
+    swap = rows([((z, lane), (z, 1 - lane)) for z, lane in every])
     first = [((0, 0), (2, 0)), ((2, 0), (3, 0)), ((3, 0), (1, 0)), ((1, 0), (0, 0)), ((0, 1), (1, 1))]
     second = [((3, 1), (1, 1)), ((1, 1), (0, 1)), ((2, 1), (3, 1)), ((1, 0), (2, 0))]
-    swap = [((z, lane), (z, 1 - lane)) for z in planes for lane in (0, 1)]
     return [
-        Move("A", "own", rows(swap), 0, 0),
         Move("R1", "own", rows(first), 0, 1),
-        Move("YX", "own", across(planes, 0), 0, 1),
-        Move("R2", "own", rows(second), 1, 2, "R1"),
-        Move("YN", "own", across(planes, 1), 1, 2, "R1"),
-        Move("V", "R1", rows([((2, 0), (3, 0))]) + across([1], 1), 1, 2),
+        Move("R2", "own", rows(second), 0, 1),
+        Move("Y", "own", across(every), 0, 1),
+        Move("A", "own", swap, 0, 0),
+        Move("R3", "own", rows([((1, 1), (2, 1)), ((2, 0), (1, 1))]), 1, 2, "R1"),
+        Move("V", "R1", rows([((2, 0), (3, 0))]) + across([(1, 1)]), 1, 2),
+        Move("F", "Y", swap, 1, 1),
         Move("W", "R1", rows([((1, 0), (1, 1)), ((1, 1), (1, 0))]), 1, 1),
-        Move("FX", "YX", rows([((z, 0), (z, 1)) for z in planes]), 1, 1),
-        Move("R3", "own", rows([((1, 1), (2, 1)), ((2, 0), (1, 1))]), 2, 3, "R2"),
-        Move("FN", "YN", rows([((z, 1), (z, 0)) for z in planes]), 2, 2),
     ]
 
 
 GRID_PAIRS = (
-    ((0, 1), (0, 4), (1, 4), (3, 4)),
-    ((0, 5), (1, 3), (3, 5)),
-    ((0, 2), (0, 3), (0, 6), (2, 3), (3, 6)),
-    ((1, 2), (2, 7), (3, 7)),
-    ((1, 5), (1, 6), (1, 12), (4, 5), (6, 12)),
-    ((1, 7), (1, 13), (2, 8), (2, 12), (2, 13), (5, 7), (5, 8), (7, 12), (7, 13)),
-    ((1, 11), (1, 14), (1, 15), (2, 6), (2, 14), (2, 15), (4, 14), (4, 15), (6, 11)),
-    ((2, 4), (2, 5), (4, 6), (4, 7), (5, 6), (5, 15), (6, 7)),
-    ((0, 10), (0, 11), (4, 8), (4, 9), (4, 10), (8, 9), (8, 11), (9, 11)),
-    ((5, 9), (5, 10), (5, 11), (9, 10)),
-    ((6, 8), (6, 9), (6, 10)),
-    ((3, 8), (3, 9), (7, 8), (7, 9), (7, 10), (7, 11), (8, 10), (10, 11)),
-    ((0, 12), (0, 13), (0, 14), (0, 15), (8, 12), (8, 13), (8, 14)),
-    ((9, 12), (9, 13), (9, 14), (9, 15), (12, 13), (13, 15)),
-    ((10, 12), (10, 13), (10, 14), (10, 15), (12, 14), (12, 15)),
-    ((3, 13), (3, 14), (3, 15), (11, 12), (11, 13), (11, 14), (11, 15), (13, 14), (14, 15)),
+    ((0, 1), (0, 4), (1, 2), (1, 4), (3, 4)),
+    ((0, 5), (1, 5), (2, 5), (3, 5)),
+    ((0, 2), (0, 6), (1, 6), (2, 6), (3, 6)),
+    ((0, 3), (1, 3), (2, 3), (2, 7), (3, 7)),
+    ((1, 7), (4, 5), (4, 7), (5, 6), (7, 12)),
+    ((1, 12), (1, 13), (2, 8), (2, 12), (2, 13), (6, 12), (7, 13), (8, 13)),
+    ((1, 11), (1, 14), (1, 15), (2, 4), (2, 14), (4, 14), (4, 15), (6, 7), (11, 15)),
+    ((2, 15), (4, 6), (5, 7), (5, 15)),
+    ((0, 10), (0, 11), (4, 8), (4, 9), (4, 10)),
+    ((5, 8), (5, 9), (5, 10), (5, 11), (8, 9), (8, 11), (9, 11)),
+    ((6, 8), (6, 9), (6, 10), (6, 11), (8, 10), (9, 10)),
+    ((3, 8), (3, 9), (7, 8), (7, 9), (7, 10), (7, 11), (10, 11)),
+    ((0, 12), (0, 13), (0, 14), (0, 15), (8, 12), (8, 14), (12, 13), (13, 14), (13, 15)),
+    ((9, 12), (9, 13), (9, 14), (9, 15), (12, 14)),
+    ((10, 12), (10, 13), (10, 14), (10, 15)),
+    ((3, 13), (3, 14), (3, 15), (11, 12), (11, 13), (11, 14), (12, 15), (14, 15)),
 )
 
 
@@ -78,7 +78,7 @@
 
 def planned(count):
     if count == 16:
-        moves, placed_pairs, sending = grid_moves(), GRID_PAIRS, (2, 3)
+        moves, placed_pairs, sending = grid_moves(), GRID_PAIRS, (1, 2)
     else:
         moves, sending = ring_moves(count), (STEPS,)
         placed_pairs = [[(b, (b + k) % count) for k in range(1, STEPS + 1)] for b in range(count)]
@@ -159,11 +159,12 @@
 
 def valid_rows(pads, order, start, count):
     rows = order.shape[1]
+    most = min(rows, MOST_PADS)
     valid_count = rows - pads[lax.axis_index("blk")]
-    position = lax.broadcasted_iota(jnp.int32, (1, rows), 1)
-    kept = jnp.where(position < valid_count, order[...], -1)
+    position = rows - most + lax.broadcasted_iota(jnp.int32, (1, most), 1)
+    padding = jnp.where(position < valid_count, -1, order[:, rows - most :])
     row = start + lax.broadcasted_iota(jnp.int32, (count, 1), 0)
-    return jnp.max(jnp.where(kept == row, 1.0, 0.0), axis=1, keepdims=True) > 0.0
+    return jnp.max(jnp.where(padding == row, 1.0, 0.0), axis=1, keepdims=True) < 1.0
 
 
 def normalized(embeddings, order, pad_counts):
@@ -230,56 +231,50 @@
     )(pad_counts, order.reshape(1, rows), unit)
 
 
-def pairs_kernel(ntaken, nslots, nsends, most, table, best, *refs):
-    refs = list(refs)
-    arrivals, slots, (out, *sent) = (
-        [refs.pop(0) for _ in range(count)] for count in (ntaken, nslots, 1 + nsends)
-    )
-    held, across, sems = refs
+def pairs_kernel(nslots, nrows, ntaken, nloads, npairs, table, best, *refs):
+    arrivals, slots, out = refs[:ntaken], refs[ntaken : ntaken + nslots], refs[ntaken + nslots]
+    sent, (held, across, sems) = refs[ntaken + nslots + 1 : -3], refs[-3:]
     rows = out.shape[1]
     here = lax.axis_index("blk")
-    fixed = 1 + nsends + ntaken
-    at = here * (fixed + 4 * most)
-    steps = table[at]
-
-    def entry(step, which):
-        return table[at + fixed + 4 * step + which]
-
-    def fetch(step):
-        for side in range(2):
-            wanted = entry(step, side)
+    loads_at = here * (2 + nrows + ntaken + nloads + 5 * npairs) + 2 + nrows + ntaken
+    pairs_at = loads_at + nloads
+    rows_at = loads_at - nrows - ntaken
+    loads, pairs = table[rows_at - 2], table[rows_at - 1]
+
+    def fetch(load):
+        @pl.when(load < loads)
+        def _():
+            wanted = table[loads_at + jnp.minimum(load, nloads - 1)]
             for index, slot in enumerate(slots):
                 @pl.when(wanted == index)
-                def _(slot=slot, side=side):
-                    pltpu.make_async_copy(slot, held.at[step % 2, side], sems.at[step % 2, side]).start()
-
-    def arrived(step):
-        for side in range(2):
-            pltpu.make_async_copy(slots[0], held.at[step % 2, side], sems.at[step % 2, side]).wait()
-
-    @pl.when(steps > 0)
-    def _():
-        fetch(0)
-
+                def _(slot=slot):
+                    for start in range(0, rows, 256):
+                        part = pl.ds(start, 256)
+                        pltpu.make_async_copy(slot.at[part], held.at[load, part], sems.at[load]).start()
+
+    for load in range(min(AHEAD, nloads)):
+        fetch(load)
     out[...] = best[...]
     own = pl.ds(here, 1)
     for index, row in enumerate(arrivals):
-        taken = table[at + 1 + nsends + index] > 0
-        out[own, :] = jnp.where(taken, jnp.maximum(out[own, :], row[...]), out[own, :])
-
-    @pl.loop(0, steps)
+        handed = table[rows_at + nrows + index] > 0
+        out[own, :] = jnp.where(handed, jnp.maximum(out[own, :], row[...]), out[own, :])
+
+    @pl.loop(0, pairs)
     def _(step):
-        arrived(step)
-
-        @pl.when(step + 1 < steps)
-        def _():
-            fetch(step + 1)
-
-        now = step % 2
-        first, second = pl.ds(entry(step, 2), 1), pl.ds(entry(step, 3), 1)
+        at = pairs_at + 5 * step
+        before = jnp.where(step == 0, 0, table[jnp.maximum(at - 1, 0)])
+
+        @pl.loop(before, table[at + 4])
+        def _(load):
+            pltpu.make_async_copy(slots[0], held.at[load], sems.at[load]).wait()
+            fetch(load + AHEAD)
+
+        left, right = table[at], table[at + 1]
+        first, second = pl.ds(table[at + 2], 1), pl.ds(table[at + 3], 1)
         for start in range(0, rows, 256):
             part = pl.ds(start, 256)
-            scores = product(held[now, 0], held[now, 1, part, :])
+            scores = product(held[left], held[right, part, :])
             down = jnp.max(scores, axis=0, keepdims=True)
             out[second, part] = jnp.maximum(out[second, part], down)
             along = jnp.maximum(scores[:, :128], scores[:, 128:])
@@ -288,24 +283,41 @@
         out[first, :] = jnp.maximum(out[first, :], found)
 
     for index, row in enumerate(sent):
-        row[...] = out[pl.ds(table[at + 1 + index], 1), :]
-
-
-def scored(best, found, permutes, slots, work, sends):
+        row[...] = out[pl.ds(table[rows_at + index], 1), :]
+
+
+def in_order_of_loads(pairs, rank):
+    left, loaded, ordered = list(pairs), [], []
+    while left:
+        pair = min(
+            left,
+            key=lambda p: (sum(s not in loaded for s in p[:2]), max(rank[s] for s in p[:2]), p[2:]),
+        )
+        left.remove(pair)
+        loaded += [slot for slot in pair[:2] if slot not in loaded]
+        ordered.append((pair, len(loaded)))
+    return loaded, ordered
+
+
+def scored(best, found, permutes, slots, rank, work, sends):
     names = sorted({slot for pairs in work for pair in pairs for slot in pair[:2]})
-    most = max(len(pairs) for pairs in work)
+    plans = [in_order_of_loads(pairs, rank) for pairs in work]
+    nloads = max(len(loaded) for loaded, _ in plans)
+    npairs = max(len(pairs) for pairs in work)
     table = []
-    for device, pairs in enumerate(work):
-        table.append(len(pairs))
+    for device, (loaded, ordered) in enumerate(plans):
+        table += [len(loaded), len(ordered)]
         table += [dict(permute).get(device, device) for permute in sends]
         table += [int(device in dict(permute).values()) for permute in permutes]
-        for slot, other, block, visitor in pairs + [(names[0], names[0], 0, 0)] * (most - len(pairs)):
-            table += [names.index(slot), names.index(other), block, visitor]
+        table += [names.index(slot) for slot in loaded] + [0] * (nloads - len(loaded))
+        for (slot, other, block, visitor), need in ordered:
+            table += [loaded.index(slot), loaded.index(other), block, visitor, need]
+        table += [0] * (5 * (npairs - len(ordered)))
     given = [slots[name] for name in names]
     rows, depth = given[0].shape
     whole = pl.BlockSpec(memory_space=pltpu.VMEM)
     return pl.pallas_call(
-        functools.partial(pairs_kernel, len(found), len(given), len(sends), most),
+        functools.partial(pairs_kernel, len(given), len(sends), len(found), nloads, npairs),
         out_shape=[jax.ShapeDtypeStruct(best.shape, jnp.float32)]
         + [jax.ShapeDtypeStruct((1, rows), jnp.float32)] * len(sends),
         in_specs=[pl.BlockSpec(memory_space=pltpu.SMEM)]
@@ -313,14 +325,14 @@
         + [pl.BlockSpec(memory_space=pl.ANY)] * len(given),
         out_specs=[whole] * (1 + len(sends)),
         scratch_shapes=[
-            pltpu.VMEM((2, 2, rows, depth), jnp.bfloat16),
+            pltpu.VMEM((nloads, rows, depth), jnp.bfloat16),
             pltpu.VMEM((rows, 128), jnp.float32),
-            pltpu.SemaphoreType.DMA((2, 2)),
+            pltpu.SemaphoreType.DMA((nloads,)),
         ],
         compiler_params=pltpu.CompilerParams(vmem_limit_bytes=VMEM),
         cost_estimate=pl.CostEstimate(
-            flops=2 * most * rows * rows * depth,
-            bytes_accessed=4 * most * rows * depth,
+            flops=2 * npairs * rows * rows * depth,
+            bytes_accessed=2 * nloads * rows * depth,
             transcendentals=0,
         ),
         name="scored",
@@ -362,6 +374,7 @@
     moves, work, sending = planned(nblocks)
     unit = normalized(embeddings, order, pad_counts)
     slots, best = {"own": unit}, None
+    rank = dict({"own": -1}, **{move.name: move.stage for move in moves})
     touched, permutes, found = [set() for _ in range(nblocks)], [], []
     for stage, pairs in enumerate(work):
         starting = [move for move in moves if move.begins == stage]
@@ -382,7 +395,7 @@
             sends = colored([(of, to) for of in range(nblocks) for to in sorted(touched[of])], nblocks)
             touched = [set() for _ in range(nblocks)]
         if any(pairs):
-            best, *rows = scored(best, found, permutes, slots, pairs, sends)
+            best, *rows = scored(best, found, permutes, slots, rank, pairs, sends)
             found = [lax.ppermute(row, "blk", permute) for row, permute in zip(rows, sends)]
             permutes = sends
     return placed(best, found, permutes, order, pad_counts)

time: 162 us -> 124 us (0.77)
  the two profiles are of different devices: /device:TPU:17 before, /device:TPU:9 now
where the time goes in v6:
time: 124 us; the launch traced here: 123 us
  waiting for transfers between devices  42.4 us (34%)
  Pallas kernels  39.7 us (32%)
  starting transfers between devices  39.3 us (32%)
    ppermute x8, waiting for transfers between devices, local(): slots[move.name] = lax.ppermute(value, 'blk', move.pairs)  37.7 us
    pallas_call x3, Pallas kernels, scored(): pl.pallas_call(functools.partial(pairs_kernel, len(given), len(sends), le...  28.7 us
    ppermute x9, starting transfers between devices, local(): lax.ppermute(row, 'blk', permute)  21.2 us
    ppermute x8, starting transfers between devices, local(): slots[move.name] = lax.ppermute(value, 'blk', move.pairs)  18.1 us
    pallas_call x1, Pallas kernels, own_block(): pl.pallas_call(own_kernel, out_shape=jax.ShapeDtypeStruct((nblocks, rows)...  4.66 us
    ppermute x9, waiting for transfers between devices, local(): lax.ppermute(row, 'blk', permute)  4.65 us
    pallas_call x1, Pallas kernels, normalized(): pl.pallas_call(unit_kernel, out_shape=jax.ShapeDtypeStruct((rows, depth),...  4.19 us
  transfers between devices with their start and end apart: 17, of which 5 were waited for; matrix products, arithmetic and copies ran while one was open for 0% of the time, Pallas kernels for 16%

profile of v6, /device:TPU:9, one launch (start us, length us, event | category | flops | bytes accessed | tf_op | source)
XLA Modules:
  0.0 122.9 jit_solution(6612588371462079766)
XLA Ops:
  0.0 4.2 %normalized.1.unit.refs_1_.refs_6_.refs_12_ = bf16[1024,1024]{1,0:T(8,128)(2,1)} custom-call(s32[16]{0:T(128)} %pads.5, s32[1024]{0:T(1024)} %order_smem.1, s32[1,1024]{1,0:T(1,128)} %bitcast.2, bf16[1024,1024]{1,0:T(8,128)(2,1)} %embeddings.1), custom_call_target="tpu_custom_call" | custom-call | flops 4194304 | bytes 4194304 | tf_op jit(solution)/shard_map/normalized/pallas_call | solution.py:174
  4.9 1.3 %collective-permute-start = (bf16[1024,1024]{1,0:T(8,128)(2,1)}, bf16[1024,1024]{1,0:T(8,128)(2,1)}, u32[]{:S(2)}, u32[]{:S(2)}) collective-permute-start(bf16[1024,1024]{1,0:T(8,128)(2,1)} %normalized.1.unit.refs_1_.refs_6_.refs_12_), channel_id=1, source_target_pairs={{0,8},{8,12},{12,4},{4,0},{1,5},{3,11},{11,15},{15,7},{7,3},{2,6},... | collective-permute-start | bytes 6291464 | tf_op jit(solution)/shard_map/ppermute | solution.py:388
  6.1 1.3 %collective-permute-start.1 = (bf16[1024,1024]{1,0:T(8,128)(2,1)}, bf16[1024,1024]{1,0:T(8,128)(2,1)}, u32[]{:S(2)}, u32[]{:S(2)}) collective-permute-start(bf16[1024,1024]{1,0:T(8,128)(2,1)} %normalized.1.unit.refs_1_.refs_6_.refs_12_), channel_id=1, source_target_pairs={{0,3},{3,0},{1,2},{2,1},{4,7},{7,4},{5,6},{6,5},{8,11},{11,8},{9,1... | collective-permute-start | bytes 6291464 | tf_op jit(solution)/shard_map/ppermute | solution.py:388
  7.4 5.5 %collective-permute-start.4 = (bf16[1024,1024]{1,0:T(8,128)(2,1)}, bf16[1024,1024]{1,0:T(8,128)(2,1)}, u32[]{:S(2)}, u32[]{:S(2)}) collective-permute-start(bf16[1024,1024]{1,0:T(8,128)(2,1)} %normalized.1.unit.refs_1_.refs_6_.refs_12_), channel_id=1, source_target_pairs={{13,5},{5,1},{9,13},{4,8},{14,6},{6,2},{10,14},{7,11},{29,21},{21,... | collective-permute-start | bytes 6291464 | tf_op jit(solution)/shard_map/ppermute | solution.py:388
  13.0 4.7 %own_block.1.best = f32[16,1024]{1,0:T(8,128)} custom-call(s32[16]{0:T(128)} %pads.5, s32[1,1024]{1,0:T(1,128)} %bitcast.3, bf16[1024,1024]{1,0:T(8,128)(2,1)} %normalized.1.unit.refs_1_.refs_6_.refs_12_), custom_call_target="tpu_custom_call" | custom-call | flops 2147483648 | bytes 2097152 | tf_op jit(solution)/shard_map/own_block/pallas_call | solution.py:221
  17.6 1.5 %scored.3.best = f32[16,1024]{1,0:T(8,128)} custom-call(s32[144]{0:T(256)} %constant.8.clone.table, f32[16,1024]{1,0:T(8,128)} %own_block.1.best, bf16[1024,1024]{1,0:T(8,128)(2,1)} %collective-permute-done.2.refs_0_.refs_5_, bf16[1024,1024]{1,0:T(8,128)(2,1)} %normalized.1.unit.refs_1_.refs_6_.refs_12_), custom_call_target="tpu_custom_call" | custom-call | flops 2147483648 | bytes 4194304 | tf_op jit(solution)/shard_map/scored/pallas_call | solution.py:319
  19.2 33.9 %collective-permute-done.refs_2_ = bf16[1024,1024]{1,0:T(8,128)(2,1)} collective-permute-done((bf16[1024,1024]{1,0:T(8,128)(2,1)}, bf16[1024,1024]{1,0:T(8,128)(2,1)}, u32[]{:S(2)}, u32[]{:S(2)}) %collective-permute-start) | collective-permute-done | bytes 2097184 | tf_op jit(solution)/shard_map/ppermute | solution.py:388
  53.0 1.6 %collective-permute-done.1.refs_5_.refs_11_ = bf16[1024,1024]{1,0:T(8,128)(2,1)} collective-permute-done((bf16[1024,1024]{1,0:T(8,128)(2,1)}, bf16[1024,1024]{1,0:T(8,128)(2,1)}, u32[]{:S(2)}, u32[]{:S(2)}) %collective-permute-start.1) | collective-permute-done | bytes 2097184 | tf_op jit(solution)/shard_map/ppermute | solution.py:388
  55.1 1.9 %collective-permute-start.5 = (bf16[1024,1024]{1,0:T(8,128)(2,1)}, bf16[1024,1024]{1,0:T(8,128)(2,1)}, u32[]{:S(2)}, u32[]{:S(2)}) collective-permute-start(bf16[1024,1024]{1,0:T(8,128)(2,1)} %collective-permute-done.refs_2_), channel_id=1, source_target_pairs={{4,5},{5,4},{7,6},{6,7},{20,21},{21,20},{23,22},{22,23}} | collective-permute-start | bytes 6291464 | tf_op jit(solution)/shard_map/ppermute | solution.py:388
  57.1 4.0 %collective-permute-start.11 = (bf16[1024,1024]{1,0:T(8,128)(2,1)}, bf16[1024,1024]{1,0:T(8,128)(2,1)}, u32[]{:S(2)}, u32[]{:S(2)}) collective-permute-start(bf16[1024,1024]{1,0:T(8,128)(2,1)} %normalized.1.unit.refs_1_.refs_6_.refs_12_), channel_id=1, source_target_pairs={{5,9},{8,5},{6,10},{11,6},{21,25},{24,21},{22,26},{27,22}} | collective-permute-start | bytes 6291464 | tf_op jit(solution)/shard_map/ppermute | solution.py:388
  61.1 2.9 %collective-permute-start.12 = (bf16[1024,1024]{1,0:T(8,128)(2,1)}, bf16[1024,1024]{1,0:T(8,128)(2,1)}, u32[]{:S(2)}, u32[]{:S(2)}) collective-permute-start(bf16[1024,1024]{1,0:T(8,128)(2,1)} %collective-permute-done.refs_2_), channel_id=1, source_target_pairs={{8,12},{11,15},{5,6},{6,5},{24,28},{27,31},{21,22},{22,21}} | collective-permute-start | bytes 6291464 | tf_op jit(solution)/shard_map/ppermute | solution.py:388
  64.0 13.6 %scored.4 = (f32[16,1024]{1,0:T(8,128)}, f32[1,1024]{1,0:T(1,128)}, f32[1,1024]{1,0:T(1,128)}, f32[1,1024]{1,0:T(1,128)}, f32[1,1024]{1,0:T(1,128)}, /*index=5*/f32[1,1024]{1,0:T(1,128)}) custom-call(s32[688]{0:T(1024)} %constant.9.clone.table, f32[16,1024]{1,0:T(8,128)} %scored.3.best, bf16[1024,1024]{1,0:T(8,128)(2,1)} %collective-permute-done.2.refs_0_.refs_5_, ...), custom_call_target="tpu_custom_call" | custom-call | flops 12884901888 | bytes 12582912 | tf_op jit(solution)/shard_map/scored/pallas_call | solution.py:319
  77.6 3.7 %collective-permute-start.10 = (f32[1,1024]{1,0:T(1,128)}, f32[1,1024]{1,0:T(1,128)S(1)}, u32[]{:S(2)}, u32[]{:S(2)}) collective-permute-start(f32[1,1024]{1,0:T(1,128)} %get-tuple-element.32), channel_id=1, source_target_pairs={{0,2},{4,1},{5,13},{6,7},{7,15},{8,11},{11,10},{14,12},{16,18},{20... | collective-permute-start | bytes 12296 | tf_op jit(solution)/shard_map/ppermute | solution.py:399
  81.3 1.9 %collective-permute-start.6 = (f32[1,1024]{1,0:T(1,128)}, f32[1,1024]{1,0:T(1,128)S(1)}, u32[]{:S(2)}, u32[]{:S(2)}) collective-permute-start(f32[1,1024]{1,0:T(1,128)} %get-tuple-element.28), channel_id=1, source_target_pairs={{0,4},{1,5},{2,6},{3,7},{4,12},{5,1},{6,15},{7,2},{8,0},{9,8},{11,... | collective-permute-start | bytes 12296 | tf_op jit(solution)/shard_map/ppermute | solution.py:399
  83.3 3.2 %collective-permute-start.7 = (f32[1,1024]{1,0:T(1,128)}, f32[1,1024]{1,0:T(1,128)S(1)}, u32[]{:S(2)}, u32[]{:S(2)}) collective-permute-start(f32[1,1024]{1,0:T(1,128)} %get-tuple-element.29), channel_id=1, source_target_pairs={{0,1},{1,2},{2,3},{3,0},{4,5},{5,7},{6,14},{7,6},{8,4},{10,9},{11,... | collective-permute-start | bytes 12296 | tf_op jit(solution)/shard_map/ppermute | solution.py:399
  86.5 2.2 %collective-permute-done.12.refs_9_ = bf16[1024,1024]{1,0:T(8,128)(2,1)} collective-permute-done((bf16[1024,1024]{1,0:T(8,128)(2,1)}, bf16[1024,1024]{1,0:T(8,128)(2,1)}, u32[]{:S(2)}, u32[]{:S(2)}) %collective-permute-start.12) | collective-permute-done | bytes 2097184 | tf_op jit(solution)/shard_map/ppermute | solution.py:388
  88.7 2.9 %collective-permute-start.9 = (f32[1,1024]{1,0:T(1,128)}, f32[1,1024]{1,0:T(1,128)S(1)}, u32[]{:S(2)}, u32[]{:S(2)}) collective-permute-start(f32[1,1024]{1,0:T(1,128)} %get-tuple-element.31), channel_id=1, source_target_pairs={{1,3},{2,0},{3,1},{4,7},{5,6},{6,2},{7,4},{8,10},{11,9},{12,8},{13... | collective-permute-start | bytes 12296 | tf_op jit(solution)/shard_map/ppermute | solution.py:399
  93.2 13.6 %scored.5 = (f32[16,1024]{1,0:T(8,128)}, f32[1,1024]{1,0:T(1,128)}, f32[1,1024]{1,0:T(1,128)}, f32[1,1024]{1,0:T(1,128)}, f32[1,1024]{1,0:T(1,128)}) custom-call(s32[576]{0:T(1024)} %constant.10.clone.table, f32[16,1024]{1,0:T(8,128)} %get-tuple-element.27.best, f32[1,1024]{1,0:T(1,128)} %copy-done.5, f32[1,1024]{1,0:T(1,128)} %copy-done.6, ...), custom_call_target="tpu_custom_call" | custom-call | flops 8589934592 | bytes 10485760 | tf_op jit(solution)/shard_map/scored/pallas_call | solution.py:319
  106.8 1.3 %collective-permute-start.13 = (f32[1,1024]{1,0:T(1,128)}, f32[1,1024]{1,0:T(1,128)S(1)}, u32[]{:S(2)}, u32[]{:S(2)}) collective-permute-start(f32[1,1024]{1,0:T(1,128)} %get-tuple-element.35), channel_id=1, source_target_pairs={{5,8},{6,15},{9,11},{10,6},{12,14},{15,3},{21,24},{22,31},{25,27},... | collective-permute-start | bytes 12296 | tf_op jit(solution)/shard_map/ppermute | solution.py:399
  108.1 1.3 %collective-permute-start.14 = (f32[1,1024]{1,0:T(1,128)}, f32[1,1024]{1,0:T(1,128)S(1)}, u32[]{:S(2)}, u32[]{:S(2)}) collective-permute-start(f32[1,1024]{1,0:T(1,128)} %get-tuple-element.36), channel_id=1, source_target_pairs={{5,2},{6,11},{9,10},{10,8},{12,0},{15,13},{21,18},{22,27},{25,26},... | collective-permute-start | bytes 12296 | tf_op jit(solution)/shard_map/ppermute | solution.py:399
  109.4 5.0 %collective-permute-start.15 = (f32[1,1024]{1,0:T(1,128)}, f32[1,1024]{1,0:T(1,128)S(1)}, u32[]{:S(2)}, u32[]{:S(2)}) collective-permute-start(f32[1,1024]{1,0:T(1,128)} %get-tuple-element.37), channel_id=1, source_target_pairs={{5,12},{6,1},{9,8},{10,9},{12,13},{15,14},{21,28},{22,17},{25,24},... | collective-permute-start | bytes 12296 | tf_op jit(solution)/shard_map/ppermute | solution.py:399
  114.4 1.9 %collective-permute-start.16 = (f32[1,1024]{1,0:T(1,128)}, f32[1,1024]{1,0:T(1,128)S(1)}, u32[]{:S(2)}, u32[]{:S(2)}) collective-permute-start(f32[1,1024]{1,0:T(1,128)} %get-tuple-element.38), channel_id=1, source_target_pairs={{5,13},{6,14},{9,5},{10,11},{12,15},{21,29},{22,30},{25,21},{26,27... | collective-permute-start | bytes 12296 | tf_op jit(solution)/shard_map/ppermute | solution.py:399
  116.4 3.8 %collective-permute-done.16.refs_3_ = f32[1,1024]{1,0:T(1,128)S(1)} collective-permute-done((f32[1,1024]{1,0:T(1,128)}, f32[1,1024]{1,0:T(1,128)S(1)}, u32[]{:S(2)}, u32[]{:S(2)}) %collective-permute-start.16) | collective-permute-done | bytes 4128 | tf_op jit(solution)/shard_map/ppermute | solution.py:399
  120.7 2.2 %placed.1 = f32[1,1024]{1,0:T(1,128)} custom-call(s32[64]{0:T(128)} %constant.11.clone.taken, s32[16]{0:T(128)} %pads.5, s32[1,1024]{1,0:T(1,128)} %bitcast.4, f32[16,1024]{1,0:T(8,128)} %get-tuple-element.34.best, f32[1,1024]{1,0:T(1,128)} %copy-done, f32[1,1024]{1,0:T(1,128)} %copy-done.1, f32[1,1024]{1,0:T(1,128)} %copy-done.2, f32[1,1024]{1,0:T(1,128)} %copy-done.3), custom_call_target="tpu_custom_call" | custom-call | tf_op jit(solution)/shard_map/placed/pallas_call | solution.py:362
  (34 shorter events, 3.3 us)
Async XLA Ops:
  4.2 13.4 %collective-permute-start.2 = (bf16[1024,1024]{1,0:T(8,128)(2,1)}, bf16[1024,1024]{1,0:T(8,128)(2,1)}, u32[]{:S(2)}, u32[]{:S(2)}) collective-permute-start(bf16[1024,1024]{1,0:T(8,128)(2,1)} %normalized.1.unit.refs_1_.refs_6_.refs_12_), channel_id=1, source_target_pairs={{0,1},{1,0},{4,5},{5,4},{8,9},{9,8},{12,13},{13,12},{3,2},{2,3},{7... | collective-permute-start | bytes 6291464 | tf_op jit(solution)/shard_map/ppermute | solution.py:388
  4.9 48.2 %collective-permute-start = (bf16[1024,1024]{1,0:T(8,128)(2,1)}, bf16[1024,1024]{1,0:T(8,128)(2,1)}, u32[]{:S(2)}, u32[]{:S(2)}) collective-permute-start(bf16[1024,1024]{1,0:T(8,128)(2,1)} %normalized.1.unit.refs_1_.refs_6_.refs_12_), channel_id=1, source_target_pairs={{0,8},{8,12},{12,4},{4,0},{1,5},{3,11},{11,15},{15,7},{7,3},{2,6},... | collective-permute-start | bytes 6291464 | tf_op jit(solution)/shard_map/ppermute | solution.py:388
  6.1 48.5 %collective-permute-start.1 = (bf16[1024,1024]{1,0:T(8,128)(2,1)}, bf16[1024,1024]{1,0:T(8,128)(2,1)}, u32[]{:S(2)}, u32[]{:S(2)}) collective-permute-start(bf16[1024,1024]{1,0:T(8,128)(2,1)} %normalized.1.unit.refs_1_.refs_6_.refs_12_), channel_id=1, source_target_pairs={{0,3},{3,0},{1,2},{2,1},{4,7},{7,4},{5,6},{6,5},{8,11},{11,8},{9,1... | collective-permute-start | bytes 6291464 | tf_op jit(solution)/shard_map/ppermute | solution.py:388
  7.4 56.6 %collective-permute-start.4 = (bf16[1024,1024]{1,0:T(8,128)(2,1)}, bf16[1024,1024]{1,0:T(8,128)(2,1)}, u32[]{:S(2)}, u32[]{:S(2)}) collective-permute-start(bf16[1024,1024]{1,0:T(8,128)(2,1)} %normalized.1.unit.refs_1_.refs_6_.refs_12_), channel_id=1, source_target_pairs={{13,5},{5,1},{9,13},{4,8},{14,6},{6,2},{10,14},{7,11},{29,21},{21,... | collective-permute-start | bytes 6291464 | tf_op jit(solution)/shard_map/ppermute | solution.py:388
  54.7 9.3 %collective-permute-start.3 = (bf16[1024,1024]{1,0:T(8,128)(2,1)}, bf16[1024,1024]{1,0:T(8,128)(2,1)}, u32[]{:S(2)}, u32[]{:S(2)}) collective-permute-start(bf16[1024,1024]{1,0:T(8,128)(2,1)} %collective-permute-done.1.refs_5_.refs_11_), channel_id=1, source_target_pairs={{0,1},{1,0},{4,5},{5,4},{8,9},{9,8},{12,13},{13,12},{3,2},{2,3},{7... | collective-permute-start | bytes 6291464 | tf_op jit(solution)/shard_map/ppermute | solution.py:388
  55.1 8.9 %collective-permute-start.5 = (bf16[1024,1024]{1,0:T(8,128)(2,1)}, bf16[1024,1024]{1,0:T(8,128)(2,1)}, u32[]{:S(2)}, u32[]{:S(2)}) collective-permute-start(bf16[1024,1024]{1,0:T(8,128)(2,1)} %collective-permute-done.refs_2_), channel_id=1, source_target_pairs={{4,5},{5,4},{7,6},{6,7},{20,21},{21,20},{23,22},{22,23}} | collective-permute-start | bytes 6291464 | tf_op jit(solution)/shard_map/ppermute | solution.py:388
  57.1 29.3 %collective-permute-start.11 = (bf16[1024,1024]{1,0:T(8,128)(2,1)}, bf16[1024,1024]{1,0:T(8,128)(2,1)}, u32[]{:S(2)}, u32[]{:S(2)}) collective-permute-start(bf16[1024,1024]{1,0:T(8,128)(2,1)} %normalized.1.unit.refs_1_.refs_6_.refs_12_), channel_id=1, source_target_pairs={{5,9},{8,5},{6,10},{11,6},{21,25},{24,21},{22,26},{27,22}} | collective-permute-start | bytes 6291464 | tf_op jit(solution)/shard_map/ppermute | solution.py:388
  61.1 27.7 %collective-permute-start.12 = (bf16[1024,1024]{1,0:T(8,128)(2,1)}, bf16[1024,1024]{1,0:T(8,128)(2,1)}, u32[]{:S(2)}, u32[]{:S(2)}) collective-permute-start(bf16[1024,1024]{1,0:T(8,128)(2,1)} %collective-permute-done.refs_2_), channel_id=1, source_target_pairs={{8,12},{11,15},{5,6},{6,5},{24,28},{27,31},{21,22},{22,21}} | collective-permute-start | bytes 6291464 | tf_op jit(solution)/shard_map/ppermute | solution.py:388
  77.6 14.0 %collective-permute-start.10 = (f32[1,1024]{1,0:T(1,128)}, f32[1,1024]{1,0:T(1,128)S(1)}, u32[]{:S(2)}, u32[]{:S(2)}) collective-permute-start(f32[1,1024]{1,0:T(1,128)} %get-tuple-element.32), channel_id=1, source_target_pairs={{0,2},{4,1},{5,13},{6,7},{7,15},{8,11},{11,10},{14,12},{16,18},{20... | collective-permute-start | bytes 12296 | tf_op jit(solution)/shard_map/ppermute | solution.py:399
  81.3 10.3 %collective-permute-start.6 = (f32[1,1024]{1,0:T(1,128)}, f32[1,1024]{1,0:T(1,128)S(1)}, u32[]{:S(2)}, u32[]{:S(2)}) collective-permute-start(f32[1,1024]{1,0:T(1,128)} %get-tuple-element.28), channel_id=1, source_target_pairs={{0,4},{1,5},{2,6},{3,7},{4,12},{5,1},{6,15},{7,2},{8,0},{9,8},{11,... | collective-permute-start | bytes 12296 | tf_op jit(solution)/shard_map/ppermute | solution.py:399
  83.3 8.4 %collective-permute-start.7 = (f32[1,1024]{1,0:T(1,128)}, f32[1,1024]{1,0:T(1,128)S(1)}, u32[]{:S(2)}, u32[]{:S(2)}) collective-permute-start(f32[1,1024]{1,0:T(1,128)} %get-tuple-element.29), channel_id=1, source_target_pairs={{0,1},{1,2},{2,3},{3,0},{4,5},{5,7},{6,14},{7,6},{8,4},{10,9},{11,... | collective-permute-start | bytes 12296 | tf_op jit(solution)/shard_map/ppermute | solution.py:399
  86.4 5.3 %collective-permute-start.8 = (f32[1,1024]{1,0:T(1,128)}, f32[1,1024]{1,0:T(1,128)S(1)}, u32[]{:S(2)}, u32[]{:S(2)}) collective-permute-start(f32[1,1024]{1,0:T(1,128)} %get-tuple-element.30), channel_id=1, source_target_pairs={{0,3},{1,0},{2,1},{3,2},{4,6},{5,12},{6,4},{7,5},{8,9},{9,11},{10,... | collective-permute-start | bytes 12296 | tf_op jit(solution)/shard_map/ppermute | solution.py:399
  88.7 3.9 %collective-permute-start.9 = (f32[1,1024]{1,0:T(1,128)}, f32[1,1024]{1,0:T(1,128)S(1)}, u32[]{:S(2)}, u32[]{:S(2)}) collective-permute-start(f32[1,1024]{1,0:T(1,128)} %get-tuple-element.31), channel_id=1, source_target_pairs={{1,3},{2,0},{3,1},{4,7},{5,6},{6,2},{7,4},{8,10},{11,9},{12,8},{13... | collective-permute-start | bytes 12296 | tf_op jit(solution)/shard_map/ppermute | solution.py:399
  91.7 0.9 copy-start.4
  91.7 0.9 copy-start.5
  91.7 0.9 copy-start.6
  91.7 0.9 copy-start.7
  106.8 9.5 %collective-permute-start.13 = (f32[1,1024]{1,0:T(1,128)}, f32[1,1024]{1,0:T(1,128)S(1)}, u32[]{:S(2)}, u32[]{:S(2)}) collective-permute-start(f32[1,1024]{1,0:T(1,128)} %get-tuple-element.35), channel_id=1, source_target_pairs={{5,8},{6,15},{9,11},{10,6},{12,14},{15,3},{21,24},{22,31},{25,27},... | collective-permute-start | bytes 12296 | tf_op jit(solution)/shard_map/ppermute | solution.py:399
  108.1 8.2 %collective-permute-start.14 = (f32[1,1024]{1,0:T(1,128)}, f32[1,1024]{1,0:T(1,128)S(1)}, u32[]{:S(2)}, u32[]{:S(2)}) collective-permute-start(f32[1,1024]{1,0:T(1,128)} %get-tuple-element.36), channel_id=1, source_target_pairs={{5,2},{6,11},{9,10},{10,8},{12,0},{15,13},{21,18},{22,27},{25,26},... | collective-permute-start | bytes 12296 | tf_op jit(solution)/shard_map/ppermute | solution.py:399
  109.4 7.0 %collective-permute-start.15 = (f32[1,1024]{1,0:T(1,128)}, f32[1,1024]{1,0:T(1,128)S(1)}, u32[]{:S(2)}, u32[]{:S(2)}) collective-permute-start(f32[1,1024]{1,0:T(1,128)} %get-tuple-element.37), channel_id=1, source_target_pairs={{5,12},{6,1},{9,8},{10,9},{12,13},{15,14},{21,28},{22,17},{25,24},... | collective-permute-start | bytes 12296 | tf_op jit(solution)/shard_map/ppermute | solution.py:399
  114.4 5.8 %collective-permute-start.16 = (f32[1,1024]{1,0:T(1,128)}, f32[1,1024]{1,0:T(1,128)S(1)}, u32[]{:S(2)}, u32[]{:S(2)}) collective-permute-start(f32[1,1024]{1,0:T(1,128)} %get-tuple-element.38), channel_id=1, source_target_pairs={{5,13},{6,14},{9,5},{10,11},{12,15},{21,29},{22,30},{25,21},{26,27... | collective-permute-start | bytes 12296 | tf_op jit(solution)/shard_map/ppermute | solution.py:399
  116.3 3.8 %copy-start = (f32[1,1024]{1,0:T(1,128)}, f32[1,1024]{1,0:T(1,128)S(1)}, u32[]{:S(2)}) copy-start(f32[1,1024]{1,0:T(1,128)S(1)} %collective-permute-done.13.refs_0_) | copy-start | bytes 12292
  116.3 3.8 %copy-start.1 = (f32[1,1024]{1,0:T(1,128)}, f32[1,1024]{1,0:T(1,128)S(1)}, u32[]{:S(2)}) copy-start(f32[1,1024]{1,0:T(1,128)S(1)} %collective-permute-done.14.refs_1_) | copy-start | bytes 12292
  116.4 3.8 %copy-start.2 = (f32[1,1024]{1,0:T(1,128)}, f32[1,1024]{1,0:T(1,128)S(1)}, u32[]{:S(2)}) copy-start(f32[1,1024]{1,0:T(1,128)S(1)} %collective-permute-done.15.refs_2_) | copy-start | bytes 12292
  (2 other events, 1.2 us)

commit v7 on v6

--- a/solution.py
+++ b/solution.py
@@ -36,13 +36,13 @@
     every = [(z, lane) for z in range(4) for lane in (0, 1)]
     swap = rows([((z, lane), (z, 1 - lane)) for z, lane in every])
     first = [((0, 0), (2, 0)), ((2, 0), (3, 0)), ((3, 0), (1, 0)), ((1, 0), (0, 0)), ((0, 1), (1, 1))]
-    second = [((3, 1), (1, 1)), ((1, 1), (0, 1)), ((2, 1), (3, 1)), ((1, 0), (2, 0))]
+    second = [((3, 1), (1, 1)), ((1, 1), (0, 1)), ((2, 1), (3, 1)), ((1, 0), (2, 1))]
     return [
         Move("R1", "own", rows(first), 0, 1),
         Move("R2", "own", rows(second), 0, 1),
         Move("Y", "own", across(every), 0, 1),
         Move("A", "own", swap, 0, 0),
-        Move("R3", "own", rows([((1, 1), (2, 1)), ((2, 0), (1, 1))]), 1, 2, "R1"),
+        Move("R3", "own", rows([((1, 1), (2, 0)), ((2, 0), (1, 1))]), 1, 2, "R1"),
         Move("V", "R1", rows([((2, 0), (3, 0))]) + across([(1, 1)]), 1, 2),
         Move("F", "Y", swap, 1, 1),
         Move("W", "R1", rows([((1, 0), (1, 1)), ((1, 1), (1, 0))]), 1, 1),
@@ -50,22 +50,22 @@
 
 
 GRID_PAIRS = (
-    ((0, 1), (0, 4), (1, 2), (1, 4), (3, 4)),
-    ((0, 5), (1, 5), (2, 5), (3, 5)),
-    ((0, 2), (0, 6), (1, 6), (2, 6), (3, 6)),
-    ((0, 3), (1, 3), (2, 3), (2, 7), (3, 7)),
-    ((1, 7), (4, 5), (4, 7), (5, 6), (7, 12)),
-    ((1, 12), (1, 13), (2, 8), (2, 12), (2, 13), (6, 12), (7, 13), (8, 13)),
-    ((1, 11), (1, 14), (1, 15), (2, 4), (2, 14), (4, 14), (4, 15), (6, 7), (11, 15)),
-    ((2, 15), (4, 6), (5, 7), (5, 15)),
-    ((0, 10), (0, 11), (4, 8), (4, 9), (4, 10)),
-    ((5, 8), (5, 9), (5, 10), (5, 11), (8, 9), (8, 11), (9, 11)),
-    ((6, 8), (6, 9), (6, 10), (6, 11), (8, 10), (9, 10)),
-    ((3, 8), (3, 9), (7, 8), (7, 9), (7, 10), (7, 11), (10, 11)),
-    ((0, 12), (0, 13), (0, 14), (0, 15), (8, 12), (8, 14), (12, 13), (13, 14), (13, 15)),
-    ((9, 12), (9, 13), (9, 14), (9, 15), (12, 14)),
-    ((10, 12), (10, 13), (10, 14), (10, 15)),
-    ((3, 13), (3, 14), (3, 15), (11, 12), (11, 13), (11, 14), (12, 15), (14, 15)),
+    ((0, 1), (0, 4), (1, 3), (1, 4), (3, 4)),
+    ((0, 5), (1, 2), (2, 5), (3, 5)),
+    ((0, 6), (1, 6), (2, 6), (3, 6)),
+    ((0, 2), (0, 3), (1, 7), (2, 3), (2, 7), (3, 7)),
+    ((4, 5), (4, 7), (5, 6), (6, 12), (7, 12)),
+    ((1, 5), (1, 12), (1, 13), (2, 8), (2, 12), (2, 13), (7, 13), (8, 12)),
+    ((1, 11), (1, 14), (1, 15), (2, 4), (2, 14), (4, 6), (4, 14), (11, 14)),
+    ((2, 15), (4, 15), (5, 7), (5, 15), (6, 7)),
+    ((0, 10), (0, 11), (5, 8), (5, 9), (5, 10), (5, 11), (8, 11)),
+    ((4, 8), (4, 9), (4, 10), (8, 9), (9, 11)),
+    ((7, 8), (7, 9), (7, 10), (7, 11)),
+    ((3, 8), (3, 9), (6, 8), (6, 9), (6, 10), (6, 11), (8, 10), (9, 10), (10, 11)),
+    ((0, 12), (0, 13), (0, 14), (0, 15), (8, 13), (8, 14), (12, 15), (13, 14)),
+    ((9, 12), (9, 13), (9, 14), (9, 15), (12, 13)),
+    ((10, 12), (10, 13), (10, 14), (10, 15), (12, 14), (14, 15)),
+    ((3, 13), (3, 14), (3, 15), (11, 12), (11, 13), (11, 15), (13, 15)),
 )
 
 
@@ -78,7 +78,7 @@
 
 def planned(count):
     if count == 16:
-        moves, placed_pairs, sending = grid_moves(), GRID_PAIRS, (1, 2)
+        moves, placed_pairs, sending = grid_moves(), GRID_PAIRS, (2,)
     else:
         moves, sending = ring_moves(count), (STEPS,)
         placed_pairs = [[(b, (b + k) % count) for k in range(1, STEPS + 1)] for b in range(count)]

time: 124 us -> 123 us (level)
  the two profiles are of different devices: /device:TPU:9 before, /device:TPU:0 now
where the time goes in v7:
time: 123 us
  starting transfers between devices  49.1 us (40%)
  waiting for transfers between devices  40.5 us (33%)
  Pallas kernels  32.3 us (26%)
    ppermute x8, waiting for transfers between devices, local(): slots[move.name] = lax.ppermute(value, 'blk', move.pairs)  33.6 us
    ppermute x6, starting transfers between devices, local(): lax.ppermute(row, 'blk', permute)  33.3 us
    pallas_call x3, Pallas kernels, scored(): pl.pallas_call(functools.partial(pairs_kernel, len(given), len(sends), le...  21.3 us
    ppermute x8, starting transfers between devices, local(): slots[move.name] = lax.ppermute(value, 'blk', move.pairs)  15.8 us
    ppermute x6, waiting for transfers between devices, local(): lax.ppermute(row, 'blk', permute)  6.91 us
    pallas_call x1, Pallas kernels, own_block(): pl.pallas_call(own_kernel, out_shape=jax.ShapeDtypeStruct((nblocks, rows)...  4.65 us
    pallas_call x1, Pallas kernels, normalized(): pl.pallas_call(unit_kernel, out_shape=jax.ShapeDtypeStruct((rows, depth),...  4.14 us
  transfers between devices with their start and end apart: 14, of which 4 were waited for; matrix products, arithmetic and copies ran while one was open for 0% of the time, Pallas kernels for 20%

profile of v7, /device:TPU:0, one launch (start us, length us, event | category | flops | bytes accessed | tf_op | source)
XLA Modules:
  0.0 122.6 jit_solution(5571451028229807166)
XLA Ops:
  0.0 4.1 %normalized.1.unit.refs_1_.refs_6_.refs_7_ = bf16[1024,1024]{1,0:T(8,128)(2,1)} custom-call(s32[16]{0:T(128)} %pads.5, s32[1024]{0:T(1024)} %order_smem.1, s32[1,1024]{1,0:T(1,128)} %bitcast.2, bf16[1024,1024]{1,0:T(8,128)(2,1)} %embeddings.1), custom_call_target="tpu_custom_call" | custom-call | flops 4194304 | bytes 4194304 | tf_op jit(solution)/shard_map/normalized/pallas_call | solution.py:174
  4.1 0.5 collective-permute-start.2
  4.7 5.5 %collective-permute-start = (bf16[1024,1024]{1,0:T(8,128)(2,1)}, bf16[1024,1024]{1,0:T(8,128)(2,1)}, u32[]{:S(2)}, u32[]{:S(2)}) collective-permute-start(bf16[1024,1024]{1,0:T(8,128)(2,1)} %normalized.1.unit.refs_1_.refs_6_.refs_7_), channel_id=1, source_target_pairs={{0,8},{8,12},{12,4},{4,0},{1,5},{3,11},{11,15},{15,7},{7,3},{2,6},... | collective-permute-start | bytes 6291464 | tf_op jit(solution)/shard_map/ppermute | solution.py:388
  10.2 1.4 %collective-permute-start.1 = (bf16[1024,1024]{1,0:T(8,128)(2,1)}, bf16[1024,1024]{1,0:T(8,128)(2,1)}, u32[]{:S(2)}, u32[]{:S(2)}) collective-permute-start(bf16[1024,1024]{1,0:T(8,128)(2,1)} %normalized.1.unit.refs_1_.refs_6_.refs_7_), channel_id=1, source_target_pairs={{0,3},{3,0},{1,2},{2,1},{4,7},{7,4},{5,6},{6,5},{8,11},{11,8},{9,1... | collective-permute-start | bytes 6291464 | tf_op jit(solution)/shard_map/ppermute | solution.py:388
  11.6 2.0 %collective-permute-start.4 = (bf16[1024,1024]{1,0:T(8,128)(2,1)}, bf16[1024,1024]{1,0:T(8,128)(2,1)}, u32[]{:S(2)}, u32[]{:S(2)}) collective-permute-start(bf16[1024,1024]{1,0:T(8,128)(2,1)} %normalized.1.unit.refs_1_.refs_6_.refs_7_), channel_id=1, source_target_pairs={{13,5},{5,1},{9,13},{4,9},{14,6},{6,2},{10,14},{7,10},{29,21},{21,... | collective-permute-start | bytes 6291464 | tf_op jit(solution)/shard_map/ppermute | solution.py:388
  13.6 4.6 %own_block.1.best = f32[16,1024]{1,0:T(8,128)} custom-call(s32[16]{0:T(128)} %pads.5, s32[1,1024]{1,0:T(1,128)} %bitcast.3, bf16[1024,1024]{1,0:T(8,128)(2,1)} %normalized.1.unit.refs_1_.refs_6_.refs_7_), custom_call_target="tpu_custom_call" | custom-call | flops 2147483648 | bytes 2097152 | tf_op jit(solution)/shard_map/own_block/pallas_call | solution.py:221
  18.2 6.1 %scored.3.best = f32[16,1024]{1,0:T(8,128)} custom-call(s32[144]{0:T(256)} %constant.8.clone.table, f32[16,1024]{1,0:T(8,128)} %own_block.1.best, bf16[1024,1024]{1,0:T(8,128)(2,1)} %collective-permute-done.2.refs_0_, bf16[1024,1024]{1,0:T(8,128)(2,1)} %normalized.1.unit.refs_1_.refs_6_.refs_7_), custom_call_target="tpu_custom_call" | custom-call | flops 2147483648 | bytes 4194304 | tf_op jit(solution)/shard_map/scored/pallas_call | solution.py:319
  24.4 30.7 %collective-permute-done.refs_2_ = bf16[1024,1024]{1,0:T(8,128)(2,1)} collective-permute-done((bf16[1024,1024]{1,0:T(8,128)(2,1)}, bf16[1024,1024]{1,0:T(8,128)(2,1)}, u32[]{:S(2)}, u32[]{:S(2)}) %collective-permute-start) | collective-permute-done | bytes 2097184 | tf_op jit(solution)/shard_map/ppermute | solution.py:388
  55.0 2.9 %collective-permute-done.1.refs_5_.refs_6_ = bf16[1024,1024]{1,0:T(8,128)(2,1)} collective-permute-done((bf16[1024,1024]{1,0:T(8,128)(2,1)}, bf16[1024,1024]{1,0:T(8,128)(2,1)}, u32[]{:S(2)}, u32[]{:S(2)}) %collective-permute-start.1) | collective-permute-done | bytes 2097184 | tf_op jit(solution)/shard_map/ppermute | solution.py:388
  58.3 2.0 %collective-permute-start.5 = (bf16[1024,1024]{1,0:T(8,128)(2,1)}, bf16[1024,1024]{1,0:T(8,128)(2,1)}, u32[]{:S(2)}, u32[]{:S(2)}) collective-permute-start(bf16[1024,1024]{1,0:T(8,128)(2,1)} %collective-permute-done.refs_2_), channel_id=1, source_target_pairs={{4,5},{5,4},{7,6},{6,7},{20,21},{21,20},{23,22},{22,23}} | collective-permute-start | bytes 6291464 | tf_op jit(solution)/shard_map/ppermute | solution.py:388
  60.3 2.0 %collective-permute-start.6 = (bf16[1024,1024]{1,0:T(8,128)(2,1)}, bf16[1024,1024]{1,0:T(8,128)(2,1)}, u32[]{:S(2)}, u32[]{:S(2)}) collective-permute-start(bf16[1024,1024]{1,0:T(8,128)(2,1)} %normalized.1.unit.refs_1_.refs_6_.refs_7_), channel_id=1, source_target_pairs={{5,8},{8,5},{6,11},{11,6},{21,24},{24,21},{22,27},{27,22}} | collective-permute-start | bytes 6291464 | tf_op jit(solution)/shard_map/ppermute | solution.py:388
  62.3 2.0 %collective-permute-start.7 = (bf16[1024,1024]{1,0:T(8,128)(2,1)}, bf16[1024,1024]{1,0:T(8,128)(2,1)}, u32[]{:S(2)}, u32[]{:S(2)}) collective-permute-start(bf16[1024,1024]{1,0:T(8,128)(2,1)} %collective-permute-done.refs_2_), channel_id=1, source_target_pairs={{8,12},{11,15},{5,6},{6,5},{24,28},{27,31},{21,22},{22,21}} | collective-permute-start | bytes 6291464 | tf_op jit(solution)/shard_map/ppermute | solution.py:388
  64.3 13.6 %scored.4.best = f32[16,1024]{1,0:T(8,128)} custom-call(s32[512]{0:T(512)} %constant.9.clone.table, f32[16,1024]{1,0:T(8,128)} %scored.3.best, bf16[1024,1024]{1,0:T(8,128)(2,1)} %collective-permute-done.2.refs_0_, bf16[1024,1024]{1,0:T(8,128)(2,1)} %collective-permute-done.3.refs_1_, bf16[1024,1024]{1,0:T(8,128)(2,1)} %collective-permute-done.refs_2_, ...), custom_call_target="tpu_custom_call" | custom-call | flops 10737418240 | bytes 10485760 | tf_op jit(solution)/shard_map/scored/pallas_call | solution.py:319
  77.9 1.6 %scored.5 = (f32[16,1024]{1,0:T(8,128)}, f32[1,1024]{1,0:T(1,128)}, f32[1,1024]{1,0:T(1,128)}, f32[1,1024]{1,0:T(1,128)}, f32[1,1024]{1,0:T(1,128)}, /*index=5*/f32[1,1024]{1,0:T(1,128)}, f32[1,1024]{1,0:T(1,128)}) custom-call(s32[528]{0:T(1024)} %constant.10.clone.table, f32[16,1024]{1,0:T(8,128)} %scored.4.best, ...), custom_call_target="tpu_custom_call" | custom-call | flops 8589934592 | bytes 10485760 | tf_op jit(solution)/shard_map/scored/pallas_call | solution.py:319
  79.5 1.3 %collective-permute-start.10 = (f32[1,1024]{1,0:T(1,128)}, f32[1,1024]{1,0:T(1,128)S(1)}, u32[]{:S(2)}, u32[]{:S(2)}) collective-permute-start(f32[1,1024]{1,0:T(1,128)} %get-tuple-element.27), channel_id=1, source_target_pairs={{2,3},{3,2},{4,7},{5,1},{6,11},{7,5},{8,0},{9,4},{10,9},{11,6},{12... | collective-permute-start | bytes 12296 | tf_op jit(solution)/shard_map/ppermute | solution.py:399
  80.8 5.1 %collective-permute-start.11 = (f32[1,1024]{1,0:T(1,128)}, f32[1,1024]{1,0:T(1,128)S(1)}, u32[]{:S(2)}, u32[]{:S(2)}) collective-permute-start(f32[1,1024]{1,0:T(1,128)} %get-tuple-element.28), channel_id=1, source_target_pairs={{0,3},{1,0},{2,1},{3,7},{4,5},{5,2},{6,4},{7,6},{8,10},{9,8},{10,1... | collective-permute-start | bytes 12296 | tf_op jit(solution)/shard_map/ppermute | solution.py:399
  85.9 23.0 %collective-permute-start.12 = (f32[1,1024]{1,0:T(1,128)}, f32[1,1024]{1,0:T(1,128)S(1)}, u32[]{:S(2)}, u32[]{:S(2)}) collective-permute-start(f32[1,1024]{1,0:T(1,128)} %get-tuple-element.29), channel_id=1, source_target_pairs={{0,4},{1,5},{3,0},{5,12},{6,1},{7,2},{8,11},{10,8},{11,3},{12,15},... | collective-permute-start | bytes 12296 | tf_op jit(solution)/shard_map/ppermute | solution.py:399
  108.9 0.7 collective-permute-start.13
  109.6 1.9 %collective-permute-start.8 = (f32[1,1024]{1,0:T(1,128)}, f32[1,1024]{1,0:T(1,128)S(1)}, u32[]{:S(2)}, u32[]{:S(2)}) collective-permute-start(f32[1,1024]{1,0:T(1,128)} %get-tuple-element.25), channel_id=1, source_target_pairs={{0,1},{1,2},{2,6},{4,12},{5,8},{6,14},{7,15},{8,5},{9,11},{10,7},{... | collective-permute-start | bytes 12296 | tf_op jit(solution)/shard_map/ppermute | solution.py:399
  111.5 1.3 %collective-permute-start.9 = (f32[1,1024]{1,0:T(1,128)}, f32[1,1024]{1,0:T(1,128)S(1)}, u32[]{:S(2)}, u32[]{:S(2)}) collective-permute-start(f32[1,1024]{1,0:T(1,128)} %get-tuple-element.26), channel_id=1, source_target_pairs={{1,3},{2,0},{3,1},{4,6},{5,7},{6,2},{7,4},{8,9},{9,10},{11,8},{12,... | collective-permute-start | bytes 12296 | tf_op jit(solution)/shard_map/ppermute | solution.py:399
  112.9 4.2 %collective-permute-done.8.refs_0_ = f32[1,1024]{1,0:T(1,128)S(1)} collective-permute-done((f32[1,1024]{1,0:T(1,128)}, f32[1,1024]{1,0:T(1,128)S(1)}, u32[]{:S(2)}, u32[]{:S(2)}) %collective-permute-start.8) | collective-permute-done | bytes 4128 | tf_op jit(solution)/shard_map/ppermute | solution.py:399
  117.1 2.7 %collective-permute-done.9.refs_1_ = f32[1,1024]{1,0:T(1,128)S(1)} collective-permute-done((f32[1,1024]{1,0:T(1,128)}, f32[1,1024]{1,0:T(1,128)S(1)}, u32[]{:S(2)}, u32[]{:S(2)}) %collective-permute-start.9) | collective-permute-done | bytes 4128 | tf_op jit(solution)/shard_map/ppermute | solution.py:399
  119.8 0.6 copy-done.5
  120.4 2.2 %placed.1 = f32[1,1024]{1,0:T(1,128)} custom-call(s32[96]{0:T(128)} %constant.11.clone.taken, s32[16]{0:T(128)} %pads.5, s32[1,1024]{1,0:T(1,128)} %bitcast.4, f32[16,1024]{1,0:T(8,128)} %get-tuple-element.24.best, f32[1,1024]{1,0:T(1,128)} %copy-done.4, f32[1,1024]{1,0:T(1,128)} %copy-done.5, f32[1,1024]{1,0:T(1,128)} %copy-done, f32[1,1024]{1,0:T(1,128)} %copy-done.1, ...), custom_call_target="tpu_custom_call" | custom-call | tf_op jit(solution)/shard_map/placed/pallas_call | solution.py:362
  (22 shorter events, 0.5 us)
Async XLA Ops:
  4.1 14.1 %collective-permute-start.2 = (bf16[1024,1024]{1,0:T(8,128)(2,1)}, bf16[1024,1024]{1,0:T(8,128)(2,1)}, u32[]{:S(2)}, u32[]{:S(2)}) collective-permute-start(bf16[1024,1024]{1,0:T(8,128)(2,1)} %normalized.1.unit.refs_1_.refs_6_.refs_7_), channel_id=1, source_target_pairs={{0,1},{1,0},{4,5},{5,4},{8,9},{9,8},{12,13},{13,12},{3,2},{2,3},{7... | collective-permute-start | bytes 6291464 | tf_op jit(solution)/shard_map/ppermute | solution.py:388
  4.7 50.4 %collective-permute-start = (bf16[1024,1024]{1,0:T(8,128)(2,1)}, bf16[1024,1024]{1,0:T(8,128)(2,1)}, u32[]{:S(2)}, u32[]{:S(2)}) collective-permute-start(bf16[1024,1024]{1,0:T(8,128)(2,1)} %normalized.1.unit.refs_1_.refs_6_.refs_7_), channel_id=1, source_target_pairs={{0,8},{8,12},{12,4},{4,0},{1,5},{3,11},{11,15},{15,7},{7,3},{2,6},... | collective-permute-start | bytes 6291464 | tf_op jit(solution)/shard_map/ppermute | solution.py:388
  10.2 47.7 %collective-permute-start.1 = (bf16[1024,1024]{1,0:T(8,128)(2,1)}, bf16[1024,1024]{1,0:T(8,128)(2,1)}, u32[]{:S(2)}, u32[]{:S(2)}) collective-permute-start(bf16[1024,1024]{1,0:T(8,128)(2,1)} %normalized.1.unit.refs_1_.refs_6_.refs_7_), channel_id=1, source_target_pairs={{0,3},{3,0},{1,2},{2,1},{4,7},{7,4},{5,6},{6,5},{8,11},{11,8},{9,1... | collective-permute-start | bytes 6291464 | tf_op jit(solution)/shard_map/ppermute | solution.py:388
  11.6 52.7 %collective-permute-start.4 = (bf16[1024,1024]{1,0:T(8,128)(2,1)}, bf16[1024,1024]{1,0:T(8,128)(2,1)}, u32[]{:S(2)}, u32[]{:S(2)}) collective-permute-start(bf16[1024,1024]{1,0:T(8,128)(2,1)} %normalized.1.unit.refs_1_.refs_6_.refs_7_), channel_id=1, source_target_pairs={{13,5},{5,1},{9,13},{4,9},{14,6},{6,2},{10,14},{7,10},{29,21},{21,... | collective-permute-start | bytes 6291464 | tf_op jit(solution)/shard_map/ppermute | solution.py:388
  57.9 6.4 %collective-permute-start.3 = (bf16[1024,1024]{1,0:T(8,128)(2,1)}, bf16[1024,1024]{1,0:T(8,128)(2,1)}, u32[]{:S(2)}, u32[]{:S(2)}) collective-permute-start(bf16[1024,1024]{1,0:T(8,128)(2,1)} %collective-permute-done.1.refs_5_.refs_6_), channel_id=1, source_target_pairs={{0,1},{1,0},{4,5},{5,4},{8,9},{9,8},{12,13},{13,12},{3,2},{2,3},{7... | collective-permute-start | bytes 6291464 | tf_op jit(solution)/shard_map/ppermute | solution.py:388
  58.3 6.0 %collective-permute-start.5 = (bf16[1024,1024]{1,0:T(8,128)(2,1)}, bf16[1024,1024]{1,0:T(8,128)(2,1)}, u32[]{:S(2)}, u32[]{:S(2)}) collective-permute-start(bf16[1024,1024]{1,0:T(8,128)(2,1)} %collective-permute-done.refs_2_), channel_id=1, source_target_pairs={{4,5},{5,4},{7,6},{6,7},{20,21},{21,20},{23,22},{22,23}} | collective-permute-start | bytes 6291464 | tf_op jit(solution)/shard_map/ppermute | solution.py:388
  60.3 17.6 %collective-permute-start.6 = (bf16[1024,1024]{1,0:T(8,128)(2,1)}, bf16[1024,1024]{1,0:T(8,128)(2,1)}, u32[]{:S(2)}, u32[]{:S(2)}) collective-permute-start(bf16[1024,1024]{1,0:T(8,128)(2,1)} %normalized.1.unit.refs_1_.refs_6_.refs_7_), channel_id=1, source_target_pairs={{5,8},{8,5},{6,11},{11,6},{21,24},{24,21},{22,27},{27,22}} | collective-permute-start | bytes 6291464 | tf_op jit(solution)/shard_map/ppermute | solution.py:388
  62.3 15.6 %collective-permute-start.7 = (bf16[1024,1024]{1,0:T(8,128)(2,1)}, bf16[1024,1024]{1,0:T(8,128)(2,1)}, u32[]{:S(2)}, u32[]{:S(2)}) collective-permute-start(bf16[1024,1024]{1,0:T(8,128)(2,1)} %collective-permute-done.refs_2_), channel_id=1, source_target_pairs={{8,12},{11,15},{5,6},{6,5},{24,28},{27,31},{21,22},{22,21}} | collective-permute-start | bytes 6291464 | tf_op jit(solution)/shard_map/ppermute | solution.py:388
  79.5 32.0 %collective-permute-start.10 = (f32[1,1024]{1,0:T(1,128)}, f32[1,1024]{1,0:T(1,128)S(1)}, u32[]{:S(2)}, u32[]{:S(2)}) collective-permute-start(f32[1,1024]{1,0:T(1,128)} %get-tuple-element.27), channel_id=1, source_target_pairs={{2,3},{3,2},{4,7},{5,1},{6,11},{7,5},{8,0},{9,4},{10,9},{11,6},{12... | collective-permute-start | bytes 12296 | tf_op jit(solution)/shard_map/ppermute | solution.py:399
  80.8 32.0 %collective-permute-start.11 = (f32[1,1024]{1,0:T(1,128)}, f32[1,1024]{1,0:T(1,128)S(1)}, u32[]{:S(2)}, u32[]{:S(2)}) collective-permute-start(f32[1,1024]{1,0:T(1,128)} %get-tuple-element.28), channel_id=1, source_target_pairs={{0,3},{1,0},{2,1},{3,7},{4,5},{5,2},{6,4},{7,6},{8,10},{9,8},{10,1... | collective-permute-start | bytes 12296 | tf_op jit(solution)/shard_map/ppermute | solution.py:399
  85.9 26.9 %collective-permute-start.12 = (f32[1,1024]{1,0:T(1,128)}, f32[1,1024]{1,0:T(1,128)S(1)}, u32[]{:S(2)}, u32[]{:S(2)}) collective-permute-start(f32[1,1024]{1,0:T(1,128)} %get-tuple-element.29), channel_id=1, source_target_pairs={{0,4},{1,5},{3,0},{5,12},{6,1},{7,2},{8,11},{10,8},{11,3},{12,15},... | collective-permute-start | bytes 12296 | tf_op jit(solution)/shard_map/ppermute | solution.py:399
  108.9 4.0 %collective-permute-start.13 = (f32[1,1024]{1,0:T(1,128)}, f32[1,1024]{1,0:T(1,128)S(1)}, u32[]{:S(2)}, u32[]{:S(2)}) collective-permute-start(f32[1,1024]{1,0:T(1,128)} %get-tuple-element.30), channel_id=1, source_target_pairs={{5,13},{6,15},{21,29},{22,31}} | collective-permute-start | bytes 12296 | tf_op jit(solution)/shard_map/ppermute | solution.py:399
  109.6 7.5 %collective-permute-start.8 = (f32[1,1024]{1,0:T(1,128)}, f32[1,1024]{1,0:T(1,128)S(1)}, u32[]{:S(2)}, u32[]{:S(2)}) collective-permute-start(f32[1,1024]{1,0:T(1,128)} %get-tuple-element.25), channel_id=1, source_target_pairs={{0,1},{1,2},{2,6},{4,12},{5,8},{6,14},{7,15},{8,5},{9,11},{10,7},{... | collective-permute-start | bytes 12296 | tf_op jit(solution)/shard_map/ppermute | solution.py:399
  111.5 8.3 %copy-start = (f32[1,1024]{1,0:T(1,128)}, f32[1,1024]{1,0:T(1,128)S(1)}, u32[]{:S(2)}) copy-start(f32[1,1024]{1,0:T(1,128)S(1)} %collective-permute-done.10.refs_2_) | copy-start | bytes 12292
  111.5 8.3 %collective-permute-start.9 = (f32[1,1024]{1,0:T(1,128)}, f32[1,1024]{1,0:T(1,128)S(1)}, u32[]{:S(2)}, u32[]{:S(2)}) collective-permute-start(f32[1,1024]{1,0:T(1,128)} %get-tuple-element.26), channel_id=1, source_target_pairs={{1,3},{2,0},{3,1},{4,6},{5,7},{6,2},{7,4},{8,9},{9,10},{11,8},{12,... | collective-permute-start | bytes 12296 | tf_op jit(solution)/shard_map/ppermute | solution.py:399
  112.8 7.0 %copy-start.1 = (f32[1,1024]{1,0:T(1,128)}, f32[1,1024]{1,0:T(1,128)S(1)}, u32[]{:S(2)}) copy-start(f32[1,1024]{1,0:T(1,128)S(1)} %collective-permute-done.11.refs_3_) | copy-start | bytes 12292
  112.8 6.9 %copy-start.2 = (f32[1,1024]{1,0:T(1,128)}, f32[1,1024]{1,0:T(1,128)S(1)}, u32[]{:S(2)}) copy-start(f32[1,1024]{1,0:T(1,128)S(1)} %collective-permute-done.12.refs_4_) | copy-start | bytes 12292
  112.9 6.9 %copy-start.3 = (f32[1,1024]{1,0:T(1,128)}, f32[1,1024]{1,0:T(1,128)S(1)}, u32[]{:S(2)}) copy-start(f32[1,1024]{1,0:T(1,128)S(1)} %collective-permute-done.13.refs_5_) | copy-start | bytes 12292
  117.1 2.7 %copy-start.4 = (f32[1,1024]{1,0:T(1,128)}, f32[1,1024]{1,0:T(1,128)S(1)}, u32[]{:S(2)}) copy-start(f32[1,1024]{1,0:T(1,128)S(1)} %collective-permute-done.8.refs_0_) | copy-start | bytes 12292
  119.8 0.6 copy-start.5

commit v8 on v7

--- a/solution.py
+++ b/solution.py
@@ -78,7 +78,7 @@
 
 def planned(count):
     if count == 16:
-        moves, placed_pairs, sending = grid_moves(), GRID_PAIRS, (2,)
+        moves, placed_pairs, sending = grid_moves(), GRID_PAIRS, (1, 2)
     else:
         moves, sending = ring_moves(count), (STEPS,)
         placed_pairs = [[(b, (b + k) % count) for k in range(1, STEPS + 1)] for b in range(count)]
@@ -123,6 +123,30 @@
         [(of, to[c]) for of, to in enumerate(sends) if c in to]
         for c in range(max((c + 1 for to in sends for c in to), default=0))
     ]
+
+
+def in_two(early, late, count):
+    early, late = set(early) - set(late), set(late)
+
+    def degrees(edges):
+        return [
+            [sum(edge[side] == device for edge in edges) for device in range(count)] for side in (0, 1)
+        ]
+
+    most = max(degrees(late)[0] + degrees(late)[1])
+    while early:
+        busy, taken = degrees(early), degrees(late)
+        top = max(busy[0] + busy[1])
+        free = [
+            (max(busy[0][of], busy[1][to]), busy[0][of] + busy[1][to], of, to)
+            for of, to in sorted(early)
+            if max(taken[0][of], taken[1][to]) < most and max(busy[0][of], busy[1][to]) == top
+        ]
+        if not free:
+            break
+        early.remove(max(free)[2:])
+        late.add(max(free)[2:])
+    return sorted(early), sorted(late)
 
 
 def unit_kernel(pads, order_smem, order, embeddings, unit, value, result, tile, into, out, sem):
@@ -375,7 +399,15 @@
     unit = normalized(embeddings, order, pad_counts)
     slots, best = {"own": unit}, None
     rank = dict({"own": -1}, **{move.name: move.stage for move in moves})
-    touched, permutes, found = [set() for _ in range(nblocks)], [], []
+    edges = [
+        {(of, to) for of in range(nblocks) for pair in pairs[of] for to in pair[2:] if to != of}
+        for pairs in work
+    ]
+    edges = {sending[-1]: set().union(*edges[sending[0] + 1 :] if len(sending) > 1 else edges),
+             sending[0]: set().union(*edges[: sending[0] + 1])}
+    if len(sending) > 1:
+        edges = dict(zip(sending, in_two(edges[sending[0]], edges[sending[1]], nblocks)))
+    permutes, found = [], []
     for stage, pairs in enumerate(work):
         starting = [move for move in moves if move.begins == stage]
         for needs in sorted({move.needs for move in starting}):
@@ -388,12 +420,7 @@
                     slots[move.name] = lax.ppermute(value, "blk", move.pairs)
         if stage == 0:
             best = own_block(unit, order, pad_counts, nblocks)
-        for device, mine in enumerate(pairs):
-            touched[device] |= {block for pair in mine for block in pair[2:] if block != device}
-        sends = []
-        if stage in sending:
-            sends = colored([(of, to) for of in range(nblocks) for to in sorted(touched[of])], nblocks)
-            touched = [set() for _ in range(nblocks)]
+        sends = colored(sorted(edges[stage]), nblocks) if stage in sending else []
         if any(pairs):
             best, *rows = scored(best, found, permutes, slots, rank, pairs, sends)
             found = [lax.ppermute(row, "blk", permute) for row, permute in zip(rows, sends)]

time: 123 us -> 120 us (0.976)
  the two profiles are of different devices: /device:TPU:0 before, /device:TPU:1 now
where the time goes in v8:
time: 120 us; the launch traced here: 119 us
  waiting for transfers between devices  45.7 us (38%)
  starting transfers between devices  44.6 us (37%)
  Pallas kernels  27.6 us (23%)
    ppermute x8, waiting for transfers between devices, local(): slots[move.name] = lax.ppermute(value, 'blk', move.pairs)  38.7 us
    ppermute x6, starting transfers between devices, local(): lax.ppermute(row, 'blk', permute)  29.8 us
    pallas_call x3, Pallas kernels, scored(): pl.pallas_call(functools.partial(pairs_kernel, len(given), len(sends), le...  16.7 us
    ppermute x8, starting transfers between devices, local(): slots[move.name] = lax.ppermute(value, 'blk', move.pairs)  14.9 us
    ppermute x6, waiting for transfers between devices, local(): lax.ppermute(row, 'blk', permute)  6.96 us
    pallas_call x1, Pallas kernels, own_block(): pl.pallas_call(own_kernel, out_shape=jax.ShapeDtypeStruct((nblocks, rows)...  4.64 us
    pallas_call x1, Pallas kernels, normalized(): pl.pallas_call(unit_kernel, out_shape=jax.ShapeDtypeStruct((rows, depth),...  4.14 us
  transfers between devices with their start and end apart: 14, of which 4 were waited for; matrix products, arithmetic and copies ran while one was open for 0% of the time, Pallas kernels for 17%

profile of v8, /device:TPU:1, one launch (start us, length us, event | category | flops | bytes accessed | tf_op | source)
XLA Modules:
  0.0 119.3 jit_solution(9140263402949108501)
XLA Ops:
  0.0 4.1 %normalized.1.unit.refs_1_.refs_6_.refs_9_ = bf16[1024,1024]{1,0:T(8,128)(2,1)} custom-call(s32[16]{0:T(128)} %pads.5, s32[1024]{0:T(1024)} %order_smem.1, s32[1,1024]{1,0:T(1,128)} %bitcast.2, bf16[1024,1024]{1,0:T(8,128)(2,1)} %embeddings.1), custom_call_target="tpu_custom_call" | custom-call | flops 4194304 | bytes 4194304 | tf_op jit(solution)/shard_map/normalized/pallas_call | solution.py:198
  4.3 6.0 %collective-permute-start = (bf16[1024,1024]{1,0:T(8,128)(2,1)}, bf16[1024,1024]{1,0:T(8,128)(2,1)}, u32[]{:S(2)}, u32[]{:S(2)}) collective-permute-start(bf16[1024,1024]{1,0:T(8,128)(2,1)} %normalized.1.unit.refs_1_.refs_6_.refs_9_), channel_id=1, source_target_pairs={{0,8},{8,12},{12,4},{4,0},{1,5},{3,11},{11,15},{15,7},{7,3},{2,6},... | collective-permute-start | bytes 6291464 | tf_op jit(solution)/shard_map/ppermute | solution.py:420
  10.2 1.4 %collective-permute-start.1 = (bf16[1024,1024]{1,0:T(8,128)(2,1)}, bf16[1024,1024]{1,0:T(8,128)(2,1)}, u32[]{:S(2)}, u32[]{:S(2)}) collective-permute-start(bf16[1024,1024]{1,0:T(8,128)(2,1)} %normalized.1.unit.refs_1_.refs_6_.refs_9_), channel_id=1, source_target_pairs={{0,3},{3,0},{1,2},{2,1},{4,7},{7,4},{5,6},{6,5},{8,11},{11,8},{9,1... | collective-permute-start | bytes 6291464 | tf_op jit(solution)/shard_map/ppermute | solution.py:420
  11.7 1.3 %collective-permute-start.4 = (bf16[1024,1024]{1,0:T(8,128)(2,1)}, bf16[1024,1024]{1,0:T(8,128)(2,1)}, u32[]{:S(2)}, u32[]{:S(2)}) collective-permute-start(bf16[1024,1024]{1,0:T(8,128)(2,1)} %normalized.1.unit.refs_1_.refs_6_.refs_9_), channel_id=1, source_target_pairs={{13,5},{5,1},{9,13},{4,9},{14,6},{6,2},{10,14},{7,10},{29,21},{21,... | collective-permute-start | bytes 6291464 | tf_op jit(solution)/shard_map/ppermute | solution.py:420
  13.0 4.6 %own_block.1.best = f32[16,1024]{1,0:T(8,128)} custom-call(s32[16]{0:T(128)} %pads.5, s32[1,1024]{1,0:T(1,128)} %bitcast.3, bf16[1024,1024]{1,0:T(8,128)(2,1)} %normalized.1.unit.refs_1_.refs_6_.refs_9_), custom_call_target="tpu_custom_call" | custom-call | flops 2147483648 | bytes 2097152 | tf_op jit(solution)/shard_map/own_block/pallas_call | solution.py:245
  17.6 1.5 %scored.3.best = f32[16,1024]{1,0:T(8,128)} custom-call(s32[144]{0:T(256)} %constant.8.clone.table, f32[16,1024]{1,0:T(8,128)} %own_block.1.best, bf16[1024,1024]{1,0:T(8,128)(2,1)} %collective-permute-done.2.refs_0_.refs_2_, bf16[1024,1024]{1,0:T(8,128)(2,1)} %normalized.1.unit.refs_1_.refs_6_.refs_9_), custom_call_target="tpu_custom_call" | custom-call | flops 2147483648 | bytes 4194304 | tf_op jit(solution)/shard_map/scored/pallas_call | solution.py:343
  19.1 34.0 %collective-permute-done.refs_2_ = bf16[1024,1024]{1,0:T(8,128)(2,1)} collective-permute-done((bf16[1024,1024]{1,0:T(8,128)(2,1)}, bf16[1024,1024]{1,0:T(8,128)(2,1)}, u32[]{:S(2)}, u32[]{:S(2)}) %collective-permute-start) | collective-permute-done | bytes 2097184 | tf_op jit(solution)/shard_map/ppermute | solution.py:420
  53.1 4.8 %collective-permute-done.1.refs_5_.refs_8_ = bf16[1024,1024]{1,0:T(8,128)(2,1)} collective-permute-done((bf16[1024,1024]{1,0:T(8,128)(2,1)}, bf16[1024,1024]{1,0:T(8,128)(2,1)}, u32[]{:S(2)}, u32[]{:S(2)}) %collective-permute-start.1) | collective-permute-done | bytes 2097184 | tf_op jit(solution)/shard_map/ppermute | solution.py:420
  58.0 2.0 %collective-permute-start.5 = (bf16[1024,1024]{1,0:T(8,128)(2,1)}, bf16[1024,1024]{1,0:T(8,128)(2,1)}, u32[]{:S(2)}, u32[]{:S(2)}) collective-permute-start(bf16[1024,1024]{1,0:T(8,128)(2,1)} %collective-permute-done.refs_2_), channel_id=1, source_target_pairs={{4,5},{5,4},{7,6},{6,7},{20,21},{21,20},{23,22},{22,23}} | collective-permute-start | bytes 6291464 | tf_op jit(solution)/shard_map/ppermute | solution.py:420
  60.0 2.0 %collective-permute-start.8 = (bf16[1024,1024]{1,0:T(8,128)(2,1)}, bf16[1024,1024]{1,0:T(8,128)(2,1)}, u32[]{:S(2)}, u32[]{:S(2)}) collective-permute-start(bf16[1024,1024]{1,0:T(8,128)(2,1)} %normalized.1.unit.refs_1_.refs_6_.refs_9_), channel_id=1, source_target_pairs={{5,8},{8,5},{6,11},{11,6},{21,24},{24,21},{22,27},{27,22}} | collective-permute-start | bytes 6291464 | tf_op jit(solution)/shard_map/ppermute | solution.py:420
  62.0 2.0 %collective-permute-start.9 = (bf16[1024,1024]{1,0:T(8,128)(2,1)}, bf16[1024,1024]{1,0:T(8,128)(2,1)}, u32[]{:S(2)}, u32[]{:S(2)}) collective-permute-start(bf16[1024,1024]{1,0:T(8,128)(2,1)} %collective-permute-done.refs_2_), channel_id=1, source_target_pairs={{8,12},{11,15},{5,6},{6,5},{24,28},{27,31},{21,22},{22,21}} | collective-permute-start | bytes 6291464 | tf_op jit(solution)/shard_map/ppermute | solution.py:420
  63.9 13.6 %scored.4 = (f32[16,1024]{1,0:T(8,128)}, f32[1,1024]{1,0:T(1,128)}, f32[1,1024]{1,0:T(1,128)}) custom-call(s32[544]{0:T(1024)} %constant.9.clone.table, f32[16,1024]{1,0:T(8,128)} %scored.3.best, bf16[1024,1024]{1,0:T(8,128)(2,1)} %collective-permute-done.2.refs_0_.refs_2_, bf16[1024,1024]{1,0:T(8,128)(2,1)} %collective-permute-done.3.refs_1_.refs_3_, ...), custom_call_target="tpu_custom_call" | custom-call | flops 10737418240 | bytes 10485760 | tf_op jit(solution)/shard_map/scored/pallas_call | solution.py:343
  77.5 1.3 %collective-permute-start.6 = (f32[1,1024]{1,0:T(1,128)}, f32[1,1024]{1,0:T(1,128)S(1)}, u32[]{:S(2)}, u32[]{:S(2)}) collective-permute-start(f32[1,1024]{1,0:T(1,128)} %get-tuple-element.25), channel_id=1, source_target_pairs={{2,6},{4,5},{5,1},{6,2},{7,15},{8,0},{9,10},{10,11},{11,3},{12,8},... | collective-permute-start | bytes 12296 | tf_op jit(solution)/shard_map/ppermute | solution.py:426
  78.8 0.7 collective-permute-start.7
  79.5 2.9 %collective-permute-done.6.refs_0_ = f32[1,1024]{1,0:T(1,128)S(1)} collective-permute-done((f32[1,1024]{1,0:T(1,128)}, f32[1,1024]{1,0:T(1,128)S(1)}, u32[]{:S(2)}, u32[]{:S(2)}) %collective-permute-start.6) | collective-permute-done | bytes 4128 | tf_op jit(solution)/shard_map/ppermute | solution.py:426
  82.4 0.6 copy-done.4
  83.0 1.6 %scored.5 = (f32[16,1024]{1,0:T(8,128)}, f32[1,1024]{1,0:T(1,128)}, f32[1,1024]{1,0:T(1,128)}, f32[1,1024]{1,0:T(1,128)}, f32[1,1024]{1,0:T(1,128)}) custom-call(s32[528]{0:T(1024)} %constant.10.clone.table, f32[16,1024]{1,0:T(8,128)} %get-tuple-element.24.best, f32[1,1024]{1,0:T(1,128)} %copy-done.4, f32[1,1024]{1,0:T(1,128)} %copy-done.5, ...), custom_call_target="tpu_custom_call" | custom-call | flops 8589934592 | bytes 10485760 | tf_op jit(solution)/shard_map/scored/pallas_call | solution.py:343
  84.6 22.2 %collective-permute-start.10 = (f32[1,1024]{1,0:T(1,128)}, f32[1,1024]{1,0:T(1,128)S(1)}, u32[]{:S(2)}, u32[]{:S(2)}) collective-permute-start(f32[1,1024]{1,0:T(1,128)} %get-tuple-element.29), channel_id=1, source_target_pairs={{1,5},{2,0},{3,1},{4,7},{5,2},{6,14},{7,4},{8,11},{10,8},{11,9},{1... | collective-permute-start | bytes 12296 | tf_op jit(solution)/shard_map/ppermute | solution.py:426
  106.8 1.9 %collective-permute-start.11 = (f32[1,1024]{1,0:T(1,128)}, f32[1,1024]{1,0:T(1,128)S(1)}, u32[]{:S(2)}, u32[]{:S(2)}) collective-permute-start(f32[1,1024]{1,0:T(1,128)} %get-tuple-element.30), channel_id=1, source_target_pairs={{0,4},{1,3},{2,1},{3,7},{4,6},{5,13},{6,15},{7,2},{8,9},{9,8},{11,... | collective-permute-start | bytes 12296 | tf_op jit(solution)/shard_map/ppermute | solution.py:426
  108.7 1.8 %collective-permute-start.12 = (f32[1,1024]{1,0:T(1,128)}, f32[1,1024]{1,0:T(1,128)S(1)}, u32[]{:S(2)}, u32[]{:S(2)}) collective-permute-start(f32[1,1024]{1,0:T(1,128)} %get-tuple-element.31), channel_id=1, source_target_pairs={{0,1},{1,2},{2,3},{3,0},{4,12},{5,8},{6,11},{7,5},{8,10},{9,4},{10... | collective-permute-start | bytes 12296 | tf_op jit(solution)/shard_map/ppermute | solution.py:426
  110.5 1.9 %collective-permute-start.13 = (f32[1,1024]{1,0:T(1,128)}, f32[1,1024]{1,0:T(1,128)S(1)}, u32[]{:S(2)}, u32[]{:S(2)}) collective-permute-start(f32[1,1024]{1,0:T(1,128)} %get-tuple-element.32), channel_id=1, source_target_pairs={{0,3},{1,0},{3,2},{5,12},{6,1},{7,6},{8,5},{9,11},{10,9},{11,8},{1... | collective-permute-start | bytes 12296 | tf_op jit(solution)/shard_map/ppermute | solution.py:426
  112.5 4.0 %collective-permute-done.13.refs_3_ = f32[1,1024]{1,0:T(1,128)S(1)} collective-permute-done((f32[1,1024]{1,0:T(1,128)}, f32[1,1024]{1,0:T(1,128)S(1)}, u32[]{:S(2)}, u32[]{:S(2)}) %collective-permute-start.13) | collective-permute-done | bytes 4128 | tf_op jit(solution)/shard_map/ppermute | solution.py:426
  116.5 0.6 copy-done.3
  117.1 2.2 %placed.1 = f32[1,1024]{1,0:T(1,128)} custom-call(s32[64]{0:T(128)} %constant.11.clone.taken, s32[16]{0:T(128)} %pads.5, s32[1,1024]{1,0:T(1,128)} %bitcast.4, f32[16,1024]{1,0:T(8,128)} %get-tuple-element.28.best, f32[1,1024]{1,0:T(1,128)} %copy-done, f32[1,1024]{1,0:T(1,128)} %copy-done.1, f32[1,1024]{1,0:T(1,128)} %copy-done.2, f32[1,1024]{1,0:T(1,128)} %copy-done.3), custom_call_target="tpu_custom_call" | custom-call | tf_op jit(solution)/shard_map/placed/pallas_call | solution.py:386
  (22 shorter events, 0.3 us)
Async XLA Ops:
  4.1 13.5 %collective-permute-start.2 = (bf16[1024,1024]{1,0:T(8,128)(2,1)}, bf16[1024,1024]{1,0:T(8,128)(2,1)}, u32[]{:S(2)}, u32[]{:S(2)}) collective-permute-start(bf16[1024,1024]{1,0:T(8,128)(2,1)} %normalized.1.unit.refs_1_.refs_6_.refs_9_), channel_id=1, source_target_pairs={{0,1},{1,0},{4,5},{5,4},{8,9},{9,8},{12,13},{13,12},{3,2},{2,3},{7... | collective-permute-start | bytes 6291464 | tf_op jit(solution)/shard_map/ppermute | solution.py:420
  4.3 48.8 %collective-permute-start = (bf16[1024,1024]{1,0:T(8,128)(2,1)}, bf16[1024,1024]{1,0:T(8,128)(2,1)}, u32[]{:S(2)}, u32[]{:S(2)}) collective-permute-start(bf16[1024,1024]{1,0:T(8,128)(2,1)} %normalized.1.unit.refs_1_.refs_6_.refs_9_), channel_id=1, source_target_pairs={{0,8},{8,12},{12,4},{4,0},{1,5},{3,11},{11,15},{15,7},{7,3},{2,6},... | collective-permute-start | bytes 6291464 | tf_op jit(solution)/shard_map/ppermute | solution.py:420
  10.2 47.6 %collective-permute-start.1 = (bf16[1024,1024]{1,0:T(8,128)(2,1)}, bf16[1024,1024]{1,0:T(8,128)(2,1)}, u32[]{:S(2)}, u32[]{:S(2)}) collective-permute-start(bf16[1024,1024]{1,0:T(8,128)(2,1)} %normalized.1.unit.refs_1_.refs_6_.refs_9_), channel_id=1, source_target_pairs={{0,3},{3,0},{1,2},{2,1},{4,7},{7,4},{5,6},{6,5},{8,11},{11,8},{9,1... | collective-permute-start | bytes 6291464 | tf_op jit(solution)/shard_map/ppermute | solution.py:420
  11.7 52.3 %collective-permute-start.4 = (bf16[1024,1024]{1,0:T(8,128)(2,1)}, bf16[1024,1024]{1,0:T(8,128)(2,1)}, u32[]{:S(2)}, u32[]{:S(2)}) collective-permute-start(bf16[1024,1024]{1,0:T(8,128)(2,1)} %normalized.1.unit.refs_1_.refs_6_.refs_9_), channel_id=1, source_target_pairs={{13,5},{5,1},{9,13},{4,9},{14,6},{6,2},{10,14},{7,10},{29,21},{21,... | collective-permute-start | bytes 6291464 | tf_op jit(solution)/shard_map/ppermute | solution.py:420
  57.9 6.1 %collective-permute-start.3 = (bf16[1024,1024]{1,0:T(8,128)(2,1)}, bf16[1024,1024]{1,0:T(8,128)(2,1)}, u32[]{:S(2)}, u32[]{:S(2)}) collective-permute-start(bf16[1024,1024]{1,0:T(8,128)(2,1)} %collective-permute-done.1.refs_5_.refs_8_), channel_id=1, source_target_pairs={{0,1},{1,0},{4,5},{5,4},{8,9},{9,8},{12,13},{13,12},{3,2},{2,3},{7... | collective-permute-start | bytes 6291464 | tf_op jit(solution)/shard_map/ppermute | solution.py:420
  58.0 6.0 %collective-permute-start.5 = (bf16[1024,1024]{1,0:T(8,128)(2,1)}, bf16[1024,1024]{1,0:T(8,128)(2,1)}, u32[]{:S(2)}, u32[]{:S(2)}) collective-permute-start(bf16[1024,1024]{1,0:T(8,128)(2,1)} %collective-permute-done.refs_2_), channel_id=1, source_target_pairs={{4,5},{5,4},{7,6},{6,7},{20,21},{21,20},{23,22},{22,23}} | collective-permute-start | bytes 6291464 | tf_op jit(solution)/shard_map/ppermute | solution.py:420
  60.0 19.5 %collective-permute-start.8 = (bf16[1024,1024]{1,0:T(8,128)(2,1)}, bf16[1024,1024]{1,0:T(8,128)(2,1)}, u32[]{:S(2)}, u32[]{:S(2)}) collective-permute-start(bf16[1024,1024]{1,0:T(8,128)(2,1)} %normalized.1.unit.refs_1_.refs_6_.refs_9_), channel_id=1, source_target_pairs={{5,8},{8,5},{6,11},{11,6},{21,24},{24,21},{22,27},{27,22}} | collective-permute-start | bytes 6291464 | tf_op jit(solution)/shard_map/ppermute | solution.py:420
  62.0 17.5 %collective-permute-start.9 = (bf16[1024,1024]{1,0:T(8,128)(2,1)}, bf16[1024,1024]{1,0:T(8,128)(2,1)}, u32[]{:S(2)}, u32[]{:S(2)}) collective-permute-start(bf16[1024,1024]{1,0:T(8,128)(2,1)} %collective-permute-done.refs_2_), channel_id=1, source_target_pairs={{8,12},{11,15},{5,6},{6,5},{24,28},{27,31},{21,22},{22,21}} | collective-permute-start | bytes 6291464 | tf_op jit(solution)/shard_map/ppermute | solution.py:420
  77.5 4.9 %collective-permute-start.6 = (f32[1,1024]{1,0:T(1,128)}, f32[1,1024]{1,0:T(1,128)S(1)}, u32[]{:S(2)}, u32[]{:S(2)}) collective-permute-start(f32[1,1024]{1,0:T(1,128)} %get-tuple-element.25), channel_id=1, source_target_pairs={{2,6},{4,5},{5,1},{6,2},{7,15},{8,0},{9,10},{10,11},{11,3},{12,8},... | collective-permute-start | bytes 12296 | tf_op jit(solution)/shard_map/ppermute | solution.py:426
  78.8 3.6 %collective-permute-start.7 = (f32[1,1024]{1,0:T(1,128)}, f32[1,1024]{1,0:T(1,128)S(1)}, u32[]{:S(2)}, u32[]{:S(2)}) collective-permute-start(f32[1,1024]{1,0:T(1,128)} %get-tuple-element.26), channel_id=1, source_target_pairs={{5,7},{6,4},{21,23},{22,20}} | collective-permute-start | bytes 12296 | tf_op jit(solution)/shard_map/ppermute | solution.py:426
  82.4 0.6 copy-start.4
  82.4 0.6 copy-start.5
  84.6 27.8 %collective-permute-start.10 = (f32[1,1024]{1,0:T(1,128)}, f32[1,1024]{1,0:T(1,128)S(1)}, u32[]{:S(2)}, u32[]{:S(2)}) collective-permute-start(f32[1,1024]{1,0:T(1,128)} %get-tuple-element.29), channel_id=1, source_target_pairs={{1,5},{2,0},{3,1},{4,7},{5,2},{6,14},{7,4},{8,11},{10,8},{11,9},{1... | collective-permute-start | bytes 12296 | tf_op jit(solution)/shard_map/ppermute | solution.py:426
  106.8 5.7 %collective-permute-start.11 = (f32[1,1024]{1,0:T(1,128)}, f32[1,1024]{1,0:T(1,128)S(1)}, u32[]{:S(2)}, u32[]{:S(2)}) collective-permute-start(f32[1,1024]{1,0:T(1,128)} %get-tuple-element.30), channel_id=1, source_target_pairs={{0,4},{1,3},{2,1},{3,7},{4,6},{5,13},{6,15},{7,2},{8,9},{9,8},{11,... | collective-permute-start | bytes 12296 | tf_op jit(solution)/shard_map/ppermute | solution.py:426
  108.7 3.8 %collective-permute-start.12 = (f32[1,1024]{1,0:T(1,128)}, f32[1,1024]{1,0:T(1,128)S(1)}, u32[]{:S(2)}, u32[]{:S(2)}) collective-permute-start(f32[1,1024]{1,0:T(1,128)} %get-tuple-element.31), channel_id=1, source_target_pairs={{0,1},{1,2},{2,3},{3,0},{4,12},{5,8},{6,11},{7,5},{8,10},{9,4},{10... | collective-permute-start | bytes 12296 | tf_op jit(solution)/shard_map/ppermute | solution.py:426
  110.5 6.0 %collective-permute-start.13 = (f32[1,1024]{1,0:T(1,128)}, f32[1,1024]{1,0:T(1,128)S(1)}, u32[]{:S(2)}, u32[]{:S(2)}) collective-permute-start(f32[1,1024]{1,0:T(1,128)} %get-tuple-element.32), channel_id=1, source_target_pairs={{0,3},{1,0},{3,2},{5,12},{6,1},{7,6},{8,5},{9,11},{10,9},{11,8},{1... | collective-permute-start | bytes 12296 | tf_op jit(solution)/shard_map/ppermute | solution.py:426
  112.4 4.1 %copy-start = (f32[1,1024]{1,0:T(1,128)}, f32[1,1024]{1,0:T(1,128)S(1)}, u32[]{:S(2)}) copy-start(f32[1,1024]{1,0:T(1,128)S(1)} %collective-permute-done.10.refs_0_) | copy-start | bytes 12292
  112.5 4.1 %copy-start.1 = (f32[1,1024]{1,0:T(1,128)}, f32[1,1024]{1,0:T(1,128)S(1)}, u32[]{:S(2)}) copy-start(f32[1,1024]{1,0:T(1,128)S(1)} %collective-permute-done.11.refs_1_) | copy-start | bytes 12292
  112.5 4.1 %copy-start.2 = (f32[1,1024]{1,0:T(1,128)}, f32[1,1024]{1,0:T(1,128)S(1)}, u32[]{:S(2)}) copy-start(f32[1,1024]{1,0:T(1,128)S(1)} %collective-permute-done.12.refs_2_) | copy-start | bytes 12292
  116.5 0.6 copy-start.3

commit v9 on v8

--- a/solution.py
+++ b/solution.py
@@ -35,37 +35,38 @@
 
     every = [(z, lane) for z in range(4) for lane in (0, 1)]
     swap = rows([((z, lane), (z, 1 - lane)) for z, lane in every])
-    first = [((0, 0), (2, 0)), ((2, 0), (3, 0)), ((3, 0), (1, 0)), ((1, 0), (0, 0)), ((0, 1), (1, 1))]
-    second = [((3, 1), (1, 1)), ((1, 1), (0, 1)), ((2, 1), (3, 1)), ((1, 0), (2, 1))]
+    crossed = [(at(1, y, lane), at(1, 1 - y, 1 - lane)) for y in (0, 1) for lane in (0, 1)]
+    first = [((0, 0), (2, 1)), ((2, 0), (3, 1)), ((3, 0), (1, 0)), ((1, 0), (0, 0)), ((0, 1), (1, 1))]
+    second = [((3, 1), (1, 1)), ((1, 1), (0, 1)), ((2, 1), (3, 0)), ((1, 0), (2, 1))]
     return [
         Move("R1", "own", rows(first), 0, 1),
         Move("R2", "own", rows(second), 0, 1),
-        Move("Y", "own", across(every), 0, 1),
+        Move("Y", "own", across([place for place in every if place[0] != 1]) + crossed, 0, 1),
         Move("A", "own", swap, 0, 0),
         Move("R3", "own", rows([((1, 1), (2, 0)), ((2, 0), (1, 1))]), 1, 2, "R1"),
-        Move("V", "R1", rows([((2, 0), (3, 0))]) + across([(1, 1)]), 1, 2),
-        Move("F", "Y", swap, 1, 1),
-        Move("W", "R1", rows([((1, 0), (1, 1)), ((1, 1), (1, 0))]), 1, 1),
+        Move("V", "R1", [(at(2, y, 1), at(3, y, 1 - y)) for y in (0, 1)] + across([(1, 1)]), 1, 2),
+        Move("F", "Y", swap, 2, 2),
+        Move("W", "R1", rows([((1, 0), (1, 1)), ((1, 1), (1, 0))]), 2, 2),
     ]
 
 
 GRID_PAIRS = (
-    ((0, 1), (0, 4), (1, 3), (1, 4), (3, 4)),
-    ((0, 5), (1, 2), (2, 5), (3, 5)),
-    ((0, 6), (1, 6), (2, 6), (3, 6)),
-    ((0, 2), (0, 3), (1, 7), (2, 3), (2, 7), (3, 7)),
-    ((4, 5), (4, 7), (5, 6), (6, 12), (7, 12)),
-    ((1, 5), (1, 12), (1, 13), (2, 8), (2, 12), (2, 13), (7, 13), (8, 12)),
-    ((1, 11), (1, 14), (1, 15), (2, 4), (2, 14), (4, 6), (4, 14), (11, 14)),
-    ((2, 15), (4, 15), (5, 7), (5, 15), (6, 7)),
-    ((0, 10), (0, 11), (5, 8), (5, 9), (5, 10), (5, 11), (8, 11)),
-    ((4, 8), (4, 9), (4, 10), (8, 9), (9, 11)),
-    ((7, 8), (7, 9), (7, 10), (7, 11)),
-    ((3, 8), (3, 9), (6, 8), (6, 9), (6, 10), (6, 11), (8, 10), (9, 10), (10, 11)),
-    ((0, 12), (0, 13), (0, 14), (0, 15), (8, 13), (8, 14), (12, 15), (13, 14)),
-    ((9, 12), (9, 13), (9, 14), (9, 15), (12, 13)),
-    ((10, 12), (10, 13), (10, 14), (10, 15), (12, 14), (14, 15)),
-    ((3, 13), (3, 14), (3, 15), (11, 12), (11, 13), (11, 15), (13, 15)),
+    ((0, 2), (0, 4), (1, 4), (2, 4), (3, 4)),
+    ((0, 1), (0, 5), (1, 3), (1, 5), (3, 5)),
+    ((0, 3), (0, 6), (1, 6), (2, 3), (2, 6), (3, 6)),
+    ((1, 2), (1, 7), (2, 7), (3, 7)),
+    ((1, 12), (4, 5), (4, 6), (4, 7), (6, 12), (7, 12)),
+    ((1, 13), (2, 8), (2, 12), (2, 13), (5, 8), (7, 13)),
+    ((1, 11), (1, 14), (1, 15), (2, 14), (4, 14)),
+    ((2, 5), (2, 15), (4, 15), (5, 6), (5, 7), (5, 15), (6, 7)),
+    ((5, 9), (5, 10), (5, 11), (9, 10), (9, 11)),
+    ((0, 10), (0, 11), (4, 8), (4, 9), (4, 10), (8, 9), (8, 11)),
+    ((3, 8), (3, 9), (7, 8), (7, 9), (7, 10), (7, 11)),
+    ((6, 8), (6, 9), (6, 10), (6, 11), (8, 10), (10, 11)),
+    ((9, 12), (9, 13), (9, 14), (9, 15), (12, 13), (12, 14), (13, 14), (13, 15)),
+    ((0, 12), (0, 13), (0, 14), (0, 15), (8, 12), (8, 13), (8, 14)),
+    ((11, 12), (11, 13), (11, 14), (11, 15), (12, 15)),
+    ((3, 13), (3, 14), (3, 15), (10, 12), (10, 13), (10, 14), (10, 15), (14, 15)),
 )
 
 
@@ -399,14 +400,12 @@
     unit = normalized(embeddings, order, pad_counts)
     slots, best = {"own": unit}, None
     rank = dict({"own": -1}, **{move.name: move.stage for move in moves})
-    edges = [
-        {(of, to) for of in range(nblocks) for pair in pairs[of] for to in pair[2:] if to != of}
-        for pairs in work
-    ]
-    edges = {sending[-1]: set().union(*edges[sending[0] + 1 :] if len(sending) > 1 else edges),
-             sending[0]: set().union(*edges[: sending[0] + 1])}
-    if len(sending) > 1:
-        edges = dict(zip(sending, in_two(edges[sending[0]], edges[sending[1]], nblocks)))
+    edges = {}
+    for stage, pairs in enumerate(work):
+        due = edges.setdefault(min(last for last in sending if last >= stage), set())
+        due |= {(of, to) for of in range(nblocks) for pair in pairs[of] for to in pair[2:] if to != of}
+    if len(sending) == 2:
+        edges = dict(zip(sending, in_two(*[edges[stage] for stage in sending], nblocks)))
     permutes, found = [], []
     for stage, pairs in enumerate(work):
         starting = [move for move in moves if move.begins == stage]

time: 120 us -> 115 us (0.958)
  the two profiles are of different devices: /device:TPU:1 before, /device:TPU:0 now
where the time goes in v9:
time: 115 us; the launch traced here: 114 us
  waiting for transfers between devices  44 us (38%)
  starting transfers between devices  36.4 us (32%)
  Pallas kernels  32.4 us (28%)
    ppermute x8, waiting for transfers between devices, local(): slots[move.name] = lax.ppermute(value, 'blk', move.pairs)  36.9 us
    pallas_call x3, Pallas kernels, scored(): pl.pallas_call(functools.partial(pairs_kernel, len(given), len(sends), le...  21.3 us
    ppermute x6, starting transfers between devices, local(): lax.ppermute(row, 'blk', permute)  21 us
    ppermute x8, starting transfers between devices, local(): slots[move.name] = lax.ppermute(value, 'blk', move.pairs)  15.4 us
    ppermute x6, waiting for transfers between devices, local(): lax.ppermute(row, 'blk', permute)  7.12 us
    pallas_call x1, Pallas kernels, own_block(): pl.pallas_call(own_kernel, out_shape=jax.ShapeDtypeStruct((nblocks, rows)...  4.65 us
    pallas_call x1, Pallas kernels, normalized(): pl.pallas_call(unit_kernel, out_shape=jax.ShapeDtypeStruct((rows, depth),...  4.22 us
  transfers between devices with their start and end apart: 14, of which 5 were waited for; matrix products, arithmetic and copies ran while one was open for 0% of the time, Pallas kernels for 15%

profile of v9, /device:TPU:0, one launch (start us, length us, event | category | flops | bytes accessed | tf_op | source)
XLA Modules:
  0.0 114.0 jit_solution(13644353872297139583)
XLA Ops:
  0.0 4.2 %normalized.1.unit.refs_1_.refs_4_.refs_10_ = bf16[1024,1024]{1,0:T(8,128)(2,1)} custom-call(s32[16]{0:T(128)} %pads.5, s32[1024]{0:T(1024)} %order_smem.1, s32[1,1024]{1,0:T(1,128)} %bitcast.2, bf16[1024,1024]{1,0:T(8,128)(2,1)} %embeddings.1), custom_call_target="tpu_custom_call" | custom-call | flops 4194304 | bytes 4194304 | tf_op jit(solution)/shard_map/normalized/pallas_call | solution.py:199
  4.7 5.6 %collective-permute-start.1 = (bf16[1024,1024]{1,0:T(8,128)(2,1)}, bf16[1024,1024]{1,0:T(8,128)(2,1)}, u32[]{:S(2)}, u32[]{:S(2)}) collective-permute-start(bf16[1024,1024]{1,0:T(8,128)(2,1)} %normalized.1.unit.refs_1_.refs_4_.refs_10_), channel_id=1, source_target_pairs={{0,9},{8,13},{12,4},{4,0},{1,5},{3,10},{11,14},{15,7},{7,3},{2,6},... | collective-permute-start | bytes 6291464 | tf_op jit(solution)/shard_map/ppermute | solution.py:419
  10.4 2.0 %collective-permute-start.3 = (bf16[1024,1024]{1,0:T(8,128)(2,1)}, bf16[1024,1024]{1,0:T(8,128)(2,1)}, u32[]{:S(2)}, u32[]{:S(2)}) collective-permute-start(bf16[1024,1024]{1,0:T(8,128)(2,1)} %normalized.1.unit.refs_1_.refs_4_.refs_10_), channel_id=1, source_target_pairs={{13,5},{5,1},{9,12},{4,9},{14,6},{6,2},{10,15},{7,10},{29,21},{21,... | collective-permute-start | bytes 6291464 | tf_op jit(solution)/shard_map/ppermute | solution.py:419
  12.4 1.1 collective-permute-start
  13.5 4.7 %own_block.1.best = f32[16,1024]{1,0:T(8,128)} custom-call(s32[16]{0:T(128)} %pads.5, s32[1,1024]{1,0:T(1,128)} %bitcast.3, bf16[1024,1024]{1,0:T(8,128)(2,1)} %normalized.1.unit.refs_1_.refs_4_.refs_10_), custom_call_target="tpu_custom_call" | custom-call | flops 2147483648 | bytes 2097152 | tf_op jit(solution)/shard_map/own_block/pallas_call | solution.py:246
  18.2 1.5 %scored.3.best = f32[16,1024]{1,0:T(8,128)} custom-call(s32[144]{0:T(256)} %constant.8.clone.table, f32[16,1024]{1,0:T(8,128)} %own_block.1.best, bf16[1024,1024]{1,0:T(8,128)(2,1)} %collective-permute-done.2.refs_0_.refs_2_, bf16[1024,1024]{1,0:T(8,128)(2,1)} %normalized.1.unit.refs_1_.refs_4_.refs_10_), custom_call_target="tpu_custom_call" | custom-call | flops 2147483648 | bytes 4194304 | tf_op jit(solution)/shard_map/scored/pallas_call | solution.py:344
  19.7 35.4 %collective-permute-done.1.refs_1_.refs_4_ = bf16[1024,1024]{1,0:T(8,128)(2,1)} collective-permute-done((bf16[1024,1024]{1,0:T(8,128)(2,1)}, bf16[1024,1024]{1,0:T(8,128)(2,1)}, u32[]{:S(2)}, u32[]{:S(2)}) %collective-permute-start.1) | collective-permute-done | bytes 2097184 | tf_op jit(solution)/shard_map/ppermute | solution.py:419
  55.1 2.0 %collective-permute-start.7 = (bf16[1024,1024]{1,0:T(8,128)(2,1)}, bf16[1024,1024]{1,0:T(8,128)(2,1)}, u32[]{:S(2)}, u32[]{:S(2)}) collective-permute-start(bf16[1024,1024]{1,0:T(8,128)(2,1)} %normalized.1.unit.refs_1_.refs_4_.refs_10_), channel_id=1, source_target_pairs={{5,8},{8,5},{6,11},{11,6},{21,24},{24,21},{22,27},{27,22}} | collective-permute-start | bytes 6291464 | tf_op jit(solution)/shard_map/ppermute | solution.py:419
  57.1 2.0 %collective-permute-start.8 = (bf16[1024,1024]{1,0:T(8,128)(2,1)}, bf16[1024,1024]{1,0:T(8,128)(2,1)}, u32[]{:S(2)}, u32[]{:S(2)}) collective-permute-start(bf16[1024,1024]{1,0:T(8,128)(2,1)} %collective-permute-done.1.refs_1_.refs_4_), channel_id=1, source_target_pairs={{9,13},{10,15},{5,6},{6,5},{25,29},{26,31},{21,22},{22,21}} | collective-permute-start | bytes 6291464 | tf_op jit(solution)/shard_map/ppermute | solution.py:419
  59.1 1.5 %collective-permute-done.refs_3_.refs_9_ = bf16[1024,1024]{1,0:T(8,128)(2,1)} collective-permute-done((bf16[1024,1024]{1,0:T(8,128)(2,1)}, bf16[1024,1024]{1,0:T(8,128)(2,1)}, u32[]{:S(2)}, u32[]{:S(2)}) %collective-permute-start) | collective-permute-done | bytes 2097184 | tf_op jit(solution)/shard_map/ppermute | solution.py:419
  60.6 11.1 %scored.4 = (f32[16,1024]{1,0:T(8,128)}, f32[1,1024]{1,0:T(1,128)}, f32[1,1024]{1,0:T(1,128)}) custom-call(s32[464]{0:T(512)} %constant.9.clone.table, f32[16,1024]{1,0:T(8,128)} %scored.3.best, bf16[1024,1024]{1,0:T(8,128)(2,1)} %collective-permute-done.2.refs_0_.refs_2_, bf16[1024,1024]{1,0:T(8,128)(2,1)} %collective-permute-done.1.refs_1_.refs_4_, ...), custom_call_target="tpu_custom_call" | custom-call | flops 8589934592 | bytes 10485760 | tf_op jit(solution)/shard_map/scored/pallas_call | solution.py:344
  71.8 2.0 %collective-permute-start.9 = (bf16[1024,1024]{1,0:T(8,128)(2,1)}, bf16[1024,1024]{1,0:T(8,128)(2,1)}, u32[]{:S(2)}, u32[]{:S(2)}) collective-permute-start(bf16[1024,1024]{1,0:T(8,128)(2,1)} %collective-permute-done.1.refs_1_.refs_4_), channel_id=1, source_target_pairs={{4,5},{5,4},{7,6},{6,7},{20,21},{21,20},{23,22},{22,23}} | collective-permute-start | bytes 6291464 | tf_op jit(solution)/shard_map/ppermute | solution.py:419
  73.8 2.4 %collective-permute-start.4 = (f32[1,1024]{1,0:T(1,128)}, f32[1,1024]{1,0:T(1,128)S(1)}, u32[]{:S(2)}, u32[]{:S(2)}) collective-permute-start(f32[1,1024]{1,0:T(1,128)} %get-tuple-element.26), channel_id=1, source_target_pairs={{0,3},{1,0},{4,5},{5,1},{6,2},{7,6},{9,10},{10,11},{12,15},{13,8},... | collective-permute-start | bytes 12296 | tf_op jit(solution)/shard_map/ppermute | solution.py:425
  76.2 1.5 %collective-permute-done.4.refs_0_ = f32[1,1024]{1,0:T(1,128)S(1)} collective-permute-done((f32[1,1024]{1,0:T(1,128)}, f32[1,1024]{1,0:T(1,128)S(1)}, u32[]{:S(2)}, u32[]{:S(2)}) %collective-permute-start.4) | collective-permute-done | bytes 4128 | tf_op jit(solution)/shard_map/ppermute | solution.py:425
  77.7 0.6 collective-permute-start.5
  78.5 0.5 copy-done.5
  79.0 8.7 %scored.5 = (f32[16,1024]{1,0:T(8,128)}, f32[1,1024]{1,0:T(1,128)}, f32[1,1024]{1,0:T(1,128)}, f32[1,1024]{1,0:T(1,128)}, f32[1,1024]{1,0:T(1,128)}) custom-call(s32[528]{0:T(1024)} %constant.10.clone.table, f32[16,1024]{1,0:T(8,128)} %get-tuple-element.25.best, f32[1,1024]{1,0:T(1,128)} %copy-done.4, f32[1,1024]{1,0:T(1,128)} %copy-done.5, ...), custom_call_target="tpu_custom_call" | custom-call | flops 8589934592 | bytes 10485760 | tf_op jit(solution)/shard_map/scored/pallas_call | solution.py:344
  87.7 13.2 %collective-permute-start.10 = (f32[1,1024]{1,0:T(1,128)}, f32[1,1024]{1,0:T(1,128)S(1)}, u32[]{:S(2)}, u32[]{:S(2)}) collective-permute-start(f32[1,1024]{1,0:T(1,128)} %get-tuple-element.33), channel_id=1, source_target_pairs={{0,4},{1,5},{3,7},{4,12},{5,2},{6,1},{7,15},{8,9},{9,0},{10,8},{11... | collective-permute-start | bytes 12296 | tf_op jit(solution)/shard_map/ppermute | solution.py:425
  100.8 3.4 %collective-permute-start.11 = (f32[1,1024]{1,0:T(1,128)}, f32[1,1024]{1,0:T(1,128)S(1)}, u32[]{:S(2)}, u32[]{:S(2)}) collective-permute-start(f32[1,1024]{1,0:T(1,128)} %get-tuple-element.34), channel_id=1, source_target_pairs={{0,1},{2,6},{3,2},{4,7},{5,13},{6,14},{7,4},{8,5},{9,11},{10,3},{1... | collective-permute-start | bytes 12296 | tf_op jit(solution)/shard_map/ppermute | solution.py:425
  104.3 1.3 %collective-permute-start.13 = (f32[1,1024]{1,0:T(1,128)}, f32[1,1024]{1,0:T(1,128)S(1)}, u32[]{:S(2)}, u32[]{:S(2)}) collective-permute-start(f32[1,1024]{1,0:T(1,128)} %get-tuple-element.36), channel_id=1, source_target_pairs={{2,3},{4,1},{5,12},{6,15},{7,2},{8,11},{9,8},{10,9},{11,10},{13,0}... | collective-permute-start | bytes 12296 | tf_op jit(solution)/shard_map/ppermute | solution.py:425
  105.7 2.5 %collective-permute-done.12.refs_2_ = f32[1,1024]{1,0:T(1,128)S(1)} collective-permute-done((f32[1,1024]{1,0:T(1,128)}, f32[1,1024]{1,0:T(1,128)S(1)}, u32[]{:S(2)}, u32[]{:S(2)}) %collective-permute-start.12) | collective-permute-done | bytes 4128 | tf_op jit(solution)/shard_map/ppermute | solution.py:425
  108.1 3.1 %collective-permute-done.13.refs_3_ = f32[1,1024]{1,0:T(1,128)S(1)} collective-permute-done((f32[1,1024]{1,0:T(1,128)}, f32[1,1024]{1,0:T(1,128)S(1)}, u32[]{:S(2)}, u32[]{:S(2)}) %collective-permute-start.13) | collective-permute-done | bytes 4128 | tf_op jit(solution)/shard_map/ppermute | solution.py:425
  111.3 0.6 copy-done.3
  111.9 2.2 %placed.1 = f32[1,1024]{1,0:T(1,128)} custom-call(s32[64]{0:T(128)} %constant.11.clone.taken, s32[16]{0:T(128)} %pads.5, s32[1,1024]{1,0:T(1,128)} %bitcast.4, f32[16,1024]{1,0:T(8,128)} %get-tuple-element.32.best, f32[1,1024]{1,0:T(1,128)} %copy-done, f32[1,1024]{1,0:T(1,128)} %copy-done.1, f32[1,1024]{1,0:T(1,128)} %copy-done.2, f32[1,1024]{1,0:T(1,128)} %copy-done.3), custom_call_target="tpu_custom_call" | custom-call | tf_op jit(solution)/shard_map/placed/pallas_call | solution.py:387
  (22 shorter events, 0.7 us)
Async XLA Ops:
  4.2 14.0 %collective-permute-start.2 = (bf16[1024,1024]{1,0:T(8,128)(2,1)}, bf16[1024,1024]{1,0:T(8,128)(2,1)}, u32[]{:S(2)}, u32[]{:S(2)}) collective-permute-start(bf16[1024,1024]{1,0:T(8,128)(2,1)} %normalized.1.unit.refs_1_.refs_4_.refs_10_), channel_id=1, source_target_pairs={{0,1},{1,0},{4,5},{5,4},{8,9},{9,8},{12,13},{13,12},{3,2},{2,3},{7... | collective-permute-start | bytes 6291464 | tf_op jit(solution)/shard_map/ppermute | solution.py:419
  4.7 50.4 %collective-permute-start.1 = (bf16[1024,1024]{1,0:T(8,128)(2,1)}, bf16[1024,1024]{1,0:T(8,128)(2,1)}, u32[]{:S(2)}, u32[]{:S(2)}) collective-permute-start(bf16[1024,1024]{1,0:T(8,128)(2,1)} %normalized.1.unit.refs_1_.refs_4_.refs_10_), channel_id=1, source_target_pairs={{0,9},{8,13},{12,4},{4,0},{1,5},{3,10},{11,14},{15,7},{7,3},{2,6},... | collective-permute-start | bytes 6291464 | tf_op jit(solution)/shard_map/ppermute | solution.py:419
  10.4 48.7 %collective-permute-start.3 = (bf16[1024,1024]{1,0:T(8,128)(2,1)}, bf16[1024,1024]{1,0:T(8,128)(2,1)}, u32[]{:S(2)}, u32[]{:S(2)}) collective-permute-start(bf16[1024,1024]{1,0:T(8,128)(2,1)} %normalized.1.unit.refs_1_.refs_4_.refs_10_), channel_id=1, source_target_pairs={{13,5},{5,1},{9,12},{4,9},{14,6},{6,2},{10,15},{7,10},{29,21},{21,... | collective-permute-start | bytes 6291464 | tf_op jit(solution)/shard_map/ppermute | solution.py:419
  12.4 48.2 %collective-permute-start = (bf16[1024,1024]{1,0:T(8,128)(2,1)}, bf16[1024,1024]{1,0:T(8,128)(2,1)}, u32[]{:S(2)}, u32[]{:S(2)}) collective-permute-start(bf16[1024,1024]{1,0:T(8,128)(2,1)} %normalized.1.unit.refs_1_.refs_4_.refs_10_), channel_id=1, source_target_pairs={{0,3},{3,0},{1,2},{2,1},{8,11},{11,8},{9,10},{10,9},{12,15},{15,12... | collective-permute-start | bytes 6291464 | tf_op jit(solution)/shard_map/ppermute | solution.py:419
  55.1 23.3 %collective-permute-start.7 = (bf16[1024,1024]{1,0:T(8,128)(2,1)}, bf16[1024,1024]{1,0:T(8,128)(2,1)}, u32[]{:S(2)}, u32[]{:S(2)}) collective-permute-start(bf16[1024,1024]{1,0:T(8,128)(2,1)} %normalized.1.unit.refs_1_.refs_4_.refs_10_), channel_id=1, source_target_pairs={{5,8},{8,5},{6,11},{11,6},{21,24},{24,21},{22,27},{27,22}} | collective-permute-start | bytes 6291464 | tf_op jit(solution)/shard_map/ppermute | solution.py:419
  57.1 21.3 %collective-permute-start.8 = (bf16[1024,1024]{1,0:T(8,128)(2,1)}, bf16[1024,1024]{1,0:T(8,128)(2,1)}, u32[]{:S(2)}, u32[]{:S(2)}) collective-permute-start(bf16[1024,1024]{1,0:T(8,128)(2,1)} %collective-permute-done.1.refs_1_.refs_4_), channel_id=1, source_target_pairs={{9,13},{10,15},{5,6},{6,5},{25,29},{26,31},{21,22},{22,21}} | collective-permute-start | bytes 6291464 | tf_op jit(solution)/shard_map/ppermute | solution.py:419
  71.7 6.7 %collective-permute-start.6 = (bf16[1024,1024]{1,0:T(8,128)(2,1)}, bf16[1024,1024]{1,0:T(8,128)(2,1)}, u32[]{:S(2)}, u32[]{:S(2)}) collective-permute-start(bf16[1024,1024]{1,0:T(8,128)(2,1)} %collective-permute-done.refs_3_.refs_9_), channel_id=1, source_target_pairs={{0,1},{1,0},{4,5},{5,4},{8,9},{9,8},{12,13},{13,12},{3,2},{2,3},{7... | collective-permute-start | bytes 6291464 | tf_op jit(solution)/shard_map/ppermute | solution.py:419
  71.8 6.7 %collective-permute-start.9 = (bf16[1024,1024]{1,0:T(8,128)(2,1)}, bf16[1024,1024]{1,0:T(8,128)(2,1)}, u32[]{:S(2)}, u32[]{:S(2)}) collective-permute-start(bf16[1024,1024]{1,0:T(8,128)(2,1)} %collective-permute-done.1.refs_1_.refs_4_), channel_id=1, source_target_pairs={{4,5},{5,4},{7,6},{6,7},{20,21},{21,20},{23,22},{22,23}} | collective-permute-start | bytes 6291464 | tf_op jit(solution)/shard_map/ppermute | solution.py:419
  73.8 3.9 %collective-permute-start.4 = (f32[1,1024]{1,0:T(1,128)}, f32[1,1024]{1,0:T(1,128)S(1)}, u32[]{:S(2)}, u32[]{:S(2)}) collective-permute-start(f32[1,1024]{1,0:T(1,128)} %get-tuple-element.26), channel_id=1, source_target_pairs={{0,3},{1,0},{4,5},{5,1},{6,2},{7,6},{9,10},{10,11},{12,15},{13,8},... | collective-permute-start | bytes 12296 | tf_op jit(solution)/shard_map/ppermute | solution.py:425
  77.7 0.7 copy-start.4
  77.7 0.7 collective-permute-start.5
  78.4 0.6 copy-start.5
  87.7 18.0 %collective-permute-start.10 = (f32[1,1024]{1,0:T(1,128)}, f32[1,1024]{1,0:T(1,128)S(1)}, u32[]{:S(2)}, u32[]{:S(2)}) collective-permute-start(f32[1,1024]{1,0:T(1,128)} %get-tuple-element.33), channel_id=1, source_target_pairs={{0,4},{1,5},{3,7},{4,12},{5,2},{6,1},{7,15},{8,9},{9,0},{10,8},{11... | collective-permute-start | bytes 12296 | tf_op jit(solution)/shard_map/ppermute | solution.py:425
  100.8 4.8 %collective-permute-start.11 = (f32[1,1024]{1,0:T(1,128)}, f32[1,1024]{1,0:T(1,128)S(1)}, u32[]{:S(2)}, u32[]{:S(2)}) collective-permute-start(f32[1,1024]{1,0:T(1,128)} %get-tuple-element.34), channel_id=1, source_target_pairs={{0,1},{2,6},{3,2},{4,7},{5,13},{6,14},{7,4},{8,5},{9,11},{10,3},{1... | collective-permute-start | bytes 12296 | tf_op jit(solution)/shard_map/ppermute | solution.py:425
  104.3 3.9 %collective-permute-start.12 = (f32[1,1024]{1,0:T(1,128)}, f32[1,1024]{1,0:T(1,128)S(1)}, u32[]{:S(2)}, u32[]{:S(2)}) collective-permute-start(f32[1,1024]{1,0:T(1,128)} %get-tuple-element.35), channel_id=1, source_target_pairs={{0,2},{1,3},{2,0},{3,1},{4,6},{5,8},{6,11},{7,5},{8,10},{9,4},{10,... | collective-permute-start | bytes 12296 | tf_op jit(solution)/shard_map/ppermute | solution.py:425
  104.3 6.9 %collective-permute-start.13 = (f32[1,1024]{1,0:T(1,128)}, f32[1,1024]{1,0:T(1,128)S(1)}, u32[]{:S(2)}, u32[]{:S(2)}) collective-permute-start(f32[1,1024]{1,0:T(1,128)} %get-tuple-element.36), channel_id=1, source_target_pairs={{2,3},{4,1},{5,12},{6,15},{7,2},{8,11},{9,8},{10,9},{11,10},{13,0}... | collective-permute-start | bytes 12296 | tf_op jit(solution)/shard_map/ppermute | solution.py:425
  105.6 5.6 %copy-start = (f32[1,1024]{1,0:T(1,128)}, f32[1,1024]{1,0:T(1,128)S(1)}, u32[]{:S(2)}) copy-start(f32[1,1024]{1,0:T(1,128)S(1)} %collective-permute-done.10.refs_0_) | copy-start | bytes 12292
  105.7 5.6 %copy-start.1 = (f32[1,1024]{1,0:T(1,128)}, f32[1,1024]{1,0:T(1,128)S(1)}, u32[]{:S(2)}) copy-start(f32[1,1024]{1,0:T(1,128)S(1)} %collective-permute-done.11.refs_1_) | copy-start | bytes 12292
  108.1 3.1 %copy-start.2 = (f32[1,1024]{1,0:T(1,128)}, f32[1,1024]{1,0:T(1,128)S(1)}, u32[]{:S(2)}) copy-start(f32[1,1024]{1,0:T(1,128)S(1)} %collective-permute-done.12.refs_2_) | copy-start | bytes 12292
  111.3 0.6 copy-start.3

commit v10 on v9

--- a/solution.py
+++ b/solution.py
@@ -40,7 +40,7 @@
     second = [((3, 1), (1, 1)), ((1, 1), (0, 1)), ((2, 1), (3, 0)), ((1, 0), (2, 1))]
     return [
         Move("R1", "own", rows(first), 0, 1),
-        Move("R2", "own", rows(second), 0, 1),
+        Move("R2", "own", rows(second), 0, 1, "best"),
         Move("Y", "own", across([place for place in every if place[0] != 1]) + crossed, 0, 1),
         Move("A", "own", swap, 0, 0),
         Move("R3", "own", rows([((1, 1), (2, 0)), ((2, 0), (1, 1))]), 1, 2, "R1"),
@@ -106,10 +106,15 @@
 
 
 def colored(edges, count):
+    ends = [of for of, _ in edges], [to for _, to in edges]
+    most = max((side.count(device) for side in ends for device in range(count)), default=0)
     sends, takes = [{} for _ in range(count)], [{} for _ in range(count)]
-    for of, to in edges:
+    for of, to in sorted(edges, key=lambda edge: (edge[0] ^ edge[1], edge)):
         a = next(c for c in range(len(edges)) if c not in sends[of])
         b = next(c for c in range(len(edges)) if c not in takes[to])
+        both = next(c for c in range(2 * len(edges)) if c not in sends[of] and c not in takes[to])
+        if both < most:
+            a = b = both
         path, node, tables, colour = [], to, (takes, sends), a
         while a != b and colour in tables[0][node]:
             end = tables[0][node][colour]
@@ -150,7 +155,7 @@
     return sorted(early), sorted(late)
 
 
-def unit_kernel(pads, order_smem, order, embeddings, unit, value, result, tile, into, out, sem):
+def unit_kernel(pads, order, embeddings, unit, value, result, tile, scalars, line, into, out, sems):
     rows = unit.shape[0]
     count = rows // into.shape[0]
     parts = [pl.ds(start, count) for start in range(0, rows, count)]
@@ -162,19 +167,25 @@
         pltpu.make_async_copy(result.at[part], unit.at[part], out.at[index])
         for index, part in enumerate(parts)
     ]
-    first = order_smem[0]
-    base = pl.multiple_of((first // 16) * 16, 16)
-    filling = pltpu.make_async_copy(embeddings.at[pl.ds(base, 16)], tile, sem)
-    filling.start()
+    to_scalars = pltpu.make_async_copy(order, scalars, sems.at[0])
+    to_line = pltpu.make_async_copy(order, line, sems.at[1])
+    to_scalars.start()
+    to_line.start()
     for load in loads:
         load.start()
+    to_scalars.wait()
+    first = scalars[0, 0]
+    base = pl.multiple_of((first // 16) * 16, 16)
+    filling = pltpu.make_async_copy(embeddings.at[pl.ds(base, 16)], tile, sems.at[2])
+    filling.start()
+    to_line.wait()
+    found = [valid_rows(pads, line, index * count, count) for index in range(len(parts))]
+    among = lax.broadcasted_iota(jnp.int32, (16, 1), 0) == first - base
     filling.wait()
-    among = lax.broadcasted_iota(jnp.int32, (16, 1), 0) == first - base
     filler = jnp.sum(jnp.where(among, tile[...].astype(jnp.float32), 0.0), axis=0, keepdims=True)
     for index, part in enumerate(parts):
-        found = valid_rows(pads, order, index * count, count)
         loads[index].wait()
-        chunk = jnp.where(found, value[part, :].astype(jnp.float32), filler)
+        chunk = jnp.where(found[index], value[part, :].astype(jnp.float32), filler)
         scale = lax.rsqrt(jnp.sum(chunk * chunk, axis=1, keepdims=True) + 1e-06)
         result[part, :] = (chunk * scale).astype(jnp.bfloat16)
         stores[index].start()
@@ -194,32 +205,29 @@
 
 def normalized(embeddings, order, pad_counts):
     rows, depth = embeddings.shape
-    chunks = 4
-    scalars = pl.BlockSpec(memory_space=pltpu.SMEM)
+    chunks = 8
+    anywhere = pl.BlockSpec(memory_space=pl.ANY)
     return pl.pallas_call(
         unit_kernel,
         out_shape=jax.ShapeDtypeStruct((rows, depth), jnp.bfloat16),
-        in_specs=[
-            scalars,
-            scalars,
-            pl.BlockSpec(memory_space=pltpu.VMEM),
-            pl.BlockSpec(memory_space=pl.ANY),
-        ],
-        out_specs=pl.BlockSpec(memory_space=pl.ANY),
+        in_specs=[pl.BlockSpec(memory_space=pltpu.SMEM), anywhere, anywhere],
+        out_specs=anywhere,
         scratch_shapes=[
             pltpu.VMEM((rows, depth), jnp.bfloat16),
             pltpu.VMEM((rows, depth), jnp.bfloat16),
             pltpu.VMEM((16, depth), jnp.bfloat16),
+            pltpu.SMEM((1, rows), jnp.int32),
+            pltpu.VMEM((1, rows), jnp.int32),
             pltpu.SemaphoreType.DMA((chunks,)),
             pltpu.SemaphoreType.DMA((chunks,)),
-            pltpu.SemaphoreType.DMA,
+            pltpu.SemaphoreType.DMA((3,)),
         ],
         compiler_params=pltpu.CompilerParams(vmem_limit_bytes=VMEM),
         cost_estimate=pl.CostEstimate(
             flops=4 * rows * depth, bytes_accessed=4 * rows * depth, transcendentals=rows
         ),
         name="normalized",
-    )(pad_counts, order, order.reshape(1, rows), embeddings)
+    )(pad_counts, order.reshape(1, rows), embeddings)
 
 
 def product(left, right):
@@ -409,15 +417,17 @@
     permutes, found = [], []
     for stage, pairs in enumerate(work):
         starting = [move for move in moves if move.begins == stage]
-        for needs in sorted({move.needs for move in starting}):
-            values = [slots[name] for name in needs]
+        for needs in sorted({move.needs for move in starting}, key=lambda needs: ("best" in needs, needs)):
+            if stage == 0 and "best" in needs:
+                best = own_block(unit, order, pad_counts, nblocks)
+            values = [slots[name] for name in needs if name != "best"]
             if best is not None:
                 *values, best = lax.optimization_barrier((*values, best))
             for move in starting:
                 if move.needs == needs:
                     value = values[needs.index(move.source)]
                     slots[move.name] = lax.ppermute(value, "blk", move.pairs)
-        if stage == 0:
+        if best is None:
             best = own_block(unit, order, pad_counts, nblocks)
         sends = colored(sorted(edges[stage]), nblocks) if stage in sending else []
         if any(pairs):

time: 115 us -> 120 us (1.043)
  waiting for transfers between devices: 44 us -> 48.6 us
    ppermute x8, waiting for transfers between devices: 36.9 us -> 41.5 us  [local(): slots[move.name] = lax.ppermute(value, 'blk', move.pairs)]
where the time goes in v10:
time: 120 us; the launch traced here: 119 us
  waiting for transfers between devices  48.6 us (40%)
  starting transfers between devices  36.7 us (31%)
  Pallas kernels  32.8 us (27%)
    ppermute x8, waiting for transfers between devices, local(): slots[move.name] = lax.ppermute(value, 'blk', move.pairs)  41.5 us
    ppermute x6, starting transfers between devices, local(): lax.ppermute(row, 'blk', permute)  21.3 us
    pallas_call x3, Pallas kernels, scored(): pl.pallas_call(functools.partial(pairs_kernel, len(given), len(sends), le...  21.3 us
    ppermute x8, starting transfers between devices, local(): slots[move.name] = lax.ppermute(value, 'blk', move.pairs)  15.4 us
    ppermute x6, waiting for transfers between devices, local(): lax.ppermute(row, 'blk', permute)  7.12 us
    pallas_call x1, Pallas kernels, own_block(): pl.pallas_call(own_kernel, out_shape=jax.ShapeDtypeStruct((nblocks, rows)...  4.67 us
    pallas_call x1, Pallas kernels, normalized(): pl.pallas_call(unit_kernel, out_shape=jax.ShapeDtypeStruct((rows, depth),...  4.63 us
  transfers between devices with their start and end apart: 14, of which 5 were waited for; matrix products, arithmetic and copies ran while one was open for 0% of the time, Pallas kernels for 15%

profile of v10, /device:TPU:0, one launch (start us, length us, event | category | flops | bytes accessed | tf_op | source)
XLA Modules:
  0.0 119.4 jit_solution(1511768807939974628)
XLA Ops:
  0.0 4.6 %normalized.1.unit.refs_1_.refs_4_.refs_10_ = bf16[1024,1024]{1,0:T(8,128)(2,1)} custom-call(s32[16]{0:T(128)} %pads.5, s32[1,1024]{1,0:T(1,128)} %bitcast.2, bf16[1024,1024]{1,0:T(8,128)(2,1)} %embeddings.1), custom_call_target="tpu_custom_call" | custom-call | flops 4194304 | bytes 4194304 | tf_op jit(solution)/shard_map/normalized/pallas_call | solution.py:210
  5.2 5.6 %collective-permute-start.1 = (bf16[1024,1024]{1,0:T(8,128)(2,1)}, bf16[1024,1024]{1,0:T(8,128)(2,1)}, u32[]{:S(2)}, u32[]{:S(2)}) collective-permute-start(bf16[1024,1024]{1,0:T(8,128)(2,1)} %normalized.1.unit.refs_1_.refs_4_.refs_10_), channel_id=1, source_target_pairs={{0,9},{8,13},{12,4},{4,0},{1,5},{3,10},{11,14},{15,7},{7,3},{2,6},... | collective-permute-start | bytes 6291464 | tf_op jit(solution)/shard_map/ppermute | solution.py:429
  10.8 4.7 %own_block.1.best = f32[16,1024]{1,0:T(8,128)} custom-call(s32[16]{0:T(128)} %pads.5, s32[1,1024]{1,0:T(1,128)} %bitcast.3, bf16[1024,1024]{1,0:T(8,128)(2,1)} %normalized.1.unit.refs_1_.refs_4_.refs_10_), custom_call_target="tpu_custom_call" | custom-call | flops 2147483648 | bytes 2097152 | tf_op jit(solution)/shard_map/own_block/pallas_call | solution.py:254
  15.4 2.0 %collective-permute-start.3 = (bf16[1024,1024]{1,0:T(8,128)(2,1)}, bf16[1024,1024]{1,0:T(8,128)(2,1)}, u32[]{:S(2)}, u32[]{:S(2)}) collective-permute-start(bf16[1024,1024]{1,0:T(8,128)(2,1)} %normalized.1.unit.refs_1_.refs_4_.refs_10_), channel_id=1, source_target_pairs={{13,5},{5,1},{9,12},{4,9},{14,6},{6,2},{10,15},{7,10},{29,21},{21,... | collective-permute-start | bytes 6291464 | tf_op jit(solution)/shard_map/ppermute | solution.py:429
  17.5 1.2 collective-permute-start
  18.6 1.5 %scored.3.best = f32[16,1024]{1,0:T(8,128)} custom-call(s32[144]{0:T(256)} %constant.8.clone.table, f32[16,1024]{1,0:T(8,128)} %own_block.1.best, bf16[1024,1024]{1,0:T(8,128)(2,1)} %collective-permute-done.2.refs_0_.refs_2_, bf16[1024,1024]{1,0:T(8,128)(2,1)} %normalized.1.unit.refs_1_.refs_4_.refs_10_), custom_call_target="tpu_custom_call" | custom-call | flops 2147483648 | bytes 4194304 | tf_op jit(solution)/shard_map/scored/pallas_call | solution.py:352
  20.1 35.4 %collective-permute-done.1.refs_1_.refs_4_ = bf16[1024,1024]{1,0:T(8,128)(2,1)} collective-permute-done((bf16[1024,1024]{1,0:T(8,128)(2,1)}, bf16[1024,1024]{1,0:T(8,128)(2,1)}, u32[]{:S(2)}, u32[]{:S(2)}) %collective-permute-start.1) | collective-permute-done | bytes 2097184 | tf_op jit(solution)/shard_map/ppermute | solution.py:429
  55.5 2.0 %collective-permute-start.7 = (bf16[1024,1024]{1,0:T(8,128)(2,1)}, bf16[1024,1024]{1,0:T(8,128)(2,1)}, u32[]{:S(2)}, u32[]{:S(2)}) collective-permute-start(bf16[1024,1024]{1,0:T(8,128)(2,1)} %normalized.1.unit.refs_1_.refs_4_.refs_10_), channel_id=1, source_target_pairs={{5,8},{8,5},{6,11},{11,6},{21,24},{24,21},{22,27},{27,22}} | collective-permute-start | bytes 6291464 | tf_op jit(solution)/shard_map/ppermute | solution.py:429
  57.5 2.0 %collective-permute-start.8 = (bf16[1024,1024]{1,0:T(8,128)(2,1)}, bf16[1024,1024]{1,0:T(8,128)(2,1)}, u32[]{:S(2)}, u32[]{:S(2)}) collective-permute-start(bf16[1024,1024]{1,0:T(8,128)(2,1)} %collective-permute-done.1.refs_1_.refs_4_), channel_id=1, source_target_pairs={{9,13},{10,15},{5,6},{6,5},{25,29},{26,31},{21,22},{22,21}} | collective-permute-start | bytes 6291464 | tf_op jit(solution)/shard_map/ppermute | solution.py:429
  59.5 6.1 %collective-permute-done.refs_3_.refs_9_ = bf16[1024,1024]{1,0:T(8,128)(2,1)} collective-permute-done((bf16[1024,1024]{1,0:T(8,128)(2,1)}, bf16[1024,1024]{1,0:T(8,128)(2,1)}, u32[]{:S(2)}, u32[]{:S(2)}) %collective-permute-start) | collective-permute-done | bytes 2097184 | tf_op jit(solution)/shard_map/ppermute | solution.py:429
  65.6 11.1 %scored.4 = (f32[16,1024]{1,0:T(8,128)}, f32[1,1024]{1,0:T(1,128)}, f32[1,1024]{1,0:T(1,128)}) custom-call(s32[464]{0:T(512)} %constant.9.clone.table, f32[16,1024]{1,0:T(8,128)} %scored.3.best, bf16[1024,1024]{1,0:T(8,128)(2,1)} %collective-permute-done.2.refs_0_.refs_2_, bf16[1024,1024]{1,0:T(8,128)(2,1)} %collective-permute-done.1.refs_1_.refs_4_, ...), custom_call_target="tpu_custom_call" | custom-call | flops 8589934592 | bytes 10485760 | tf_op jit(solution)/shard_map/scored/pallas_call | solution.py:352
  76.8 2.0 %collective-permute-start.9 = (bf16[1024,1024]{1,0:T(8,128)(2,1)}, bf16[1024,1024]{1,0:T(8,128)(2,1)}, u32[]{:S(2)}, u32[]{:S(2)}) collective-permute-start(bf16[1024,1024]{1,0:T(8,128)(2,1)} %collective-permute-done.1.refs_1_.refs_4_), channel_id=1, source_target_pairs={{4,5},{5,4},{7,6},{6,7},{20,21},{21,20},{23,22},{22,23}} | collective-permute-start | bytes 6291464 | tf_op jit(solution)/shard_map/ppermute | solution.py:429
  78.8 2.5 %collective-permute-start.4 = (f32[1,1024]{1,0:T(1,128)}, f32[1,1024]{1,0:T(1,128)S(1)}, u32[]{:S(2)}, u32[]{:S(2)}) collective-permute-start(f32[1,1024]{1,0:T(1,128)} %get-tuple-element.30), channel_id=1, source_target_pairs={{0,3},{1,0},{2,1},{4,5},{5,7},{6,4},{7,6},{9,10},{10,11},{12,15},{... | collective-permute-start | bytes 12296 | tf_op jit(solution)/shard_map/ppermute | solution.py:435
  81.3 1.5 %collective-permute-done.4.refs_0_ = f32[1,1024]{1,0:T(1,128)S(1)} collective-permute-done((f32[1,1024]{1,0:T(1,128)}, f32[1,1024]{1,0:T(1,128)S(1)}, u32[]{:S(2)}, u32[]{:S(2)}) %collective-permute-start.4) | collective-permute-done | bytes 4128 | tf_op jit(solution)/shard_map/ppermute | solution.py:435
  82.9 0.6 collective-permute-start.5
  84.1 8.7 %scored.5 = (f32[16,1024]{1,0:T(8,128)}, f32[1,1024]{1,0:T(1,128)}, f32[1,1024]{1,0:T(1,128)}, f32[1,1024]{1,0:T(1,128)}, f32[1,1024]{1,0:T(1,128)}) custom-call(s32[528]{0:T(1024)} %constant.10.clone.table, f32[16,1024]{1,0:T(8,128)} %get-tuple-element.29.best, f32[1,1024]{1,0:T(1,128)} %copy-done.4, f32[1,1024]{1,0:T(1,128)} %copy-done.5, ...), custom_call_target="tpu_custom_call" | custom-call | flops 8589934592 | bytes 10485760 | tf_op jit(solution)/shard_map/scored/pallas_call | solution.py:352
  92.8 11.3 %collective-permute-start.10 = (f32[1,1024]{1,0:T(1,128)}, f32[1,1024]{1,0:T(1,128)S(1)}, u32[]{:S(2)}, u32[]{:S(2)}) collective-permute-start(f32[1,1024]{1,0:T(1,128)} %get-tuple-element.37), channel_id=1, source_target_pairs={{0,4},{2,6},{3,2},{4,1},{5,8},{6,15},{7,5},{8,9},{9,11},{10,7},{11... | collective-permute-start | bytes 12296 | tf_op jit(solution)/shard_map/ppermute | solution.py:435
  104.1 3.7 %collective-permute-start.11 = (f32[1,1024]{1,0:T(1,128)}, f32[1,1024]{1,0:T(1,128)S(1)}, u32[]{:S(2)}, u32[]{:S(2)}) collective-permute-start(f32[1,1024]{1,0:T(1,128)} %get-tuple-element.38), channel_id=1, source_target_pairs={{0,2},{2,0},{3,1},{4,7},{5,12},{6,11},{7,4},{8,10},{9,8},{10,3},{1... | collective-permute-start | bytes 12296 | tf_op jit(solution)/shard_map/ppermute | solution.py:435
  107.8 1.9 %collective-permute-start.12 = (f32[1,1024]{1,0:T(1,128)}, f32[1,1024]{1,0:T(1,128)S(1)}, u32[]{:S(2)}, u32[]{:S(2)}) collective-permute-start(f32[1,1024]{1,0:T(1,128)} %get-tuple-element.39), channel_id=1, source_target_pairs={{0,1},{1,5},{2,3},{3,7},{4,6},{5,13},{6,14},{7,2},{8,11},{9,0},{10... | collective-permute-start | bytes 12296 | tf_op jit(solution)/shard_map/ppermute | solution.py:435
  109.7 1.3 %collective-permute-start.13 = (f32[1,1024]{1,0:T(1,128)}, f32[1,1024]{1,0:T(1,128)S(1)}, u32[]{:S(2)}, u32[]{:S(2)}) collective-permute-start(f32[1,1024]{1,0:T(1,128)} %get-tuple-element.40), channel_id=1, source_target_pairs={{1,3},{4,12},{5,2},{6,1},{7,15},{8,5},{9,4},{10,8},{11,6},{12,9},{... | collective-permute-start | bytes 12296 | tf_op jit(solution)/shard_map/ppermute | solution.py:435
  111.1 2.8 %collective-permute-done.12.refs_2_ = f32[1,1024]{1,0:T(1,128)S(1)} collective-permute-done((f32[1,1024]{1,0:T(1,128)}, f32[1,1024]{1,0:T(1,128)S(1)}, u32[]{:S(2)}, u32[]{:S(2)}) %collective-permute-start.12) | collective-permute-done | bytes 4128 | tf_op jit(solution)/shard_map/ppermute | solution.py:435
  113.8 2.8 %collective-permute-done.13.refs_3_ = f32[1,1024]{1,0:T(1,128)S(1)} collective-permute-done((f32[1,1024]{1,0:T(1,128)}, f32[1,1024]{1,0:T(1,128)S(1)}, u32[]{:S(2)}, u32[]{:S(2)}) %collective-permute-start.13) | collective-permute-done | bytes 4128 | tf_op jit(solution)/shard_map/ppermute | solution.py:435
  116.7 0.6 copy-done.3
  117.2 2.2 %placed.1 = f32[1,1024]{1,0:T(1,128)} custom-call(s32[64]{0:T(128)} %constant.11.clone.taken, s32[16]{0:T(128)} %pads.5, s32[1,1024]{1,0:T(1,128)} %bitcast.4, f32[16,1024]{1,0:T(8,128)} %get-tuple-element.36.best, f32[1,1024]{1,0:T(1,128)} %copy-done, f32[1,1024]{1,0:T(1,128)} %copy-done.1, f32[1,1024]{1,0:T(1,128)} %copy-done.2, f32[1,1024]{1,0:T(1,128)} %copy-done.3), custom_call_target="tpu_custom_call" | custom-call | tf_op jit(solution)/shard_map/placed/pallas_call | solution.py:395
  (22 shorter events, 1.2 us)
Async XLA Ops:
  4.6 14.0 %collective-permute-start.2 = (bf16[1024,1024]{1,0:T(8,128)(2,1)}, bf16[1024,1024]{1,0:T(8,128)(2,1)}, u32[]{:S(2)}, u32[]{:S(2)}) collective-permute-start(bf16[1024,1024]{1,0:T(8,128)(2,1)} %normalized.1.unit.refs_1_.refs_4_.refs_10_), channel_id=1, source_target_pairs={{0,1},{1,0},{4,5},{5,4},{8,9},{9,8},{12,13},{13,12},{3,2},{2,3},{7... | collective-permute-start | bytes 6291464 | tf_op jit(solution)/shard_map/ppermute | solution.py:429
  5.2 50.4 %collective-permute-start.1 = (bf16[1024,1024]{1,0:T(8,128)(2,1)}, bf16[1024,1024]{1,0:T(8,128)(2,1)}, u32[]{:S(2)}, u32[]{:S(2)}) collective-permute-start(bf16[1024,1024]{1,0:T(8,128)(2,1)} %normalized.1.unit.refs_1_.refs_4_.refs_10_), channel_id=1, source_target_pairs={{0,9},{8,13},{12,4},{4,0},{1,5},{3,10},{11,14},{15,7},{7,3},{2,6},... | collective-permute-start | bytes 6291464 | tf_op jit(solution)/shard_map/ppermute | solution.py:429
  15.4 44.1 %collective-permute-start.3 = (bf16[1024,1024]{1,0:T(8,128)(2,1)}, bf16[1024,1024]{1,0:T(8,128)(2,1)}, u32[]{:S(2)}, u32[]{:S(2)}) collective-permute-start(bf16[1024,1024]{1,0:T(8,128)(2,1)} %normalized.1.unit.refs_1_.refs_4_.refs_10_), channel_id=1, source_target_pairs={{13,5},{5,1},{9,12},{4,9},{14,6},{6,2},{10,15},{7,10},{29,21},{21,... | collective-permute-start | bytes 6291464 | tf_op jit(solution)/shard_map/ppermute | solution.py:429
  17.5 48.2 %collective-permute-start = (bf16[1024,1024]{1,0:T(8,128)(2,1)}, bf16[1024,1024]{1,0:T(8,128)(2,1)}, u32[]{:S(2)}, u32[]{:S(2)}) collective-permute-start(bf16[1024,1024]{1,0:T(8,128)(2,1)} %normalized.1.unit.refs_1_.refs_4_.refs_10_), channel_id=1, source_target_pairs={{0,3},{3,0},{1,2},{2,1},{8,11},{11,8},{9,10},{10,9},{12,15},{15,12... | collective-permute-start | bytes 6291464 | tf_op jit(solution)/shard_map/ppermute | solution.py:429
  55.5 28.0 %collective-permute-start.7 = (bf16[1024,1024]{1,0:T(8,128)(2,1)}, bf16[1024,1024]{1,0:T(8,128)(2,1)}, u32[]{:S(2)}, u32[]{:S(2)}) collective-permute-start(bf16[1024,1024]{1,0:T(8,128)(2,1)} %normalized.1.unit.refs_1_.refs_4_.refs_10_), channel_id=1, source_target_pairs={{5,8},{8,5},{6,11},{11,6},{21,24},{24,21},{22,27},{27,22}} | collective-permute-start | bytes 6291464 | tf_op jit(solution)/shard_map/ppermute | solution.py:429
  57.5 26.0 %collective-permute-start.8 = (bf16[1024,1024]{1,0:T(8,128)(2,1)}, bf16[1024,1024]{1,0:T(8,128)(2,1)}, u32[]{:S(2)}, u32[]{:S(2)}) collective-permute-start(bf16[1024,1024]{1,0:T(8,128)(2,1)} %collective-permute-done.1.refs_1_.refs_4_), channel_id=1, source_target_pairs={{9,13},{10,15},{5,6},{6,5},{25,29},{26,31},{21,22},{22,21}} | collective-permute-start | bytes 6291464 | tf_op jit(solution)/shard_map/ppermute | solution.py:429
  76.8 6.8 %collective-permute-start.6 = (bf16[1024,1024]{1,0:T(8,128)(2,1)}, bf16[1024,1024]{1,0:T(8,128)(2,1)}, u32[]{:S(2)}, u32[]{:S(2)}) collective-permute-start(bf16[1024,1024]{1,0:T(8,128)(2,1)} %collective-permute-done.refs_3_.refs_9_), channel_id=1, source_target_pairs={{0,1},{1,0},{4,5},{5,4},{8,9},{9,8},{12,13},{13,12},{3,2},{2,3},{7... | collective-permute-start | bytes 6291464 | tf_op jit(solution)/shard_map/ppermute | solution.py:429
  76.8 6.7 %collective-permute-start.9 = (bf16[1024,1024]{1,0:T(8,128)(2,1)}, bf16[1024,1024]{1,0:T(8,128)(2,1)}, u32[]{:S(2)}, u32[]{:S(2)}) collective-permute-start(bf16[1024,1024]{1,0:T(8,128)(2,1)} %collective-permute-done.1.refs_1_.refs_4_), channel_id=1, source_target_pairs={{4,5},{5,4},{7,6},{6,7},{20,21},{21,20},{23,22},{22,23}} | collective-permute-start | bytes 6291464 | tf_op jit(solution)/shard_map/ppermute | solution.py:429
  78.8 4.0 %collective-permute-start.4 = (f32[1,1024]{1,0:T(1,128)}, f32[1,1024]{1,0:T(1,128)S(1)}, u32[]{:S(2)}, u32[]{:S(2)}) collective-permute-start(f32[1,1024]{1,0:T(1,128)} %get-tuple-element.30), channel_id=1, source_target_pairs={{0,3},{1,0},{2,1},{4,5},{5,7},{6,4},{7,6},{9,10},{10,11},{12,15},{... | collective-permute-start | bytes 12296 | tf_op jit(solution)/shard_map/ppermute | solution.py:435
  82.9 0.7 copy-start.4
  82.9 0.7 collective-permute-start.5
  83.5 0.6 copy-start.5
  92.8 18.2 %collective-permute-start.10 = (f32[1,1024]{1,0:T(1,128)}, f32[1,1024]{1,0:T(1,128)S(1)}, u32[]{:S(2)}, u32[]{:S(2)}) collective-permute-start(f32[1,1024]{1,0:T(1,128)} %get-tuple-element.37), channel_id=1, source_target_pairs={{0,4},{2,6},{3,2},{4,1},{5,8},{6,15},{7,5},{8,9},{9,11},{10,7},{11... | collective-permute-start | bytes 12296 | tf_op jit(solution)/shard_map/ppermute | solution.py:435
  104.1 6.9 %collective-permute-start.11 = (f32[1,1024]{1,0:T(1,128)}, f32[1,1024]{1,0:T(1,128)S(1)}, u32[]{:S(2)}, u32[]{:S(2)}) collective-permute-start(f32[1,1024]{1,0:T(1,128)} %get-tuple-element.38), channel_id=1, source_target_pairs={{0,2},{2,0},{3,1},{4,7},{5,12},{6,11},{7,4},{8,10},{9,8},{10,3},{1... | collective-permute-start | bytes 12296 | tf_op jit(solution)/shard_map/ppermute | solution.py:435
  107.8 6.0 %collective-permute-start.12 = (f32[1,1024]{1,0:T(1,128)}, f32[1,1024]{1,0:T(1,128)S(1)}, u32[]{:S(2)}, u32[]{:S(2)}) collective-permute-start(f32[1,1024]{1,0:T(1,128)} %get-tuple-element.39), channel_id=1, source_target_pairs={{0,1},{1,5},{2,3},{3,7},{4,6},{5,13},{6,14},{7,2},{8,11},{9,0},{10... | collective-permute-start | bytes 12296 | tf_op jit(solution)/shard_map/ppermute | solution.py:435
  109.7 6.9 %collective-permute-start.13 = (f32[1,1024]{1,0:T(1,128)}, f32[1,1024]{1,0:T(1,128)S(1)}, u32[]{:S(2)}, u32[]{:S(2)}) collective-permute-start(f32[1,1024]{1,0:T(1,128)} %get-tuple-element.40), channel_id=1, source_target_pairs={{1,3},{4,12},{5,2},{6,1},{7,15},{8,5},{9,4},{10,8},{11,6},{12,9},{... | collective-permute-start | bytes 12296 | tf_op jit(solution)/shard_map/ppermute | solution.py:435
  111.0 5.6 %copy-start = (f32[1,1024]{1,0:T(1,128)}, f32[1,1024]{1,0:T(1,128)S(1)}, u32[]{:S(2)}) copy-start(f32[1,1024]{1,0:T(1,128)S(1)} %collective-permute-done.10.refs_0_) | copy-start | bytes 12292
  111.1 5.6 %copy-start.1 = (f32[1,1024]{1,0:T(1,128)}, f32[1,1024]{1,0:T(1,128)S(1)}, u32[]{:S(2)}) copy-start(f32[1,1024]{1,0:T(1,128)S(1)} %collective-permute-done.11.refs_1_) | copy-start | bytes 12292
  113.8 2.8 %copy-start.2 = (f32[1,1024]{1,0:T(1,128)}, f32[1,1024]{1,0:T(1,128)S(1)}, u32[]{:S(2)}) copy-start(f32[1,1024]{1,0:T(1,128)S(1)} %collective-permute-done.12.refs_2_) | copy-start | bytes 12292
  116.7 0.6 copy-start.3

commit v11 on v9

--- a/solution.py
+++ b/solution.py
@@ -258,10 +258,10 @@
 
 def pairs_kernel(nslots, nrows, ntaken, nloads, npairs, table, best, *refs):
     arrivals, slots, out = refs[:ntaken], refs[ntaken : ntaken + nslots], refs[ntaken + nslots]
-    sent, (held, across, sems) = refs[ntaken + nslots + 1 : -3], refs[-3:]
+    sent, (held, turned, across, sems) = refs[ntaken + nslots + 1 : -4], refs[-4:]
     rows = out.shape[1]
     here = lax.axis_index("blk")
-    loads_at = here * (2 + nrows + ntaken + nloads + 5 * npairs) + 2 + nrows + ntaken
+    loads_at = here * (2 + nrows + ntaken + nloads + 6 * npairs) + 2 + nrows + ntaken
     pairs_at = loads_at + nloads
     rows_at = loads_at - nrows - ntaken
     loads, pairs = table[rows_at - 2], table[rows_at - 1]
@@ -287,19 +287,28 @@
 
     @pl.loop(0, pairs)
     def _(step):
-        at = pairs_at + 5 * step
-        before = jnp.where(step == 0, 0, table[jnp.maximum(at - 1, 0)])
-
-        @pl.loop(before, table[at + 4])
-        def _(load):
+        at = pairs_at + 6 * step
+        before = jnp.where(step == 0, 0, table[jnp.maximum(at - 2, 0)])
+        turn = table[at + 5]
+
+        def arrived(load):
             pltpu.make_async_copy(slots[0], held.at[load], sems.at[load]).wait()
             fetch(load + AHEAD)
 
+        pl.loop(before, jnp.maximum(before, turn))(arrived)
+
+        @pl.when(turn > 0)
+        def _():
+            for start in range(0, rows, 256):
+                part = pl.ds(start, 256)
+                turned[:, part] = held[table[at + 1], part, :].T
+
+        pl.loop(jnp.maximum(before, turn), table[at + 4])(arrived)
         left, right = table[at], table[at + 1]
         first, second = pl.ds(table[at + 2], 1), pl.ds(table[at + 3], 1)
         for start in range(0, rows, 256):
             part = pl.ds(start, 256)
-            scores = product(held[left], held[right, part, :])
+            scores = jnp.dot(held[left], turned[:, part], preferred_element_type=jnp.float32)
             down = jnp.max(scores, axis=0, keepdims=True)
             out[second, part] = jnp.maximum(out[second, part], down)
             along = jnp.maximum(scores[:, :128], scores[:, 128:])
@@ -312,15 +321,27 @@
 
 
 def in_order_of_loads(pairs, rank):
-    left, loaded, ordered = list(pairs), [], []
-    while left:
+    waiting, loaded, ordered, right = list(pairs), [], [], None
+    while waiting:
         pair = min(
-            left,
-            key=lambda p: (sum(s not in loaded for s in p[:2]), max(rank[s] for s in p[:2]), p[2:]),
+            waiting,
+            key=lambda p: (
+                right not in p[:2],
+                sum(s not in loaded for s in p[:2]),
+                max(rank[s] for s in p[:2]),
+                p[2:],
+            ),
         )
-        left.remove(pair)
-        loaded += [slot for slot in pair[:2] if slot not in loaded]
-        ordered.append((pair, len(loaded)))
+        turn = right not in pair[:2]
+        if turn:
+            uses = [sum(slot in p[:2] for p in waiting) for slot in pair[:2]]
+            right = pair[0] if uses[0] > uses[1] else pair[1]
+        waiting.remove(pair)
+        if pair[1] != right:
+            pair = (pair[1], pair[0], pair[3], pair[2])
+        loaded += [slot for slot in pair[1::-1] if slot not in loaded]
+        index = [loaded.index(slot) for slot in pair[:2]]
+        ordered.append((*index, *pair[2:], len(loaded), (index[1] + 1) * turn))
     return loaded, ordered
 
 
@@ -335,9 +356,9 @@
         table += [dict(permute).get(device, device) for permute in sends]
         table += [int(device in dict(permute).values()) for permute in permutes]
         table += [names.index(slot) for slot in loaded] + [0] * (nloads - len(loaded))
-        for (slot, other, block, visitor), need in ordered:
-            table += [loaded.index(slot), loaded.index(other), block, visitor, need]
-        table += [0] * (5 * (npairs - len(ordered)))
+        for entry in ordered:
+            table += entry
+        table += [0] * (6 * (npairs - len(ordered)))
     given = [slots[name] for name in names]
     rows, depth = given[0].shape
     whole = pl.BlockSpec(memory_space=pltpu.VMEM)
@@ -351,6 +372,7 @@
         out_specs=[whole] * (1 + len(sends)),
         scratch_shapes=[
             pltpu.VMEM((nloads, rows, depth), jnp.bfloat16),
+            pltpu.VMEM((depth, rows), jnp.bfloat16),
             pltpu.VMEM((rows, 128), jnp.float32),
             pltpu.SemaphoreType.DMA((nloads,)),
         ],

time: 115 us -> 115 us (level)
  no operation moved by 1% of the time
where the time goes in v11:
time: 115 us
  waiting for transfers between devices  44.1 us (38%)
  starting transfers between devices  37 us (32%)
  Pallas kernels  32.3 us (28%)
    ppermute x8, waiting for transfers between devices, local(): slots[move.name] = lax.ppermute(value, 'blk', move.pairs)  37 us
    ppermute x6, starting transfers between devices, local(): lax.ppermute(row, 'blk', permute)  21.7 us
    pallas_call x3, Pallas kernels, scored(): pl.pallas_call(functools.partial(pairs_kernel, len(given), len(sends), le...  21.2 us
    ppermute x8, starting transfers between devices, local(): slots[move.name] = lax.ppermute(value, 'blk', move.pairs)  15.3 us
    ppermute x6, waiting for transfers between devices, local(): lax.ppermute(row, 'blk', permute)  7.12 us
    pallas_call x1, Pallas kernels, own_block(): pl.pallas_call(own_kernel, out_shape=jax.ShapeDtypeStruct((nblocks, rows)...  4.65 us
    pallas_call x1, Pallas kernels, normalized(): pl.pallas_call(unit_kernel, out_shape=jax.ShapeDtypeStruct((rows, depth),...  4.22 us
  transfers between devices with their start and end apart: 14, of which 5 were waited for; matrix products, arithmetic and copies ran while one was open for 0% of the time, Pallas kernels for 15%

profile of v11, /device:TPU:0, one launch (start us, length us, event | category | flops | bytes accessed | tf_op | source)
XLA Modules:
  0.0 114.6 jit_solution(8187523865988309825)
XLA Ops:
  0.0 4.2 %normalized.1.unit.refs_1_.refs_4_.refs_10_ = bf16[1024,1024]{1,0:T(8,128)(2,1)} custom-call(s32[16]{0:T(128)} %pads.5, s32[1024]{0:T(1024)} %order_smem.1, s32[1,1024]{1,0:T(1,128)} %bitcast.2, bf16[1024,1024]{1,0:T(8,128)(2,1)} %embeddings.1), custom_call_target="tpu_custom_call" | custom-call | flops 4194304 | bytes 4194304 | tf_op jit(solution)/shard_map/normalized/pallas_call | solution.py:199
  4.7 5.6 %collective-permute-start.1 = (bf16[1024,1024]{1,0:T(8,128)(2,1)}, bf16[1024,1024]{1,0:T(8,128)(2,1)}, u32[]{:S(2)}, u32[]{:S(2)}) collective-permute-start(bf16[1024,1024]{1,0:T(8,128)(2,1)} %normalized.1.unit.refs_1_.refs_4_.refs_10_), channel_id=1, source_target_pairs={{0,9},{8,13},{12,4},{4,0},{1,5},{3,10},{11,14},{15,7},{7,3},{2,6},... | collective-permute-start | bytes 6291464 | tf_op jit(solution)/shard_map/ppermute | solution.py:441
  10.3 2.0 %collective-permute-start.3 = (bf16[1024,1024]{1,0:T(8,128)(2,1)}, bf16[1024,1024]{1,0:T(8,128)(2,1)}, u32[]{:S(2)}, u32[]{:S(2)}) collective-permute-start(bf16[1024,1024]{1,0:T(8,128)(2,1)} %normalized.1.unit.refs_1_.refs_4_.refs_10_), channel_id=1, source_target_pairs={{13,5},{5,1},{9,12},{4,9},{14,6},{6,2},{10,15},{7,10},{29,21},{21,... | collective-permute-start | bytes 6291464 | tf_op jit(solution)/shard_map/ppermute | solution.py:441
  12.4 1.1 collective-permute-start
  13.5 4.7 %own_block.1.best = f32[16,1024]{1,0:T(8,128)} custom-call(s32[16]{0:T(128)} %pads.5, s32[1,1024]{1,0:T(1,128)} %bitcast.3, bf16[1024,1024]{1,0:T(8,128)(2,1)} %normalized.1.unit.refs_1_.refs_4_.refs_10_), custom_call_target="tpu_custom_call" | custom-call | flops 2147483648 | bytes 2097152 | tf_op jit(solution)/shard_map/own_block/pallas_call | solution.py:246
  18.1 1.5 %scored.3.best = f32[16,1024]{1,0:T(8,128)} custom-call(s32[160]{0:T(256)} %constant.8.clone.table, f32[16,1024]{1,0:T(8,128)} %own_block.1.best, bf16[1024,1024]{1,0:T(8,128)(2,1)} %collective-permute-done.2.refs_0_.refs_2_, bf16[1024,1024]{1,0:T(8,128)(2,1)} %normalized.1.unit.refs_1_.refs_4_.refs_10_), custom_call_target="tpu_custom_call" | custom-call | flops 2147483648 | bytes 4194304 | tf_op jit(solution)/shard_map/scored/pallas_call | solution.py:365
  19.6 35.5 %collective-permute-done.1.refs_1_.refs_4_ = bf16[1024,1024]{1,0:T(8,128)(2,1)} collective-permute-done((bf16[1024,1024]{1,0:T(8,128)(2,1)}, bf16[1024,1024]{1,0:T(8,128)(2,1)}, u32[]{:S(2)}, u32[]{:S(2)}) %collective-permute-start.1) | collective-permute-done | bytes 2097184 | tf_op jit(solution)/shard_map/ppermute | solution.py:441
  55.1 2.0 %collective-permute-start.7 = (bf16[1024,1024]{1,0:T(8,128)(2,1)}, bf16[1024,1024]{1,0:T(8,128)(2,1)}, u32[]{:S(2)}, u32[]{:S(2)}) collective-permute-start(bf16[1024,1024]{1,0:T(8,128)(2,1)} %normalized.1.unit.refs_1_.refs_4_.refs_10_), channel_id=1, source_target_pairs={{5,8},{8,5},{6,11},{11,6},{21,24},{24,21},{22,27},{27,22}} | collective-permute-start | bytes 6291464 | tf_op jit(solution)/shard_map/ppermute | solution.py:441
  57.1 2.0 %collective-permute-start.8 = (bf16[1024,1024]{1,0:T(8,128)(2,1)}, bf16[1024,1024]{1,0:T(8,128)(2,1)}, u32[]{:S(2)}, u32[]{:S(2)}) collective-permute-start(bf16[1024,1024]{1,0:T(8,128)(2,1)} %collective-permute-done.1.refs_1_.refs_4_), channel_id=1, source_target_pairs={{9,13},{10,15},{5,6},{6,5},{25,29},{26,31},{21,22},{22,21}} | collective-permute-start | bytes 6291464 | tf_op jit(solution)/shard_map/ppermute | solution.py:441
  59.1 1.5 %collective-permute-done.refs_3_.refs_9_ = bf16[1024,1024]{1,0:T(8,128)(2,1)} collective-permute-done((bf16[1024,1024]{1,0:T(8,128)(2,1)}, bf16[1024,1024]{1,0:T(8,128)(2,1)}, u32[]{:S(2)}, u32[]{:S(2)}) %collective-permute-start) | collective-permute-done | bytes 2097184 | tf_op jit(solution)/shard_map/ppermute | solution.py:441
  60.6 11.1 %scored.4 = (f32[16,1024]{1,0:T(8,128)}, f32[1,1024]{1,0:T(1,128)}, f32[1,1024]{1,0:T(1,128)}) custom-call(s32[528]{0:T(1024)} %constant.9.clone.table, f32[16,1024]{1,0:T(8,128)} %scored.3.best, bf16[1024,1024]{1,0:T(8,128)(2,1)} %collective-permute-done.2.refs_0_.refs_2_, bf16[1024,1024]{1,0:T(8,128)(2,1)} %collective-permute-done.1.refs_1_.refs_4_, ...), custom_call_target="tpu_custom_call" | custom-call | flops 8589934592 | bytes 10485760 | tf_op jit(solution)/shard_map/scored/pallas_call | solution.py:365
  71.7 2.0 %collective-permute-start.9 = (bf16[1024,1024]{1,0:T(8,128)(2,1)}, bf16[1024,1024]{1,0:T(8,128)(2,1)}, u32[]{:S(2)}, u32[]{:S(2)}) collective-permute-start(bf16[1024,1024]{1,0:T(8,128)(2,1)} %collective-permute-done.1.refs_1_.refs_4_), channel_id=1, source_target_pairs={{4,5},{5,4},{7,6},{6,7},{20,21},{21,20},{23,22},{22,23}} | collective-permute-start | bytes 6291464 | tf_op jit(solution)/shard_map/ppermute | solution.py:441
  73.7 2.5 %collective-permute-start.4 = (f32[1,1024]{1,0:T(1,128)}, f32[1,1024]{1,0:T(1,128)S(1)}, u32[]{:S(2)}, u32[]{:S(2)}) collective-permute-start(f32[1,1024]{1,0:T(1,128)} %get-tuple-element.26), channel_id=1, source_target_pairs={{0,3},{1,0},{4,5},{5,1},{6,2},{7,6},{9,10},{10,11},{12,15},{13,8},... | collective-permute-start | bytes 12296 | tf_op jit(solution)/shard_map/ppermute | solution.py:447
  76.2 1.5 %collective-permute-done.4.refs_0_ = f32[1,1024]{1,0:T(1,128)S(1)} collective-permute-done((f32[1,1024]{1,0:T(1,128)}, f32[1,1024]{1,0:T(1,128)S(1)}, u32[]{:S(2)}, u32[]{:S(2)}) %collective-permute-start.4) | collective-permute-done | bytes 4128 | tf_op jit(solution)/shard_map/ppermute | solution.py:447
  77.7 0.6 collective-permute-start.5
  78.5 0.5 copy-done.5
  79.0 8.6 %scored.5 = (f32[16,1024]{1,0:T(8,128)}, f32[1,1024]{1,0:T(1,128)}, f32[1,1024]{1,0:T(1,128)}, f32[1,1024]{1,0:T(1,128)}, f32[1,1024]{1,0:T(1,128)}) custom-call(s32[592]{0:T(1024)} %constant.10.clone.table, f32[16,1024]{1,0:T(8,128)} %get-tuple-element.25.best, f32[1,1024]{1,0:T(1,128)} %copy-done.4, f32[1,1024]{1,0:T(1,128)} %copy-done.5, ...), custom_call_target="tpu_custom_call" | custom-call | flops 8589934592 | bytes 10485760 | tf_op jit(solution)/shard_map/scored/pallas_call | solution.py:365
  87.6 13.8 %collective-permute-start.10 = (f32[1,1024]{1,0:T(1,128)}, f32[1,1024]{1,0:T(1,128)S(1)}, u32[]{:S(2)}, u32[]{:S(2)}) collective-permute-start(f32[1,1024]{1,0:T(1,128)} %get-tuple-element.33), channel_id=1, source_target_pairs={{0,4},{1,5},{3,7},{4,12},{5,2},{6,1},{7,15},{8,9},{9,0},{10,8},{11... | collective-permute-start | bytes 12296 | tf_op jit(solution)/shard_map/ppermute | solution.py:447
  101.4 3.4 %collective-permute-start.11 = (f32[1,1024]{1,0:T(1,128)}, f32[1,1024]{1,0:T(1,128)S(1)}, u32[]{:S(2)}, u32[]{:S(2)}) collective-permute-start(f32[1,1024]{1,0:T(1,128)} %get-tuple-element.34), channel_id=1, source_target_pairs={{0,1},{2,6},{3,2},{4,7},{5,13},{6,14},{7,4},{8,5},{9,11},{10,3},{1... | collective-permute-start | bytes 12296 | tf_op jit(solution)/shard_map/ppermute | solution.py:447
  104.9 1.3 %collective-permute-start.13 = (f32[1,1024]{1,0:T(1,128)}, f32[1,1024]{1,0:T(1,128)S(1)}, u32[]{:S(2)}, u32[]{:S(2)}) collective-permute-start(f32[1,1024]{1,0:T(1,128)} %get-tuple-element.36), channel_id=1, source_target_pairs={{2,3},{4,1},{5,12},{6,15},{7,2},{8,11},{9,8},{10,9},{11,10},{13,0}... | collective-permute-start | bytes 12296 | tf_op jit(solution)/shard_map/ppermute | solution.py:447
  106.3 2.5 %collective-permute-done.12.refs_2_ = f32[1,1024]{1,0:T(1,128)S(1)} collective-permute-done((f32[1,1024]{1,0:T(1,128)}, f32[1,1024]{1,0:T(1,128)S(1)}, u32[]{:S(2)}, u32[]{:S(2)}) %collective-permute-start.12) | collective-permute-done | bytes 4128 | tf_op jit(solution)/shard_map/ppermute | solution.py:447
  108.7 3.1 %collective-permute-done.13.refs_3_ = f32[1,1024]{1,0:T(1,128)S(1)} collective-permute-done((f32[1,1024]{1,0:T(1,128)}, f32[1,1024]{1,0:T(1,128)S(1)}, u32[]{:S(2)}, u32[]{:S(2)}) %collective-permute-start.13) | collective-permute-done | bytes 4128 | tf_op jit(solution)/shard_map/ppermute | solution.py:447
  111.9 0.6 copy-done.3
  112.5 2.2 %placed.1 = f32[1,1024]{1,0:T(1,128)} custom-call(s32[64]{0:T(128)} %constant.11.clone.taken, s32[16]{0:T(128)} %pads.5, s32[1,1024]{1,0:T(1,128)} %bitcast.4, f32[16,1024]{1,0:T(8,128)} %get-tuple-element.32.best, f32[1,1024]{1,0:T(1,128)} %copy-done, f32[1,1024]{1,0:T(1,128)} %copy-done.1, f32[1,1024]{1,0:T(1,128)} %copy-done.2, f32[1,1024]{1,0:T(1,128)} %copy-done.3), custom_call_target="tpu_custom_call" | custom-call | tf_op jit(solution)/shard_map/placed/pallas_call | solution.py:409
  (22 shorter events, 0.7 us)
Async XLA Ops:
  4.2 13.9 %collective-permute-start.2 = (bf16[1024,1024]{1,0:T(8,128)(2,1)}, bf16[1024,1024]{1,0:T(8,128)(2,1)}, u32[]{:S(2)}, u32[]{:S(2)}) collective-permute-start(bf16[1024,1024]{1,0:T(8,128)(2,1)} %normalized.1.unit.refs_1_.refs_4_.refs_10_), channel_id=1, source_target_pairs={{0,1},{1,0},{4,5},{5,4},{8,9},{9,8},{12,13},{13,12},{3,2},{2,3},{7... | collective-permute-start | bytes 6291464 | tf_op jit(solution)/shard_map/ppermute | solution.py:441
  4.7 50.4 %collective-permute-start.1 = (bf16[1024,1024]{1,0:T(8,128)(2,1)}, bf16[1024,1024]{1,0:T(8,128)(2,1)}, u32[]{:S(2)}, u32[]{:S(2)}) collective-permute-start(bf16[1024,1024]{1,0:T(8,128)(2,1)} %normalized.1.unit.refs_1_.refs_4_.refs_10_), channel_id=1, source_target_pairs={{0,9},{8,13},{12,4},{4,0},{1,5},{3,10},{11,14},{15,7},{7,3},{2,6},... | collective-permute-start | bytes 6291464 | tf_op jit(solution)/shard_map/ppermute | solution.py:441
  10.3 48.8 %collective-permute-start.3 = (bf16[1024,1024]{1,0:T(8,128)(2,1)}, bf16[1024,1024]{1,0:T(8,128)(2,1)}, u32[]{:S(2)}, u32[]{:S(2)}) collective-permute-start(bf16[1024,1024]{1,0:T(8,128)(2,1)} %normalized.1.unit.refs_1_.refs_4_.refs_10_), channel_id=1, source_target_pairs={{13,5},{5,1},{9,12},{4,9},{14,6},{6,2},{10,15},{7,10},{29,21},{21,... | collective-permute-start | bytes 6291464 | tf_op jit(solution)/shard_map/ppermute | solution.py:441
  12.4 48.2 %collective-permute-start = (bf16[1024,1024]{1,0:T(8,128)(2,1)}, bf16[1024,1024]{1,0:T(8,128)(2,1)}, u32[]{:S(2)}, u32[]{:S(2)}) collective-permute-start(bf16[1024,1024]{1,0:T(8,128)(2,1)} %normalized.1.unit.refs_1_.refs_4_.refs_10_), channel_id=1, source_target_pairs={{0,3},{3,0},{1,2},{2,1},{8,11},{11,8},{9,10},{10,9},{12,15},{15,12... | collective-permute-start | bytes 6291464 | tf_op jit(solution)/shard_map/ppermute | solution.py:441
  55.1 23.3 %collective-permute-start.7 = (bf16[1024,1024]{1,0:T(8,128)(2,1)}, bf16[1024,1024]{1,0:T(8,128)(2,1)}, u32[]{:S(2)}, u32[]{:S(2)}) collective-permute-start(bf16[1024,1024]{1,0:T(8,128)(2,1)} %normalized.1.unit.refs_1_.refs_4_.refs_10_), channel_id=1, source_target_pairs={{5,8},{8,5},{6,11},{11,6},{21,24},{24,21},{22,27},{27,22}} | collective-permute-start | bytes 6291464 | tf_op jit(solution)/shard_map/ppermute | solution.py:441
  57.1 21.3 %collective-permute-start.8 = (bf16[1024,1024]{1,0:T(8,128)(2,1)}, bf16[1024,1024]{1,0:T(8,128)(2,1)}, u32[]{:S(2)}, u32[]{:S(2)}) collective-permute-start(bf16[1024,1024]{1,0:T(8,128)(2,1)} %collective-permute-done.1.refs_1_.refs_4_), channel_id=1, source_target_pairs={{9,13},{10,15},{5,6},{6,5},{25,29},{26,31},{21,22},{22,21}} | collective-permute-start | bytes 6291464 | tf_op jit(solution)/shard_map/ppermute | solution.py:441
  71.7 6.8 %collective-permute-start.6 = (bf16[1024,1024]{1,0:T(8,128)(2,1)}, bf16[1024,1024]{1,0:T(8,128)(2,1)}, u32[]{:S(2)}, u32[]{:S(2)}) collective-permute-start(bf16[1024,1024]{1,0:T(8,128)(2,1)} %collective-permute-done.refs_3_.refs_9_), channel_id=1, source_target_pairs={{0,1},{1,0},{4,5},{5,4},{8,9},{9,8},{12,13},{13,12},{3,2},{2,3},{7... | collective-permute-start | bytes 6291464 | tf_op jit(solution)/shard_map/ppermute | solution.py:441
  71.7 6.7 %collective-permute-start.9 = (bf16[1024,1024]{1,0:T(8,128)(2,1)}, bf16[1024,1024]{1,0:T(8,128)(2,1)}, u32[]{:S(2)}, u32[]{:S(2)}) collective-permute-start(bf16[1024,1024]{1,0:T(8,128)(2,1)} %collective-permute-done.1.refs_1_.refs_4_), channel_id=1, source_target_pairs={{4,5},{5,4},{7,6},{6,7},{20,21},{21,20},{23,22},{22,23}} | collective-permute-start | bytes 6291464 | tf_op jit(solution)/shard_map/ppermute | solution.py:441
  73.7 4.0 %collective-permute-start.4 = (f32[1,1024]{1,0:T(1,128)}, f32[1,1024]{1,0:T(1,128)S(1)}, u32[]{:S(2)}, u32[]{:S(2)}) collective-permute-start(f32[1,1024]{1,0:T(1,128)} %get-tuple-element.26), channel_id=1, source_target_pairs={{0,3},{1,0},{4,5},{5,1},{6,2},{7,6},{9,10},{10,11},{12,15},{13,8},... | collective-permute-start | bytes 12296 | tf_op jit(solution)/shard_map/ppermute | solution.py:447
  77.7 0.7 copy-start.4
  77.7 0.7 collective-permute-start.5
  78.4 0.6 copy-start.5
  87.6 18.6 %collective-permute-start.10 = (f32[1,1024]{1,0:T(1,128)}, f32[1,1024]{1,0:T(1,128)S(1)}, u32[]{:S(2)}, u32[]{:S(2)}) collective-permute-start(f32[1,1024]{1,0:T(1,128)} %get-tuple-element.33), channel_id=1, source_target_pairs={{0,4},{1,5},{3,7},{4,12},{5,2},{6,1},{7,15},{8,9},{9,0},{10,8},{11... | collective-permute-start | bytes 12296 | tf_op jit(solution)/shard_map/ppermute | solution.py:447
  101.4 4.8 %collective-permute-start.11 = (f32[1,1024]{1,0:T(1,128)}, f32[1,1024]{1,0:T(1,128)S(1)}, u32[]{:S(2)}, u32[]{:S(2)}) collective-permute-start(f32[1,1024]{1,0:T(1,128)} %get-tuple-element.34), channel_id=1, source_target_pairs={{0,1},{2,6},{3,2},{4,7},{5,13},{6,14},{7,4},{8,5},{9,11},{10,3},{1... | collective-permute-start | bytes 12296 | tf_op jit(solution)/shard_map/ppermute | solution.py:447
  104.9 3.9 %collective-permute-start.12 = (f32[1,1024]{1,0:T(1,128)}, f32[1,1024]{1,0:T(1,128)S(1)}, u32[]{:S(2)}, u32[]{:S(2)}) collective-permute-start(f32[1,1024]{1,0:T(1,128)} %get-tuple-element.35), channel_id=1, source_target_pairs={{0,2},{1,3},{2,0},{3,1},{4,6},{5,8},{6,11},{7,5},{8,10},{9,4},{10,... | collective-permute-start | bytes 12296 | tf_op jit(solution)/shard_map/ppermute | solution.py:447
  104.9 6.9 %collective-permute-start.13 = (f32[1,1024]{1,0:T(1,128)}, f32[1,1024]{1,0:T(1,128)S(1)}, u32[]{:S(2)}, u32[]{:S(2)}) collective-permute-start(f32[1,1024]{1,0:T(1,128)} %get-tuple-element.36), channel_id=1, source_target_pairs={{2,3},{4,1},{5,12},{6,15},{7,2},{8,11},{9,8},{10,9},{11,10},{13,0}... | collective-permute-start | bytes 12296 | tf_op jit(solution)/shard_map/ppermute | solution.py:447
  106.2 5.6 %copy-start = (f32[1,1024]{1,0:T(1,128)}, f32[1,1024]{1,0:T(1,128)S(1)}, u32[]{:S(2)}) copy-start(f32[1,1024]{1,0:T(1,128)S(1)} %collective-permute-done.10.refs_0_) | copy-start | bytes 12292
  106.3 5.6 %copy-start.1 = (f32[1,1024]{1,0:T(1,128)}, f32[1,1024]{1,0:T(1,128)S(1)}, u32[]{:S(2)}) copy-start(f32[1,1024]{1,0:T(1,128)S(1)} %collective-permute-done.11.refs_1_) | copy-start | bytes 12292
  108.7 3.1 %copy-start.2 = (f32[1,1024]{1,0:T(1,128)}, f32[1,1024]{1,0:T(1,128)S(1)}, u32[]{:S(2)}) copy-start(f32[1,1024]{1,0:T(1,128)S(1)} %collective-permute-done.12.refs_2_) | copy-start | bytes 12292
  111.9 0.6 copy-start.3

commit v12 on v10

--- a/solution.py
+++ b/solution.py
@@ -9,10 +9,10 @@
 from jax.sharding import PartitionSpec as P
 
 STEPS = 6
-VMEM = 62 * 2**20
+VMEM = 64 * 2**20 - 2**16
 FLOOR = -2.0
 MOST_PADS = 256
-AHEAD = 3
+AHEAD = 2
 
 
 class Move:
@@ -40,7 +40,7 @@
     second = [((3, 1), (1, 1)), ((1, 1), (0, 1)), ((2, 1), (3, 0)), ((1, 0), (2, 1))]
     return [
         Move("R1", "own", rows(first), 0, 1),
-        Move("R2", "own", rows(second), 0, 1, "best"),
+        Move("R2", "own", rows(second), 0, 1),
         Move("Y", "own", across([place for place in every if place[0] != 1]) + crossed, 0, 1),
         Move("A", "own", swap, 0, 0),
         Move("R3", "own", rows([((1, 1), (2, 0)), ((2, 0), (1, 1))]), 1, 2, "R1"),
@@ -106,15 +106,10 @@
 
 
 def colored(edges, count):
-    ends = [of for of, _ in edges], [to for _, to in edges]
-    most = max((side.count(device) for side in ends for device in range(count)), default=0)
     sends, takes = [{} for _ in range(count)], [{} for _ in range(count)]
-    for of, to in sorted(edges, key=lambda edge: (edge[0] ^ edge[1], edge)):
+    for of, to in edges:
         a = next(c for c in range(len(edges)) if c not in sends[of])
         b = next(c for c in range(len(edges)) if c not in takes[to])
-        both = next(c for c in range(2 * len(edges)) if c not in sends[of] and c not in takes[to])
-        if both < most:
-            a = b = both
         path, node, tables, colour = [], to, (takes, sends), a
         while a != b and colour in tables[0][node]:
             end = tables[0][node][colour]
@@ -205,7 +200,7 @@
 
 def normalized(embeddings, order, pad_counts):
     rows, depth = embeddings.shape
-    chunks = 8
+    chunks = 4
     anywhere = pl.BlockSpec(memory_space=pl.ANY)
     return pl.pallas_call(
         unit_kernel,
@@ -417,23 +412,23 @@
     permutes, found = [], []
     for stage, pairs in enumerate(work):
         starting = [move for move in moves if move.begins == stage]
-        for needs in sorted({move.needs for move in starting}, key=lambda needs: ("best" in needs, needs)):
-            if stage == 0 and "best" in needs:
-                best = own_block(unit, order, pad_counts, nblocks)
-            values = [slots[name] for name in needs if name != "best"]
+        for needs in sorted({move.needs for move in starting}):
+            values = [slots[name] for name in needs]
             if best is not None:
                 *values, best = lax.optimization_barrier((*values, best))
             for move in starting:
                 if move.needs == needs:
                     value = values[needs.index(move.source)]
                     slots[move.name] = lax.ppermute(value, "blk", move.pairs)
-        if best is None:
+        if stage == 0:
             best = own_block(unit, order, pad_counts, nblocks)
         sends = colored(sorted(edges[stage]), nblocks) if stage in sending else []
         if any(pairs):
-            best, *rows = scored(best, found, permutes, slots, rank, pairs, sends)
-            found = [lax.ppermute(row, "blk", permute) for row, permute in zip(rows, sends)]
-            permutes = sends
+            if found:
+                *found, best = lax.optimization_barrier((*found, best))
+            best, *rows = scored(best, [], [], slots, rank, pairs, sends)
+            found += [lax.ppermute(row, "blk", permute) for row, permute in zip(rows, sends)]
+            permutes += sends
     return placed(best, found, permutes, order, pad_counts)
 
 

time: 120 us -> 134 us (1.12)
  starting transfers between devices: 36.7 us -> 55.4 us
  waiting for transfers between devices: 48.6 us -> 45.7 us
    ppermute x6, starting transfers between devices: 21.3 us -> 40.1 us  [local(): lax.ppermute(row, 'blk', permute)]
    ppermute x8, waiting for transfers between devices: 41.5 us -> 38.5 us  [local(): slots[move.name] = lax.ppermute(value, 'blk', move.pairs)]
  transfers between devices with their start and end apart: 14 -> 14, of which waited for: 5 -> 5; matrix products, arithmetic and copies ran while one was open for 0% -> 0% of each run, Pallas kernels for 15% -> 5%
where the time goes in v12:
time: 134 us
  starting transfers between devices  55.4 us (41%)
  waiting for transfers between devices  45.7 us (34%)
  Pallas kernels  32.4 us (24%)
    ppermute x6, starting transfers between devices, local(): lax.ppermute(row, 'blk', permute)  40.1 us
    ppermute x8, waiting for transfers between devices, local(): slots[move.name] = lax.ppermute(value, 'blk', move.pairs)  38.5 us
    pallas_call x3, Pallas kernels, scored(): pl.pallas_call(functools.partial(pairs_kernel, len(given), len(sends), le...  21.3 us
    ppermute x8, starting transfers between devices, local(): slots[move.name] = lax.ppermute(value, 'blk', move.pairs)  15.4 us
    ppermute x6, waiting for transfers between devices, local(): lax.ppermute(row, 'blk', permute)  7.24 us
    pallas_call x1, Pallas kernels, own_block(): pl.pallas_call(own_kernel, out_shape=jax.ShapeDtypeStruct((nblocks, rows)...  4.63 us
    pallas_call x1, Pallas kernels, normalized(): pl.pallas_call(unit_kernel, out_shape=jax.ShapeDtypeStruct((rows, depth),...  4.29 us
  transfers between devices with their start and end apart: 14, of which 5 were waited for; matrix products, arithmetic and copies ran while one was open for 0% of the time, Pallas kernels for 5%

profile of v12, /device:TPU:0, one launch (start us, length us, event | category | flops | bytes accessed | tf_op | source)
XLA Modules:
  0.0 133.7 jit_solution(10682840291777506566)
XLA Ops:
  0.0 4.3 %normalized.1.unit.refs_1_.refs_4_.refs_8_ = bf16[1024,1024]{1,0:T(8,128)(2,1)} custom-call(s32[16]{0:T(128)} %pads.5, s32[1,1024]{1,0:T(1,128)} %bitcast.2, bf16[1024,1024]{1,0:T(8,128)(2,1)} %embeddings.1), custom_call_target="tpu_custom_call" | custom-call | flops 4194304 | bytes 4194304 | tf_op jit(solution)/shard_map/normalized/pallas_call | solution.py:205
  4.3 0.5 collective-permute-start.1
  4.8 5.6 %collective-permute-start = (bf16[1024,1024]{1,0:T(8,128)(2,1)}, bf16[1024,1024]{1,0:T(8,128)(2,1)}, u32[]{:S(2)}, u32[]{:S(2)}) collective-permute-start(bf16[1024,1024]{1,0:T(8,128)(2,1)} %normalized.1.unit.refs_1_.refs_4_.refs_8_), channel_id=1, source_target_pairs={{0,9},{8,13},{12,4},{4,0},{1,5},{3,10},{11,14},{15,7},{7,3},{2,6},... | collective-permute-start | bytes 6291464 | tf_op jit(solution)/shard_map/ppermute | solution.py:422
  10.4 1.2 collective-permute-start.3
  11.6 2.0 %collective-permute-start.2 = (bf16[1024,1024]{1,0:T(8,128)(2,1)}, bf16[1024,1024]{1,0:T(8,128)(2,1)}, u32[]{:S(2)}, u32[]{:S(2)}) collective-permute-start(bf16[1024,1024]{1,0:T(8,128)(2,1)} %normalized.1.unit.refs_1_.refs_4_.refs_8_), channel_id=1, source_target_pairs={{13,5},{5,1},{9,12},{4,9},{14,6},{6,2},{10,15},{7,10},{29,21},{21,... | collective-permute-start | bytes 6291464 | tf_op jit(solution)/shard_map/ppermute | solution.py:422
  13.6 4.6 %own_block.1.best = f32[16,1024]{1,0:T(8,128)} custom-call(s32[16]{0:T(128)} %pads.5, s32[1,1024]{1,0:T(1,128)} %bitcast.3, bf16[1024,1024]{1,0:T(8,128)(2,1)} %normalized.1.unit.refs_1_.refs_4_.refs_8_), custom_call_target="tpu_custom_call" | custom-call | flops 2147483648 | bytes 2097152 | tf_op jit(solution)/shard_map/own_block/pallas_call | solution.py:249
  18.3 1.5 %scored.3.best = f32[16,1024]{1,0:T(8,128)} custom-call(s32[144]{0:T(256)} %constant.8.clone.table, f32[16,1024]{1,0:T(8,128)} %own_block.1.best, bf16[1024,1024]{1,0:T(8,128)(2,1)} %collective-permute-done.1.refs_0_, bf16[1024,1024]{1,0:T(8,128)(2,1)} %normalized.1.unit.refs_1_.refs_4_.refs_8_), custom_call_target="tpu_custom_call" | custom-call | flops 2147483648 | bytes 4194304 | tf_op jit(solution)/shard_map/scored/pallas_call | solution.py:347
  19.8 35.4 %collective-permute-done.refs_1_.refs_2_ = bf16[1024,1024]{1,0:T(8,128)(2,1)} collective-permute-done((bf16[1024,1024]{1,0:T(8,128)(2,1)}, bf16[1024,1024]{1,0:T(8,128)(2,1)}, u32[]{:S(2)}, u32[]{:S(2)}) %collective-permute-start) | collective-permute-done | bytes 2097184 | tf_op jit(solution)/shard_map/ppermute | solution.py:422
  55.2 3.1 %collective-permute-done.3.refs_3_.refs_7_ = bf16[1024,1024]{1,0:T(8,128)(2,1)} collective-permute-done((bf16[1024,1024]{1,0:T(8,128)(2,1)}, bf16[1024,1024]{1,0:T(8,128)(2,1)}, u32[]{:S(2)}, u32[]{:S(2)}) %collective-permute-start.3) | collective-permute-done | bytes 2097184 | tf_op jit(solution)/shard_map/ppermute | solution.py:422
  58.3 11.1 %scored.4 = (f32[16,1024]{1,0:T(8,128)}, f32[1,1024]{1,0:T(1,128)}, f32[1,1024]{1,0:T(1,128)}) custom-call(s32[464]{0:T(512)} %constant.9.clone.table, f32[16,1024]{1,0:T(8,128)} %scored.3.best, bf16[1024,1024]{1,0:T(8,128)(2,1)} %collective-permute-done.1.refs_0_, bf16[1024,1024]{1,0:T(8,128)(2,1)} %collective-permute-done.refs_1_.refs_2_, ...), custom_call_target="tpu_custom_call" | custom-call | flops 8589934592 | bytes 10485760 | tf_op jit(solution)/shard_map/scored/pallas_call | solution.py:347
  69.4 0.1 collective-permute-start.6
  69.5 2.0 %collective-permute-start.9 = (bf16[1024,1024]{1,0:T(8,128)(2,1)}, bf16[1024,1024]{1,0:T(8,128)(2,1)}, u32[]{:S(2)}, u32[]{:S(2)}) collective-permute-start(bf16[1024,1024]{1,0:T(8,128)(2,1)} %collective-permute-done.refs_1_.refs_2_), channel_id=1, source_target_pairs={{4,5},{5,4},{7,6},{6,7},{20,21},{21,20},{23,22},{22,23}} | collective-permute-start | bytes 6291464 | tf_op jit(solution)/shard_map/ppermute | solution.py:422
  71.5 2.0 %collective-permute-start.7 = (bf16[1024,1024]{1,0:T(8,128)(2,1)}, bf16[1024,1024]{1,0:T(8,128)(2,1)}, u32[]{:S(2)}, u32[]{:S(2)}) collective-permute-start(bf16[1024,1024]{1,0:T(8,128)(2,1)} %normalized.1.unit.refs_1_.refs_4_.refs_8_), channel_id=1, source_target_pairs={{5,8},{8,5},{6,11},{11,6},{21,24},{24,21},{22,27},{27,22}} | collective-permute-start | bytes 6291464 | tf_op jit(solution)/shard_map/ppermute | solution.py:422
  73.5 2.0 %collective-permute-start.8 = (bf16[1024,1024]{1,0:T(8,128)(2,1)}, bf16[1024,1024]{1,0:T(8,128)(2,1)}, u32[]{:S(2)}, u32[]{:S(2)}) collective-permute-start(bf16[1024,1024]{1,0:T(8,128)(2,1)} %collective-permute-done.refs_1_.refs_2_), channel_id=1, source_target_pairs={{9,13},{10,15},{5,6},{6,5},{25,29},{26,31},{21,22},{22,21}} | collective-permute-start | bytes 6291464 | tf_op jit(solution)/shard_map/ppermute | solution.py:422
  75.4 4.1 %collective-permute-start.4 = (f32[1,1024]{1,0:T(1,128)}, f32[1,1024]{1,0:T(1,128)}, u32[]{:S(2)}, u32[]{:S(2)}) collective-permute-start(f32[1,1024]{1,0:T(1,128)} %get-tuple-element.26), channel_id=1, source_target_pairs={{0,3},{1,0},{4,5},{5,1},{6,2},{7,6},{9,10},{10,11},{12,15},{13,8},... | collective-permute-start | bytes 12296 | tf_op jit(solution)/shard_map/ppermute | solution.py:430
  79.5 1.5 %collective-permute-done.4.refs_0_ = f32[1,1024]{1,0:T(1,128)} collective-permute-done((f32[1,1024]{1,0:T(1,128)}, f32[1,1024]{1,0:T(1,128)}, u32[]{:S(2)}, u32[]{:S(2)}) %collective-permute-start.4) | collective-permute-done | bytes 4128 | tf_op jit(solution)/shard_map/ppermute | solution.py:430
  81.1 1.2 collective-permute-start.5
  82.3 8.7 %scored.5 = (f32[16,1024]{1,0:T(8,128)}, f32[1,1024]{1,0:T(1,128)}, f32[1,1024]{1,0:T(1,128)}, f32[1,1024]{1,0:T(1,128)}, f32[1,1024]{1,0:T(1,128)}) custom-call(s32[496]{0:T(512)} %constant.10.clone.table, f32[16,1024]{1,0:T(8,128)} %get-tuple-element.31.best, bf16[1024,1024]{1,0:T(8,128)(2,1)} %collective-permute-done.1.refs_0_, ...), custom_call_target="tpu_custom_call" | custom-call | flops 8589934592 | bytes 10485760 | tf_op jit(solution)/shard_map/scored/pallas_call | solution.py:347
  91.0 29.0 %collective-permute-start.10 = (f32[1,1024]{1,0:T(1,128)}, f32[1,1024]{1,0:T(1,128)}, u32[]{:S(2)}, u32[]{:S(2)}) collective-permute-start(f32[1,1024]{1,0:T(1,128)} %get-tuple-element.39), channel_id=1, source_target_pairs={{0,4},{1,5},{3,7},{4,12},{5,2},{6,1},{7,15},{8,9},{9,0},{10,8},{11... | collective-permute-start | bytes 12296 | tf_op jit(solution)/shard_map/ppermute | solution.py:430
  120.0 4.5 %collective-permute-start.11 = (f32[1,1024]{1,0:T(1,128)}, f32[1,1024]{1,0:T(1,128)}, u32[]{:S(2)}, u32[]{:S(2)}) collective-permute-start(f32[1,1024]{1,0:T(1,128)} %get-tuple-element.40), channel_id=1, source_target_pairs={{0,1},{2,6},{3,2},{4,7},{5,13},{6,14},{7,4},{8,5},{9,11},{10,3},{1... | collective-permute-start | bytes 12296 | tf_op jit(solution)/shard_map/ppermute | solution.py:430
  124.5 1.3 collective-permute-start.13
  125.8 2.6 %collective-permute-done.12.refs_4_ = f32[1,1024]{1,0:T(1,128)} collective-permute-done((f32[1,1024]{1,0:T(1,128)}, f32[1,1024]{1,0:T(1,128)}, u32[]{:S(2)}, u32[]{:S(2)}) %collective-permute-start.12) | collective-permute-done | bytes 4128 | tf_op jit(solution)/shard_map/ppermute | solution.py:430
  128.4 3.1 %collective-permute-done.13.refs_5_ = f32[1,1024]{1,0:T(1,128)} collective-permute-done((f32[1,1024]{1,0:T(1,128)}, f32[1,1024]{1,0:T(1,128)}, u32[]{:S(2)}, u32[]{:S(2)}) %collective-permute-start.13) | collective-permute-done | bytes 4128 | tf_op jit(solution)/shard_map/ppermute | solution.py:430
  131.5 2.2 %placed.1 = f32[1,1024]{1,0:T(1,128)} custom-call(s32[96]{0:T(128)} %constant.11.clone.taken, s32[16]{0:T(128)} %pads.5, s32[1,1024]{1,0:T(1,128)} %bitcast.4, f32[16,1024]{1,0:T(8,128)} %get-tuple-element.36.best, f32[1,1024]{1,0:T(1,128)} %collective-permute-done.4.refs_0_, f32[1,1024]{1,0:T(1,128)} %collective-permute-done.5.refs_1_, ...), custom_call_target="tpu_custom_call" | custom-call | tf_op jit(solution)/shard_map/placed/pallas_call | solution.py:390
  (10 shorter events, 0.0 us)
Async XLA Ops:
  4.3 14.0 %collective-permute-start.1 = (bf16[1024,1024]{1,0:T(8,128)(2,1)}, bf16[1024,1024]{1,0:T(8,128)(2,1)}, u32[]{:S(2)}, u32[]{:S(2)}) collective-permute-start(bf16[1024,1024]{1,0:T(8,128)(2,1)} %normalized.1.unit.refs_1_.refs_4_.refs_8_), channel_id=1, source_target_pairs={{0,1},{1,0},{4,5},{5,4},{8,9},{9,8},{12,13},{13,12},{3,2},{2,3},{7... | collective-permute-start | bytes 6291464 | tf_op jit(solution)/shard_map/ppermute | solution.py:422
  4.8 50.4 %collective-permute-start = (bf16[1024,1024]{1,0:T(8,128)(2,1)}, bf16[1024,1024]{1,0:T(8,128)(2,1)}, u32[]{:S(2)}, u32[]{:S(2)}) collective-permute-start(bf16[1024,1024]{1,0:T(8,128)(2,1)} %normalized.1.unit.refs_1_.refs_4_.refs_8_), channel_id=1, source_target_pairs={{0,9},{8,13},{12,4},{4,0},{1,5},{3,10},{11,14},{15,7},{7,3},{2,6},... | collective-permute-start | bytes 6291464 | tf_op jit(solution)/shard_map/ppermute | solution.py:422
  10.4 47.8 %collective-permute-start.3 = (bf16[1024,1024]{1,0:T(8,128)(2,1)}, bf16[1024,1024]{1,0:T(8,128)(2,1)}, u32[]{:S(2)}, u32[]{:S(2)}) collective-permute-start(bf16[1024,1024]{1,0:T(8,128)(2,1)} %normalized.1.unit.refs_1_.refs_4_.refs_8_), channel_id=1, source_target_pairs={{0,3},{3,0},{1,2},{2,1},{8,11},{11,8},{9,10},{10,9},{12,15},{15,12... | collective-permute-start | bytes 6291464 | tf_op jit(solution)/shard_map/ppermute | solution.py:422
  11.6 46.6 %collective-permute-start.2 = (bf16[1024,1024]{1,0:T(8,128)(2,1)}, bf16[1024,1024]{1,0:T(8,128)(2,1)}, u32[]{:S(2)}, u32[]{:S(2)}) collective-permute-start(bf16[1024,1024]{1,0:T(8,128)(2,1)} %normalized.1.unit.refs_1_.refs_4_.refs_8_), channel_id=1, source_target_pairs={{13,5},{5,1},{9,12},{4,9},{14,6},{6,2},{10,15},{7,10},{29,21},{21,... | collective-permute-start | bytes 6291464 | tf_op jit(solution)/shard_map/ppermute | solution.py:422
  69.4 12.9 %collective-permute-start.6 = (bf16[1024,1024]{1,0:T(8,128)(2,1)}, bf16[1024,1024]{1,0:T(8,128)(2,1)}, u32[]{:S(2)}, u32[]{:S(2)}) collective-permute-start(bf16[1024,1024]{1,0:T(8,128)(2,1)} %collective-permute-done.3.refs_3_.refs_7_), channel_id=1, source_target_pairs={{0,1},{1,0},{4,5},{5,4},{8,9},{9,8},{12,13},{13,12},{3,2},{2,3},{7... | collective-permute-start | bytes 6291464 | tf_op jit(solution)/shard_map/ppermute | solution.py:422
  69.5 12.8 %collective-permute-start.9 = (bf16[1024,1024]{1,0:T(8,128)(2,1)}, bf16[1024,1024]{1,0:T(8,128)(2,1)}, u32[]{:S(2)}, u32[]{:S(2)}) collective-permute-start(bf16[1024,1024]{1,0:T(8,128)(2,1)} %collective-permute-done.refs_1_.refs_2_), channel_id=1, source_target_pairs={{4,5},{5,4},{7,6},{6,7},{20,21},{21,20},{23,22},{22,23}} | collective-permute-start | bytes 6291464 | tf_op jit(solution)/shard_map/ppermute | solution.py:422
  71.5 10.8 %collective-permute-start.7 = (bf16[1024,1024]{1,0:T(8,128)(2,1)}, bf16[1024,1024]{1,0:T(8,128)(2,1)}, u32[]{:S(2)}, u32[]{:S(2)}) collective-permute-start(bf16[1024,1024]{1,0:T(8,128)(2,1)} %normalized.1.unit.refs_1_.refs_4_.refs_8_), channel_id=1, source_target_pairs={{5,8},{8,5},{6,11},{11,6},{21,24},{24,21},{22,27},{27,22}} | collective-permute-start | bytes 6291464 | tf_op jit(solution)/shard_map/ppermute | solution.py:422
  73.5 8.8 %collective-permute-start.8 = (bf16[1024,1024]{1,0:T(8,128)(2,1)}, bf16[1024,1024]{1,0:T(8,128)(2,1)}, u32[]{:S(2)}, u32[]{:S(2)}) collective-permute-start(bf16[1024,1024]{1,0:T(8,128)(2,1)} %collective-permute-done.refs_1_.refs_2_), channel_id=1, source_target_pairs={{9,13},{10,15},{5,6},{6,5},{25,29},{26,31},{21,22},{22,21}} | collective-permute-start | bytes 6291464 | tf_op jit(solution)/shard_map/ppermute | solution.py:422
  75.4 5.6 %collective-permute-start.4 = (f32[1,1024]{1,0:T(1,128)}, f32[1,1024]{1,0:T(1,128)}, u32[]{:S(2)}, u32[]{:S(2)}) collective-permute-start(f32[1,1024]{1,0:T(1,128)} %get-tuple-element.26), channel_id=1, source_target_pairs={{0,3},{1,0},{4,5},{5,1},{6,2},{7,6},{9,10},{10,11},{12,15},{13,8},... | collective-permute-start | bytes 12296 | tf_op jit(solution)/shard_map/ppermute | solution.py:430
  81.1 1.2 collective-permute-start.5
  91.0 34.8 %collective-permute-start.10 = (f32[1,1024]{1,0:T(1,128)}, f32[1,1024]{1,0:T(1,128)}, u32[]{:S(2)}, u32[]{:S(2)}) collective-permute-start(f32[1,1024]{1,0:T(1,128)} %get-tuple-element.39), channel_id=1, source_target_pairs={{0,4},{1,5},{3,7},{4,12},{5,2},{6,1},{7,15},{8,9},{9,0},{10,8},{11... | collective-permute-start | bytes 12296 | tf_op jit(solution)/shard_map/ppermute | solution.py:430
  120.0 5.8 %collective-permute-start.11 = (f32[1,1024]{1,0:T(1,128)}, f32[1,1024]{1,0:T(1,128)}, u32[]{:S(2)}, u32[]{:S(2)}) collective-permute-start(f32[1,1024]{1,0:T(1,128)} %get-tuple-element.40), channel_id=1, source_target_pairs={{0,1},{2,6},{3,2},{4,7},{5,13},{6,14},{7,4},{8,5},{9,11},{10,3},{1... | collective-permute-start | bytes 12296 | tf_op jit(solution)/shard_map/ppermute | solution.py:430
  124.5 3.9 %collective-permute-start.12 = (f32[1,1024]{1,0:T(1,128)}, f32[1,1024]{1,0:T(1,128)}, u32[]{:S(2)}, u32[]{:S(2)}) collective-permute-start(f32[1,1024]{1,0:T(1,128)} %get-tuple-element.41), channel_id=1, source_target_pairs={{0,2},{1,3},{2,0},{3,1},{4,6},{5,8},{6,11},{7,5},{8,10},{9,4},{10,... | collective-permute-start | bytes 12296 | tf_op jit(solution)/shard_map/ppermute | solution.py:430
  124.5 7.0 %collective-permute-start.13 = (f32[1,1024]{1,0:T(1,128)}, f32[1,1024]{1,0:T(1,128)}, u32[]{:S(2)}, u32[]{:S(2)}) collective-permute-start(f32[1,1024]{1,0:T(1,128)} %get-tuple-element.42), channel_id=1, source_target_pairs={{2,3},{4,1},{5,12},{6,15},{7,2},{8,11},{9,8},{10,9},{11,10},{13,0}... | collective-permute-start | bytes 12296 | tf_op jit(solution)/shard_map/ppermute | solution.py:430

commit v13 on v9

--- a/solution.py
+++ b/solution.py
@@ -9,10 +9,10 @@
 from jax.sharding import PartitionSpec as P
 
 STEPS = 6
-VMEM = 62 * 2**20
+VMEM = 64 * 2**20 - 2**16
 FLOOR = -2.0
 MOST_PADS = 256
-AHEAD = 3
+AHEAD = 2
 
 
 class Move:

time: 115 us -> 115 us (level)
    ppermute x6, starting transfers between devices: 21 us -> 22.2 us  [local(): lax.ppermute(row, 'blk', permute)]
where the time goes in v13:
time: 115 us; the launch traced here: 114 us
  waiting for transfers between devices  44.2 us (38%)
  starting transfers between devices  37.5 us (33%)
  Pallas kernels  32.3 us (28%)
    ppermute x8, waiting for transfers between devices, local(): slots[move.name] = lax.ppermute(value, 'blk', move.pairs)  36.9 us
    ppermute x6, starting transfers between devices, local(): lax.ppermute(row, 'blk', permute)  22.2 us
    pallas_call x3, Pallas kernels, scored(): pl.pallas_call(functools.partial(pairs_kernel, len(given), len(sends), le...  21.3 us
    ppermute x8, starting transfers between devices, local(): slots[move.name] = lax.ppermute(value, 'blk', move.pairs)  15.3 us
    ppermute x6, waiting for transfers between devices, local(): lax.ppermute(row, 'blk', permute)  7.24 us
    pallas_call x1, Pallas kernels, own_block(): pl.pallas_call(own_kernel, out_shape=jax.ShapeDtypeStruct((nblocks, rows)...  4.64 us
    pallas_call x1, Pallas kernels, normalized(): pl.pallas_call(unit_kernel, out_shape=jax.ShapeDtypeStruct((rows, depth),...  4.13 us
  transfers between devices with their start and end apart: 14, of which 5 were waited for; matrix products, arithmetic and copies ran while one was open for 0% of the time, Pallas kernels for 15%

profile of v13, /device:TPU:0, one launch (start us, length us, event | category | flops | bytes accessed | tf_op | source)
XLA Modules:
  0.0 114.1 jit_solution(5017414109993938442)
XLA Ops:
  0.0 4.1 %normalized.1.unit.refs_1_.refs_4_.refs_10_ = bf16[1024,1024]{1,0:T(8,128)(2,1)} custom-call(s32[16]{0:T(128)} %pads.5, s32[1024]{0:T(1024)} %order_smem.1, s32[1,1024]{1,0:T(1,128)} %bitcast.2, bf16[1024,1024]{1,0:T(8,128)(2,1)} %embeddings.1), custom_call_target="tpu_custom_call" | custom-call | flops 4194304 | bytes 4194304 | tf_op jit(solution)/shard_map/normalized/pallas_call | solution.py:199
  4.1 0.5 collective-permute-start.2
  4.7 5.6 %collective-permute-start.1 = (bf16[1024,1024]{1,0:T(8,128)(2,1)}, bf16[1024,1024]{1,0:T(8,128)(2,1)}, u32[]{:S(2)}, u32[]{:S(2)}) collective-permute-start(bf16[1024,1024]{1,0:T(8,128)(2,1)} %normalized.1.unit.refs_1_.refs_4_.refs_10_), channel_id=1, source_target_pairs={{0,9},{8,13},{12,4},{4,0},{1,5},{3,10},{11,14},{15,7},{7,3},{2,6},... | collective-permute-start | bytes 6291464 | tf_op jit(solution)/shard_map/ppermute | solution.py:419
  10.3 2.0 %collective-permute-start.3 = (bf16[1024,1024]{1,0:T(8,128)(2,1)}, bf16[1024,1024]{1,0:T(8,128)(2,1)}, u32[]{:S(2)}, u32[]{:S(2)}) collective-permute-start(bf16[1024,1024]{1,0:T(8,128)(2,1)} %normalized.1.unit.refs_1_.refs_4_.refs_10_), channel_id=1, source_target_pairs={{13,5},{5,1},{9,12},{4,9},{14,6},{6,2},{10,15},{7,10},{29,21},{21,... | collective-permute-start | bytes 6291464 | tf_op jit(solution)/shard_map/ppermute | solution.py:419
  12.3 1.2 %collective-permute-start = (bf16[1024,1024]{1,0:T(8,128)(2,1)}, bf16[1024,1024]{1,0:T(8,128)(2,1)}, u32[]{:S(2)}, u32[]{:S(2)}) collective-permute-start(bf16[1024,1024]{1,0:T(8,128)(2,1)} %normalized.1.unit.refs_1_.refs_4_.refs_10_), channel_id=1, source_target_pairs={{0,3},{3,0},{1,2},{2,1},{8,11},{11,8},{9,10},{10,9},{12,15},{15,12... | collective-permute-start | bytes 6291464 | tf_op jit(solution)/shard_map/ppermute | solution.py:419
  13.4 4.6 %own_block.1.best = f32[16,1024]{1,0:T(8,128)} custom-call(s32[16]{0:T(128)} %pads.5, s32[1,1024]{1,0:T(1,128)} %bitcast.3, bf16[1024,1024]{1,0:T(8,128)(2,1)} %normalized.1.unit.refs_1_.refs_4_.refs_10_), custom_call_target="tpu_custom_call" | custom-call | flops 2147483648 | bytes 2097152 | tf_op jit(solution)/shard_map/own_block/pallas_call | solution.py:246
  18.1 1.5 %scored.3.best = f32[16,1024]{1,0:T(8,128)} custom-call(s32[144]{0:T(256)} %constant.8.clone.table, f32[16,1024]{1,0:T(8,128)} %own_block.1.best, bf16[1024,1024]{1,0:T(8,128)(2,1)} %collective-permute-done.2.refs_0_.refs_2_, bf16[1024,1024]{1,0:T(8,128)(2,1)} %normalized.1.unit.refs_1_.refs_4_.refs_10_), custom_call_target="tpu_custom_call" | custom-call | flops 2147483648 | bytes 4194304 | tf_op jit(solution)/shard_map/scored/pallas_call | solution.py:344
  19.6 35.4 %collective-permute-done.1.refs_1_.refs_4_ = bf16[1024,1024]{1,0:T(8,128)(2,1)} collective-permute-done((bf16[1024,1024]{1,0:T(8,128)(2,1)}, bf16[1024,1024]{1,0:T(8,128)(2,1)}, u32[]{:S(2)}, u32[]{:S(2)}) %collective-permute-start.1) | collective-permute-done | bytes 2097184 | tf_op jit(solution)/shard_map/ppermute | solution.py:419
  55.0 2.0 %collective-permute-start.7 = (bf16[1024,1024]{1,0:T(8,128)(2,1)}, bf16[1024,1024]{1,0:T(8,128)(2,1)}, u32[]{:S(2)}, u32[]{:S(2)}) collective-permute-start(bf16[1024,1024]{1,0:T(8,128)(2,1)} %normalized.1.unit.refs_1_.refs_4_.refs_10_), channel_id=1, source_target_pairs={{5,8},{8,5},{6,11},{11,6},{21,24},{24,21},{22,27},{27,22}} | collective-permute-start | bytes 6291464 | tf_op jit(solution)/shard_map/ppermute | solution.py:419
  57.0 2.0 %collective-permute-start.8 = (bf16[1024,1024]{1,0:T(8,128)(2,1)}, bf16[1024,1024]{1,0:T(8,128)(2,1)}, u32[]{:S(2)}, u32[]{:S(2)}) collective-permute-start(bf16[1024,1024]{1,0:T(8,128)(2,1)} %collective-permute-done.1.refs_1_.refs_4_), channel_id=1, source_target_pairs={{9,13},{10,15},{5,6},{6,5},{25,29},{26,31},{21,22},{22,21}} | collective-permute-start | bytes 6291464 | tf_op jit(solution)/shard_map/ppermute | solution.py:419
  59.0 1.5 %collective-permute-done.refs_3_.refs_9_ = bf16[1024,1024]{1,0:T(8,128)(2,1)} collective-permute-done((bf16[1024,1024]{1,0:T(8,128)(2,1)}, bf16[1024,1024]{1,0:T(8,128)(2,1)}, u32[]{:S(2)}, u32[]{:S(2)}) %collective-permute-start) | collective-permute-done | bytes 2097184 | tf_op jit(solution)/shard_map/ppermute | solution.py:419
  60.5 11.1 %scored.4 = (f32[16,1024]{1,0:T(8,128)}, f32[1,1024]{1,0:T(1,128)}, f32[1,1024]{1,0:T(1,128)}) custom-call(s32[464]{0:T(512)} %constant.9.clone.table, f32[16,1024]{1,0:T(8,128)} %scored.3.best, bf16[1024,1024]{1,0:T(8,128)(2,1)} %collective-permute-done.2.refs_0_.refs_2_, bf16[1024,1024]{1,0:T(8,128)(2,1)} %collective-permute-done.1.refs_1_.refs_4_, ...), custom_call_target="tpu_custom_call" | custom-call | flops 8589934592 | bytes 10485760 | tf_op jit(solution)/shard_map/scored/pallas_call | solution.py:344
  71.6 0.1 collective-permute-start.6
  71.7 2.0 %collective-permute-start.9 = (bf16[1024,1024]{1,0:T(8,128)(2,1)}, bf16[1024,1024]{1,0:T(8,128)(2,1)}, u32[]{:S(2)}, u32[]{:S(2)}) collective-permute-start(bf16[1024,1024]{1,0:T(8,128)(2,1)} %collective-permute-done.1.refs_1_.refs_4_), channel_id=1, source_target_pairs={{4,5},{5,4},{7,6},{6,7},{20,21},{21,20},{23,22},{22,23}} | collective-permute-start | bytes 6291464 | tf_op jit(solution)/shard_map/ppermute | solution.py:419
  73.7 2.6 %collective-permute-start.4 = (f32[1,1024]{1,0:T(1,128)}, f32[1,1024]{1,0:T(1,128)}, u32[]{:S(2)}, u32[]{:S(2)}) collective-permute-start(f32[1,1024]{1,0:T(1,128)} %get-tuple-element.26), channel_id=1, source_target_pairs={{0,3},{1,0},{4,5},{5,1},{6,2},{7,6},{9,10},{10,11},{12,15},{13,8},... | collective-permute-start | bytes 12296 | tf_op jit(solution)/shard_map/ppermute | solution.py:425
  76.3 1.5 %collective-permute-done.4.refs_0_ = f32[1,1024]{1,0:T(1,128)} collective-permute-done((f32[1,1024]{1,0:T(1,128)}, f32[1,1024]{1,0:T(1,128)}, u32[]{:S(2)}, u32[]{:S(2)}) %collective-permute-start.4) | collective-permute-done | bytes 4128 | tf_op jit(solution)/shard_map/ppermute | solution.py:425
  77.8 1.2 %collective-permute-start.5 = (f32[1,1024]{1,0:T(1,128)}, f32[1,1024]{1,0:T(1,128)}, u32[]{:S(2)}, u32[]{:S(2)}) collective-permute-start(f32[1,1024]{1,0:T(1,128)} %get-tuple-element.27), channel_id=1, source_target_pairs={{2,1},{5,7},{6,4},{18,17},{21,23},{22,20}} | collective-permute-start | bytes 12296 | tf_op jit(solution)/shard_map/ppermute | solution.py:425
  79.0 8.7 %scored.5 = (f32[16,1024]{1,0:T(8,128)}, f32[1,1024]{1,0:T(1,128)}, f32[1,1024]{1,0:T(1,128)}, f32[1,1024]{1,0:T(1,128)}, f32[1,1024]{1,0:T(1,128)}) custom-call(s32[528]{0:T(1024)} %constant.10.clone.table, f32[16,1024]{1,0:T(8,128)} %get-tuple-element.25.best, f32[1,1024]{1,0:T(1,128)} %collective-permute-done.4.refs_0_, ...), custom_call_target="tpu_custom_call" | custom-call | flops 8589934592 | bytes 10485760 | tf_op jit(solution)/shard_map/scored/pallas_call | solution.py:344
  87.7 12.7 %collective-permute-start.10 = (f32[1,1024]{1,0:T(1,128)}, f32[1,1024]{1,0:T(1,128)}, u32[]{:S(2)}, u32[]{:S(2)}) collective-permute-start(f32[1,1024]{1,0:T(1,128)} %get-tuple-element.33), channel_id=1, source_target_pairs={{0,4},{1,5},{3,7},{4,12},{5,2},{6,1},{7,15},{8,9},{9,0},{10,8},{11... | collective-permute-start | bytes 12296 | tf_op jit(solution)/shard_map/ppermute | solution.py:425
  100.4 4.5 %collective-permute-start.11 = (f32[1,1024]{1,0:T(1,128)}, f32[1,1024]{1,0:T(1,128)}, u32[]{:S(2)}, u32[]{:S(2)}) collective-permute-start(f32[1,1024]{1,0:T(1,128)} %get-tuple-element.34), channel_id=1, source_target_pairs={{0,1},{2,6},{3,2},{4,7},{5,13},{6,14},{7,4},{8,5},{9,11},{10,3},{1... | collective-permute-start | bytes 12296 | tf_op jit(solution)/shard_map/ppermute | solution.py:425
  104.8 1.3 %collective-permute-start.13 = (f32[1,1024]{1,0:T(1,128)}, f32[1,1024]{1,0:T(1,128)}, u32[]{:S(2)}, u32[]{:S(2)}) collective-permute-start(f32[1,1024]{1,0:T(1,128)} %get-tuple-element.36), channel_id=1, source_target_pairs={{2,3},{4,1},{5,12},{6,15},{7,2},{8,11},{9,8},{10,9},{11,10},{13,0}... | collective-permute-start | bytes 12296 | tf_op jit(solution)/shard_map/ppermute | solution.py:425
  106.2 2.6 %collective-permute-done.12.refs_2_ = f32[1,1024]{1,0:T(1,128)} collective-permute-done((f32[1,1024]{1,0:T(1,128)}, f32[1,1024]{1,0:T(1,128)}, u32[]{:S(2)}, u32[]{:S(2)}) %collective-permute-start.12) | collective-permute-done | bytes 4128 | tf_op jit(solution)/shard_map/ppermute | solution.py:425
  108.8 3.1 %collective-permute-done.13.refs_3_ = f32[1,1024]{1,0:T(1,128)} collective-permute-done((f32[1,1024]{1,0:T(1,128)}, f32[1,1024]{1,0:T(1,128)}, u32[]{:S(2)}, u32[]{:S(2)}) %collective-permute-start.13) | collective-permute-done | bytes 4128 | tf_op jit(solution)/shard_map/ppermute | solution.py:425
  111.9 2.2 %placed.1 = f32[1,1024]{1,0:T(1,128)} custom-call(s32[64]{0:T(128)} %constant.11.clone.taken, s32[16]{0:T(128)} %pads.5, s32[1,1024]{1,0:T(1,128)} %bitcast.4, f32[16,1024]{1,0:T(8,128)} %get-tuple-element.32.best, f32[1,1024]{1,0:T(1,128)} %collective-permute-done.10.refs_0_, f32[1,1024]{1,0:T(1,128)} %collective-permute-done.11.refs_1_, ...), custom_call_target="tpu_custom_call" | custom-call | tf_op jit(solution)/shard_map/placed/pallas_call | solution.py:387
  (10 shorter events, 0.0 us)
Async XLA Ops:
  4.1 13.9 %collective-permute-start.2 = (bf16[1024,1024]{1,0:T(8,128)(2,1)}, bf16[1024,1024]{1,0:T(8,128)(2,1)}, u32[]{:S(2)}, u32[]{:S(2)}) collective-permute-start(bf16[1024,1024]{1,0:T(8,128)(2,1)} %normalized.1.unit.refs_1_.refs_4_.refs_10_), channel_id=1, source_target_pairs={{0,1},{1,0},{4,5},{5,4},{8,9},{9,8},{12,13},{13,12},{3,2},{2,3},{7... | collective-permute-start | bytes 6291464 | tf_op jit(solution)/shard_map/ppermute | solution.py:419
  4.7 50.4 %collective-permute-start.1 = (bf16[1024,1024]{1,0:T(8,128)(2,1)}, bf16[1024,1024]{1,0:T(8,128)(2,1)}, u32[]{:S(2)}, u32[]{:S(2)}) collective-permute-start(bf16[1024,1024]{1,0:T(8,128)(2,1)} %normalized.1.unit.refs_1_.refs_4_.refs_10_), channel_id=1, source_target_pairs={{0,9},{8,13},{12,4},{4,0},{1,5},{3,10},{11,14},{15,7},{7,3},{2,6},... | collective-permute-start | bytes 6291464 | tf_op jit(solution)/shard_map/ppermute | solution.py:419
  10.3 48.8 %collective-permute-start.3 = (bf16[1024,1024]{1,0:T(8,128)(2,1)}, bf16[1024,1024]{1,0:T(8,128)(2,1)}, u32[]{:S(2)}, u32[]{:S(2)}) collective-permute-start(bf16[1024,1024]{1,0:T(8,128)(2,1)} %normalized.1.unit.refs_1_.refs_4_.refs_10_), channel_id=1, source_target_pairs={{13,5},{5,1},{9,12},{4,9},{14,6},{6,2},{10,15},{7,10},{29,21},{21,... | collective-permute-start | bytes 6291464 | tf_op jit(solution)/shard_map/ppermute | solution.py:419
  12.3 48.2 %collective-permute-start = (bf16[1024,1024]{1,0:T(8,128)(2,1)}, bf16[1024,1024]{1,0:T(8,128)(2,1)}, u32[]{:S(2)}, u32[]{:S(2)}) collective-permute-start(bf16[1024,1024]{1,0:T(8,128)(2,1)} %normalized.1.unit.refs_1_.refs_4_.refs_10_), channel_id=1, source_target_pairs={{0,3},{3,0},{1,2},{2,1},{8,11},{11,8},{9,10},{10,9},{12,15},{15,12... | collective-permute-start | bytes 6291464 | tf_op jit(solution)/shard_map/ppermute | solution.py:419
  55.0 24.0 %collective-permute-start.7 = (bf16[1024,1024]{1,0:T(8,128)(2,1)}, bf16[1024,1024]{1,0:T(8,128)(2,1)}, u32[]{:S(2)}, u32[]{:S(2)}) collective-permute-start(bf16[1024,1024]{1,0:T(8,128)(2,1)} %normalized.1.unit.refs_1_.refs_4_.refs_10_), channel_id=1, source_target_pairs={{5,8},{8,5},{6,11},{11,6},{21,24},{24,21},{22,27},{27,22}} | collective-permute-start | bytes 6291464 | tf_op jit(solution)/shard_map/ppermute | solution.py:419
  57.0 22.0 %collective-permute-start.8 = (bf16[1024,1024]{1,0:T(8,128)(2,1)}, bf16[1024,1024]{1,0:T(8,128)(2,1)}, u32[]{:S(2)}, u32[]{:S(2)}) collective-permute-start(bf16[1024,1024]{1,0:T(8,128)(2,1)} %collective-permute-done.1.refs_1_.refs_4_), channel_id=1, source_target_pairs={{9,13},{10,15},{5,6},{6,5},{25,29},{26,31},{21,22},{22,21}} | collective-permute-start | bytes 6291464 | tf_op jit(solution)/shard_map/ppermute | solution.py:419
  71.6 7.4 %collective-permute-start.6 = (bf16[1024,1024]{1,0:T(8,128)(2,1)}, bf16[1024,1024]{1,0:T(8,128)(2,1)}, u32[]{:S(2)}, u32[]{:S(2)}) collective-permute-start(bf16[1024,1024]{1,0:T(8,128)(2,1)} %collective-permute-done.refs_3_.refs_9_), channel_id=1, source_target_pairs={{0,1},{1,0},{4,5},{5,4},{8,9},{9,8},{12,13},{13,12},{3,2},{2,3},{7... | collective-permute-start | bytes 6291464 | tf_op jit(solution)/shard_map/ppermute | solution.py:419
  71.7 7.4 %collective-permute-start.9 = (bf16[1024,1024]{1,0:T(8,128)(2,1)}, bf16[1024,1024]{1,0:T(8,128)(2,1)}, u32[]{:S(2)}, u32[]{:S(2)}) collective-permute-start(bf16[1024,1024]{1,0:T(8,128)(2,1)} %collective-permute-done.1.refs_1_.refs_4_), channel_id=1, source_target_pairs={{4,5},{5,4},{7,6},{6,7},{20,21},{21,20},{23,22},{22,23}} | collective-permute-start | bytes 6291464 | tf_op jit(solution)/shard_map/ppermute | solution.py:419
  73.7 4.1 %collective-permute-start.4 = (f32[1,1024]{1,0:T(1,128)}, f32[1,1024]{1,0:T(1,128)}, u32[]{:S(2)}, u32[]{:S(2)}) collective-permute-start(f32[1,1024]{1,0:T(1,128)} %get-tuple-element.26), channel_id=1, source_target_pairs={{0,3},{1,0},{4,5},{5,1},{6,2},{7,6},{9,10},{10,11},{12,15},{13,8},... | collective-permute-start | bytes 12296 | tf_op jit(solution)/shard_map/ppermute | solution.py:425
  77.8 1.2 %collective-permute-start.5 = (f32[1,1024]{1,0:T(1,128)}, f32[1,1024]{1,0:T(1,128)}, u32[]{:S(2)}, u32[]{:S(2)}) collective-permute-start(f32[1,1024]{1,0:T(1,128)} %get-tuple-element.27), channel_id=1, source_target_pairs={{2,1},{5,7},{6,4},{18,17},{21,23},{22,20}} | collective-permute-start | bytes 12296 | tf_op jit(solution)/shard_map/ppermute | solution.py:425
  87.7 18.4 %collective-permute-start.10 = (f32[1,1024]{1,0:T(1,128)}, f32[1,1024]{1,0:T(1,128)}, u32[]{:S(2)}, u32[]{:S(2)}) collective-permute-start(f32[1,1024]{1,0:T(1,128)} %get-tuple-element.33), channel_id=1, source_target_pairs={{0,4},{1,5},{3,7},{4,12},{5,2},{6,1},{7,15},{8,9},{9,0},{10,8},{11... | collective-permute-start | bytes 12296 | tf_op jit(solution)/shard_map/ppermute | solution.py:425
  100.4 5.8 %collective-permute-start.11 = (f32[1,1024]{1,0:T(1,128)}, f32[1,1024]{1,0:T(1,128)}, u32[]{:S(2)}, u32[]{:S(2)}) collective-permute-start(f32[1,1024]{1,0:T(1,128)} %get-tuple-element.34), channel_id=1, source_target_pairs={{0,1},{2,6},{3,2},{4,7},{5,13},{6,14},{7,4},{8,5},{9,11},{10,3},{1... | collective-permute-start | bytes 12296 | tf_op jit(solution)/shard_map/ppermute | solution.py:425
  104.8 3.9 %collective-permute-start.12 = (f32[1,1024]{1,0:T(1,128)}, f32[1,1024]{1,0:T(1,128)}, u32[]{:S(2)}, u32[]{:S(2)}) collective-permute-start(f32[1,1024]{1,0:T(1,128)} %get-tuple-element.35), channel_id=1, source_target_pairs={{0,2},{1,3},{2,0},{3,1},{4,6},{5,8},{6,11},{7,5},{8,10},{9,4},{10,... | collective-permute-start | bytes 12296 | tf_op jit(solution)/shard_map/ppermute | solution.py:425
  104.8 7.0 %collective-permute-start.13 = (f32[1,1024]{1,0:T(1,128)}, f32[1,1024]{1,0:T(1,128)}, u32[]{:S(2)}, u32[]{:S(2)}) collective-permute-start(f32[1,1024]{1,0:T(1,128)} %get-tuple-element.36), channel_id=1, source_target_pairs={{2,3},{4,1},{5,12},{6,15},{7,2},{8,11},{9,8},{10,9},{11,10},{13,0}... | collective-permute-start | bytes 12296 | tf_op jit(solution)/shard_map/ppermute | solution.py:425

commit v14 on v13

--- a/solution.py
+++ b/solution.py
@@ -13,6 +13,7 @@
 FLOOR = -2.0
 MOST_PADS = 256
 AHEAD = 2
+FIRST, EARLY = 4, 3
 
 
 class Move:
@@ -106,10 +107,15 @@
 
 
 def colored(edges, count):
+    ends = [of for of, _ in edges], [to for _, to in edges]
+    most = max((side.count(device) for side in ends for device in range(count)), default=0)
     sends, takes = [{} for _ in range(count)], [{} for _ in range(count)]
-    for of, to in edges:
+    for of, to in sorted(edges, key=lambda edge: (min(edge) >= FIRST, edge)):
+        both = next(c for c in range(2 * len(edges)) if c not in sends[of] and c not in takes[to])
         a = next(c for c in range(len(edges)) if c not in sends[of])
         b = next(c for c in range(len(edges)) if c not in takes[to])
+        if both < most:
+            a = b = both
         path, node, tables, colour = [], to, (takes, sends), a
         while a != b and colour in tables[0][node]:
             end = tables[0][node][colour]
@@ -139,14 +145,14 @@
         busy, taken = degrees(early), degrees(late)
         top = max(busy[0] + busy[1])
         free = [
-            (max(busy[0][of], busy[1][to]), busy[0][of] + busy[1][to], of, to)
+            (min(of, to) >= FIRST, max(busy[0][of], busy[1][to]), busy[0][of] + busy[1][to], of, to)
             for of, to in sorted(early)
             if max(taken[0][of], taken[1][to]) < most and max(busy[0][of], busy[1][to]) == top
         ]
-        if not free:
+        if not free or top <= EARLY:
             break
-        early.remove(max(free)[2:])
-        late.add(max(free)[2:])
+        early.remove(max(free)[3:])
+        late.add(max(free)[3:])
     return sorted(early), sorted(late)
 
 

time: 115 us -> 116 us (level)
    ppermute x6 -> x7, starting transfers between devices: 22.2 us -> 23.1 us  [local(): lax.ppermute(row, 'blk', permute)]
    ppermute x6 -> x7, waiting for transfers between devices: 7.24 us -> 6.41 us  [local(): lax.ppermute(row, 'blk', permute)]
  transfers between devices with their start and end apart: 14 -> 15, of which waited for: 5 -> 5; matrix products, arithmetic and copies ran while one was open for 0% -> 0% of each run, Pallas kernels for 15% -> 15%
where the time goes in v14:
time: 116 us; the launch traced here: 114 us
  waiting for transfers between devices  43.3 us (37%)
  starting transfers between devices  38.5 us (33%)
  Pallas kernels  32.3 us (28%)
    ppermute x8, waiting for transfers between devices, local(): slots[move.name] = lax.ppermute(value, 'blk', move.pairs)  36.9 us
    ppermute x7, starting transfers between devices, local(): lax.ppermute(row, 'blk', permute)  23.1 us
    pallas_call x3, Pallas kernels, scored(): pl.pallas_call(functools.partial(pairs_kernel, len(given), len(sends), le...  21.3 us
    ppermute x8, starting transfers between devices, local(): slots[move.name] = lax.ppermute(value, 'blk', move.pairs)  15.4 us
    ppermute x7, waiting for transfers between devices, local(): lax.ppermute(row, 'blk', permute)  6.41 us
    pallas_call x1, Pallas kernels, own_block(): pl.pallas_call(own_kernel, out_shape=jax.ShapeDtypeStruct((nblocks, rows)...  4.64 us
    pallas_call x1, Pallas kernels, normalized(): pl.pallas_call(unit_kernel, out_shape=jax.ShapeDtypeStruct((rows, depth),...  4.14 us
  transfers between devices with their start and end apart: 15, of which 5 were waited for; matrix products, arithmetic and copies ran while one was open for 0% of the time, Pallas kernels for 15%

profile of v14, /device:TPU:0, one launch (start us, length us, event | category | flops | bytes accessed | tf_op | source)
XLA Modules:
  0.0 114.2 jit_solution(3992832112603533234)
XLA Ops:
  0.0 4.1 %normalized.1.unit.refs_1_.refs_4_.refs_11_ = bf16[1024,1024]{1,0:T(8,128)(2,1)} custom-call(s32[16]{0:T(128)} %pads.5, s32[1024]{0:T(1024)} %order_smem.1, s32[1,1024]{1,0:T(1,128)} %bitcast.2, bf16[1024,1024]{1,0:T(8,128)(2,1)} %embeddings.1), custom_call_target="tpu_custom_call" | custom-call | flops 4194304 | bytes 4194304 | tf_op jit(solution)/shard_map/normalized/pallas_call | solution.py:205
  4.7 5.6 %collective-permute-start.1 = (bf16[1024,1024]{1,0:T(8,128)(2,1)}, bf16[1024,1024]{1,0:T(8,128)(2,1)}, u32[]{:S(2)}, u32[]{:S(2)}) collective-permute-start(bf16[1024,1024]{1,0:T(8,128)(2,1)} %normalized.1.unit.refs_1_.refs_4_.refs_11_), channel_id=1, source_target_pairs={{0,9},{8,13},{12,4},{4,0},{1,5},{3,10},{11,14},{15,7},{7,3},{2,6},... | collective-permute-start | bytes 6291464 | tf_op jit(solution)/shard_map/ppermute | solution.py:425
  10.3 2.0 %collective-permute-start.3 = (bf16[1024,1024]{1,0:T(8,128)(2,1)}, bf16[1024,1024]{1,0:T(8,128)(2,1)}, u32[]{:S(2)}, u32[]{:S(2)}) collective-permute-start(bf16[1024,1024]{1,0:T(8,128)(2,1)} %normalized.1.unit.refs_1_.refs_4_.refs_11_), channel_id=1, source_target_pairs={{13,5},{5,1},{9,12},{4,9},{14,6},{6,2},{10,15},{7,10},{29,21},{21,... | collective-permute-start | bytes 6291464 | tf_op jit(solution)/shard_map/ppermute | solution.py:425
  12.3 1.2 %collective-permute-start = (bf16[1024,1024]{1,0:T(8,128)(2,1)}, bf16[1024,1024]{1,0:T(8,128)(2,1)}, u32[]{:S(2)}, u32[]{:S(2)}) collective-permute-start(bf16[1024,1024]{1,0:T(8,128)(2,1)} %normalized.1.unit.refs_1_.refs_4_.refs_11_), channel_id=1, source_target_pairs={{0,3},{3,0},{1,2},{2,1},{8,11},{11,8},{9,10},{10,9},{12,15},{15,12... | collective-permute-start | bytes 6291464 | tf_op jit(solution)/shard_map/ppermute | solution.py:425
  13.4 4.6 %own_block.1.best = f32[16,1024]{1,0:T(8,128)} custom-call(s32[16]{0:T(128)} %pads.5, s32[1,1024]{1,0:T(1,128)} %bitcast.3, bf16[1024,1024]{1,0:T(8,128)(2,1)} %normalized.1.unit.refs_1_.refs_4_.refs_11_), custom_call_target="tpu_custom_call" | custom-call | flops 2147483648 | bytes 2097152 | tf_op jit(solution)/shard_map/own_block/pallas_call | solution.py:252
  18.1 1.5 %scored.3.best = f32[16,1024]{1,0:T(8,128)} custom-call(s32[144]{0:T(256)} %constant.8.clone.table, f32[16,1024]{1,0:T(8,128)} %own_block.1.best, bf16[1024,1024]{1,0:T(8,128)(2,1)} %collective-permute-done.2.refs_0_.refs_3_, bf16[1024,1024]{1,0:T(8,128)(2,1)} %normalized.1.unit.refs_1_.refs_4_.refs_11_), custom_call_target="tpu_custom_call" | custom-call | flops 2147483648 | bytes 4194304 | tf_op jit(solution)/shard_map/scored/pallas_call | solution.py:350
  19.6 35.4 %collective-permute-done.1.refs_1_.refs_5_ = bf16[1024,1024]{1,0:T(8,128)(2,1)} collective-permute-done((bf16[1024,1024]{1,0:T(8,128)(2,1)}, bf16[1024,1024]{1,0:T(8,128)(2,1)}, u32[]{:S(2)}, u32[]{:S(2)}) %collective-permute-start.1) | collective-permute-done | bytes 2097184 | tf_op jit(solution)/shard_map/ppermute | solution.py:425
  55.0 2.0 %collective-permute-start.8 = (bf16[1024,1024]{1,0:T(8,128)(2,1)}, bf16[1024,1024]{1,0:T(8,128)(2,1)}, u32[]{:S(2)}, u32[]{:S(2)}) collective-permute-start(bf16[1024,1024]{1,0:T(8,128)(2,1)} %normalized.1.unit.refs_1_.refs_4_.refs_11_), channel_id=1, source_target_pairs={{5,8},{8,5},{6,11},{11,6},{21,24},{24,21},{22,27},{27,22}} | collective-permute-start | bytes 6291464 | tf_op jit(solution)/shard_map/ppermute | solution.py:425
  57.0 2.0 %collective-permute-start.9 = (bf16[1024,1024]{1,0:T(8,128)(2,1)}, bf16[1024,1024]{1,0:T(8,128)(2,1)}, u32[]{:S(2)}, u32[]{:S(2)}) collective-permute-start(bf16[1024,1024]{1,0:T(8,128)(2,1)} %collective-permute-done.1.refs_1_.refs_5_), channel_id=1, source_target_pairs={{9,13},{10,15},{5,6},{6,5},{25,29},{26,31},{21,22},{22,21}} | collective-permute-start | bytes 6291464 | tf_op jit(solution)/shard_map/ppermute | solution.py:425
  59.1 1.5 %collective-permute-done.refs_3_.refs_10_ = bf16[1024,1024]{1,0:T(8,128)(2,1)} collective-permute-done((bf16[1024,1024]{1,0:T(8,128)(2,1)}, bf16[1024,1024]{1,0:T(8,128)(2,1)}, u32[]{:S(2)}, u32[]{:S(2)}) %collective-permute-start) | collective-permute-done | bytes 2097184 | tf_op jit(solution)/shard_map/ppermute | solution.py:425
  60.5 11.2 %scored.4 = (f32[16,1024]{1,0:T(8,128)}, f32[1,1024]{1,0:T(1,128)}, f32[1,1024]{1,0:T(1,128)}, f32[1,1024]{1,0:T(1,128)}) custom-call(s32[480]{0:T(512)} %constant.9.clone.table, f32[16,1024]{1,0:T(8,128)} %scored.3.best, bf16[1024,1024]{1,0:T(8,128)(2,1)} %collective-permute-done.2.refs_0_.refs_3_, ...), custom_call_target="tpu_custom_call" | custom-call | flops 8589934592 | bytes 10485760 | tf_op jit(solution)/shard_map/scored/pallas_call | solution.py:350
  71.7 2.0 %collective-permute-start.10 = (bf16[1024,1024]{1,0:T(8,128)(2,1)}, bf16[1024,1024]{1,0:T(8,128)(2,1)}, u32[]{:S(2)}, u32[]{:S(2)}) collective-permute-start(bf16[1024,1024]{1,0:T(8,128)(2,1)} %collective-permute-done.1.refs_1_.refs_5_), channel_id=1, source_target_pairs={{4,5},{5,4},{7,6},{6,7},{20,21},{21,20},{23,22},{22,23}} | collective-permute-start | bytes 6291464 | tf_op jit(solution)/shard_map/ppermute | solution.py:425
  73.7 2.4 %collective-permute-start.4 = (f32[1,1024]{1,0:T(1,128)}, f32[1,1024]{1,0:T(1,128)}, u32[]{:S(2)}, u32[]{:S(2)}) collective-permute-start(f32[1,1024]{1,0:T(1,128)} %get-tuple-element.27), channel_id=1, source_target_pairs={{0,1},{1,0},{4,5},{5,7},{6,2},{7,6},{9,4},{10,9},{12,15},{13,8},{1... | collective-permute-start | bytes 12296 | tf_op jit(solution)/shard_map/ppermute | solution.py:431
  76.1 1.1 %collective-permute-done.4.refs_0_ = f32[1,1024]{1,0:T(1,128)} collective-permute-done((f32[1,1024]{1,0:T(1,128)}, f32[1,1024]{1,0:T(1,128)}, u32[]{:S(2)}, u32[]{:S(2)}) %collective-permute-start.4) | collective-permute-done | bytes 4128 | tf_op jit(solution)/shard_map/ppermute | solution.py:431
  77.3 1.9 %collective-permute-start.5 = (f32[1,1024]{1,0:T(1,128)}, f32[1,1024]{1,0:T(1,128)}, u32[]{:S(2)}, u32[]{:S(2)}) collective-permute-start(f32[1,1024]{1,0:T(1,128)} %get-tuple-element.28), channel_id=1, source_target_pairs={{0,3},{2,1},{4,6},{6,4},{9,10},{10,11},{16,19},{18,17},{20,22},{22... | collective-permute-start | bytes 12296 | tf_op jit(solution)/shard_map/ppermute | solution.py:431
  79.1 0.9 collective-permute-done.5.refs_1_
  80.1 1.2 %collective-permute-start.6 = (f32[1,1024]{1,0:T(1,128)}, f32[1,1024]{1,0:T(1,128)}, u32[]{:S(2)}, u32[]{:S(2)}) collective-permute-start(f32[1,1024]{1,0:T(1,128)} %get-tuple-element.29), channel_id=1, source_target_pairs={{5,1},{21,17}} | collective-permute-start | bytes 12296 | tf_op jit(solution)/shard_map/ppermute | solution.py:431
  81.4 8.7 %scored.5 = (f32[16,1024]{1,0:T(8,128)}, f32[1,1024]{1,0:T(1,128)}, f32[1,1024]{1,0:T(1,128)}, f32[1,1024]{1,0:T(1,128)}, f32[1,1024]{1,0:T(1,128)}) custom-call(s32[544]{0:T(1024)} %constant.10.clone.table, f32[16,1024]{1,0:T(8,128)} %get-tuple-element.26.best, f32[1,1024]{1,0:T(1,128)} %collective-permute-done.4.refs_0_, ...), custom_call_target="tpu_custom_call" | custom-call | flops 8589934592 | bytes 10485760 | tf_op jit(solution)/shard_map/scored/pallas_call | solution.py:350
  90.0 4.7 %collective-permute-start.11 = (f32[1,1024]{1,0:T(1,128)}, f32[1,1024]{1,0:T(1,128)}, u32[]{:S(2)}, u32[]{:S(2)}) collective-permute-start(f32[1,1024]{1,0:T(1,128)} %get-tuple-element.35), channel_id=1, source_target_pairs={{0,2},{1,3},{2,6},{3,7},{4,12},{5,8},{6,1},{7,4},{8,5},{9,11},{11,... | collective-permute-start | bytes 12296 | tf_op jit(solution)/shard_map/ppermute | solution.py:431
  94.8 10.4 %collective-permute-start.12 = (f32[1,1024]{1,0:T(1,128)}, f32[1,1024]{1,0:T(1,128)}, u32[]{:S(2)}, u32[]{:S(2)}) collective-permute-start(f32[1,1024]{1,0:T(1,128)} %get-tuple-element.36), channel_id=1, source_target_pairs={{0,4},{1,5},{2,0},{3,1},{4,7},{5,2},{6,11},{7,15},{8,9},{9,8},{10,... | collective-permute-start | bytes 12296 | tf_op jit(solution)/shard_map/ppermute | solution.py:431
  105.2 1.3 %collective-permute-start.13 = (f32[1,1024]{1,0:T(1,128)}, f32[1,1024]{1,0:T(1,128)}, u32[]{:S(2)}, u32[]{:S(2)}) collective-permute-start(f32[1,1024]{1,0:T(1,128)} %get-tuple-element.37), channel_id=1, source_target_pairs={{2,3},{3,2},{4,1},{5,12},{6,15},{7,5},{8,10},{9,0},{10,7},{11,8},{... | collective-permute-start | bytes 12296 | tf_op jit(solution)/shard_map/ppermute | solution.py:431
  106.5 1.2 %collective-permute-start.14 = (f32[1,1024]{1,0:T(1,128)}, f32[1,1024]{1,0:T(1,128)}, u32[]{:S(2)}, u32[]{:S(2)}) collective-permute-start(f32[1,1024]{1,0:T(1,128)} %get-tuple-element.38), channel_id=1, source_target_pairs={{5,13},{6,14},{7,2},{8,11},{10,8},{11,10},{13,15},{14,12},{15,3},{... | collective-permute-start | bytes 12296 | tf_op jit(solution)/shard_map/ppermute | solution.py:431
  107.7 4.3 %collective-permute-done.13.refs_2_ = f32[1,1024]{1,0:T(1,128)} collective-permute-done((f32[1,1024]{1,0:T(1,128)}, f32[1,1024]{1,0:T(1,128)}, u32[]{:S(2)}, u32[]{:S(2)}) %collective-permute-start.13) | collective-permute-done | bytes 4128 | tf_op jit(solution)/shard_map/ppermute | solution.py:431
  112.0 2.2 %placed.1 = f32[1,1024]{1,0:T(1,128)} custom-call(s32[64]{0:T(128)} %constant.11.clone.taken, s32[16]{0:T(128)} %pads.5, s32[1,1024]{1,0:T(1,128)} %bitcast.4, f32[16,1024]{1,0:T(8,128)} %get-tuple-element.34.best, f32[1,1024]{1,0:T(1,128)} %collective-permute-done.11.refs_0_, f32[1,1024]{1,0:T(1,128)} %collective-permute-done.12.refs_1_, ...), custom_call_target="tpu_custom_call" | custom-call | tf_op jit(solution)/shard_map/placed/pallas_call | solution.py:393
  (12 shorter events, 0.6 us)
Async XLA Ops:
  4.2 13.9 %collective-permute-start.2 = (bf16[1024,1024]{1,0:T(8,128)(2,1)}, bf16[1024,1024]{1,0:T(8,128)(2,1)}, u32[]{:S(2)}, u32[]{:S(2)}) collective-permute-start(bf16[1024,1024]{1,0:T(8,128)(2,1)} %normalized.1.unit.refs_1_.refs_4_.refs_11_), channel_id=1, source_target_pairs={{0,1},{1,0},{4,5},{5,4},{8,9},{9,8},{12,13},{13,12},{3,2},{2,3},{7... | collective-permute-start | bytes 6291464 | tf_op jit(solution)/shard_map/ppermute | solution.py:425
  4.7 50.4 %collective-permute-start.1 = (bf16[1024,1024]{1,0:T(8,128)(2,1)}, bf16[1024,1024]{1,0:T(8,128)(2,1)}, u32[]{:S(2)}, u32[]{:S(2)}) collective-permute-start(bf16[1024,1024]{1,0:T(8,128)(2,1)} %normalized.1.unit.refs_1_.refs_4_.refs_11_), channel_id=1, source_target_pairs={{0,9},{8,13},{12,4},{4,0},{1,5},{3,10},{11,14},{15,7},{7,3},{2,6},... | collective-permute-start | bytes 6291464 | tf_op jit(solution)/shard_map/ppermute | solution.py:425
  10.3 48.8 %collective-permute-start.3 = (bf16[1024,1024]{1,0:T(8,128)(2,1)}, bf16[1024,1024]{1,0:T(8,128)(2,1)}, u32[]{:S(2)}, u32[]{:S(2)}) collective-permute-start(bf16[1024,1024]{1,0:T(8,128)(2,1)} %normalized.1.unit.refs_1_.refs_4_.refs_11_), channel_id=1, source_target_pairs={{13,5},{5,1},{9,12},{4,9},{14,6},{6,2},{10,15},{7,10},{29,21},{21,... | collective-permute-start | bytes 6291464 | tf_op jit(solution)/shard_map/ppermute | solution.py:425
  12.3 48.2 %collective-permute-start = (bf16[1024,1024]{1,0:T(8,128)(2,1)}, bf16[1024,1024]{1,0:T(8,128)(2,1)}, u32[]{:S(2)}, u32[]{:S(2)}) collective-permute-start(bf16[1024,1024]{1,0:T(8,128)(2,1)} %normalized.1.unit.refs_1_.refs_4_.refs_11_), channel_id=1, source_target_pairs={{0,3},{3,0},{1,2},{2,1},{8,11},{11,8},{9,10},{10,9},{12,15},{15,12... | collective-permute-start | bytes 6291464 | tf_op jit(solution)/shard_map/ppermute | solution.py:425
  55.0 26.3 %collective-permute-start.8 = (bf16[1024,1024]{1,0:T(8,128)(2,1)}, bf16[1024,1024]{1,0:T(8,128)(2,1)}, u32[]{:S(2)}, u32[]{:S(2)}) collective-permute-start(bf16[1024,1024]{1,0:T(8,128)(2,1)} %normalized.1.unit.refs_1_.refs_4_.refs_11_), channel_id=1, source_target_pairs={{5,8},{8,5},{6,11},{11,6},{21,24},{24,21},{22,27},{27,22}} | collective-permute-start | bytes 6291464 | tf_op jit(solution)/shard_map/ppermute | solution.py:425
  57.0 24.3 %collective-permute-start.9 = (bf16[1024,1024]{1,0:T(8,128)(2,1)}, bf16[1024,1024]{1,0:T(8,128)(2,1)}, u32[]{:S(2)}, u32[]{:S(2)}) collective-permute-start(bf16[1024,1024]{1,0:T(8,128)(2,1)} %collective-permute-done.1.refs_1_.refs_5_), channel_id=1, source_target_pairs={{9,13},{10,15},{5,6},{6,5},{25,29},{26,31},{21,22},{22,21}} | collective-permute-start | bytes 6291464 | tf_op jit(solution)/shard_map/ppermute | solution.py:425
  71.7 9.7 %collective-permute-start.7 = (bf16[1024,1024]{1,0:T(8,128)(2,1)}, bf16[1024,1024]{1,0:T(8,128)(2,1)}, u32[]{:S(2)}, u32[]{:S(2)}) collective-permute-start(bf16[1024,1024]{1,0:T(8,128)(2,1)} %collective-permute-done.refs_3_.refs_10_), channel_id=1, source_target_pairs={{0,1},{1,0},{4,5},{5,4},{8,9},{9,8},{12,13},{13,12},{3,2},{2,3},{7... | collective-permute-start | bytes 6291464 | tf_op jit(solution)/shard_map/ppermute | solution.py:425
  71.7 9.6 %collective-permute-start.10 = (bf16[1024,1024]{1,0:T(8,128)(2,1)}, bf16[1024,1024]{1,0:T(8,128)(2,1)}, u32[]{:S(2)}, u32[]{:S(2)}) collective-permute-start(bf16[1024,1024]{1,0:T(8,128)(2,1)} %collective-permute-done.1.refs_1_.refs_5_), channel_id=1, source_target_pairs={{4,5},{5,4},{7,6},{6,7},{20,21},{21,20},{23,22},{22,23}} | collective-permute-start | bytes 6291464 | tf_op jit(solution)/shard_map/ppermute | solution.py:425
  73.7 3.5 %collective-permute-start.4 = (f32[1,1024]{1,0:T(1,128)}, f32[1,1024]{1,0:T(1,128)}, u32[]{:S(2)}, u32[]{:S(2)}) collective-permute-start(f32[1,1024]{1,0:T(1,128)} %get-tuple-element.27), channel_id=1, source_target_pairs={{0,1},{1,0},{4,5},{5,7},{6,2},{7,6},{9,4},{10,9},{12,15},{13,8},{1... | collective-permute-start | bytes 12296 | tf_op jit(solution)/shard_map/ppermute | solution.py:431
  77.3 2.8 %collective-permute-start.5 = (f32[1,1024]{1,0:T(1,128)}, f32[1,1024]{1,0:T(1,128)}, u32[]{:S(2)}, u32[]{:S(2)}) collective-permute-start(f32[1,1024]{1,0:T(1,128)} %get-tuple-element.28), channel_id=1, source_target_pairs={{0,3},{2,1},{4,6},{6,4},{9,10},{10,11},{16,19},{18,17},{20,22},{22... | collective-permute-start | bytes 12296 | tf_op jit(solution)/shard_map/ppermute | solution.py:431
  80.1 1.2 %collective-permute-start.6 = (f32[1,1024]{1,0:T(1,128)}, f32[1,1024]{1,0:T(1,128)}, u32[]{:S(2)}, u32[]{:S(2)}) collective-permute-start(f32[1,1024]{1,0:T(1,128)} %get-tuple-element.29), channel_id=1, source_target_pairs={{5,1},{21,17}} | collective-permute-start | bytes 12296 | tf_op jit(solution)/shard_map/ppermute | solution.py:431
  90.0 17.7 %collective-permute-start.11 = (f32[1,1024]{1,0:T(1,128)}, f32[1,1024]{1,0:T(1,128)}, u32[]{:S(2)}, u32[]{:S(2)}) collective-permute-start(f32[1,1024]{1,0:T(1,128)} %get-tuple-element.35), channel_id=1, source_target_pairs={{0,2},{1,3},{2,6},{3,7},{4,12},{5,8},{6,1},{7,4},{8,5},{9,11},{11,... | collective-permute-start | bytes 12296 | tf_op jit(solution)/shard_map/ppermute | solution.py:431
  94.8 12.9 %collective-permute-start.12 = (f32[1,1024]{1,0:T(1,128)}, f32[1,1024]{1,0:T(1,128)}, u32[]{:S(2)}, u32[]{:S(2)}) collective-permute-start(f32[1,1024]{1,0:T(1,128)} %get-tuple-element.36), channel_id=1, source_target_pairs={{0,4},{1,5},{2,0},{3,1},{4,7},{5,2},{6,11},{7,15},{8,9},{9,8},{10,... | collective-permute-start | bytes 12296 | tf_op jit(solution)/shard_map/ppermute | solution.py:431
  105.2 6.9 %collective-permute-start.13 = (f32[1,1024]{1,0:T(1,128)}, f32[1,1024]{1,0:T(1,128)}, u32[]{:S(2)}, u32[]{:S(2)}) collective-permute-start(f32[1,1024]{1,0:T(1,128)} %get-tuple-element.37), channel_id=1, source_target_pairs={{2,3},{3,2},{4,1},{5,12},{6,15},{7,5},{8,10},{9,0},{10,7},{11,8},{... | collective-permute-start | bytes 12296 | tf_op jit(solution)/shard_map/ppermute | solution.py:431
  106.5 5.6 %collective-permute-start.14 = (f32[1,1024]{1,0:T(1,128)}, f32[1,1024]{1,0:T(1,128)}, u32[]{:S(2)}, u32[]{:S(2)}) collective-permute-start(f32[1,1024]{1,0:T(1,128)} %get-tuple-element.38), channel_id=1, source_target_pairs={{5,13},{6,14},{7,2},{8,11},{10,8},{11,10},{13,15},{14,12},{15,3},{... | collective-permute-start | bytes 12296 | tf_op jit(solution)/shard_map/ppermute | solution.py:431

commit v15 on v14

--- a/solution.py
+++ b/solution.py
@@ -13,7 +13,7 @@
 FLOOR = -2.0
 MOST_PADS = 256
 AHEAD = 2
-FIRST, EARLY = 4, 3
+FIRST, EARLY = 2, 2
 
 
 class Move:

time: 116 us -> 116 us (level)
  the two profiles are of different devices: /device:TPU:0 before, /device:TPU:1 now
where the time goes in v15:
time: 116 us; the launch traced here: 115 us
  waiting for transfers between devices  48.4 us (42%)
  Pallas kernels  34.3 us (30%)
  starting transfers between devices  32.1 us (28%)
    ppermute x8, waiting for transfers between devices, local(): slots[move.name] = lax.ppermute(value, 'blk', move.pairs)  32.4 us
    pallas_call x3, Pallas kernels, scored(): pl.pallas_call(functools.partial(pairs_kernel, len(given), len(sends), le...  23.4 us
    ppermute x8, starting transfers between devices, local(): slots[move.name] = lax.ppermute(value, 'blk', move.pairs)  17.8 us
    ppermute x6, waiting for transfers between devices, local(): lax.ppermute(row, 'blk', permute)  16.1 us
    ppermute x6, starting transfers between devices, local(): lax.ppermute(row, 'blk', permute)  14.2 us
    pallas_call x1, Pallas kernels, own_block(): pl.pallas_call(own_kernel, out_shape=jax.ShapeDtypeStruct((nblocks, rows)...  4.65 us
    pallas_call x1, Pallas kernels, normalized(): pl.pallas_call(unit_kernel, out_shape=jax.ShapeDtypeStruct((rows, depth),...  4.13 us
  transfers between devices with their start and end apart: 14, of which 6 were waited for; matrix products, arithmetic and copies ran while one was open for 0% of the time, Pallas kernels for 17%

profile of v15, /device:TPU:1, one launch (start us, length us, event | category | flops | bytes accessed | tf_op | source)
XLA Modules:
  0.0 115.0 jit_solution(1537895255586254620)
XLA Ops:
  0.0 4.1 %normalized.1.unit.refs_1_.refs_4_.refs_10_ = bf16[1024,1024]{1,0:T(8,128)(2,1)} custom-call(s32[16]{0:T(128)} %pads.5, s32[1024]{0:T(1024)} %order_smem.1, s32[1,1024]{1,0:T(1,128)} %bitcast.2, bf16[1024,1024]{1,0:T(8,128)(2,1)} %embeddings.1), custom_call_target="tpu_custom_call" | custom-call | flops 4194304 | bytes 4194304 | tf_op jit(solution)/shard_map/normalized/pallas_call | solution.py:205
  4.3 6.0 %collective-permute-start.1 = (bf16[1024,1024]{1,0:T(8,128)(2,1)}, bf16[1024,1024]{1,0:T(8,128)(2,1)}, u32[]{:S(2)}, u32[]{:S(2)}) collective-permute-start(bf16[1024,1024]{1,0:T(8,128)(2,1)} %normalized.1.unit.refs_1_.refs_4_.refs_10_), channel_id=1, source_target_pairs={{0,9},{8,13},{12,4},{4,0},{1,5},{3,10},{11,14},{15,7},{7,3},{2,6},... | collective-permute-start | bytes 6291464 | tf_op jit(solution)/shard_map/ppermute | solution.py:425
  11.5 1.5 %collective-permute-start = (bf16[1024,1024]{1,0:T(8,128)(2,1)}, bf16[1024,1024]{1,0:T(8,128)(2,1)}, u32[]{:S(2)}, u32[]{:S(2)}) collective-permute-start(bf16[1024,1024]{1,0:T(8,128)(2,1)} %normalized.1.unit.refs_1_.refs_4_.refs_10_), channel_id=1, source_target_pairs={{0,3},{3,0},{1,2},{2,1},{8,11},{11,8},{9,10},{10,9},{12,15},{15,12... | collective-permute-start | bytes 6291464 | tf_op jit(solution)/shard_map/ppermute | solution.py:425
  13.0 4.6 %own_block.1.best = f32[16,1024]{1,0:T(8,128)} custom-call(s32[16]{0:T(128)} %pads.5, s32[1,1024]{1,0:T(1,128)} %bitcast.3, bf16[1024,1024]{1,0:T(8,128)(2,1)} %normalized.1.unit.refs_1_.refs_4_.refs_10_), custom_call_target="tpu_custom_call" | custom-call | flops 2147483648 | bytes 2097152 | tf_op jit(solution)/shard_map/own_block/pallas_call | solution.py:252
  17.7 6.1 %scored.3.best = f32[16,1024]{1,0:T(8,128)} custom-call(s32[144]{0:T(256)} %constant.8.clone.table, f32[16,1024]{1,0:T(8,128)} %own_block.1.best, bf16[1024,1024]{1,0:T(8,128)(2,1)} %collective-permute-done.2.refs_0_.refs_2_, bf16[1024,1024]{1,0:T(8,128)(2,1)} %normalized.1.unit.refs_1_.refs_4_.refs_10_), custom_call_target="tpu_custom_call" | custom-call | flops 2147483648 | bytes 4194304 | tf_op jit(solution)/shard_map/scored/pallas_call | solution.py:350
  23.8 29.2 %collective-permute-done.1.refs_1_.refs_4_ = bf16[1024,1024]{1,0:T(8,128)(2,1)} collective-permute-done((bf16[1024,1024]{1,0:T(8,128)(2,1)}, bf16[1024,1024]{1,0:T(8,128)(2,1)}, u32[]{:S(2)}, u32[]{:S(2)}) %collective-permute-start.1) | collective-permute-done | bytes 2097184 | tf_op jit(solution)/shard_map/ppermute | solution.py:425
  53.0 2.0 %collective-permute-start.7 = (bf16[1024,1024]{1,0:T(8,128)(2,1)}, bf16[1024,1024]{1,0:T(8,128)(2,1)}, u32[]{:S(2)}, u32[]{:S(2)}) collective-permute-start(bf16[1024,1024]{1,0:T(8,128)(2,1)} %normalized.1.unit.refs_1_.refs_4_.refs_10_), channel_id=1, source_target_pairs={{5,8},{8,5},{6,11},{11,6},{21,24},{24,21},{22,27},{27,22}} | collective-permute-start | bytes 6291464 | tf_op jit(solution)/shard_map/ppermute | solution.py:425
  55.0 2.0 %collective-permute-start.8 = (bf16[1024,1024]{1,0:T(8,128)(2,1)}, bf16[1024,1024]{1,0:T(8,128)(2,1)}, u32[]{:S(2)}, u32[]{:S(2)}) collective-permute-start(bf16[1024,1024]{1,0:T(8,128)(2,1)} %collective-permute-done.1.refs_1_.refs_4_), channel_id=1, source_target_pairs={{9,13},{10,15},{5,6},{6,5},{25,29},{26,31},{21,22},{22,21}} | collective-permute-start | bytes 6291464 | tf_op jit(solution)/shard_map/ppermute | solution.py:425
  57.0 3.1 %collective-permute-done.refs_3_.refs_9_ = bf16[1024,1024]{1,0:T(8,128)(2,1)} collective-permute-done((bf16[1024,1024]{1,0:T(8,128)(2,1)}, bf16[1024,1024]{1,0:T(8,128)(2,1)}, u32[]{:S(2)}, u32[]{:S(2)}) %collective-permute-start) | collective-permute-done | bytes 2097184 | tf_op jit(solution)/shard_map/ppermute | solution.py:425
  60.1 8.6 %scored.4 = (f32[16,1024]{1,0:T(8,128)}, f32[1,1024]{1,0:T(1,128)}, f32[1,1024]{1,0:T(1,128)}) custom-call(s32[464]{0:T(512)} %constant.9.clone.table, f32[16,1024]{1,0:T(8,128)} %scored.3.best, bf16[1024,1024]{1,0:T(8,128)(2,1)} %collective-permute-done.2.refs_0_.refs_2_, bf16[1024,1024]{1,0:T(8,128)(2,1)} %collective-permute-done.1.refs_1_.refs_4_, ...), custom_call_target="tpu_custom_call" | custom-call | flops 8589934592 | bytes 10485760 | tf_op jit(solution)/shard_map/scored/pallas_call | solution.py:350
  68.7 3.0 %collective-permute-start.6 = (bf16[1024,1024]{1,0:T(8,128)(2,1)}, bf16[1024,1024]{1,0:T(8,128)(2,1)}, u32[]{:S(2)}, u32[]{:S(2)}) collective-permute-start(bf16[1024,1024]{1,0:T(8,128)(2,1)} %collective-permute-done.refs_3_.refs_9_), channel_id=1, source_target_pairs={{0,1},{1,0},{4,5},{5,4},{8,9},{9,8},{12,13},{13,12},{3,2},{2,3},{7... | collective-permute-start | bytes 6291464 | tf_op jit(solution)/shard_map/ppermute | solution.py:425
  71.7 2.0 %collective-permute-start.9 = (bf16[1024,1024]{1,0:T(8,128)(2,1)}, bf16[1024,1024]{1,0:T(8,128)(2,1)}, u32[]{:S(2)}, u32[]{:S(2)}) collective-permute-start(bf16[1024,1024]{1,0:T(8,128)(2,1)} %collective-permute-done.1.refs_1_.refs_4_), channel_id=1, source_target_pairs={{4,5},{5,4},{7,6},{6,7},{20,21},{21,20},{23,22},{22,23}} | collective-permute-start | bytes 6291464 | tf_op jit(solution)/shard_map/ppermute | solution.py:425
  73.7 1.9 %collective-permute-start.4 = (f32[1,1024]{1,0:T(1,128)}, f32[1,1024]{1,0:T(1,128)}, u32[]{:S(2)}, u32[]{:S(2)}) collective-permute-start(f32[1,1024]{1,0:T(1,128)} %get-tuple-element.26), channel_id=1, source_target_pairs={{0,3},{1,0},{2,1},{4,5},{5,7},{6,2},{7,6},{9,4},{10,9},{12,15},{13... | collective-permute-start | bytes 12296 | tf_op jit(solution)/shard_map/ppermute | solution.py:431
  75.7 3.3 %collective-permute-done.4.refs_0_ = f32[1,1024]{1,0:T(1,128)} collective-permute-done((f32[1,1024]{1,0:T(1,128)}, f32[1,1024]{1,0:T(1,128)}, u32[]{:S(2)}, u32[]{:S(2)}) %collective-permute-start.4) | collective-permute-done | bytes 4128 | tf_op jit(solution)/shard_map/ppermute | solution.py:431
  79.0 1.3 %collective-permute-start.5 = (f32[1,1024]{1,0:T(1,128)}, f32[1,1024]{1,0:T(1,128)}, u32[]{:S(2)}, u32[]{:S(2)}) collective-permute-start(f32[1,1024]{1,0:T(1,128)} %get-tuple-element.27), channel_id=1, source_target_pairs={{4,6},{5,1},{6,4},{9,10},{10,11},{20,22},{21,17},{22,20},{25,26},{... | collective-permute-start | bytes 12296 | tf_op jit(solution)/shard_map/ppermute | solution.py:431
  80.2 7.9 %collective-permute-done.5.refs_1_ = f32[1,1024]{1,0:T(1,128)} collective-permute-done((f32[1,1024]{1,0:T(1,128)}, f32[1,1024]{1,0:T(1,128)}, u32[]{:S(2)}, u32[]{:S(2)}) %collective-permute-start.5) | collective-permute-done | bytes 4128 | tf_op jit(solution)/shard_map/ppermute | solution.py:431
  88.2 8.7 %scored.5 = (f32[16,1024]{1,0:T(8,128)}, f32[1,1024]{1,0:T(1,128)}, f32[1,1024]{1,0:T(1,128)}, f32[1,1024]{1,0:T(1,128)}, f32[1,1024]{1,0:T(1,128)}) custom-call(s32[528]{0:T(1024)} %constant.10.clone.table, f32[16,1024]{1,0:T(8,128)} %get-tuple-element.25.best, f32[1,1024]{1,0:T(1,128)} %collective-permute-done.4.refs_0_, ...), custom_call_target="tpu_custom_call" | custom-call | flops 8589934592 | bytes 10485760 | tf_op jit(solution)/shard_map/scored/pallas_call | solution.py:350
  96.9 1.9 %collective-permute-start.10 = (f32[1,1024]{1,0:T(1,128)}, f32[1,1024]{1,0:T(1,128)}, u32[]{:S(2)}, u32[]{:S(2)}) collective-permute-start(f32[1,1024]{1,0:T(1,128)} %get-tuple-element.33), channel_id=1, source_target_pairs={{0,1},{1,3},{2,6},{3,2},{4,7},{5,8},{6,14},{7,15},{8,5},{9,11},{11... | collective-permute-start | bytes 12296 | tf_op jit(solution)/shard_map/ppermute | solution.py:431
  98.8 6.5 %collective-permute-start.11 = (f32[1,1024]{1,0:T(1,128)}, f32[1,1024]{1,0:T(1,128)}, u32[]{:S(2)}, u32[]{:S(2)}) collective-permute-start(f32[1,1024]{1,0:T(1,128)} %get-tuple-element.34), channel_id=1, source_target_pairs={{0,2},{1,5},{2,3},{3,1},{4,12},{5,13},{6,11},{7,4},{8,10},{9,0},{1... | collective-permute-start | bytes 12296 | tf_op jit(solution)/shard_map/ppermute | solution.py:431
  105.3 1.3 %collective-permute-start.12 = (f32[1,1024]{1,0:T(1,128)}, f32[1,1024]{1,0:T(1,128)}, u32[]{:S(2)}, u32[]{:S(2)}) collective-permute-start(f32[1,1024]{1,0:T(1,128)} %get-tuple-element.35), channel_id=1, source_target_pairs={{0,4},{2,0},{3,7},{4,1},{5,2},{6,15},{7,5},{8,9},{9,8},{10,3},{11,... | collective-permute-start | bytes 12296 | tf_op jit(solution)/shard_map/ppermute | solution.py:431
  106.6 1.3 %collective-permute-start.13 = (f32[1,1024]{1,0:T(1,128)}, f32[1,1024]{1,0:T(1,128)}, u32[]{:S(2)}, u32[]{:S(2)}) collective-permute-start(f32[1,1024]{1,0:T(1,128)} %get-tuple-element.36), channel_id=1, source_target_pairs={{5,12},{6,1},{7,2},{8,11},{10,8},{11,10},{13,14},{14,15},{15,3},{2... | collective-permute-start | bytes 12296 | tf_op jit(solution)/shard_map/ppermute | solution.py:431
  108.0 2.6 %collective-permute-done.12.refs_2_ = f32[1,1024]{1,0:T(1,128)} collective-permute-done((f32[1,1024]{1,0:T(1,128)}, f32[1,1024]{1,0:T(1,128)}, u32[]{:S(2)}, u32[]{:S(2)}) %collective-permute-start.12) | collective-permute-done | bytes 4128 | tf_op jit(solution)/shard_map/ppermute | solution.py:431
  110.6 2.2 %collective-permute-done.13.refs_3_ = f32[1,1024]{1,0:T(1,128)} collective-permute-done((f32[1,1024]{1,0:T(1,128)}, f32[1,1024]{1,0:T(1,128)}, u32[]{:S(2)}, u32[]{:S(2)}) %collective-permute-start.13) | collective-permute-done | bytes 4128 | tf_op jit(solution)/shard_map/ppermute | solution.py:431
  112.8 2.2 %placed.1 = f32[1,1024]{1,0:T(1,128)} custom-call(s32[64]{0:T(128)} %constant.11.clone.taken, s32[16]{0:T(128)} %pads.5, s32[1,1024]{1,0:T(1,128)} %bitcast.4, f32[16,1024]{1,0:T(8,128)} %get-tuple-element.32.best, f32[1,1024]{1,0:T(1,128)} %collective-permute-done.10.refs_0_, f32[1,1024]{1,0:T(1,128)} %collective-permute-done.11.refs_1_, ...), custom_call_target="tpu_custom_call" | custom-call | tf_op jit(solution)/shard_map/placed/pallas_call | solution.py:393
  (10 shorter events, 1.4 us)
Async XLA Ops:
  4.1 13.5 %collective-permute-start.2 = (bf16[1024,1024]{1,0:T(8,128)(2,1)}, bf16[1024,1024]{1,0:T(8,128)(2,1)}, u32[]{:S(2)}, u32[]{:S(2)}) collective-permute-start(bf16[1024,1024]{1,0:T(8,128)(2,1)} %normalized.1.unit.refs_1_.refs_4_.refs_10_), channel_id=1, source_target_pairs={{0,1},{1,0},{4,5},{5,4},{8,9},{9,8},{12,13},{13,12},{3,2},{2,3},{7... | collective-permute-start | bytes 6291464 | tf_op jit(solution)/shard_map/ppermute | solution.py:425
  4.3 48.7 %collective-permute-start.1 = (bf16[1024,1024]{1,0:T(8,128)(2,1)}, bf16[1024,1024]{1,0:T(8,128)(2,1)}, u32[]{:S(2)}, u32[]{:S(2)}) collective-permute-start(bf16[1024,1024]{1,0:T(8,128)(2,1)} %normalized.1.unit.refs_1_.refs_4_.refs_10_), channel_id=1, source_target_pairs={{0,9},{8,13},{12,4},{4,0},{1,5},{3,10},{11,14},{15,7},{7,3},{2,6},... | collective-permute-start | bytes 6291464 | tf_op jit(solution)/shard_map/ppermute | solution.py:425
  10.2 46.7 %collective-permute-start.3 = (bf16[1024,1024]{1,0:T(8,128)(2,1)}, bf16[1024,1024]{1,0:T(8,128)(2,1)}, u32[]{:S(2)}, u32[]{:S(2)}) collective-permute-start(bf16[1024,1024]{1,0:T(8,128)(2,1)} %normalized.1.unit.refs_1_.refs_4_.refs_10_), channel_id=1, source_target_pairs={{13,5},{5,1},{9,12},{4,9},{14,6},{6,2},{10,15},{7,10},{29,21},{21,... | collective-permute-start | bytes 6291464 | tf_op jit(solution)/shard_map/ppermute | solution.py:425
  11.5 48.6 %collective-permute-start = (bf16[1024,1024]{1,0:T(8,128)(2,1)}, bf16[1024,1024]{1,0:T(8,128)(2,1)}, u32[]{:S(2)}, u32[]{:S(2)}) collective-permute-start(bf16[1024,1024]{1,0:T(8,128)(2,1)} %normalized.1.unit.refs_1_.refs_4_.refs_10_), channel_id=1, source_target_pairs={{0,3},{3,0},{1,2},{2,1},{8,11},{11,8},{9,10},{10,9},{12,15},{15,12... | collective-permute-start | bytes 6291464 | tf_op jit(solution)/shard_map/ppermute | solution.py:425
  53.0 35.2 %collective-permute-start.7 = (bf16[1024,1024]{1,0:T(8,128)(2,1)}, bf16[1024,1024]{1,0:T(8,128)(2,1)}, u32[]{:S(2)}, u32[]{:S(2)}) collective-permute-start(bf16[1024,1024]{1,0:T(8,128)(2,1)} %normalized.1.unit.refs_1_.refs_4_.refs_10_), channel_id=1, source_target_pairs={{5,8},{8,5},{6,11},{11,6},{21,24},{24,21},{22,27},{27,22}} | collective-permute-start | bytes 6291464 | tf_op jit(solution)/shard_map/ppermute | solution.py:425
  55.0 33.2 %collective-permute-start.8 = (bf16[1024,1024]{1,0:T(8,128)(2,1)}, bf16[1024,1024]{1,0:T(8,128)(2,1)}, u32[]{:S(2)}, u32[]{:S(2)}) collective-permute-start(bf16[1024,1024]{1,0:T(8,128)(2,1)} %collective-permute-done.1.refs_1_.refs_4_), channel_id=1, source_target_pairs={{9,13},{10,15},{5,6},{6,5},{25,29},{26,31},{21,22},{22,21}} | collective-permute-start | bytes 6291464 | tf_op jit(solution)/shard_map/ppermute | solution.py:425
  68.7 19.5 %collective-permute-start.6 = (bf16[1024,1024]{1,0:T(8,128)(2,1)}, bf16[1024,1024]{1,0:T(8,128)(2,1)}, u32[]{:S(2)}, u32[]{:S(2)}) collective-permute-start(bf16[1024,1024]{1,0:T(8,128)(2,1)} %collective-permute-done.refs_3_.refs_9_), channel_id=1, source_target_pairs={{0,1},{1,0},{4,5},{5,4},{8,9},{9,8},{12,13},{13,12},{3,2},{2,3},{7... | collective-permute-start | bytes 6291464 | tf_op jit(solution)/shard_map/ppermute | solution.py:425
  71.7 16.5 %collective-permute-start.9 = (bf16[1024,1024]{1,0:T(8,128)(2,1)}, bf16[1024,1024]{1,0:T(8,128)(2,1)}, u32[]{:S(2)}, u32[]{:S(2)}) collective-permute-start(bf16[1024,1024]{1,0:T(8,128)(2,1)} %collective-permute-done.1.refs_1_.refs_4_), channel_id=1, source_target_pairs={{4,5},{5,4},{7,6},{6,7},{20,21},{21,20},{23,22},{22,23}} | collective-permute-start | bytes 6291464 | tf_op jit(solution)/shard_map/ppermute | solution.py:425
  73.7 5.2 %collective-permute-start.4 = (f32[1,1024]{1,0:T(1,128)}, f32[1,1024]{1,0:T(1,128)}, u32[]{:S(2)}, u32[]{:S(2)}) collective-permute-start(f32[1,1024]{1,0:T(1,128)} %get-tuple-element.26), channel_id=1, source_target_pairs={{0,3},{1,0},{2,1},{4,5},{5,7},{6,2},{7,6},{9,4},{10,9},{12,15},{13... | collective-permute-start | bytes 12296 | tf_op jit(solution)/shard_map/ppermute | solution.py:431
  79.0 9.2 %collective-permute-start.5 = (f32[1,1024]{1,0:T(1,128)}, f32[1,1024]{1,0:T(1,128)}, u32[]{:S(2)}, u32[]{:S(2)}) collective-permute-start(f32[1,1024]{1,0:T(1,128)} %get-tuple-element.27), channel_id=1, source_target_pairs={{4,6},{5,1},{6,4},{9,10},{10,11},{20,22},{21,17},{22,20},{25,26},{... | collective-permute-start | bytes 12296 | tf_op jit(solution)/shard_map/ppermute | solution.py:431
  96.9 11.1 %collective-permute-start.10 = (f32[1,1024]{1,0:T(1,128)}, f32[1,1024]{1,0:T(1,128)}, u32[]{:S(2)}, u32[]{:S(2)}) collective-permute-start(f32[1,1024]{1,0:T(1,128)} %get-tuple-element.33), channel_id=1, source_target_pairs={{0,1},{1,3},{2,6},{3,2},{4,7},{5,8},{6,14},{7,15},{8,5},{9,11},{11... | collective-permute-start | bytes 12296 | tf_op jit(solution)/shard_map/ppermute | solution.py:431
  98.8 9.2 %collective-permute-start.11 = (f32[1,1024]{1,0:T(1,128)}, f32[1,1024]{1,0:T(1,128)}, u32[]{:S(2)}, u32[]{:S(2)}) collective-permute-start(f32[1,1024]{1,0:T(1,128)} %get-tuple-element.34), channel_id=1, source_target_pairs={{0,2},{1,5},{2,3},{3,1},{4,12},{5,13},{6,11},{7,4},{8,10},{9,0},{1... | collective-permute-start | bytes 12296 | tf_op jit(solution)/shard_map/ppermute | solution.py:431
  105.3 5.2 %collective-permute-start.12 = (f32[1,1024]{1,0:T(1,128)}, f32[1,1024]{1,0:T(1,128)}, u32[]{:S(2)}, u32[]{:S(2)}) collective-permute-start(f32[1,1024]{1,0:T(1,128)} %get-tuple-element.35), channel_id=1, source_target_pairs={{0,4},{2,0},{3,7},{4,1},{5,2},{6,15},{7,5},{8,9},{9,8},{10,3},{11,... | collective-permute-start | bytes 12296 | tf_op jit(solution)/shard_map/ppermute | solution.py:431
  106.6 6.1 %collective-permute-start.13 = (f32[1,1024]{1,0:T(1,128)}, f32[1,1024]{1,0:T(1,128)}, u32[]{:S(2)}, u32[]{:S(2)}) collective-permute-start(f32[1,1024]{1,0:T(1,128)} %get-tuple-element.36), channel_id=1, source_target_pairs={{5,12},{6,1},{7,2},{8,11},{10,8},{11,10},{13,14},{14,15},{15,3},{2... | collective-permute-start | bytes 12296 | tf_op jit(solution)/shard_map/ppermute | solution.py:431

commit v16 on v15

--- a/solution.py
+++ b/solution.py
@@ -13,7 +13,7 @@
 FLOOR = -2.0
 MOST_PADS = 256
 AHEAD = 2
-FIRST, EARLY = 2, 2
+FIRST, EARLY = 4, 2
 
 
 class Move:
@@ -110,7 +110,7 @@
     ends = [of for of, _ in edges], [to for _, to in edges]
     most = max((side.count(device) for side in ends for device in range(count)), default=0)
     sends, takes = [{} for _ in range(count)], [{} for _ in range(count)]
-    for of, to in sorted(edges, key=lambda edge: (min(edge) >= FIRST, edge)):
+    for of, to in sorted(edges, key=lambda edge: (-abs(edge[0] - edge[1]) * (min(edge) < FIRST), edge)):
         both = next(c for c in range(2 * len(edges)) if c not in sends[of] and c not in takes[to])
         a = next(c for c in range(len(edges)) if c not in sends[of])
         b = next(c for c in range(len(edges)) if c not in takes[to])

time: 116 us -> 114 us (0.983)
  the two profiles are of different devices: /device:TPU:1 before, /device:TPU:8 now
where the time goes in v16:
time: 114 us
  waiting for transfers between devices  46.2 us (41%)
  Pallas kernels  36.8 us (32%)
  starting transfers between devices  30.4 us (27%)
    ppermute x8, waiting for transfers between devices, local(): slots[move.name] = lax.ppermute(value, 'blk', move.pairs)  31.5 us
    pallas_call x3, Pallas kernels, scored(): pl.pallas_call(functools.partial(pairs_kernel, len(given), len(sends), le...  25.9 us
    ppermute x8, starting transfers between devices, local(): slots[move.name] = lax.ppermute(value, 'blk', move.pairs)  15.6 us
    ppermute x6, starting transfers between devices, local(): lax.ppermute(row, 'blk', permute)  14.7 us
    ppermute x6, waiting for transfers between devices, local(): lax.ppermute(row, 'blk', permute)  14.7 us
    pallas_call x1, Pallas kernels, own_block(): pl.pallas_call(own_kernel, out_shape=jax.ShapeDtypeStruct((nblocks, rows)...  4.65 us
    pallas_call x1, Pallas kernels, normalized(): pl.pallas_call(unit_kernel, out_shape=jax.ShapeDtypeStruct((rows, depth),...  4.13 us
  transfers between devices with their start and end apart: 14, of which 5 were waited for; matrix products, arithmetic and copies ran while one was open for 0% of the time, Pallas kernels for 17%

profile of v16, /device:TPU:8, one launch (start us, length us, event | category | flops | bytes accessed | tf_op | source)
XLA Modules:
  0.0 113.5 jit_solution(4077788616060826557)
XLA Ops:
  0.0 4.1 %normalized.1.unit.refs_1_.refs_4_.refs_10_ = bf16[1024,1024]{1,0:T(8,128)(2,1)} custom-call(s32[16]{0:T(128)} %pads.5, s32[1024]{0:T(1024)} %order_smem.1, s32[1,1024]{1,0:T(1,128)} %bitcast.2, bf16[1024,1024]{1,0:T(8,128)(2,1)} %embeddings.1), custom_call_target="tpu_custom_call" | custom-call | flops 4194304 | bytes 4194304 | tf_op jit(solution)/shard_map/normalized/pallas_call | solution.py:205
  4.2 1.9 %collective-permute-start.1 = (bf16[1024,1024]{1,0:T(8,128)(2,1)}, bf16[1024,1024]{1,0:T(8,128)(2,1)}, u32[]{:S(2)}, u32[]{:S(2)}) collective-permute-start(bf16[1024,1024]{1,0:T(8,128)(2,1)} %normalized.1.unit.refs_1_.refs_4_.refs_10_), channel_id=1, source_target_pairs={{0,9},{8,13},{12,4},{4,0},{1,5},{3,10},{11,14},{15,7},{7,3},{2,6},... | collective-permute-start | bytes 6291464 | tf_op jit(solution)/shard_map/ppermute | solution.py:425
  6.1 4.3 %collective-permute-start.3 = (bf16[1024,1024]{1,0:T(8,128)(2,1)}, bf16[1024,1024]{1,0:T(8,128)(2,1)}, u32[]{:S(2)}, u32[]{:S(2)}) collective-permute-start(bf16[1024,1024]{1,0:T(8,128)(2,1)} %normalized.1.unit.refs_1_.refs_4_.refs_10_), channel_id=1, source_target_pairs={{13,5},{5,1},{9,12},{4,9},{14,6},{6,2},{10,15},{7,10},{29,21},{21,... | collective-permute-start | bytes 6291464 | tf_op jit(solution)/shard_map/ppermute | solution.py:425
  10.4 2.6 %collective-permute-start = (bf16[1024,1024]{1,0:T(8,128)(2,1)}, bf16[1024,1024]{1,0:T(8,128)(2,1)}, u32[]{:S(2)}, u32[]{:S(2)}) collective-permute-start(bf16[1024,1024]{1,0:T(8,128)(2,1)} %normalized.1.unit.refs_1_.refs_4_.refs_10_), channel_id=1, source_target_pairs={{0,3},{3,0},{1,2},{2,1},{8,11},{11,8},{9,10},{10,9},{12,15},{15,12... | collective-permute-start | bytes 6291464 | tf_op jit(solution)/shard_map/ppermute | solution.py:425
  13.0 4.6 %own_block.1.best = f32[16,1024]{1,0:T(8,128)} custom-call(s32[16]{0:T(128)} %pads.5, s32[1,1024]{1,0:T(1,128)} %bitcast.3, bf16[1024,1024]{1,0:T(8,128)(2,1)} %normalized.1.unit.refs_1_.refs_4_.refs_10_), custom_call_target="tpu_custom_call" | custom-call | flops 2147483648 | bytes 2097152 | tf_op jit(solution)/shard_map/own_block/pallas_call | solution.py:252
  17.6 6.1 %scored.3.best = f32[16,1024]{1,0:T(8,128)} custom-call(s32[144]{0:T(256)} %constant.8.clone.table, f32[16,1024]{1,0:T(8,128)} %own_block.1.best, bf16[1024,1024]{1,0:T(8,128)(2,1)} %collective-permute-done.2.refs_0_.refs_2_, bf16[1024,1024]{1,0:T(8,128)(2,1)} %normalized.1.unit.refs_1_.refs_4_.refs_10_), custom_call_target="tpu_custom_call" | custom-call | flops 2147483648 | bytes 4194304 | tf_op jit(solution)/shard_map/scored/pallas_call | solution.py:350
  23.7 31.3 %collective-permute-done.1.refs_1_.refs_4_ = bf16[1024,1024]{1,0:T(8,128)(2,1)} collective-permute-done((bf16[1024,1024]{1,0:T(8,128)(2,1)}, bf16[1024,1024]{1,0:T(8,128)(2,1)}, u32[]{:S(2)}, u32[]{:S(2)}) %collective-permute-start.1) | collective-permute-done | bytes 2097184 | tf_op jit(solution)/shard_map/ppermute | solution.py:425
  55.0 2.0 %collective-permute-start.7 = (bf16[1024,1024]{1,0:T(8,128)(2,1)}, bf16[1024,1024]{1,0:T(8,128)(2,1)}, u32[]{:S(2)}, u32[]{:S(2)}) collective-permute-start(bf16[1024,1024]{1,0:T(8,128)(2,1)} %normalized.1.unit.refs_1_.refs_4_.refs_10_), channel_id=1, source_target_pairs={{5,8},{8,5},{6,11},{11,6},{21,24},{24,21},{22,27},{27,22}} | collective-permute-start | bytes 6291464 | tf_op jit(solution)/shard_map/ppermute | solution.py:425
  57.0 2.0 %collective-permute-start.8 = (bf16[1024,1024]{1,0:T(8,128)(2,1)}, bf16[1024,1024]{1,0:T(8,128)(2,1)}, u32[]{:S(2)}, u32[]{:S(2)}) collective-permute-start(bf16[1024,1024]{1,0:T(8,128)(2,1)} %collective-permute-done.1.refs_1_.refs_4_), channel_id=1, source_target_pairs={{9,13},{10,15},{5,6},{6,5},{25,29},{26,31},{21,22},{22,21}} | collective-permute-start | bytes 6291464 | tf_op jit(solution)/shard_map/ppermute | solution.py:425
  59.0 0.2 collective-permute-done.refs_3_.refs_9_
  59.2 8.6 %scored.4 = (f32[16,1024]{1,0:T(8,128)}, f32[1,1024]{1,0:T(1,128)}, f32[1,1024]{1,0:T(1,128)}) custom-call(s32[464]{0:T(512)} %constant.9.clone.table, f32[16,1024]{1,0:T(8,128)} %scored.3.best, bf16[1024,1024]{1,0:T(8,128)(2,1)} %collective-permute-done.2.refs_0_.refs_2_, bf16[1024,1024]{1,0:T(8,128)(2,1)} %collective-permute-done.1.refs_1_.refs_4_, ...), custom_call_target="tpu_custom_call" | custom-call | flops 8589934592 | bytes 10485760 | tf_op jit(solution)/shard_map/scored/pallas_call | solution.py:350
  67.9 0.9 collective-permute-start.6
  68.8 1.9 %collective-permute-start.9 = (bf16[1024,1024]{1,0:T(8,128)(2,1)}, bf16[1024,1024]{1,0:T(8,128)(2,1)}, u32[]{:S(2)}, u32[]{:S(2)}) collective-permute-start(bf16[1024,1024]{1,0:T(8,128)(2,1)} %collective-permute-done.1.refs_1_.refs_4_), channel_id=1, source_target_pairs={{4,5},{5,4},{7,6},{6,7},{20,21},{21,20},{23,22},{22,23}} | collective-permute-start | bytes 6291464 | tf_op jit(solution)/shard_map/ppermute | solution.py:425
  70.7 2.4 %collective-permute-start.4 = (f32[1,1024]{1,0:T(1,128)}, f32[1,1024]{1,0:T(1,128)}, u32[]{:S(2)}, u32[]{:S(2)}) collective-permute-start(f32[1,1024]{1,0:T(1,128)} %get-tuple-element.26), channel_id=1, source_target_pairs={{0,3},{1,0},{4,5},{5,1},{6,2},{7,6},{9,4},{10,9},{12,15},{13,8},{1... | collective-permute-start | bytes 12296 | tf_op jit(solution)/shard_map/ppermute | solution.py:431
  73.1 6.9 %collective-permute-done.4.refs_0_ = f32[1,1024]{1,0:T(1,128)} collective-permute-done((f32[1,1024]{1,0:T(1,128)}, f32[1,1024]{1,0:T(1,128)}, u32[]{:S(2)}, u32[]{:S(2)}) %collective-permute-start.4) | collective-permute-done | bytes 4128 | tf_op jit(solution)/shard_map/ppermute | solution.py:431
  80.0 1.9 %collective-permute-start.5 = (f32[1,1024]{1,0:T(1,128)}, f32[1,1024]{1,0:T(1,128)}, u32[]{:S(2)}, u32[]{:S(2)}) collective-permute-start(f32[1,1024]{1,0:T(1,128)} %get-tuple-element.27), channel_id=1, source_target_pairs={{2,1},{4,6},{5,7},{6,4},{9,10},{10,11},{18,17},{20,22},{21,23},{22... | collective-permute-start | bytes 12296 | tf_op jit(solution)/shard_map/ppermute | solution.py:431
  81.9 3.9 %collective-permute-done.5.refs_1_ = f32[1,1024]{1,0:T(1,128)} collective-permute-done((f32[1,1024]{1,0:T(1,128)}, f32[1,1024]{1,0:T(1,128)}, u32[]{:S(2)}, u32[]{:S(2)}) %collective-permute-start.5) | collective-permute-done | bytes 4128 | tf_op jit(solution)/shard_map/ppermute | solution.py:431
  85.8 11.1 %scored.5 = (f32[16,1024]{1,0:T(8,128)}, f32[1,1024]{1,0:T(1,128)}, f32[1,1024]{1,0:T(1,128)}, f32[1,1024]{1,0:T(1,128)}, f32[1,1024]{1,0:T(1,128)}) custom-call(s32[528]{0:T(1024)} %constant.10.clone.table, f32[16,1024]{1,0:T(8,128)} %get-tuple-element.25.best, f32[1,1024]{1,0:T(1,128)} %collective-permute-done.4.refs_0_, ...), custom_call_target="tpu_custom_call" | custom-call | flops 8589934592 | bytes 10485760 | tf_op jit(solution)/shard_map/scored/pallas_call | solution.py:350
  96.9 1.9 %collective-permute-start.10 = (f32[1,1024]{1,0:T(1,128)}, f32[1,1024]{1,0:T(1,128)}, u32[]{:S(2)}, u32[]{:S(2)}) collective-permute-start(f32[1,1024]{1,0:T(1,128)} %get-tuple-element.33), channel_id=1, source_target_pairs={{0,4},{1,5},{2,6},{3,2},{4,12},{5,13},{6,1},{7,15},{8,9},{9,11},{1... | collective-permute-start | bytes 12296 | tf_op jit(solution)/shard_map/ppermute | solution.py:431
  98.9 4.6 %collective-permute-start.11 = (f32[1,1024]{1,0:T(1,128)}, f32[1,1024]{1,0:T(1,128)}, u32[]{:S(2)}, u32[]{:S(2)}) collective-permute-start(f32[1,1024]{1,0:T(1,128)} %get-tuple-element.34), channel_id=1, source_target_pairs={{4,1},{5,8},{6,14},{7,2},{8,11},{9,0},{10,3},{11,6},{12,9},{13,12}... | collective-permute-start | bytes 12296 | tf_op jit(solution)/shard_map/ppermute | solution.py:431
  103.5 2.7 %collective-permute-start.12 = (f32[1,1024]{1,0:T(1,128)}, f32[1,1024]{1,0:T(1,128)}, u32[]{:S(2)}, u32[]{:S(2)}) collective-permute-start(f32[1,1024]{1,0:T(1,128)} %get-tuple-element.35), channel_id=1, source_target_pairs={{0,2},{1,3},{2,0},{3,1},{4,7},{5,12},{6,15},{7,5},{8,10},{9,8},{11... | collective-permute-start | bytes 12296 | tf_op jit(solution)/shard_map/ppermute | solution.py:431
  106.1 1.3 %collective-permute-start.13 = (f32[1,1024]{1,0:T(1,128)}, f32[1,1024]{1,0:T(1,128)}, u32[]{:S(2)}, u32[]{:S(2)}) collective-permute-start(f32[1,1024]{1,0:T(1,128)} %get-tuple-element.36), channel_id=1, source_target_pairs={{0,1},{2,3},{3,7},{5,2},{6,11},{7,4},{8,5},{10,8},{11,10},{12,13},... | collective-permute-start | bytes 12296 | tf_op jit(solution)/shard_map/ppermute | solution.py:431
  107.4 3.9 %collective-permute-done.13.refs_3_ = f32[1,1024]{1,0:T(1,128)} collective-permute-done((f32[1,1024]{1,0:T(1,128)}, f32[1,1024]{1,0:T(1,128)}, u32[]{:S(2)}, u32[]{:S(2)}) %collective-permute-start.13) | collective-permute-done | bytes 4128 | tf_op jit(solution)/shard_map/ppermute | solution.py:431
  111.3 2.2 %placed.1 = f32[1,1024]{1,0:T(1,128)} custom-call(s32[64]{0:T(128)} %constant.11.clone.taken, s32[16]{0:T(128)} %pads.5, s32[1,1024]{1,0:T(1,128)} %bitcast.4, f32[16,1024]{1,0:T(8,128)} %get-tuple-element.32.best, f32[1,1024]{1,0:T(1,128)} %collective-permute-done.10.refs_0_, f32[1,1024]{1,0:T(1,128)} %collective-permute-done.11.refs_1_, ...), custom_call_target="tpu_custom_call" | custom-call | tf_op jit(solution)/shard_map/placed/pallas_call | solution.py:393
  (10 shorter events, 0.1 us)
Async XLA Ops:
  4.1 13.5 %collective-permute-start.2 = (bf16[1024,1024]{1,0:T(8,128)(2,1)}, bf16[1024,1024]{1,0:T(8,128)(2,1)}, u32[]{:S(2)}, u32[]{:S(2)}) collective-permute-start(bf16[1024,1024]{1,0:T(8,128)(2,1)} %normalized.1.unit.refs_1_.refs_4_.refs_10_), channel_id=1, source_target_pairs={{0,1},{1,0},{4,5},{5,4},{8,9},{9,8},{12,13},{13,12},{3,2},{2,3},{7... | collective-permute-start | bytes 6291464 | tf_op jit(solution)/shard_map/ppermute | solution.py:425
  4.2 50.8 %collective-permute-start.1 = (bf16[1024,1024]{1,0:T(8,128)(2,1)}, bf16[1024,1024]{1,0:T(8,128)(2,1)}, u32[]{:S(2)}, u32[]{:S(2)}) collective-permute-start(bf16[1024,1024]{1,0:T(8,128)(2,1)} %normalized.1.unit.refs_1_.refs_4_.refs_10_), channel_id=1, source_target_pairs={{0,9},{8,13},{12,4},{4,0},{1,5},{3,10},{11,14},{15,7},{7,3},{2,6},... | collective-permute-start | bytes 6291464 | tf_op jit(solution)/shard_map/ppermute | solution.py:425
  6.1 52.9 %collective-permute-start.3 = (bf16[1024,1024]{1,0:T(8,128)(2,1)}, bf16[1024,1024]{1,0:T(8,128)(2,1)}, u32[]{:S(2)}, u32[]{:S(2)}) collective-permute-start(bf16[1024,1024]{1,0:T(8,128)(2,1)} %normalized.1.unit.refs_1_.refs_4_.refs_10_), channel_id=1, source_target_pairs={{13,5},{5,1},{9,12},{4,9},{14,6},{6,2},{10,15},{7,10},{29,21},{21,... | collective-permute-start | bytes 6291464 | tf_op jit(solution)/shard_map/ppermute | solution.py:425
  10.4 48.8 %collective-permute-start = (bf16[1024,1024]{1,0:T(8,128)(2,1)}, bf16[1024,1024]{1,0:T(8,128)(2,1)}, u32[]{:S(2)}, u32[]{:S(2)}) collective-permute-start(bf16[1024,1024]{1,0:T(8,128)(2,1)} %normalized.1.unit.refs_1_.refs_4_.refs_10_), channel_id=1, source_target_pairs={{0,3},{3,0},{1,2},{2,1},{8,11},{11,8},{9,10},{10,9},{12,15},{15,12... | collective-permute-start | bytes 6291464 | tf_op jit(solution)/shard_map/ppermute | solution.py:425
  55.0 30.7 %collective-permute-start.7 = (bf16[1024,1024]{1,0:T(8,128)(2,1)}, bf16[1024,1024]{1,0:T(8,128)(2,1)}, u32[]{:S(2)}, u32[]{:S(2)}) collective-permute-start(bf16[1024,1024]{1,0:T(8,128)(2,1)} %normalized.1.unit.refs_1_.refs_4_.refs_10_), channel_id=1, source_target_pairs={{5,8},{8,5},{6,11},{11,6},{21,24},{24,21},{22,27},{27,22}} | collective-permute-start | bytes 6291464 | tf_op jit(solution)/shard_map/ppermute | solution.py:425
  57.0 28.8 %collective-permute-start.8 = (bf16[1024,1024]{1,0:T(8,128)(2,1)}, bf16[1024,1024]{1,0:T(8,128)(2,1)}, u32[]{:S(2)}, u32[]{:S(2)}) collective-permute-start(bf16[1024,1024]{1,0:T(8,128)(2,1)} %collective-permute-done.1.refs_1_.refs_4_), channel_id=1, source_target_pairs={{9,13},{10,15},{5,6},{6,5},{25,29},{26,31},{21,22},{22,21}} | collective-permute-start | bytes 6291464 | tf_op jit(solution)/shard_map/ppermute | solution.py:425
  67.9 17.9 %collective-permute-start.6 = (bf16[1024,1024]{1,0:T(8,128)(2,1)}, bf16[1024,1024]{1,0:T(8,128)(2,1)}, u32[]{:S(2)}, u32[]{:S(2)}) collective-permute-start(bf16[1024,1024]{1,0:T(8,128)(2,1)} %collective-permute-done.refs_3_.refs_9_), channel_id=1, source_target_pairs={{0,1},{1,0},{4,5},{5,4},{8,9},{9,8},{12,13},{13,12},{3,2},{2,3},{7... | collective-permute-start | bytes 6291464 | tf_op jit(solution)/shard_map/ppermute | solution.py:425
  68.8 17.0 %collective-permute-start.9 = (bf16[1024,1024]{1,0:T(8,128)(2,1)}, bf16[1024,1024]{1,0:T(8,128)(2,1)}, u32[]{:S(2)}, u32[]{:S(2)}) collective-permute-start(bf16[1024,1024]{1,0:T(8,128)(2,1)} %collective-permute-done.1.refs_1_.refs_4_), channel_id=1, source_target_pairs={{4,5},{5,4},{7,6},{6,7},{20,21},{21,20},{23,22},{22,23}} | collective-permute-start | bytes 6291464 | tf_op jit(solution)/shard_map/ppermute | solution.py:425
  70.7 9.3 %collective-permute-start.4 = (f32[1,1024]{1,0:T(1,128)}, f32[1,1024]{1,0:T(1,128)}, u32[]{:S(2)}, u32[]{:S(2)}) collective-permute-start(f32[1,1024]{1,0:T(1,128)} %get-tuple-element.26), channel_id=1, source_target_pairs={{0,3},{1,0},{4,5},{5,1},{6,2},{7,6},{9,4},{10,9},{12,15},{13,8},{1... | collective-permute-start | bytes 12296 | tf_op jit(solution)/shard_map/ppermute | solution.py:431
  80.0 5.8 %collective-permute-start.5 = (f32[1,1024]{1,0:T(1,128)}, f32[1,1024]{1,0:T(1,128)}, u32[]{:S(2)}, u32[]{:S(2)}) collective-permute-start(f32[1,1024]{1,0:T(1,128)} %get-tuple-element.27), channel_id=1, source_target_pairs={{2,1},{4,6},{5,7},{6,4},{9,10},{10,11},{18,17},{20,22},{21,23},{22... | collective-permute-start | bytes 12296 | tf_op jit(solution)/shard_map/ppermute | solution.py:431
  96.9 10.5 %collective-permute-start.10 = (f32[1,1024]{1,0:T(1,128)}, f32[1,1024]{1,0:T(1,128)}, u32[]{:S(2)}, u32[]{:S(2)}) collective-permute-start(f32[1,1024]{1,0:T(1,128)} %get-tuple-element.33), channel_id=1, source_target_pairs={{0,4},{1,5},{2,6},{3,2},{4,12},{5,13},{6,1},{7,15},{8,9},{9,11},{1... | collective-permute-start | bytes 12296 | tf_op jit(solution)/shard_map/ppermute | solution.py:431
  98.9 8.5 %collective-permute-start.11 = (f32[1,1024]{1,0:T(1,128)}, f32[1,1024]{1,0:T(1,128)}, u32[]{:S(2)}, u32[]{:S(2)}) collective-permute-start(f32[1,1024]{1,0:T(1,128)} %get-tuple-element.34), channel_id=1, source_target_pairs={{4,1},{5,8},{6,14},{7,2},{8,11},{9,0},{10,3},{11,6},{12,9},{13,12}... | collective-permute-start | bytes 12296 | tf_op jit(solution)/shard_map/ppermute | solution.py:431
  103.5 4.0 %collective-permute-start.12 = (f32[1,1024]{1,0:T(1,128)}, f32[1,1024]{1,0:T(1,128)}, u32[]{:S(2)}, u32[]{:S(2)}) collective-permute-start(f32[1,1024]{1,0:T(1,128)} %get-tuple-element.35), channel_id=1, source_target_pairs={{0,2},{1,3},{2,0},{3,1},{4,7},{5,12},{6,15},{7,5},{8,10},{9,8},{11... | collective-permute-start | bytes 12296 | tf_op jit(solution)/shard_map/ppermute | solution.py:431
  106.1 5.2 %collective-permute-start.13 = (f32[1,1024]{1,0:T(1,128)}, f32[1,1024]{1,0:T(1,128)}, u32[]{:S(2)}, u32[]{:S(2)}) collective-permute-start(f32[1,1024]{1,0:T(1,128)} %get-tuple-element.36), channel_id=1, source_target_pairs={{0,1},{2,3},{3,7},{5,2},{6,11},{7,4},{8,5},{10,8},{11,10},{12,13},... | collective-permute-start | bytes 12296 | tf_op jit(solution)/shard_map/ppermute | solution.py:431

commit v17 on v16

--- a/solution.py
+++ b/solution.py
@@ -110,7 +110,7 @@
     ends = [of for of, _ in edges], [to for _, to in edges]
     most = max((side.count(device) for side in ends for device in range(count)), default=0)
     sends, takes = [{} for _ in range(count)], [{} for _ in range(count)]
-    for of, to in sorted(edges, key=lambda edge: (-abs(edge[0] - edge[1]) * (min(edge) < FIRST), edge)):
+    for of, to in sorted(edges, key=lambda edge: (min(edge) >= FIRST, -abs(edge[0] - edge[1]), edge)):
         both = next(c for c in range(2 * len(edges)) if c not in sends[of] and c not in takes[to])
         a = next(c for c in range(len(edges)) if c not in sends[of])
         b = next(c for c in range(len(edges)) if c not in takes[to])

time: 114 us -> 114 us (level)
  the two profiles are of different devices: /device:TPU:8 before, /device:TPU:21 now
where the time goes in v17:
time: 114 us; the launch traced here: 113 us
  starting transfers between devices  41.6 us (36%)
  Pallas kernels  36.8 us (32%)
  waiting for transfers between devices  34.5 us (30%)
    ppermute x8, starting transfers between devices, local(): slots[move.name] = lax.ppermute(value, 'blk', move.pairs)  27.5 us
    ppermute x8, waiting for transfers between devices, local(): slots[move.name] = lax.ppermute(value, 'blk', move.pairs)  27.3 us
    pallas_call x3, Pallas kernels, scored(): pl.pallas_call(functools.partial(pairs_kernel, len(given), len(sends), le...  25.9 us
    ppermute x6, starting transfers between devices, local(): lax.ppermute(row, 'blk', permute)  14.1 us
    ppermute x6, waiting for transfers between devices, local(): lax.ppermute(row, 'blk', permute)  7.19 us
    pallas_call x1, Pallas kernels, own_block(): pl.pallas_call(own_kernel, out_shape=jax.ShapeDtypeStruct((nblocks, rows)...  4.65 us
    pallas_call x1, Pallas kernels, normalized(): pl.pallas_call(unit_kernel, out_shape=jax.ShapeDtypeStruct((rows, depth),...  4.13 us
  transfers between devices with their start and end apart: 14, of which 4 were waited for; matrix products, arithmetic and copies ran while one was open for 0% of the time, Pallas kernels for 15%

profile of v17, /device:TPU:21, one launch (start us, length us, event | category | flops | bytes accessed | tf_op | source)
XLA Modules:
  0.0 113.1 jit_solution(7579796231308987556)
XLA Ops:
  0.0 4.1 %normalized.1.unit.refs_1_.refs_4_.refs_10_ = bf16[1024,1024]{1,0:T(8,128)(2,1)} custom-call(s32[16]{0:T(128)} %pads.5, s32[1024]{0:T(1024)} %order_smem.1, s32[1,1024]{1,0:T(1,128)} %bitcast.2, bf16[1024,1024]{1,0:T(8,128)(2,1)} %embeddings.1), custom_call_target="tpu_custom_call" | custom-call | flops 4194304 | bytes 4194304 | tf_op jit(solution)/shard_map/normalized/pallas_call | solution.py:205
  4.1 0.7 collective-permute-start.2
  4.9 4.5 %collective-permute-start.1 = (bf16[1024,1024]{1,0:T(8,128)(2,1)}, bf16[1024,1024]{1,0:T(8,128)(2,1)}, u32[]{:S(2)}, u32[]{:S(2)}) collective-permute-start(bf16[1024,1024]{1,0:T(8,128)(2,1)} %normalized.1.unit.refs_1_.refs_4_.refs_10_), channel_id=1, source_target_pairs={{0,9},{8,13},{12,4},{4,0},{1,5},{3,10},{11,14},{15,7},{7,3},{2,6},... | collective-permute-start | bytes 6291464 | tf_op jit(solution)/shard_map/ppermute | solution.py:425
  9.3 2.0 %collective-permute-start.3 = (bf16[1024,1024]{1,0:T(8,128)(2,1)}, bf16[1024,1024]{1,0:T(8,128)(2,1)}, u32[]{:S(2)}, u32[]{:S(2)}) collective-permute-start(bf16[1024,1024]{1,0:T(8,128)(2,1)} %normalized.1.unit.refs_1_.refs_4_.refs_10_), channel_id=1, source_target_pairs={{13,5},{5,1},{9,12},{4,9},{14,6},{6,2},{10,15},{7,10},{29,21},{21,... | collective-permute-start | bytes 6291464 | tf_op jit(solution)/shard_map/ppermute | solution.py:425
  11.3 0.6 collective-permute-start
  11.9 4.6 %own_block.1.best = f32[16,1024]{1,0:T(8,128)} custom-call(s32[16]{0:T(128)} %pads.5, s32[1,1024]{1,0:T(1,128)} %bitcast.3, bf16[1024,1024]{1,0:T(8,128)(2,1)} %normalized.1.unit.refs_1_.refs_4_.refs_10_), custom_call_target="tpu_custom_call" | custom-call | flops 2147483648 | bytes 2097152 | tf_op jit(solution)/shard_map/own_block/pallas_call | solution.py:252
  16.6 6.1 %scored.3.best = f32[16,1024]{1,0:T(8,128)} custom-call(s32[144]{0:T(256)} %constant.8.clone.table, f32[16,1024]{1,0:T(8,128)} %own_block.1.best, bf16[1024,1024]{1,0:T(8,128)(2,1)} %collective-permute-done.2.refs_0_.refs_2_, bf16[1024,1024]{1,0:T(8,128)(2,1)} %normalized.1.unit.refs_1_.refs_4_.refs_10_), custom_call_target="tpu_custom_call" | custom-call | flops 2147483648 | bytes 4194304 | tf_op jit(solution)/shard_map/scored/pallas_call | solution.py:350
  22.7 27.0 %collective-permute-done.1.refs_1_.refs_4_ = bf16[1024,1024]{1,0:T(8,128)(2,1)} collective-permute-done((bf16[1024,1024]{1,0:T(8,128)(2,1)}, bf16[1024,1024]{1,0:T(8,128)(2,1)}, u32[]{:S(2)}, u32[]{:S(2)}) %collective-permute-start.1) | collective-permute-done | bytes 2097184 | tf_op jit(solution)/shard_map/ppermute | solution.py:425
  49.7 7.5 %collective-permute-start.7 = (bf16[1024,1024]{1,0:T(8,128)(2,1)}, bf16[1024,1024]{1,0:T(8,128)(2,1)}, u32[]{:S(2)}, u32[]{:S(2)}) collective-permute-start(bf16[1024,1024]{1,0:T(8,128)(2,1)} %normalized.1.unit.refs_1_.refs_4_.refs_10_), channel_id=1, source_target_pairs={{5,8},{8,5},{6,11},{11,6},{21,24},{24,21},{22,27},{27,22}} | collective-permute-start | bytes 6291464 | tf_op jit(solution)/shard_map/ppermute | solution.py:425
  57.2 2.0 %collective-permute-start.8 = (bf16[1024,1024]{1,0:T(8,128)(2,1)}, bf16[1024,1024]{1,0:T(8,128)(2,1)}, u32[]{:S(2)}, u32[]{:S(2)}) collective-permute-start(bf16[1024,1024]{1,0:T(8,128)(2,1)} %collective-permute-done.1.refs_1_.refs_4_), channel_id=1, source_target_pairs={{9,13},{10,15},{5,6},{6,5},{25,29},{26,31},{21,22},{22,21}} | collective-permute-start | bytes 6291464 | tf_op jit(solution)/shard_map/ppermute | solution.py:425
  59.2 0.3 collective-permute-done.refs_3_.refs_9_
  59.5 6.1 %scored.4 = (f32[16,1024]{1,0:T(8,128)}, f32[1,1024]{1,0:T(1,128)}, f32[1,1024]{1,0:T(1,128)}) custom-call(s32[464]{0:T(512)} %constant.9.clone.table, f32[16,1024]{1,0:T(8,128)} %scored.3.best, bf16[1024,1024]{1,0:T(8,128)(2,1)} %collective-permute-done.2.refs_0_.refs_2_, bf16[1024,1024]{1,0:T(8,128)(2,1)} %collective-permute-done.1.refs_1_.refs_4_, ...), custom_call_target="tpu_custom_call" | custom-call | flops 8589934592 | bytes 10485760 | tf_op jit(solution)/shard_map/scored/pallas_call | solution.py:350
  65.7 8.2 %collective-permute-start.6 = (bf16[1024,1024]{1,0:T(8,128)(2,1)}, bf16[1024,1024]{1,0:T(8,128)(2,1)}, u32[]{:S(2)}, u32[]{:S(2)}) collective-permute-start(bf16[1024,1024]{1,0:T(8,128)(2,1)} %collective-permute-done.refs_3_.refs_9_), channel_id=1, source_target_pairs={{0,1},{1,0},{4,5},{5,4},{8,9},{9,8},{12,13},{13,12},{3,2},{2,3},{7... | collective-permute-start | bytes 6291464 | tf_op jit(solution)/shard_map/ppermute | solution.py:425
  73.9 2.0 %collective-permute-start.9 = (bf16[1024,1024]{1,0:T(8,128)(2,1)}, bf16[1024,1024]{1,0:T(8,128)(2,1)}, u32[]{:S(2)}, u32[]{:S(2)}) collective-permute-start(bf16[1024,1024]{1,0:T(8,128)(2,1)} %collective-permute-done.1.refs_1_.refs_4_), channel_id=1, source_target_pairs={{4,5},{5,4},{7,6},{6,7},{20,21},{21,20},{23,22},{22,23}} | collective-permute-start | bytes 6291464 | tf_op jit(solution)/shard_map/ppermute | solution.py:425
  75.9 1.2 %collective-permute-start.4 = (f32[1,1024]{1,0:T(1,128)}, f32[1,1024]{1,0:T(1,128)}, u32[]{:S(2)}, u32[]{:S(2)}) collective-permute-start(f32[1,1024]{1,0:T(1,128)} %get-tuple-element.26), channel_id=1, source_target_pairs={{0,3},{1,0},{4,6},{5,1},{6,2},{9,4},{10,9},{12,15},{13,8},{14,13},... | collective-permute-start | bytes 12296 | tf_op jit(solution)/shard_map/ppermute | solution.py:431
  77.1 1.3 %collective-permute-start.5 = (f32[1,1024]{1,0:T(1,128)}, f32[1,1024]{1,0:T(1,128)}, u32[]{:S(2)}, u32[]{:S(2)}) collective-permute-start(f32[1,1024]{1,0:T(1,128)} %get-tuple-element.27), channel_id=1, source_target_pairs={{2,1},{4,5},{5,7},{6,4},{7,6},{9,10},{10,11},{18,17},{20,21},{21,2... | collective-permute-start | bytes 12296 | tf_op jit(solution)/shard_map/ppermute | solution.py:431
  78.4 3.9 %collective-permute-done.5.refs_1_ = f32[1,1024]{1,0:T(1,128)} collective-permute-done((f32[1,1024]{1,0:T(1,128)}, f32[1,1024]{1,0:T(1,128)}, u32[]{:S(2)}, u32[]{:S(2)}) %collective-permute-start.5) | collective-permute-done | bytes 4128 | tf_op jit(solution)/shard_map/ppermute | solution.py:431
  82.3 13.6 %scored.5 = (f32[16,1024]{1,0:T(8,128)}, f32[1,1024]{1,0:T(1,128)}, f32[1,1024]{1,0:T(1,128)}, f32[1,1024]{1,0:T(1,128)}, f32[1,1024]{1,0:T(1,128)}) custom-call(s32[528]{0:T(1024)} %constant.10.clone.table, f32[16,1024]{1,0:T(8,128)} %get-tuple-element.25.best, f32[1,1024]{1,0:T(1,128)} %collective-permute-done.4.refs_0_, ...), custom_call_target="tpu_custom_call" | custom-call | flops 8589934592 | bytes 10485760 | tf_op jit(solution)/shard_map/scored/pallas_call | solution.py:350
  96.0 2.0 %collective-permute-start.10 = (f32[1,1024]{1,0:T(1,128)}, f32[1,1024]{1,0:T(1,128)}, u32[]{:S(2)}, u32[]{:S(2)}) collective-permute-start(f32[1,1024]{1,0:T(1,128)} %get-tuple-element.33), channel_id=1, source_target_pairs={{0,4},{1,3},{3,1},{4,7},{5,12},{6,14},{7,2},{8,11},{9,8},{11,6},{1... | collective-permute-start | bytes 12296 | tf_op jit(solution)/shard_map/ppermute | solution.py:431
  98.0 3.5 %collective-permute-start.11 = (f32[1,1024]{1,0:T(1,128)}, f32[1,1024]{1,0:T(1,128)}, u32[]{:S(2)}, u32[]{:S(2)}) collective-permute-start(f32[1,1024]{1,0:T(1,128)} %get-tuple-element.34), channel_id=1, source_target_pairs={{2,6},{4,1},{5,2},{6,15},{7,4},{8,5},{9,0},{10,3},{11,8},{12,14},{... | collective-permute-start | bytes 12296 | tf_op jit(solution)/shard_map/ppermute | solution.py:431
  101.5 4.1 %collective-permute-start.12 = (f32[1,1024]{1,0:T(1,128)}, f32[1,1024]{1,0:T(1,128)}, u32[]{:S(2)}, u32[]{:S(2)}) collective-permute-start(f32[1,1024]{1,0:T(1,128)} %get-tuple-element.35), channel_id=1, source_target_pairs={{0,2},{1,5},{2,0},{3,7},{4,12},{5,13},{6,1},{7,15},{8,10},{9,11},{... | collective-permute-start | bytes 12296 | tf_op jit(solution)/shard_map/ppermute | solution.py:431
  105.7 1.9 %collective-permute-start.13 = (f32[1,1024]{1,0:T(1,128)}, f32[1,1024]{1,0:T(1,128)}, u32[]{:S(2)}, u32[]{:S(2)}) collective-permute-start(f32[1,1024]{1,0:T(1,128)} %get-tuple-element.36), channel_id=1, source_target_pairs={{0,1},{2,3},{3,2},{5,8},{6,11},{7,5},{8,9},{10,7},{11,10},{12,13},... | collective-permute-start | bytes 12296 | tf_op jit(solution)/shard_map/ppermute | solution.py:431
  107.6 3.3 %collective-permute-done.13.refs_3_ = f32[1,1024]{1,0:T(1,128)} collective-permute-done((f32[1,1024]{1,0:T(1,128)}, f32[1,1024]{1,0:T(1,128)}, u32[]{:S(2)}, u32[]{:S(2)}) %collective-permute-start.13) | collective-permute-done | bytes 4128 | tf_op jit(solution)/shard_map/ppermute | solution.py:431
  110.9 2.2 %placed.1 = f32[1,1024]{1,0:T(1,128)} custom-call(s32[64]{0:T(128)} %constant.11.clone.taken, s32[16]{0:T(128)} %pads.5, s32[1,1024]{1,0:T(1,128)} %bitcast.4, f32[16,1024]{1,0:T(8,128)} %get-tuple-element.32.best, f32[1,1024]{1,0:T(1,128)} %collective-permute-done.10.refs_0_, f32[1,1024]{1,0:T(1,128)} %collective-permute-done.11.refs_1_, ...), custom_call_target="tpu_custom_call" | custom-call | tf_op jit(solution)/shard_map/placed/pallas_call | solution.py:393
  (10 shorter events, 0.0 us)
Async XLA Ops:
  4.1 12.4 %collective-permute-start.2 = (bf16[1024,1024]{1,0:T(8,128)(2,1)}, bf16[1024,1024]{1,0:T(8,128)(2,1)}, u32[]{:S(2)}, u32[]{:S(2)}) collective-permute-start(bf16[1024,1024]{1,0:T(8,128)(2,1)} %normalized.1.unit.refs_1_.refs_4_.refs_10_), channel_id=1, source_target_pairs={{0,1},{1,0},{4,5},{5,4},{8,9},{9,8},{12,13},{13,12},{3,2},{2,3},{7... | collective-permute-start | bytes 6291464 | tf_op jit(solution)/shard_map/ppermute | solution.py:425
  4.9 44.8 %collective-permute-start.1 = (bf16[1024,1024]{1,0:T(8,128)(2,1)}, bf16[1024,1024]{1,0:T(8,128)(2,1)}, u32[]{:S(2)}, u32[]{:S(2)}) collective-permute-start(bf16[1024,1024]{1,0:T(8,128)(2,1)} %normalized.1.unit.refs_1_.refs_4_.refs_10_), channel_id=1, source_target_pairs={{0,9},{8,13},{12,4},{4,0},{1,5},{3,10},{11,14},{15,7},{7,3},{2,6},... | collective-permute-start | bytes 6291464 | tf_op jit(solution)/shard_map/ppermute | solution.py:425
  9.3 49.9 %collective-permute-start.3 = (bf16[1024,1024]{1,0:T(8,128)(2,1)}, bf16[1024,1024]{1,0:T(8,128)(2,1)}, u32[]{:S(2)}, u32[]{:S(2)}) collective-permute-start(bf16[1024,1024]{1,0:T(8,128)(2,1)} %normalized.1.unit.refs_1_.refs_4_.refs_10_), channel_id=1, source_target_pairs={{13,5},{5,1},{9,12},{4,9},{14,6},{6,2},{10,15},{7,10},{29,21},{21,... | collective-permute-start | bytes 6291464 | tf_op jit(solution)/shard_map/ppermute | solution.py:425
  11.3 48.2 %collective-permute-start = (bf16[1024,1024]{1,0:T(8,128)(2,1)}, bf16[1024,1024]{1,0:T(8,128)(2,1)}, u32[]{:S(2)}, u32[]{:S(2)}) collective-permute-start(bf16[1024,1024]{1,0:T(8,128)(2,1)} %normalized.1.unit.refs_1_.refs_4_.refs_10_), channel_id=1, source_target_pairs={{0,3},{3,0},{1,2},{2,1},{8,11},{11,8},{9,10},{10,9},{12,15},{15,12... | collective-permute-start | bytes 6291464 | tf_op jit(solution)/shard_map/ppermute | solution.py:425
  49.7 32.6 %collective-permute-start.7 = (bf16[1024,1024]{1,0:T(8,128)(2,1)}, bf16[1024,1024]{1,0:T(8,128)(2,1)}, u32[]{:S(2)}, u32[]{:S(2)}) collective-permute-start(bf16[1024,1024]{1,0:T(8,128)(2,1)} %normalized.1.unit.refs_1_.refs_4_.refs_10_), channel_id=1, source_target_pairs={{5,8},{8,5},{6,11},{11,6},{21,24},{24,21},{22,27},{27,22}} | collective-permute-start | bytes 6291464 | tf_op jit(solution)/shard_map/ppermute | solution.py:425
  57.2 25.1 %collective-permute-start.8 = (bf16[1024,1024]{1,0:T(8,128)(2,1)}, bf16[1024,1024]{1,0:T(8,128)(2,1)}, u32[]{:S(2)}, u32[]{:S(2)}) collective-permute-start(bf16[1024,1024]{1,0:T(8,128)(2,1)} %collective-permute-done.1.refs_1_.refs_4_), channel_id=1, source_target_pairs={{9,13},{10,15},{5,6},{6,5},{25,29},{26,31},{21,22},{22,21}} | collective-permute-start | bytes 6291464 | tf_op jit(solution)/shard_map/ppermute | solution.py:425
  65.7 16.6 %collective-permute-start.6 = (bf16[1024,1024]{1,0:T(8,128)(2,1)}, bf16[1024,1024]{1,0:T(8,128)(2,1)}, u32[]{:S(2)}, u32[]{:S(2)}) collective-permute-start(bf16[1024,1024]{1,0:T(8,128)(2,1)} %collective-permute-done.refs_3_.refs_9_), channel_id=1, source_target_pairs={{0,1},{1,0},{4,5},{5,4},{8,9},{9,8},{12,13},{13,12},{3,2},{2,3},{7... | collective-permute-start | bytes 6291464 | tf_op jit(solution)/shard_map/ppermute | solution.py:425
  73.9 8.4 %collective-permute-start.9 = (bf16[1024,1024]{1,0:T(8,128)(2,1)}, bf16[1024,1024]{1,0:T(8,128)(2,1)}, u32[]{:S(2)}, u32[]{:S(2)}) collective-permute-start(bf16[1024,1024]{1,0:T(8,128)(2,1)} %collective-permute-done.1.refs_1_.refs_4_), channel_id=1, source_target_pairs={{4,5},{5,4},{7,6},{6,7},{20,21},{21,20},{23,22},{22,23}} | collective-permute-start | bytes 6291464 | tf_op jit(solution)/shard_map/ppermute | solution.py:425
  75.9 1.2 %collective-permute-start.4 = (f32[1,1024]{1,0:T(1,128)}, f32[1,1024]{1,0:T(1,128)}, u32[]{:S(2)}, u32[]{:S(2)}) collective-permute-start(f32[1,1024]{1,0:T(1,128)} %get-tuple-element.26), channel_id=1, source_target_pairs={{0,3},{1,0},{4,6},{5,1},{6,2},{9,4},{10,9},{12,15},{13,8},{14,13},... | collective-permute-start | bytes 12296 | tf_op jit(solution)/shard_map/ppermute | solution.py:431
  77.1 5.2 %collective-permute-start.5 = (f32[1,1024]{1,0:T(1,128)}, f32[1,1024]{1,0:T(1,128)}, u32[]{:S(2)}, u32[]{:S(2)}) collective-permute-start(f32[1,1024]{1,0:T(1,128)} %get-tuple-element.27), channel_id=1, source_target_pairs={{2,1},{4,5},{5,7},{6,4},{7,6},{9,10},{10,11},{18,17},{20,21},{21,2... | collective-permute-start | bytes 12296 | tf_op jit(solution)/shard_map/ppermute | solution.py:431
  96.0 11.7 %collective-permute-start.10 = (f32[1,1024]{1,0:T(1,128)}, f32[1,1024]{1,0:T(1,128)}, u32[]{:S(2)}, u32[]{:S(2)}) collective-permute-start(f32[1,1024]{1,0:T(1,128)} %get-tuple-element.33), channel_id=1, source_target_pairs={{0,4},{1,3},{3,1},{4,7},{5,12},{6,14},{7,2},{8,11},{9,8},{11,6},{1... | collective-permute-start | bytes 12296 | tf_op jit(solution)/shard_map/ppermute | solution.py:431
  98.0 9.6 %collective-permute-start.11 = (f32[1,1024]{1,0:T(1,128)}, f32[1,1024]{1,0:T(1,128)}, u32[]{:S(2)}, u32[]{:S(2)}) collective-permute-start(f32[1,1024]{1,0:T(1,128)} %get-tuple-element.34), channel_id=1, source_target_pairs={{2,6},{4,1},{5,2},{6,15},{7,4},{8,5},{9,0},{10,3},{11,8},{12,14},{... | collective-permute-start | bytes 12296 | tf_op jit(solution)/shard_map/ppermute | solution.py:431
  101.5 6.1 %collective-permute-start.12 = (f32[1,1024]{1,0:T(1,128)}, f32[1,1024]{1,0:T(1,128)}, u32[]{:S(2)}, u32[]{:S(2)}) collective-permute-start(f32[1,1024]{1,0:T(1,128)} %get-tuple-element.35), channel_id=1, source_target_pairs={{0,2},{1,5},{2,0},{3,7},{4,12},{5,13},{6,1},{7,15},{8,10},{9,11},{... | collective-permute-start | bytes 12296 | tf_op jit(solution)/shard_map/ppermute | solution.py:431
  105.7 5.2 %collective-permute-start.13 = (f32[1,1024]{1,0:T(1,128)}, f32[1,1024]{1,0:T(1,128)}, u32[]{:S(2)}, u32[]{:S(2)}) collective-permute-start(f32[1,1024]{1,0:T(1,128)} %get-tuple-element.36), channel_id=1, source_target_pairs={{0,1},{2,3},{3,2},{5,8},{6,11},{7,5},{8,9},{10,7},{11,10},{12,13},... | collective-permute-start | bytes 12296 | tf_op jit(solution)/shard_map/ppermute | solution.py:431

commit v18 on v17

--- a/solution.py
+++ b/solution.py
@@ -262,9 +262,10 @@
     )(pad_counts, order.reshape(1, rows), unit)
 
 
-def pairs_kernel(nslots, nrows, ntaken, nloads, npairs, table, best, *refs):
+def pairs_kernel(nslots, nrows, ntaken, nloads, npairs, final, table, best, *refs):
     arrivals, slots, out = refs[:ntaken], refs[ntaken : ntaken + nslots], refs[ntaken + nslots]
-    sent, (held, across, sems) = refs[ntaken + nslots + 1 : -3], refs[-3:]
+    sent, (held, across, total, sems) = refs[ntaken + nslots + 1 : -4], refs[-4:]
+    result, out = out, total if final else out
     rows = out.shape[1]
     here = lax.axis_index("blk")
     loads_at = here * (2 + nrows + ntaken + nloads + 5 * npairs) + 2 + nrows + ntaken
@@ -315,6 +316,8 @@
 
     for index, row in enumerate(sent):
         row[...] = out[pl.ds(table[rows_at + index], 1), :]
+    if final:
+        result[...] = out[own, :]
 
 
 def in_order_of_loads(pairs, rank):
@@ -330,7 +333,7 @@
     return loaded, ordered
 
 
-def scored(best, found, permutes, slots, rank, work, sends):
+def scored(best, found, permutes, slots, rank, work, sends, final):
     names = sorted({slot for pairs in work for pair in pairs for slot in pair[:2]})
     plans = [in_order_of_loads(pairs, rank) for pairs in work]
     nloads = max(len(loaded) for loaded, _ in plans)
@@ -348,8 +351,8 @@
     rows, depth = given[0].shape
     whole = pl.BlockSpec(memory_space=pltpu.VMEM)
     return pl.pallas_call(
-        functools.partial(pairs_kernel, len(given), len(sends), len(found), nloads, npairs),
-        out_shape=[jax.ShapeDtypeStruct(best.shape, jnp.float32)]
+        functools.partial(pairs_kernel, len(given), len(sends), len(found), nloads, npairs, final),
+        out_shape=[jax.ShapeDtypeStruct((1, rows) if final else best.shape, jnp.float32)]
         + [jax.ShapeDtypeStruct((1, rows), jnp.float32)] * len(sends),
         in_specs=[pl.BlockSpec(memory_space=pltpu.SMEM)]
         + [whole] * (1 + len(found))
@@ -358,6 +361,7 @@
         scratch_shapes=[
             pltpu.VMEM((nloads, rows, depth), jnp.bfloat16),
             pltpu.VMEM((rows, 128), jnp.float32),
+            pltpu.VMEM(best.shape if final else (8, 128), jnp.float32),
             pltpu.SemaphoreType.DMA((nloads,)),
         ],
         compiler_params=pltpu.CompilerParams(vmem_limit_bytes=VMEM),
@@ -374,7 +378,7 @@
     found, out = refs[:-1], refs[-1]
     rows = order.shape[1]
     here = lax.axis_index("blk")
-    total = best[pl.ds(here, 1), :]
+    total = best[...]
     for index, row in enumerate(found):
         total = jnp.where(taken[here * len(found) + index] > 0, jnp.maximum(total, row[...]), total)
     column = jnp.broadcast_to(total, (128, rows)).T[:, :1]
@@ -384,9 +388,9 @@
     out[...] = jnp.where(position < rows - pads[here], in_order, 0.0)
 
 
-def placed(best, found, permutes, order, pad_counts):
+def placed(best, found, permutes, order, pad_counts, nblocks):
     rows = order.shape[0]
-    taken = np.zeros((best.shape[0], len(permutes)), np.int32)
+    taken = np.zeros((nblocks, len(permutes)), np.int32)
     for index, permute in enumerate(permutes):
         taken[[to for _, to in permute], index] = 1
     whole, scalars = pl.BlockSpec(memory_space=pltpu.VMEM), pl.BlockSpec(memory_space=pltpu.SMEM)
@@ -427,10 +431,10 @@
             best = own_block(unit, order, pad_counts, nblocks)
         sends = colored(sorted(edges[stage]), nblocks) if stage in sending else []
         if any(pairs):
-            best, *rows = scored(best, found, permutes, slots, rank, pairs, sends)
+            best, *rows = scored(best, found, permutes, slots, rank, pairs, sends, stage == len(work) - 1)
             found = [lax.ppermute(row, "blk", permute) for row, permute in zip(rows, sends)]
             permutes = sends
-    return placed(best, found, permutes, order, pad_counts)
+    return placed(best, found, permutes, order, pad_counts, nblocks)
 
 
 def solution(mesh):

time: 114 us -> 114 us (level)
  no operation moved by 1% of the time
where the time goes in v18:
time: 114 us; the launch traced here: 113 us
  starting transfers between devices  41.7 us (37%)
  Pallas kernels  36.8 us (32%)
  waiting for transfers between devices  34.5 us (30%)
    ppermute x8, starting transfers between devices, local(): slots[move.name] = lax.ppermute(value, 'blk', move.pairs)  27.5 us
    ppermute x8, waiting for transfers between devices, local(): slots[move.name] = lax.ppermute(value, 'blk', move.pairs)  27.3 us
    pallas_call x3, Pallas kernels, scored(): pl.pallas_call(functools.partial(pairs_kernel, len(given), len(sends), le...  25.9 us
    ppermute x6, starting transfers between devices, local(): lax.ppermute(row, 'blk', permute)  14.2 us
    ppermute x6, waiting for transfers between devices, local(): lax.ppermute(row, 'blk', permute)  7.17 us
    pallas_call x1, Pallas kernels, own_block(): pl.pallas_call(own_kernel, out_shape=jax.ShapeDtypeStruct((nblocks, rows)...  4.65 us
    pallas_call x1, Pallas kernels, normalized(): pl.pallas_call(unit_kernel, out_shape=jax.ShapeDtypeStruct((rows, depth),...  4.13 us
  transfers between devices with their start and end apart: 14, of which 4 were waited for; matrix products, arithmetic and copies ran while one was open for 0% of the time, Pallas kernels for 15%

profile of v18, /device:TPU:21, one launch (start us, length us, event | category | flops | bytes accessed | tf_op | source)
XLA Modules:
  0.0 113.1 jit_solution(14746373304264038479)
XLA Ops:
  0.0 4.1 %normalized.1.unit.refs_1_.refs_4_.refs_10_ = bf16[1024,1024]{1,0:T(8,128)(2,1)} custom-call(s32[16]{0:T(128)} %pads.5, s32[1024]{0:T(1024)} %order_smem.1, s32[1,1024]{1,0:T(1,128)} %bitcast.2, bf16[1024,1024]{1,0:T(8,128)(2,1)} %embeddings.1), custom_call_target="tpu_custom_call" | custom-call | flops 4194304 | bytes 4194304 | tf_op jit(solution)/shard_map/normalized/pallas_call | solution.py:205
  4.1 0.7 collective-permute-start.2
  4.9 4.5 %collective-permute-start.1 = (bf16[1024,1024]{1,0:T(8,128)(2,1)}, bf16[1024,1024]{1,0:T(8,128)(2,1)}, u32[]{:S(2)}, u32[]{:S(2)}) collective-permute-start(bf16[1024,1024]{1,0:T(8,128)(2,1)} %normalized.1.unit.refs_1_.refs_4_.refs_10_), channel_id=1, source_target_pairs={{0,9},{8,13},{12,4},{4,0},{1,5},{3,10},{11,14},{15,7},{7,3},{2,6},... | collective-permute-start | bytes 6291464 | tf_op jit(solution)/shard_map/ppermute | solution.py:429
  9.3 2.0 %collective-permute-start.3 = (bf16[1024,1024]{1,0:T(8,128)(2,1)}, bf16[1024,1024]{1,0:T(8,128)(2,1)}, u32[]{:S(2)}, u32[]{:S(2)}) collective-permute-start(bf16[1024,1024]{1,0:T(8,128)(2,1)} %normalized.1.unit.refs_1_.refs_4_.refs_10_), channel_id=1, source_target_pairs={{13,5},{5,1},{9,12},{4,9},{14,6},{6,2},{10,15},{7,10},{29,21},{21,... | collective-permute-start | bytes 6291464 | tf_op jit(solution)/shard_map/ppermute | solution.py:429
  11.3 0.6 collective-permute-start
  11.9 4.6 %own_block.1.best = f32[16,1024]{1,0:T(8,128)} custom-call(s32[16]{0:T(128)} %pads.5, s32[1,1024]{1,0:T(1,128)} %bitcast.3, bf16[1024,1024]{1,0:T(8,128)(2,1)} %normalized.1.unit.refs_1_.refs_4_.refs_10_), custom_call_target="tpu_custom_call" | custom-call | flops 2147483648 | bytes 2097152 | tf_op jit(solution)/shard_map/own_block/pallas_call | solution.py:252
  16.6 6.1 %scored.3.best = f32[16,1024]{1,0:T(8,128)} custom-call(s32[144]{0:T(256)} %constant.8.clone.table, f32[16,1024]{1,0:T(8,128)} %own_block.1.best, bf16[1024,1024]{1,0:T(8,128)(2,1)} %collective-permute-done.2.refs_0_.refs_2_, bf16[1024,1024]{1,0:T(8,128)(2,1)} %normalized.1.unit.refs_1_.refs_4_.refs_10_), custom_call_target="tpu_custom_call" | custom-call | flops 2147483648 | bytes 4194304 | tf_op jit(solution)/shard_map/scored/pallas_call | solution.py:353
  22.7 27.0 %collective-permute-done.1.refs_1_.refs_4_ = bf16[1024,1024]{1,0:T(8,128)(2,1)} collective-permute-done((bf16[1024,1024]{1,0:T(8,128)(2,1)}, bf16[1024,1024]{1,0:T(8,128)(2,1)}, u32[]{:S(2)}, u32[]{:S(2)}) %collective-permute-start.1) | collective-permute-done | bytes 2097184 | tf_op jit(solution)/shard_map/ppermute | solution.py:429
  49.7 7.5 %collective-permute-start.7 = (bf16[1024,1024]{1,0:T(8,128)(2,1)}, bf16[1024,1024]{1,0:T(8,128)(2,1)}, u32[]{:S(2)}, u32[]{:S(2)}) collective-permute-start(bf16[1024,1024]{1,0:T(8,128)(2,1)} %normalized.1.unit.refs_1_.refs_4_.refs_10_), channel_id=1, source_target_pairs={{5,8},{8,5},{6,11},{11,6},{21,24},{24,21},{22,27},{27,22}} | collective-permute-start | bytes 6291464 | tf_op jit(solution)/shard_map/ppermute | solution.py:429
  57.2 2.0 %collective-permute-start.8 = (bf16[1024,1024]{1,0:T(8,128)(2,1)}, bf16[1024,1024]{1,0:T(8,128)(2,1)}, u32[]{:S(2)}, u32[]{:S(2)}) collective-permute-start(bf16[1024,1024]{1,0:T(8,128)(2,1)} %collective-permute-done.1.refs_1_.refs_4_), channel_id=1, source_target_pairs={{9,13},{10,15},{5,6},{6,5},{25,29},{26,31},{21,22},{22,21}} | collective-permute-start | bytes 6291464 | tf_op jit(solution)/shard_map/ppermute | solution.py:429
  59.2 0.3 collective-permute-done.refs_3_.refs_9_
  59.5 6.1 %scored.4 = (f32[16,1024]{1,0:T(8,128)}, f32[1,1024]{1,0:T(1,128)}, f32[1,1024]{1,0:T(1,128)}) custom-call(s32[464]{0:T(512)} %constant.9.clone.table, f32[16,1024]{1,0:T(8,128)} %scored.3.best, bf16[1024,1024]{1,0:T(8,128)(2,1)} %collective-permute-done.2.refs_0_.refs_2_, bf16[1024,1024]{1,0:T(8,128)(2,1)} %collective-permute-done.1.refs_1_.refs_4_, ...), custom_call_target="tpu_custom_call" | custom-call | flops 8589934592 | bytes 10485760 | tf_op jit(solution)/shard_map/scored/pallas_call | solution.py:353
  65.7 8.2 %collective-permute-start.6 = (bf16[1024,1024]{1,0:T(8,128)(2,1)}, bf16[1024,1024]{1,0:T(8,128)(2,1)}, u32[]{:S(2)}, u32[]{:S(2)}) collective-permute-start(bf16[1024,1024]{1,0:T(8,128)(2,1)} %collective-permute-done.refs_3_.refs_9_), channel_id=1, source_target_pairs={{0,1},{1,0},{4,5},{5,4},{8,9},{9,8},{12,13},{13,12},{3,2},{2,3},{7... | collective-permute-start | bytes 6291464 | tf_op jit(solution)/shard_map/ppermute | solution.py:429
  73.9 2.0 %collective-permute-start.9 = (bf16[1024,1024]{1,0:T(8,128)(2,1)}, bf16[1024,1024]{1,0:T(8,128)(2,1)}, u32[]{:S(2)}, u32[]{:S(2)}) collective-permute-start(bf16[1024,1024]{1,0:T(8,128)(2,1)} %collective-permute-done.1.refs_1_.refs_4_), channel_id=1, source_target_pairs={{4,5},{5,4},{7,6},{6,7},{20,21},{21,20},{23,22},{22,23}} | collective-permute-start | bytes 6291464 | tf_op jit(solution)/shard_map/ppermute | solution.py:429
  75.9 1.2 %collective-permute-start.4 = (f32[1,1024]{1,0:T(1,128)}, f32[1,1024]{1,0:T(1,128)}, u32[]{:S(2)}, u32[]{:S(2)}) collective-permute-start(f32[1,1024]{1,0:T(1,128)} %get-tuple-element.26), channel_id=1, source_target_pairs={{0,3},{1,0},{4,6},{5,1},{6,2},{9,4},{10,9},{12,15},{13,8},{14,13},... | collective-permute-start | bytes 12296 | tf_op jit(solution)/shard_map/ppermute | solution.py:435
  77.1 1.3 %collective-permute-start.5 = (f32[1,1024]{1,0:T(1,128)}, f32[1,1024]{1,0:T(1,128)}, u32[]{:S(2)}, u32[]{:S(2)}) collective-permute-start(f32[1,1024]{1,0:T(1,128)} %get-tuple-element.27), channel_id=1, source_target_pairs={{2,1},{4,5},{5,7},{6,4},{7,6},{9,10},{10,11},{18,17},{20,21},{21,2... | collective-permute-start | bytes 12296 | tf_op jit(solution)/shard_map/ppermute | solution.py:435
  78.4 3.9 %collective-permute-done.5.refs_1_ = f32[1,1024]{1,0:T(1,128)} collective-permute-done((f32[1,1024]{1,0:T(1,128)}, f32[1,1024]{1,0:T(1,128)}, u32[]{:S(2)}, u32[]{:S(2)}) %collective-permute-start.5) | collective-permute-done | bytes 4128 | tf_op jit(solution)/shard_map/ppermute | solution.py:435
  82.3 13.6 %scored.5 = (f32[1,1024]{1,0:T(1,128)}, f32[1,1024]{1,0:T(1,128)}, f32[1,1024]{1,0:T(1,128)}, f32[1,1024]{1,0:T(1,128)}, f32[1,1024]{1,0:T(1,128)}) custom-call(s32[528]{0:T(1024)} %constant.10.clone.table, f32[16,1024]{1,0:T(8,128)} %get-tuple-element.25.best, f32[1,1024]{1,0:T(1,128)} %collective-permute-done.4.refs_0_, ...), custom_call_target="tpu_custom_call" | custom-call | flops 8589934592 | bytes 10485760 | tf_op jit(solution)/shard_map/scored/pallas_call | solution.py:353
  95.9 2.0 %collective-permute-start.10 = (f32[1,1024]{1,0:T(1,128)}, f32[1,1024]{1,0:T(1,128)}, u32[]{:S(2)}, u32[]{:S(2)}) collective-permute-start(f32[1,1024]{1,0:T(1,128)} %get-tuple-element.33), channel_id=1, source_target_pairs={{0,4},{1,3},{3,1},{4,7},{5,12},{6,14},{7,2},{8,11},{9,8},{11,6},{1... | collective-permute-start | bytes 12296 | tf_op jit(solution)/shard_map/ppermute | solution.py:435
  98.0 3.5 %collective-permute-start.11 = (f32[1,1024]{1,0:T(1,128)}, f32[1,1024]{1,0:T(1,128)}, u32[]{:S(2)}, u32[]{:S(2)}) collective-permute-start(f32[1,1024]{1,0:T(1,128)} %get-tuple-element.34), channel_id=1, source_target_pairs={{2,6},{4,1},{5,2},{6,15},{7,4},{8,5},{9,0},{10,3},{11,8},{12,14},{... | collective-permute-start | bytes 12296 | tf_op jit(solution)/shard_map/ppermute | solution.py:435
  101.5 4.1 %collective-permute-start.12 = (f32[1,1024]{1,0:T(1,128)}, f32[1,1024]{1,0:T(1,128)}, u32[]{:S(2)}, u32[]{:S(2)}) collective-permute-start(f32[1,1024]{1,0:T(1,128)} %get-tuple-element.35), channel_id=1, source_target_pairs={{0,2},{1,5},{2,0},{3,7},{4,12},{5,13},{6,1},{7,15},{8,10},{9,11},{... | collective-permute-start | bytes 12296 | tf_op jit(solution)/shard_map/ppermute | solution.py:435
  105.7 1.9 %collective-permute-start.13 = (f32[1,1024]{1,0:T(1,128)}, f32[1,1024]{1,0:T(1,128)}, u32[]{:S(2)}, u32[]{:S(2)}) collective-permute-start(f32[1,1024]{1,0:T(1,128)} %get-tuple-element.36), channel_id=1, source_target_pairs={{0,1},{2,3},{3,2},{5,8},{6,11},{7,5},{8,9},{10,7},{11,10},{12,13},... | collective-permute-start | bytes 12296 | tf_op jit(solution)/shard_map/ppermute | solution.py:435
  107.6 3.3 %collective-permute-done.13.refs_3_ = f32[1,1024]{1,0:T(1,128)} collective-permute-done((f32[1,1024]{1,0:T(1,128)}, f32[1,1024]{1,0:T(1,128)}, u32[]{:S(2)}, u32[]{:S(2)}) %collective-permute-start.13) | collective-permute-done | bytes 4128 | tf_op jit(solution)/shard_map/ppermute | solution.py:435
  110.9 2.1 %placed.1 = f32[1,1024]{1,0:T(1,128)} custom-call(s32[64]{0:T(128)} %constant.11.clone.taken, s32[16]{0:T(128)} %pads.5, s32[1,1024]{1,0:T(1,128)} %bitcast.4, f32[1,1024]{1,0:T(1,128)} %get-tuple-element.32.best, f32[1,1024]{1,0:T(1,128)} %collective-permute-done.10.refs_0_, f32[1,1024]{1,0:T(1,128)} %collective-permute-done.11.refs_1_, ...), custom_call_target="tpu_custom_call" | custom-call | tf_op jit(solution)/shard_map/placed/pallas_call | solution.py:397
  (10 shorter events, 0.0 us)
Async XLA Ops:
  4.1 12.4 %collective-permute-start.2 = (bf16[1024,1024]{1,0:T(8,128)(2,1)}, bf16[1024,1024]{1,0:T(8,128)(2,1)}, u32[]{:S(2)}, u32[]{:S(2)}) collective-permute-start(bf16[1024,1024]{1,0:T(8,128)(2,1)} %normalized.1.unit.refs_1_.refs_4_.refs_10_), channel_id=1, source_target_pairs={{0,1},{1,0},{4,5},{5,4},{8,9},{9,8},{12,13},{13,12},{3,2},{2,3},{7... | collective-permute-start | bytes 6291464 | tf_op jit(solution)/shard_map/ppermute | solution.py:429
  4.9 44.8 %collective-permute-start.1 = (bf16[1024,1024]{1,0:T(8,128)(2,1)}, bf16[1024,1024]{1,0:T(8,128)(2,1)}, u32[]{:S(2)}, u32[]{:S(2)}) collective-permute-start(bf16[1024,1024]{1,0:T(8,128)(2,1)} %normalized.1.unit.refs_1_.refs_4_.refs_10_), channel_id=1, source_target_pairs={{0,9},{8,13},{12,4},{4,0},{1,5},{3,10},{11,14},{15,7},{7,3},{2,6},... | collective-permute-start | bytes 6291464 | tf_op jit(solution)/shard_map/ppermute | solution.py:429
  9.3 49.9 %collective-permute-start.3 = (bf16[1024,1024]{1,0:T(8,128)(2,1)}, bf16[1024,1024]{1,0:T(8,128)(2,1)}, u32[]{:S(2)}, u32[]{:S(2)}) collective-permute-start(bf16[1024,1024]{1,0:T(8,128)(2,1)} %normalized.1.unit.refs_1_.refs_4_.refs_10_), channel_id=1, source_target_pairs={{13,5},{5,1},{9,12},{4,9},{14,6},{6,2},{10,15},{7,10},{29,21},{21,... | collective-permute-start | bytes 6291464 | tf_op jit(solution)/shard_map/ppermute | solution.py:429
  11.3 48.2 %collective-permute-start = (bf16[1024,1024]{1,0:T(8,128)(2,1)}, bf16[1024,1024]{1,0:T(8,128)(2,1)}, u32[]{:S(2)}, u32[]{:S(2)}) collective-permute-start(bf16[1024,1024]{1,0:T(8,128)(2,1)} %normalized.1.unit.refs_1_.refs_4_.refs_10_), channel_id=1, source_target_pairs={{0,3},{3,0},{1,2},{2,1},{8,11},{11,8},{9,10},{10,9},{12,15},{15,12... | collective-permute-start | bytes 6291464 | tf_op jit(solution)/shard_map/ppermute | solution.py:429
  49.7 32.6 %collective-permute-start.7 = (bf16[1024,1024]{1,0:T(8,128)(2,1)}, bf16[1024,1024]{1,0:T(8,128)(2,1)}, u32[]{:S(2)}, u32[]{:S(2)}) collective-permute-start(bf16[1024,1024]{1,0:T(8,128)(2,1)} %normalized.1.unit.refs_1_.refs_4_.refs_10_), channel_id=1, source_target_pairs={{5,8},{8,5},{6,11},{11,6},{21,24},{24,21},{22,27},{27,22}} | collective-permute-start | bytes 6291464 | tf_op jit(solution)/shard_map/ppermute | solution.py:429
  57.2 25.1 %collective-permute-start.8 = (bf16[1024,1024]{1,0:T(8,128)(2,1)}, bf16[1024,1024]{1,0:T(8,128)(2,1)}, u32[]{:S(2)}, u32[]{:S(2)}) collective-permute-start(bf16[1024,1024]{1,0:T(8,128)(2,1)} %collective-permute-done.1.refs_1_.refs_4_), channel_id=1, source_target_pairs={{9,13},{10,15},{5,6},{6,5},{25,29},{26,31},{21,22},{22,21}} | collective-permute-start | bytes 6291464 | tf_op jit(solution)/shard_map/ppermute | solution.py:429
  65.7 16.6 %collective-permute-start.6 = (bf16[1024,1024]{1,0:T(8,128)(2,1)}, bf16[1024,1024]{1,0:T(8,128)(2,1)}, u32[]{:S(2)}, u32[]{:S(2)}) collective-permute-start(bf16[1024,1024]{1,0:T(8,128)(2,1)} %collective-permute-done.refs_3_.refs_9_), channel_id=1, source_target_pairs={{0,1},{1,0},{4,5},{5,4},{8,9},{9,8},{12,13},{13,12},{3,2},{2,3},{7... | collective-permute-start | bytes 6291464 | tf_op jit(solution)/shard_map/ppermute | solution.py:429
  73.9 8.4 %collective-permute-start.9 = (bf16[1024,1024]{1,0:T(8,128)(2,1)}, bf16[1024,1024]{1,0:T(8,128)(2,1)}, u32[]{:S(2)}, u32[]{:S(2)}) collective-permute-start(bf16[1024,1024]{1,0:T(8,128)(2,1)} %collective-permute-done.1.refs_1_.refs_4_), channel_id=1, source_target_pairs={{4,5},{5,4},{7,6},{6,7},{20,21},{21,20},{23,22},{22,23}} | collective-permute-start | bytes 6291464 | tf_op jit(solution)/shard_map/ppermute | solution.py:429
  75.9 1.2 %collective-permute-start.4 = (f32[1,1024]{1,0:T(1,128)}, f32[1,1024]{1,0:T(1,128)}, u32[]{:S(2)}, u32[]{:S(2)}) collective-permute-start(f32[1,1024]{1,0:T(1,128)} %get-tuple-element.26), channel_id=1, source_target_pairs={{0,3},{1,0},{4,6},{5,1},{6,2},{9,4},{10,9},{12,15},{13,8},{14,13},... | collective-permute-start | bytes 12296 | tf_op jit(solution)/shard_map/ppermute | solution.py:435
  77.1 5.2 %collective-permute-start.5 = (f32[1,1024]{1,0:T(1,128)}, f32[1,1024]{1,0:T(1,128)}, u32[]{:S(2)}, u32[]{:S(2)}) collective-permute-start(f32[1,1024]{1,0:T(1,128)} %get-tuple-element.27), channel_id=1, source_target_pairs={{2,1},{4,5},{5,7},{6,4},{7,6},{9,10},{10,11},{18,17},{20,21},{21,2... | collective-permute-start | bytes 12296 | tf_op jit(solution)/shard_map/ppermute | solution.py:435
  95.9 11.7 %collective-permute-start.10 = (f32[1,1024]{1,0:T(1,128)}, f32[1,1024]{1,0:T(1,128)}, u32[]{:S(2)}, u32[]{:S(2)}) collective-permute-start(f32[1,1024]{1,0:T(1,128)} %get-tuple-element.33), channel_id=1, source_target_pairs={{0,4},{1,3},{3,1},{4,7},{5,12},{6,14},{7,2},{8,11},{9,8},{11,6},{1... | collective-permute-start | bytes 12296 | tf_op jit(solution)/shard_map/ppermute | solution.py:435
  98.0 9.7 %collective-permute-start.11 = (f32[1,1024]{1,0:T(1,128)}, f32[1,1024]{1,0:T(1,128)}, u32[]{:S(2)}, u32[]{:S(2)}) collective-permute-start(f32[1,1024]{1,0:T(1,128)} %get-tuple-element.34), channel_id=1, source_target_pairs={{2,6},{4,1},{5,2},{6,15},{7,4},{8,5},{9,0},{10,3},{11,8},{12,14},{... | collective-permute-start | bytes 12296 | tf_op jit(solution)/shard_map/ppermute | solution.py:435
  101.5 6.1 %collective-permute-start.12 = (f32[1,1024]{1,0:T(1,128)}, f32[1,1024]{1,0:T(1,128)}, u32[]{:S(2)}, u32[]{:S(2)}) collective-permute-start(f32[1,1024]{1,0:T(1,128)} %get-tuple-element.35), channel_id=1, source_target_pairs={{0,2},{1,5},{2,0},{3,7},{4,12},{5,13},{6,1},{7,15},{8,10},{9,11},{... | collective-permute-start | bytes 12296 | tf_op jit(solution)/shard_map/ppermute | solution.py:435
  105.7 5.2 %collective-permute-start.13 = (f32[1,1024]{1,0:T(1,128)}, f32[1,1024]{1,0:T(1,128)}, u32[]{:S(2)}, u32[]{:S(2)}) collective-permute-start(f32[1,1024]{1,0:T(1,128)} %get-tuple-element.36), channel_id=1, source_target_pairs={{0,1},{2,3},{3,2},{5,8},{6,11},{7,5},{8,9},{10,7},{11,10},{12,13},... | collective-permute-start | bytes 12296 | tf_op jit(solution)/shard_map/ppermute | solution.py:435

commit v19 on v18

--- a/solution.py
+++ b/solution.py
@@ -200,7 +200,7 @@
 
 def normalized(embeddings, order, pad_counts):
     rows, depth = embeddings.shape
-    chunks = 4
+    chunks = 2
     scalars = pl.BlockSpec(memory_space=pltpu.SMEM)
     return pl.pallas_call(
         unit_kernel,

time: 114 us -> 114 us (level)
  no operation moved by 1% of the time
where the time goes in v19:
time: 114 us; the launch traced here: 113 us
  starting transfers between devices  41.7 us (37%)
  Pallas kernels  36.9 us (32%)
  waiting for transfers between devices  34.5 us (30%)
    ppermute x8, starting transfers between devices, local(): slots[move.name] = lax.ppermute(value, 'blk', move.pairs)  27.5 us
    ppermute x8, waiting for transfers between devices, local(): slots[move.name] = lax.ppermute(value, 'blk', move.pairs)  27.3 us
    pallas_call x3, Pallas kernels, scored(): pl.pallas_call(functools.partial(pairs_kernel, len(given), len(sends), le...  25.9 us
    ppermute x6, starting transfers between devices, local(): lax.ppermute(row, 'blk', permute)  14.2 us
    ppermute x6, waiting for transfers between devices, local(): lax.ppermute(row, 'blk', permute)  7.17 us
    pallas_call x1, Pallas kernels, own_block(): pl.pallas_call(own_kernel, out_shape=jax.ShapeDtypeStruct((nblocks, rows)...  4.65 us
    pallas_call x1, Pallas kernels, normalized(): pl.pallas_call(unit_kernel, out_shape=jax.ShapeDtypeStruct((rows, depth),...  4.26 us
  transfers between devices with their start and end apart: 14, of which 4 were waited for; matrix products, arithmetic and copies ran while one was open for 0% of the time, Pallas kernels for 15%

profile of v19, /device:TPU:21, one launch (start us, length us, event | category | flops | bytes accessed | tf_op | source)
XLA Modules:
  0.0 113.2 jit_solution(14136819908247644149)
XLA Ops:
  0.0 4.3 %normalized.1.unit.refs_1_.refs_4_.refs_10_ = bf16[1024,1024]{1,0:T(8,128)(2,1)} custom-call(s32[16]{0:T(128)} %pads.5, s32[1024]{0:T(1024)} %order_smem.1, s32[1,1024]{1,0:T(1,128)} %bitcast.2, bf16[1024,1024]{1,0:T(8,128)(2,1)} %embeddings.1), custom_call_target="tpu_custom_call" | custom-call | flops 4194304 | bytes 4194304 | tf_op jit(solution)/shard_map/normalized/pallas_call | solution.py:205
  4.3 0.7 collective-permute-start.2
  5.0 4.5 %collective-permute-start.1 = (bf16[1024,1024]{1,0:T(8,128)(2,1)}, bf16[1024,1024]{1,0:T(8,128)(2,1)}, u32[]{:S(2)}, u32[]{:S(2)}) collective-permute-start(bf16[1024,1024]{1,0:T(8,128)(2,1)} %normalized.1.unit.refs_1_.refs_4_.refs_10_), channel_id=1, source_target_pairs={{0,9},{8,13},{12,4},{4,0},{1,5},{3,10},{11,14},{15,7},{7,3},{2,6},... | collective-permute-start | bytes 6291464 | tf_op jit(solution)/shard_map/ppermute | solution.py:429
  9.5 2.0 %collective-permute-start.3 = (bf16[1024,1024]{1,0:T(8,128)(2,1)}, bf16[1024,1024]{1,0:T(8,128)(2,1)}, u32[]{:S(2)}, u32[]{:S(2)}) collective-permute-start(bf16[1024,1024]{1,0:T(8,128)(2,1)} %normalized.1.unit.refs_1_.refs_4_.refs_10_), channel_id=1, source_target_pairs={{13,5},{5,1},{9,12},{4,9},{14,6},{6,2},{10,15},{7,10},{29,21},{21,... | collective-permute-start | bytes 6291464 | tf_op jit(solution)/shard_map/ppermute | solution.py:429
  11.5 0.6 collective-permute-start
  12.0 4.6 %own_block.1.best = f32[16,1024]{1,0:T(8,128)} custom-call(s32[16]{0:T(128)} %pads.5, s32[1,1024]{1,0:T(1,128)} %bitcast.3, bf16[1024,1024]{1,0:T(8,128)(2,1)} %normalized.1.unit.refs_1_.refs_4_.refs_10_), custom_call_target="tpu_custom_call" | custom-call | flops 2147483648 | bytes 2097152 | tf_op jit(solution)/shard_map/own_block/pallas_call | solution.py:252
  16.7 6.1 %scored.3.best = f32[16,1024]{1,0:T(8,128)} custom-call(s32[144]{0:T(256)} %constant.8.clone.table, f32[16,1024]{1,0:T(8,128)} %own_block.1.best, bf16[1024,1024]{1,0:T(8,128)(2,1)} %collective-permute-done.2.refs_0_.refs_2_, bf16[1024,1024]{1,0:T(8,128)(2,1)} %normalized.1.unit.refs_1_.refs_4_.refs_10_), custom_call_target="tpu_custom_call" | custom-call | flops 2147483648 | bytes 4194304 | tf_op jit(solution)/shard_map/scored/pallas_call | solution.py:353
  22.8 27.0 %collective-permute-done.1.refs_1_.refs_4_ = bf16[1024,1024]{1,0:T(8,128)(2,1)} collective-permute-done((bf16[1024,1024]{1,0:T(8,128)(2,1)}, bf16[1024,1024]{1,0:T(8,128)(2,1)}, u32[]{:S(2)}, u32[]{:S(2)}) %collective-permute-start.1) | collective-permute-done | bytes 2097184 | tf_op jit(solution)/shard_map/ppermute | solution.py:429
  49.8 7.5 %collective-permute-start.7 = (bf16[1024,1024]{1,0:T(8,128)(2,1)}, bf16[1024,1024]{1,0:T(8,128)(2,1)}, u32[]{:S(2)}, u32[]{:S(2)}) collective-permute-start(bf16[1024,1024]{1,0:T(8,128)(2,1)} %normalized.1.unit.refs_1_.refs_4_.refs_10_), channel_id=1, source_target_pairs={{5,8},{8,5},{6,11},{11,6},{21,24},{24,21},{22,27},{27,22}} | collective-permute-start | bytes 6291464 | tf_op jit(solution)/shard_map/ppermute | solution.py:429
  57.3 2.0 %collective-permute-start.8 = (bf16[1024,1024]{1,0:T(8,128)(2,1)}, bf16[1024,1024]{1,0:T(8,128)(2,1)}, u32[]{:S(2)}, u32[]{:S(2)}) collective-permute-start(bf16[1024,1024]{1,0:T(8,128)(2,1)} %collective-permute-done.1.refs_1_.refs_4_), channel_id=1, source_target_pairs={{9,13},{10,15},{5,6},{6,5},{25,29},{26,31},{21,22},{22,21}} | collective-permute-start | bytes 6291464 | tf_op jit(solution)/shard_map/ppermute | solution.py:429
  59.4 0.3 collective-permute-done.refs_3_.refs_9_
  59.6 6.1 %scored.4 = (f32[16,1024]{1,0:T(8,128)}, f32[1,1024]{1,0:T(1,128)}, f32[1,1024]{1,0:T(1,128)}) custom-call(s32[464]{0:T(512)} %constant.9.clone.table, f32[16,1024]{1,0:T(8,128)} %scored.3.best, bf16[1024,1024]{1,0:T(8,128)(2,1)} %collective-permute-done.2.refs_0_.refs_2_, bf16[1024,1024]{1,0:T(8,128)(2,1)} %collective-permute-done.1.refs_1_.refs_4_, ...), custom_call_target="tpu_custom_call" | custom-call | flops 8589934592 | bytes 10485760 | tf_op jit(solution)/shard_map/scored/pallas_call | solution.py:353
  65.8 8.2 %collective-permute-start.6 = (bf16[1024,1024]{1,0:T(8,128)(2,1)}, bf16[1024,1024]{1,0:T(8,128)(2,1)}, u32[]{:S(2)}, u32[]{:S(2)}) collective-permute-start(bf16[1024,1024]{1,0:T(8,128)(2,1)} %collective-permute-done.refs_3_.refs_9_), channel_id=1, source_target_pairs={{0,1},{1,0},{4,5},{5,4},{8,9},{9,8},{12,13},{13,12},{3,2},{2,3},{7... | collective-permute-start | bytes 6291464 | tf_op jit(solution)/shard_map/ppermute | solution.py:429
  74.0 2.0 %collective-permute-start.9 = (bf16[1024,1024]{1,0:T(8,128)(2,1)}, bf16[1024,1024]{1,0:T(8,128)(2,1)}, u32[]{:S(2)}, u32[]{:S(2)}) collective-permute-start(bf16[1024,1024]{1,0:T(8,128)(2,1)} %collective-permute-done.1.refs_1_.refs_4_), channel_id=1, source_target_pairs={{4,5},{5,4},{7,6},{6,7},{20,21},{21,20},{23,22},{22,23}} | collective-permute-start | bytes 6291464 | tf_op jit(solution)/shard_map/ppermute | solution.py:429
  76.0 1.2 %collective-permute-start.4 = (f32[1,1024]{1,0:T(1,128)}, f32[1,1024]{1,0:T(1,128)}, u32[]{:S(2)}, u32[]{:S(2)}) collective-permute-start(f32[1,1024]{1,0:T(1,128)} %get-tuple-element.26), channel_id=1, source_target_pairs={{0,3},{1,0},{4,6},{5,1},{6,2},{9,4},{10,9},{12,15},{13,8},{14,13},... | collective-permute-start | bytes 12296 | tf_op jit(solution)/shard_map/ppermute | solution.py:435
  77.3 1.3 %collective-permute-start.5 = (f32[1,1024]{1,0:T(1,128)}, f32[1,1024]{1,0:T(1,128)}, u32[]{:S(2)}, u32[]{:S(2)}) collective-permute-start(f32[1,1024]{1,0:T(1,128)} %get-tuple-element.27), channel_id=1, source_target_pairs={{2,1},{4,5},{5,7},{6,4},{7,6},{9,10},{10,11},{18,17},{20,21},{21,2... | collective-permute-start | bytes 12296 | tf_op jit(solution)/shard_map/ppermute | solution.py:435
  78.5 3.9 %collective-permute-done.5.refs_1_ = f32[1,1024]{1,0:T(1,128)} collective-permute-done((f32[1,1024]{1,0:T(1,128)}, f32[1,1024]{1,0:T(1,128)}, u32[]{:S(2)}, u32[]{:S(2)}) %collective-permute-start.5) | collective-permute-done | bytes 4128 | tf_op jit(solution)/shard_map/ppermute | solution.py:435
  82.4 13.6 %scored.5 = (f32[1,1024]{1,0:T(1,128)}, f32[1,1024]{1,0:T(1,128)}, f32[1,1024]{1,0:T(1,128)}, f32[1,1024]{1,0:T(1,128)}, f32[1,1024]{1,0:T(1,128)}) custom-call(s32[528]{0:T(1024)} %constant.10.clone.table, f32[16,1024]{1,0:T(8,128)} %get-tuple-element.25.best, f32[1,1024]{1,0:T(1,128)} %collective-permute-done.4.refs_0_, ...), custom_call_target="tpu_custom_call" | custom-call | flops 8589934592 | bytes 10485760 | tf_op jit(solution)/shard_map/scored/pallas_call | solution.py:353
  96.1 2.0 %collective-permute-start.10 = (f32[1,1024]{1,0:T(1,128)}, f32[1,1024]{1,0:T(1,128)}, u32[]{:S(2)}, u32[]{:S(2)}) collective-permute-start(f32[1,1024]{1,0:T(1,128)} %get-tuple-element.33), channel_id=1, source_target_pairs={{0,4},{1,3},{3,1},{4,7},{5,12},{6,14},{7,2},{8,11},{9,8},{11,6},{1... | collective-permute-start | bytes 12296 | tf_op jit(solution)/shard_map/ppermute | solution.py:435
  98.1 3.5 %collective-permute-start.11 = (f32[1,1024]{1,0:T(1,128)}, f32[1,1024]{1,0:T(1,128)}, u32[]{:S(2)}, u32[]{:S(2)}) collective-permute-start(f32[1,1024]{1,0:T(1,128)} %get-tuple-element.34), channel_id=1, source_target_pairs={{2,6},{4,1},{5,2},{6,15},{7,4},{8,5},{9,0},{10,3},{11,8},{12,14},{... | collective-permute-start | bytes 12296 | tf_op jit(solution)/shard_map/ppermute | solution.py:435
  101.7 4.1 %collective-permute-start.12 = (f32[1,1024]{1,0:T(1,128)}, f32[1,1024]{1,0:T(1,128)}, u32[]{:S(2)}, u32[]{:S(2)}) collective-permute-start(f32[1,1024]{1,0:T(1,128)} %get-tuple-element.35), channel_id=1, source_target_pairs={{0,2},{1,5},{2,0},{3,7},{4,12},{5,13},{6,1},{7,15},{8,10},{9,11},{... | collective-permute-start | bytes 12296 | tf_op jit(solution)/shard_map/ppermute | solution.py:435
  105.8 1.9 %collective-permute-start.13 = (f32[1,1024]{1,0:T(1,128)}, f32[1,1024]{1,0:T(1,128)}, u32[]{:S(2)}, u32[]{:S(2)}) collective-permute-start(f32[1,1024]{1,0:T(1,128)} %get-tuple-element.36), channel_id=1, source_target_pairs={{0,1},{2,3},{3,2},{5,8},{6,11},{7,5},{8,9},{10,7},{11,10},{12,13},... | collective-permute-start | bytes 12296 | tf_op jit(solution)/shard_map/ppermute | solution.py:435
  107.8 3.3 %collective-permute-done.13.refs_3_ = f32[1,1024]{1,0:T(1,128)} collective-permute-done((f32[1,1024]{1,0:T(1,128)}, f32[1,1024]{1,0:T(1,128)}, u32[]{:S(2)}, u32[]{:S(2)}) %collective-permute-start.13) | collective-permute-done | bytes 4128 | tf_op jit(solution)/shard_map/ppermute | solution.py:435
  111.1 2.1 %placed.1 = f32[1,1024]{1,0:T(1,128)} custom-call(s32[64]{0:T(128)} %constant.11.clone.taken, s32[16]{0:T(128)} %pads.5, s32[1,1024]{1,0:T(1,128)} %bitcast.4, f32[1,1024]{1,0:T(1,128)} %get-tuple-element.32.best, f32[1,1024]{1,0:T(1,128)} %collective-permute-done.10.refs_0_, f32[1,1024]{1,0:T(1,128)} %collective-permute-done.11.refs_1_, ...), custom_call_target="tpu_custom_call" | custom-call | tf_op jit(solution)/shard_map/placed/pallas_call | solution.py:397
  (10 shorter events, 0.0 us)
Async XLA Ops:
  4.3 12.4 %collective-permute-start.2 = (bf16[1024,1024]{1,0:T(8,128)(2,1)}, bf16[1024,1024]{1,0:T(8,128)(2,1)}, u32[]{:S(2)}, u32[]{:S(2)}) collective-permute-start(bf16[1024,1024]{1,0:T(8,128)(2,1)} %normalized.1.unit.refs_1_.refs_4_.refs_10_), channel_id=1, source_target_pairs={{0,1},{1,0},{4,5},{5,4},{8,9},{9,8},{12,13},{13,12},{3,2},{2,3},{7... | collective-permute-start | bytes 6291464 | tf_op jit(solution)/shard_map/ppermute | solution.py:429
  5.0 44.8 %collective-permute-start.1 = (bf16[1024,1024]{1,0:T(8,128)(2,1)}, bf16[1024,1024]{1,0:T(8,128)(2,1)}, u32[]{:S(2)}, u32[]{:S(2)}) collective-permute-start(bf16[1024,1024]{1,0:T(8,128)(2,1)} %normalized.1.unit.refs_1_.refs_4_.refs_10_), channel_id=1, source_target_pairs={{0,9},{8,13},{12,4},{4,0},{1,5},{3,10},{11,14},{15,7},{7,3},{2,6},... | collective-permute-start | bytes 6291464 | tf_op jit(solution)/shard_map/ppermute | solution.py:429
  9.5 49.9 %collective-permute-start.3 = (bf16[1024,1024]{1,0:T(8,128)(2,1)}, bf16[1024,1024]{1,0:T(8,128)(2,1)}, u32[]{:S(2)}, u32[]{:S(2)}) collective-permute-start(bf16[1024,1024]{1,0:T(8,128)(2,1)} %normalized.1.unit.refs_1_.refs_4_.refs_10_), channel_id=1, source_target_pairs={{13,5},{5,1},{9,12},{4,9},{14,6},{6,2},{10,15},{7,10},{29,21},{21,... | collective-permute-start | bytes 6291464 | tf_op jit(solution)/shard_map/ppermute | solution.py:429
  11.5 48.2 %collective-permute-start = (bf16[1024,1024]{1,0:T(8,128)(2,1)}, bf16[1024,1024]{1,0:T(8,128)(2,1)}, u32[]{:S(2)}, u32[]{:S(2)}) collective-permute-start(bf16[1024,1024]{1,0:T(8,128)(2,1)} %normalized.1.unit.refs_1_.refs_4_.refs_10_), channel_id=1, source_target_pairs={{0,3},{3,0},{1,2},{2,1},{8,11},{11,8},{9,10},{10,9},{12,15},{15,12... | collective-permute-start | bytes 6291464 | tf_op jit(solution)/shard_map/ppermute | solution.py:429
  49.8 32.6 %collective-permute-start.7 = (bf16[1024,1024]{1,0:T(8,128)(2,1)}, bf16[1024,1024]{1,0:T(8,128)(2,1)}, u32[]{:S(2)}, u32[]{:S(2)}) collective-permute-start(bf16[1024,1024]{1,0:T(8,128)(2,1)} %normalized.1.unit.refs_1_.refs_4_.refs_10_), channel_id=1, source_target_pairs={{5,8},{8,5},{6,11},{11,6},{21,24},{24,21},{22,27},{27,22}} | collective-permute-start | bytes 6291464 | tf_op jit(solution)/shard_map/ppermute | solution.py:429
  57.3 25.1 %collective-permute-start.8 = (bf16[1024,1024]{1,0:T(8,128)(2,1)}, bf16[1024,1024]{1,0:T(8,128)(2,1)}, u32[]{:S(2)}, u32[]{:S(2)}) collective-permute-start(bf16[1024,1024]{1,0:T(8,128)(2,1)} %collective-permute-done.1.refs_1_.refs_4_), channel_id=1, source_target_pairs={{9,13},{10,15},{5,6},{6,5},{25,29},{26,31},{21,22},{22,21}} | collective-permute-start | bytes 6291464 | tf_op jit(solution)/shard_map/ppermute | solution.py:429
  65.8 16.6 %collective-permute-start.6 = (bf16[1024,1024]{1,0:T(8,128)(2,1)}, bf16[1024,1024]{1,0:T(8,128)(2,1)}, u32[]{:S(2)}, u32[]{:S(2)}) collective-permute-start(bf16[1024,1024]{1,0:T(8,128)(2,1)} %collective-permute-done.refs_3_.refs_9_), channel_id=1, source_target_pairs={{0,1},{1,0},{4,5},{5,4},{8,9},{9,8},{12,13},{13,12},{3,2},{2,3},{7... | collective-permute-start | bytes 6291464 | tf_op jit(solution)/shard_map/ppermute | solution.py:429
  74.0 8.4 %collective-permute-start.9 = (bf16[1024,1024]{1,0:T(8,128)(2,1)}, bf16[1024,1024]{1,0:T(8,128)(2,1)}, u32[]{:S(2)}, u32[]{:S(2)}) collective-permute-start(bf16[1024,1024]{1,0:T(8,128)(2,1)} %collective-permute-done.1.refs_1_.refs_4_), channel_id=1, source_target_pairs={{4,5},{5,4},{7,6},{6,7},{20,21},{21,20},{23,22},{22,23}} | collective-permute-start | bytes 6291464 | tf_op jit(solution)/shard_map/ppermute | solution.py:429
  76.0 1.2 %collective-permute-start.4 = (f32[1,1024]{1,0:T(1,128)}, f32[1,1024]{1,0:T(1,128)}, u32[]{:S(2)}, u32[]{:S(2)}) collective-permute-start(f32[1,1024]{1,0:T(1,128)} %get-tuple-element.26), channel_id=1, source_target_pairs={{0,3},{1,0},{4,6},{5,1},{6,2},{9,4},{10,9},{12,15},{13,8},{14,13},... | collective-permute-start | bytes 12296 | tf_op jit(solution)/shard_map/ppermute | solution.py:435
  77.3 5.2 %collective-permute-start.5 = (f32[1,1024]{1,0:T(1,128)}, f32[1,1024]{1,0:T(1,128)}, u32[]{:S(2)}, u32[]{:S(2)}) collective-permute-start(f32[1,1024]{1,0:T(1,128)} %get-tuple-element.27), channel_id=1, source_target_pairs={{2,1},{4,5},{5,7},{6,4},{7,6},{9,10},{10,11},{18,17},{20,21},{21,2... | collective-permute-start | bytes 12296 | tf_op jit(solution)/shard_map/ppermute | solution.py:435
  96.1 11.7 %collective-permute-start.10 = (f32[1,1024]{1,0:T(1,128)}, f32[1,1024]{1,0:T(1,128)}, u32[]{:S(2)}, u32[]{:S(2)}) collective-permute-start(f32[1,1024]{1,0:T(1,128)} %get-tuple-element.33), channel_id=1, source_target_pairs={{0,4},{1,3},{3,1},{4,7},{5,12},{6,14},{7,2},{8,11},{9,8},{11,6},{1... | collective-permute-start | bytes 12296 | tf_op jit(solution)/shard_map/ppermute | solution.py:435
  98.1 9.6 %collective-permute-start.11 = (f32[1,1024]{1,0:T(1,128)}, f32[1,1024]{1,0:T(1,128)}, u32[]{:S(2)}, u32[]{:S(2)}) collective-permute-start(f32[1,1024]{1,0:T(1,128)} %get-tuple-element.34), channel_id=1, source_target_pairs={{2,6},{4,1},{5,2},{6,15},{7,4},{8,5},{9,0},{10,3},{11,8},{12,14},{... | collective-permute-start | bytes 12296 | tf_op jit(solution)/shard_map/ppermute | solution.py:435
  101.7 6.1 %collective-permute-start.12 = (f32[1,1024]{1,0:T(1,128)}, f32[1,1024]{1,0:T(1,128)}, u32[]{:S(2)}, u32[]{:S(2)}) collective-permute-start(f32[1,1024]{1,0:T(1,128)} %get-tuple-element.35), channel_id=1, source_target_pairs={{0,2},{1,5},{2,0},{3,7},{4,12},{5,13},{6,1},{7,15},{8,10},{9,11},{... | collective-permute-start | bytes 12296 | tf_op jit(solution)/shard_map/ppermute | solution.py:435
  105.8 5.2 %collective-permute-start.13 = (f32[1,1024]{1,0:T(1,128)}, f32[1,1024]{1,0:T(1,128)}, u32[]{:S(2)}, u32[]{:S(2)}) collective-permute-start(f32[1,1024]{1,0:T(1,128)} %get-tuple-element.36), channel_id=1, source_target_pairs={{0,1},{2,3},{3,2},{5,8},{6,11},{7,5},{8,9},{10,7},{11,10},{12,13},... | collective-permute-start | bytes 12296 | tf_op jit(solution)/shard_map/ppermute | solution.py:435
